TPU v7x, 32 devices: a whole 2x2x4 slice. The times are simulated.
32 devices in a mesh: row: 4 (over y, x), col: 8 (over z, core).
Axes of the slice: x: 2, y: 2, z: 4, core: 2. Of those that a mesh axis runs over, the one named last changes fastest.
Arguments:
- amplitudes: float32 [8, 8, 256, 256], P('row', 'col'), may hold values from -6 to 6
- coulomb: bfloat16 [8, 8, 256, 256], P('row'), may hold values from -6 to 6
- inner_list: int32 [8, 8, 8], P('row', 'col'), may hold values from 0 to 7, as said below
- inner_count: int32 [8, 8], P('row', 'col'), may hold values from 4 to 8
- reader_list: int32 [8, 8, 8], P('row'), may hold values from 0 to 7, as said below
- reader_count: int32 [8, 8], P('row'), may hold values from 4 to 8
- virtual_energy: float32 [256], replicated, may hold values from 0.5 to 2.5
- occupied_energy: float32 [8], replicated, may hold values from -1.5 to -0.3
Outputs:
- new_amplitudes: float32 [8, 8, 256, 256], P('row', 'col')
Inputs may be any that keep to these rules, and one draw needn't show every extreme that they name: `inner_list`: for each pair block the 8 entries are distinct orbitals; only the first inner_count of them are used. `reader_list`: for each pair block the 8 entries are distinct orbitals; only the first reader_count of them are used.
All inputs are finite; a program needn't handle non-finite values.
Results may differ from a plain program's by a relative error of at most 0.0015.
Values may be sent and summed in bfloat16 or wider, within the bound.
No kernel may reach another device: no remote copies, remote signals or barrier semaphores. Data moves between devices by JAX's collectives and lax.ppermute only.
A program may use at most 64 MiB of HBM per device.

v0:
```python
import functools

import jax
import jax.numpy as jnp
from jax import lax
from jax.experimental import pallas as pl
from jax.experimental.pallas import tpu as pltpu
from jax.sharding import PartitionSpec as P

ITERS = 2


damping = 0.5
coupling = 0.03125
ANY = pl.BlockSpec(memory_space=pl.ANY)
SMEM = pl.BlockSpec(memory_space=pltpu.SMEM)
VMEM = pl.BlockSpec(memory_space=pltpu.VMEM)
VMEM_BYTES = 32 * 1024 * 1024


def call(body, out_shape, in_specs, flops, moved, *operands):
    single = isinstance(out_shape, jax.ShapeDtypeStruct)
    return pl.pallas_call(
        body,
        out_shape=out_shape,
        in_specs=in_specs,
        out_specs=VMEM if single else (VMEM,) * len(out_shape),
        compiler_params=pltpu.CompilerParams(vmem_limit_bytes=VMEM_BYTES),
        cost_estimate=pl.CostEstimate(flops=flops, bytes_accessed=moved, transcendentals=0),
    )(*operands)


def prologue_body(meta, occupied, k_ref, virt_row, virt_col, kept_ref, own_ref, inverse_ref):
    orb_rows, _, virt, _ = k_ref.shape
    my_row = meta[2 * orb_rows, 0]
    my_col = meta[2 * orb_rows, 1]
    for step in range(kept_ref.shape[0]):
        for t in range(orb_rows):
            orbital = (my_row ^ step) * orb_rows + t
            for i in range(orb_rows):
                block = k_ref[i, orbital]
                keep = jnp.where(meta[i, orbital] > 0, block, jnp.zeros_like(block))
                kept_ref[step, i * virt : (i + 1) * virt, t * virt : (t + 1) * virt] = keep
    virt_pair = virt_col[...] + virt_row[...]
    for i in range(orb_rows):
        own_ref[i] = k_ref[i, my_col]
        inverse_ref[i] = 1.0 / (virt_pair - occupied[0, my_row * orb_rows + i] - occupied[0, my_col])


def prologue(rows, meta, coulomb, virtual_energy, occupied_energy):
    orb_rows, count, virt, _ = coulomb.shape
    shape = (
        jax.ShapeDtypeStruct((rows, orb_rows * virt, orb_rows * virt), jnp.bfloat16),
        jax.ShapeDtypeStruct((orb_rows, virt, virt), jnp.bfloat16),
        jax.ShapeDtypeStruct((orb_rows, virt, virt), jnp.float32),
    )
    return call(
        prologue_body, shape, [SMEM, SMEM, VMEM, VMEM, VMEM], 0, 4 * orb_rows * count * virt**2,
        meta, occupied_energy[None], coulomb, virtual_energy[None], virtual_energy[:, None],
    )


def piece_blocks(refs, rows):
    found, refs, size = [], list(refs), refs[0].shape[0]
    for step in range(rows):
        blocks = []
        while len(blocks) < size:
            ref = refs.pop(0)
            blocks += [(ref, at) for at in range(ref.shape[0])]
        found.append(blocks)
    return found


def coupled_body(rows, k_ref, *refs):
    out_ref = refs[-1]
    orb_rows, virt, _ = out_ref.shape
    blocks = piece_blocks(refs[:-1], rows)
    total = None
    for step in range(rows):
        for t in range(orb_rows):
            ref, at = blocks[step][t]
            left = k_ref[step, :, t * virt : (t + 1) * virt]
            part = jnp.dot(left, ref[at], preferred_element_type=jnp.float32)
            total = part if total is None else total + part
    out_ref[...] = total.astype(out_ref.dtype).reshape(out_ref.shape)


def coupled_blocks(rows, kept, pieces):
    orb_rows, virt, _ = pieces[0].shape
    count = rows * orb_rows
    shape = jax.ShapeDtypeStruct((orb_rows, virt, virt), jnp.bfloat16)
    body = functools.partial(coupled_body, rows)
    flops, moved = 2 * orb_rows * count * virt**3, 2 * (orb_rows + 1) * count * virt**2
    return call(body, shape, [VMEM] * (1 + len(pieces)), flops, moved, kept, *pieces)


def column_body(meta, crossing_ref, *refs):
    out_ref, same_ref, other_ref = refs[-3:]
    orb_rows = crossing_ref.shape[0]
    my_col = meta[2 * orb_rows, 1]
    for step in range(out_ref.shape[0] // orb_rows):
        out_ref[pl.ds((my_col // 2 ^ step) * orb_rows, orb_rows)] = refs[step][...]
    same_ref[...] = crossing_ref[my_col % 2]
    other_ref[...] = crossing_ref[1 - my_col % 2]


def whole_column(meta, pieces, crossing, others):
    orb_rows, virt, _ = crossing.shape
    block = jax.ShapeDtypeStruct((virt, virt), jnp.bfloat16)
    shape = (jax.ShapeDtypeStruct((orb_rows * len(pieces), virt, virt), jnp.bfloat16), block, block)
    operands = [crossing, *pieces, *others]
    moved = 4 * orb_rows * (len(pieces) + 1) * virt**2
    return call(column_body, shape, [SMEM] + [VMEM] * len(operands), 0, moved, meta, *operands)


def tied_body(*refs):
    pass


def tied(x, *others):
    return pl.pallas_call(
        tied_body,
        out_shape=jax.ShapeDtypeStruct(x.shape, x.dtype),
        in_specs=[VMEM] * (1 + len(others)),
        out_specs=VMEM,
        input_output_aliases={0: 0},
        compiler_params=pltpu.CompilerParams(vmem_limit_bytes=VMEM_BYTES),
    )(x, *others)


def masked_pair(meta, orbital, blocks):
    orb_rows = len(blocks)
    kept = [jnp.where(meta[orb_rows + i, orbital] > 0, block, jnp.zeros_like(block)) for i, block in enumerate(blocks)]
    return jnp.concatenate(kept, axis=0)


def turned(block):
    return jnp.transpose(block.astype(jnp.float32), (1, 0))


def first_body(rows, meta, own_ref, other_ref, *refs):
    state_ref, coulomb_ref, inverse_ref, out_ref = refs[-4:]
    orb_rows = out_ref.shape[0]
    blocks = piece_blocks(refs[:-4], rows)
    my_row, side = meta[2 * orb_rows, 0], meta[2 * orb_rows, 1] % 2
    total = None
    for step in range(rows):
        at = my_row ^ step
        for t in range(orb_rows):
            left = [
                jnp.where(side == t, own_ref[at * orb_rows + i], other_ref[at * orb_rows + i]) for i in range(orb_rows)
            ]
            ref, place = blocks[step][t]
            left = masked_pair(meta, at * orb_rows + t, left)
            part = jnp.dot(left, ref[place], preferred_element_type=jnp.float32)
            total = part if total is None else total + part
    linear = coulomb_ref[...].astype(jnp.float32) + coupling * refs[0][...].astype(jnp.float32)
    residual = linear + coupling * coupling * total.reshape(out_ref.shape)
    out_ref[...] = damping * state_ref[...] - residual * inverse_ref[...]


def second_body(meta, same_ref, other_ref, part_ref, inverse_ref, out_ref, half_ref):
    side = meta[2 * out_ref.shape[0], 1] % 2
    for ref, at in ((same_ref, side), (other_ref, 1 - side)):
        state = part_ref[at] - coupling * turned(ref[...]) * inverse_ref[at]
        out_ref[at] = state
        half_ref[at] = state.astype(half_ref.dtype)


def first_update(rows, meta, own, other, c_pieces, state, coulomb_own, inverse):
    orb_rows, virt, _ = state.shape
    shape = jax.ShapeDtypeStruct(state.shape, jnp.float32)
    flops, moved = 2 * orb_rows**2 * rows * virt**3, 4 * (orb_rows + 1) * orb_rows * rows * virt**2
    return call(
        functools.partial(first_body, rows), shape, [SMEM] + [VMEM] * (len(c_pieces) + 5), flops, moved,
        meta, own, other, *c_pieces, state, coulomb_own, inverse,
    )


def second_update(meta, same, other, part, inverse):
    shape = (jax.ShapeDtypeStruct(part.shape, jnp.float32), jax.ShapeDtypeStruct(part.shape, jnp.bfloat16))
    return call(second_body, shape, [SMEM] + [VMEM] * 4, 0, 16 * part.size, meta, same, other, part, inverse)


def on_device(
    rows,
    cols,
    amplitudes,
    coulomb,
    inner_list,
    inner_count,
    reader_list,
    reader_count,
    virtual_energy,
    occupied_energy,
):
    orb_rows, orb_cols, virt, _ = amplitudes.shape
    count = coulomb.shape[1]
    slots = inner_list.shape[2]
    assert orb_cols == 1 and count == cols == rows * orb_rows and orb_rows == 2
    halves = cols // 2
    my_row = lax.axis_index("row")
    my_col = lax.axis_index("col")

    def from_row(x, step):
        return lax.ppermute(x, "row", [(r ^ step, r) for r in range(rows)])

    def row_gathered(x):
        return [x] + [from_row(x, step) for step in range(1, rows)]

    def swapped(x):
        return lax.ppermute(x, "col", [(c ^ 1, c) for c in range(cols)])

    def from_chip(x, step):
        return lax.ppermute(x, "col", [(c ^ 2 * step, c) for c in range(cols)])

    def crossing(x, place, flip=0):
        pairs = []
        for r in range(rows):
            for c in range(cols):
                to_r, to_z = place(r, c // 2)
                pairs.append((r * cols + c, to_r * cols + 2 * to_z + (c % 2 ^ flip)))
        return lax.ppermute(x, ("row", "col"), pairs)

    def high_parts(r, z):
        return z - z % 2 + r % 2, r - r % 2 + z % 2

    def last_bits(r, z):
        return r - r % 2 + z % 2, z - z % 2 + r % 2

    state = amplitudes[:, 0]
    half = state.astype(jnp.bfloat16)

    slot_iota = jnp.arange(slots, dtype=jnp.int32)
    orbital_iota = jnp.arange(count, dtype=jnp.int32)

    def used(lists, counts):
        live = slot_iota[None] < counts[:, None]
        hit = (lists[:, :, None] == orbital_iota) & live[:, :, None]
        return jnp.any(hit, axis=1).astype(jnp.int32)

    inner_used = used(inner_list[:, 0], inner_count[:, 0])
    reader_used = used(
        lax.dynamic_index_in_dim(reader_list, my_col, 1, False), lax.dynamic_index_in_dim(reader_count, my_col, 1, False)
    )
    place = jnp.where(orbital_iota == 0, my_row, my_col).astype(jnp.int32)
    meta = jnp.concatenate([inner_used, reader_used, place[None]], axis=0)

    kept, coulomb_own, inverse = prologue(rows, meta, coulomb, virtual_energy, occupied_energy)

    for sweep_index in range(ITERS):
        a_pieces = row_gathered(half)
        column = {0: half, 1: from_chip(half, 1)}
        for step in range(2, halves, 2):
            column[step] = from_chip(half, step)
        coupled = coupled_blocks(rows, kept, a_pieces)
        c_pieces = row_gathered(coupled)
        half_way = crossing(coupled, high_parts)
        for step in range(2, halves, 2):
            column[step] = tied(column[step], coupled)
            column[step + 1] = from_chip(column[step], 1)
        column = [column[step] for step in range(halves)]
        own, same, other = whole_column(meta, column, half_way, c_pieces[1:])
        same, other = crossing(same, last_bits), crossing(other, last_bits, 1)
        part = first_update(rows, meta, own, swapped(own), c_pieces, state, coulomb_own, inverse)
        state, half = second_update(meta, same, other, part, inverse)
    return state[:, None]


def solution(mesh):
    return jax.shard_map(
        functools.partial(on_device, mesh.shape["row"], mesh.shape["col"]),
        mesh=mesh,
        in_specs=(
            P("row", "col", None, None),
            P("row", None, None, None),
            P("row", "col", None),
            P("row", "col"),
            P("row", None, None),
            P("row", None),
            P(),
            P(),
        ),
        out_specs=P("row", "col", None, None),
        check_vma=False,
    )
```

profile of v0, /device:TPU:7, one launch (start us, length us, event | category | flops | bytes accessed | tf_op | source)
XLA Modules:
  0.0 101.0 jit_solution(7176277509856454032)
XLA Ops:
  1.1 2.4 %collective-permute-start.5 = (bf16[2,256,256]{2,1,0:T(8,128)(2,1)S(1)}, bf16[2,256,256]{2,1,0:T(8,128)(2,1)S(1)}, u32[]{:S(2)}, u32[]{:S(2)}) collective-permute-start(bf16[2,256,256]{2,1,0:T(8,128)(2,1)S(1)} %bitcast_convert_fusion.refs_0_), channel_id=1, source_target_pairs={{4,0},{5,1},{6,2},{7,3},{0,4},{1,5},{2,6},{3,7},{12,8},{13,9},{14,... | collective-permute-start | bytes 786440 | tf_op jit(solution)/shard_map/ppermute | solution.py:215
  3.5 1.3 %collective-permute-start.4 = (bf16[2,256,256]{2,1,0:T(8,128)(2,1)S(1)}, bf16[2,256,256]{2,1,0:T(8,128)(2,1)S(1)}, u32[]{:S(2)}, u32[]{:S(2)}) collective-permute-start(bf16[2,256,256]{2,1,0:T(8,128)(2,1)S(1)} %bitcast_convert_fusion.refs_0_), channel_id=1, source_target_pairs={{2,0},{3,1},{0,2},{1,3},{6,4},{7,5},{4,6},{5,7},{10,8},{11,9},{8,1... | collective-permute-start | bytes 786440 | tf_op jit(solution)/shard_map/ppermute | solution.py:215
  5.0 1.2 %collective-permute-start.1 = (bf16[2,256,256]{2,1,0:T(8,128)(2,1)S(1)}, bf16[2,256,256]{2,1,0:T(8,128)(2,1)S(1)}, u32[]{:S(2)}, u32[]{:S(2)}) collective-permute-start(bf16[2,256,256]{2,1,0:T(8,128)(2,1)S(1)} %bitcast_convert_fusion.refs_0_), channel_id=1, source_target_pairs={{16,0},{24,8},{0,16},{8,24},{17,1},{25,9},{1,17},{9,25},{18,2},{26... | collective-permute-start | bytes 786440 | tf_op jit(solution)/shard_map/ppermute | solution.py:206
  10.8 1.6 %copy-done.1 = bf16[2,8,256,256]{3,2,1,0:T(8,128)(2,1)S(1)} copy-done((bf16[2,8,256,256]{3,2,1,0:T(8,128)(2,1)S(1)}, bf16[2,8,256,256]{3,2,1,0:T(8,128)(2,1)}, u32[]{:S(2)}) %copy-start.1) | copy-done | bytes 2097176
  14.7 3.3 %collective-permute-done.1.refs_2_ = bf16[2,256,256]{2,1,0:T(8,128)(2,1)S(1)} collective-permute-done((bf16[2,256,256]{2,1,0:T(8,128)(2,1)S(1)}, bf16[2,256,256]{2,1,0:T(8,128)(2,1)S(1)}, u32[]{:S(2)}, u32[]{:S(2)}) %collective-permute-start.1) | collective-permute-done | bytes 262176 | tf_op jit(solution)/shard_map/ppermute | solution.py:206
  18.8 1.7 %collective-permute-start.9 = (bf16[2,256,256]{2,1,0:T(8,128)(2,1)S(1)}, bf16[2,256,256]{2,1,0:T(8,128)(2,1)S(1)}, u32[]{:S(2)}, u32[]{:S(2)}) collective-permute-start(bf16[2,256,256]{2,1,0:T(8,128)(2,1)S(1)} %shard_map.86.refs_1_.refs_0_), channel_id=1, source_target_pairs={{24,0},{16,8},{8,16},{0,24},{25,1},{17,9},{9,17},{1,25},{26,2},{18... | collective-permute-start | bytes 786440 | tf_op jit(solution)/shard_map/ppermute | solution.py:206
  21.9 3.1 %collective-permute-start.3 = (bf16[2,256,256]{2,1,0:T(8,128)(2,1)S(1)}, bf16[2,256,256]{2,1,0:T(8,128)(2,1)S(1)}, u32[]{:S(2)}, u32[]{:S(2)}) collective-permute-start(bf16[2,256,256]{2,1,0:T(8,128)(2,1)S(1)} %shard_map.86.refs_1_.refs_0_), channel_id=1, source_target_pairs={{0,0},{1,1},{2,2},{3,3},{4,16},{5,17},{6,18},{7,19},{8,8},{9,9},{1... | collective-permute-start | bytes 786440 | tf_op jit(solution)/shard_map/ppermute | solution.py:223
  25.1 2.4 %collective-permute-done.6.refs_3_ = bf16[2,256,256]{2,1,0:T(8,128)(2,1)S(1)} collective-permute-done((bf16[2,256,256]{2,1,0:T(8,128)(2,1)S(1)}, bf16[2,256,256]{2,1,0:T(8,128)(2,1)S(1)}, u32[]{:S(2)}, u32[]{:S(2)}) %collective-permute-start.6) | collective-permute-done | bytes 262176 | tf_op jit(solution)/shard_map/ppermute | solution.py:215
  27.5 7.4 %collective-permute-done.8.refs_5_.refs_2_ = bf16[2,256,256]{2,1,0:T(8,128)(2,1)S(1)} collective-permute-done((bf16[2,256,256]{2,1,0:T(8,128)(2,1)S(1)}, bf16[2,256,256]{2,1,0:T(8,128)(2,1)S(1)}, u32[]{:S(2)}, u32[]{:S(2)}) %collective-permute-start.8) | collective-permute-done | bytes 262176 | tf_op jit(solution)/shard_map/ppermute | solution.py:206
  34.9 3.3 %collective-permute-done.3.crossing_ref = bf16[2,256,256]{2,1,0:T(8,128)(2,1)S(1)} collective-permute-done((bf16[2,256,256]{2,1,0:T(8,128)(2,1)S(1)}, bf16[2,256,256]{2,1,0:T(8,128)(2,1)S(1)}, u32[]{:S(2)}, u32[]{:S(2)}) %collective-permute-start.3) | collective-permute-done | bytes 262176 | tf_op jit(solution)/shard_map/ppermute | solution.py:223
  38.9 1.9 %collective-permute-start.12 = (bf16[8,256,256]{2,1,0:T(8,128)(2,1)S(1)}, bf16[8,256,256]{2,1,0:T(8,128)(2,1)S(1)}, u32[]{:S(2)}, u32[]{:S(2)}) collective-permute-start(bf16[8,256,256]{2,1,0:T(8,128)(2,1)S(1)} %get-tuple-element.20.own_ref), channel_id=1, source_target_pairs={{1,0},{0,1},{3,2},{2,3},{5,4},{4,5},{7,6},{6,7},{9,8},{8,9},{11,10... | collective-permute-start | bytes 3145736 | tf_op jit(solution)/shard_map/ppermute | solution.py:212
  40.8 3.2 %collective-permute-start.10 = (bf16[256,256]{1,0:T(8,128)(2,1)S(1)}, bf16[256,256]{1,0:T(8,128)(2,1)S(1)}, u32[]{:S(2)}, u32[]{:S(2)}) collective-permute-start(bf16[256,256]{1,0:T(8,128)(2,1)S(1)} %get-tuple-element.18), channel_id=1, source_target_pairs={{0,0},{1,1},{2,8},{3,9},{4,4},{5,5},{6,12},{7,13},{8,2},{9,3},{10,... | collective-permute-start | bytes 393224 | tf_op jit(solution)/shard_map/ppermute | solution.py:223
  44.0 1.3 %collective-permute-start.11 = (bf16[256,256]{1,0:T(8,128)(2,1)S(1)}, bf16[256,256]{1,0:T(8,128)(2,1)S(1)}, u32[]{:S(2)}, u32[]{:S(2)}) collective-permute-start(bf16[256,256]{1,0:T(8,128)(2,1)S(1)} %get-tuple-element.19), channel_id=1, source_target_pairs={{0,1},{1,0},{2,9},{3,8},{4,5},{5,4},{6,13},{7,12},{8,3},{9,2},{10,... | collective-permute-start | bytes 393224 | tf_op jit(solution)/shard_map/ppermute | solution.py:223
  45.3 1.4 %shard_map.89.part_ref = f32[2,256,256]{2,1,0:T(8,128)S(1)} custom-call(s32[5,8]{1,0:T(8,128)S(1)} %pad_add_fusion.meta, bf16[8,256,256]{2,1,0:T(8,128)(2,1)S(1)} %get-tuple-element.20.own_ref, bf16[8,256,256]{2,1,0:T(8,128)(2,1)S(1)} %collective-permute-done.12.other_ref, bf16[2,256,256]{2,1,0:T(8,128)(2,1)S(1)} %shard_map.86.refs_1_.refs_0_, ...), custom_call_target="tpu_custom_call" | custom-call | flops 536870912 | bytes 6291456 | tf_op jit(solution)/shard_map/pallas_call | solution.py:23
  46.7 2.0 %collective-permute-done.10.same_ref = bf16[256,256]{1,0:T(8,128)(2,1)S(1)} collective-permute-done((bf16[256,256]{1,0:T(8,128)(2,1)S(1)}, bf16[256,256]{1,0:T(8,128)(2,1)S(1)}, u32[]{:S(2)}, u32[]{:S(2)}) %collective-permute-start.10) | collective-permute-done | bytes 131104 | tf_op jit(solution)/shard_map/ppermute | solution.py:223
  48.6 2.9 %collective-permute-done.11.other_ref = bf16[256,256]{1,0:T(8,128)(2,1)S(1)} collective-permute-done((bf16[256,256]{1,0:T(8,128)(2,1)S(1)}, bf16[256,256]{1,0:T(8,128)(2,1)S(1)}, u32[]{:S(2)}, u32[]{:S(2)}) %collective-permute-start.11) | collective-permute-done | bytes 131104 | tf_op jit(solution)/shard_map/ppermute | solution.py:223
  52.5 2.6 %collective-permute-start.13 = (bf16[2,256,256]{2,1,0:T(8,128)(2,1)S(1)}, bf16[2,256,256]{2,1,0:T(8,128)(2,1)S(1)}, u32[]{:S(2)}, u32[]{:S(2)}) collective-permute-start(bf16[2,256,256]{2,1,0:T(8,128)(2,1)S(1)} %get-tuple-element.23.refs_0_), channel_id=1, source_target_pairs={{8,0},{0,8},{24,16},{16,24},{9,1},{1,9},{25,17},{17,25},{10,2},{2,... | collective-permute-start | bytes 786440 | tf_op jit(solution)/shard_map/ppermute | solution.py:206
  55.5 5.5 %collective-permute-done.15.refs_3_ = bf16[2,256,256]{2,1,0:T(8,128)(2,1)S(1)} collective-permute-done((bf16[2,256,256]{2,1,0:T(8,128)(2,1)S(1)}, bf16[2,256,256]{2,1,0:T(8,128)(2,1)S(1)}, u32[]{:S(2)}, u32[]{:S(2)}) %collective-permute-start.15) | collective-permute-done | bytes 262176 | tf_op jit(solution)/shard_map/ppermute | solution.py:206
  61.0 4.8 %collective-permute-done.14.refs_2_ = bf16[2,256,256]{2,1,0:T(8,128)(2,1)S(1)} collective-permute-done((bf16[2,256,256]{2,1,0:T(8,128)(2,1)S(1)}, bf16[2,256,256]{2,1,0:T(8,128)(2,1)S(1)}, u32[]{:S(2)}, u32[]{:S(2)}) %collective-permute-start.14) | collective-permute-done | bytes 262176 | tf_op jit(solution)/shard_map/ppermute | solution.py:206
  66.4 1.5 %collective-permute-start.22 = (bf16[2,256,256]{2,1,0:T(8,128)(2,1)S(1)}, bf16[2,256,256]{2,1,0:T(8,128)(2,1)S(1)}, u32[]{:S(2)}, u32[]{:S(2)}) collective-permute-start(bf16[2,256,256]{2,1,0:T(8,128)(2,1)S(1)} %shard_map.91.refs_1_.refs_0_), channel_id=1, source_target_pairs={{24,0},{16,8},{8,16},{0,24},{25,1},{17,9},{9,17},{1,25},{26,2},{18... | collective-permute-start | bytes 786440 | tf_op jit(solution)/shard_map/ppermute | solution.py:206
  67.9 1.7 %collective-permute-done.18.refs_0_ = bf16[2,256,256]{2,1,0:T(8,128)(2,1)S(1)} collective-permute-done((bf16[2,256,256]{2,1,0:T(8,128)(2,1)S(1)}, bf16[2,256,256]{2,1,0:T(8,128)(2,1)S(1)}, u32[]{:S(2)}, u32[]{:S(2)}) %collective-permute-start.18) | collective-permute-done | bytes 262176 | tf_op jit(solution)/shard_map/ppermute | solution.py:215
  69.7 4.7 %collective-permute-start.16 = (bf16[2,256,256]{2,1,0:T(8,128)(2,1)S(1)}, bf16[2,256,256]{2,1,0:T(8,128)(2,1)S(1)}, u32[]{:S(2)}, u32[]{:S(2)}) collective-permute-start(bf16[2,256,256]{2,1,0:T(8,128)(2,1)S(1)} %shard_map.91.refs_1_.refs_0_), channel_id=1, source_target_pairs={{0,0},{1,1},{2,2},{3,3},{4,16},{5,17},{6,18},{7,19},{8,8},{9,9},{1... | collective-permute-start | bytes 786440 | tf_op jit(solution)/shard_map/ppermute | solution.py:223
  74.5 2.5 %collective-permute-done.19.refs_3_ = bf16[2,256,256]{2,1,0:T(8,128)(2,1)S(1)} collective-permute-done((bf16[2,256,256]{2,1,0:T(8,128)(2,1)S(1)}, bf16[2,256,256]{2,1,0:T(8,128)(2,1)S(1)}, u32[]{:S(2)}, u32[]{:S(2)}) %collective-permute-start.19) | collective-permute-done | bytes 262176 | tf_op jit(solution)/shard_map/ppermute | solution.py:215
  77.0 5.4 %collective-permute-done.21.refs_5_.refs_2_ = bf16[2,256,256]{2,1,0:T(8,128)(2,1)S(1)} collective-permute-done((bf16[2,256,256]{2,1,0:T(8,128)(2,1)S(1)}, bf16[2,256,256]{2,1,0:T(8,128)(2,1)S(1)}, u32[]{:S(2)}, u32[]{:S(2)}) %collective-permute-start.21) | collective-permute-done | bytes 262176 | tf_op jit(solution)/shard_map/ppermute | solution.py:206
  82.4 3.8 %collective-permute-done.16.crossing_ref = bf16[2,256,256]{2,1,0:T(8,128)(2,1)S(1)} collective-permute-done((bf16[2,256,256]{2,1,0:T(8,128)(2,1)S(1)}, bf16[2,256,256]{2,1,0:T(8,128)(2,1)S(1)}, u32[]{:S(2)}, u32[]{:S(2)}) %collective-permute-start.16) | collective-permute-done | bytes 262176 | tf_op jit(solution)/shard_map/ppermute | solution.py:223
  86.9 1.7 %collective-permute-start.25 = (bf16[8,256,256]{2,1,0:T(8,128)(2,1)S(1)}, bf16[8,256,256]{2,1,0:T(8,128)(2,1)S(1)}, u32[]{:S(2)}, u32[]{:S(2)}) collective-permute-start(bf16[8,256,256]{2,1,0:T(8,128)(2,1)S(1)} %get-tuple-element.26.own_ref), channel_id=1, source_target_pairs={{1,0},{0,1},{3,2},{2,3},{5,4},{4,5},{7,6},{6,7},{9,8},{8,9},{11,10... | collective-permute-start | bytes 3145736 | tf_op jit(solution)/shard_map/ppermute | solution.py:212
  88.6 2.8 %collective-permute-start.23 = (bf16[256,256]{1,0:T(8,128)(2,1)S(1)}, bf16[256,256]{1,0:T(8,128)(2,1)S(1)}, u32[]{:S(2)}, u32[]{:S(2)}) collective-permute-start(bf16[256,256]{1,0:T(8,128)(2,1)S(1)} %get-tuple-element.24), channel_id=1, source_target_pairs={{0,0},{1,1},{2,8},{3,9},{4,4},{5,5},{6,12},{7,13},{8,2},{9,3},{10,... | collective-permute-start | bytes 393224 | tf_op jit(solution)/shard_map/ppermute | solution.py:223
  91.4 1.7 %collective-permute-start.24 = (bf16[256,256]{1,0:T(8,128)(2,1)S(1)}, bf16[256,256]{1,0:T(8,128)(2,1)S(1)}, u32[]{:S(2)}, u32[]{:S(2)}) collective-permute-start(bf16[256,256]{1,0:T(8,128)(2,1)S(1)} %get-tuple-element.25), channel_id=1, source_target_pairs={{0,1},{1,0},{2,9},{3,8},{4,5},{5,4},{6,13},{7,12},{8,3},{9,2},{10,... | collective-permute-start | bytes 393224 | tf_op jit(solution)/shard_map/ppermute | solution.py:223
  93.1 1.4 %shard_map.94.part_ref = f32[2,256,256]{2,1,0:T(8,128)S(1)} custom-call(s32[5,8]{1,0:T(8,128)S(1)} %pad_add_fusion.meta, bf16[8,256,256]{2,1,0:T(8,128)(2,1)S(1)} %get-tuple-element.26.own_ref, bf16[8,256,256]{2,1,0:T(8,128)(2,1)S(1)} %collective-permute-done.25.other_ref, bf16[2,256,256]{2,1,0:T(8,128)(2,1)S(1)} %shard_map.91.refs_1_.refs_0_, ...), custom_call_target="tpu_custom_call" | custom-call | flops 536870912 | bytes 6291456 | tf_op jit(solution)/shard_map/pallas_call | solution.py:23
  94.5 2.0 %collective-permute-done.23.same_ref = bf16[256,256]{1,0:T(8,128)(2,1)S(1)} collective-permute-done((bf16[256,256]{1,0:T(8,128)(2,1)S(1)}, bf16[256,256]{1,0:T(8,128)(2,1)S(1)}, u32[]{:S(2)}, u32[]{:S(2)}) %collective-permute-start.23) | collective-permute-done | bytes 131104 | tf_op jit(solution)/shard_map/ppermute | solution.py:223
  96.5 2.9 %collective-permute-done.24.other_ref = bf16[256,256]{1,0:T(8,128)(2,1)S(1)} collective-permute-done((bf16[256,256]{1,0:T(8,128)(2,1)S(1)}, bf16[256,256]{1,0:T(8,128)(2,1)S(1)}, u32[]{:S(2)}, u32[]{:S(2)}) %collective-permute-start.24) | collective-permute-done | bytes 131104 | tf_op jit(solution)/shard_map/ppermute | solution.py:223
  99.4 1.6 %shard_map.95 = (f32[2,256,256]{2,1,0:T(8,128)}, bf16[2,256,256]{2,1,0:T(8,128)(2,1)}) custom-call(s32[5,8]{1,0:T(8,128)S(1)} %pad_add_fusion.meta, bf16[256,256]{1,0:T(8,128)(2,1)S(1)} %collective-permute-done.23.same_ref, bf16[256,256]{1,0:T(8,128)(2,1)S(1)} %collective-permute-done.24.other_ref, f32[2,256,256]{2,1,0:T(8,128)S(1)} %shard_map.94.part_ref, ...), custom_call_target="tpu_custom_call" | custom-call | bytes 2097152 | tf_op jit(solution)/shard_map/pallas_call | solution.py:23
  (53 shorter events, 13.8 us)
Async XLA Ops:
  0.0 9.1 %copy-start = (s32[2,8,8]{2,1,0:T(8,128)S(1)}, s32[2,8,8]{2,1,0:T(8,128)}, u32[]{:S(2)}) copy-start(s32[2,8,8]{2,1,0:T(8,128)} %param.12) | copy-start | bytes 1540
  1.1 19.4 %collective-permute-start.5 = (bf16[2,256,256]{2,1,0:T(8,128)(2,1)S(1)}, bf16[2,256,256]{2,1,0:T(8,128)(2,1)S(1)}, u32[]{:S(2)}, u32[]{:S(2)}) collective-permute-start(bf16[2,256,256]{2,1,0:T(8,128)(2,1)S(1)} %bitcast_convert_fusion.refs_0_), channel_id=1, source_target_pairs={{4,0},{5,1},{6,2},{7,3},{0,4},{1,5},{2,6},{3,7},{12,8},{13,9},{14,... | collective-permute-start | bytes 786440 | tf_op jit(solution)/shard_map/ppermute | solution.py:215
  3.5 18.5 %collective-permute-start.4 = (bf16[2,256,256]{2,1,0:T(8,128)(2,1)S(1)}, bf16[2,256,256]{2,1,0:T(8,128)(2,1)S(1)}, u32[]{:S(2)}, u32[]{:S(2)}) collective-permute-start(bf16[2,256,256]{2,1,0:T(8,128)(2,1)S(1)} %bitcast_convert_fusion.refs_0_), channel_id=1, source_target_pairs={{2,0},{3,1},{0,2},{1,3},{6,4},{7,5},{4,6},{5,7},{10,8},{11,9},{8,1... | collective-permute-start | bytes 786440 | tf_op jit(solution)/shard_map/ppermute | solution.py:215
  4.8 9.9 %collective-permute-start.2 = (bf16[2,256,256]{2,1,0:T(8,128)(2,1)S(1)}, bf16[2,256,256]{2,1,0:T(8,128)(2,1)S(1)}, u32[]{:S(2)}, u32[]{:S(2)}) collective-permute-start(bf16[2,256,256]{2,1,0:T(8,128)(2,1)S(1)} %bitcast_convert_fusion.refs_0_), channel_id=1, source_target_pairs={{24,0},{16,8},{8,16},{0,24},{25,1},{17,9},{9,17},{1,25},{26,2},{18... | collective-permute-start | bytes 786440 | tf_op jit(solution)/shard_map/ppermute | solution.py:206
  5.0 13.1 %collective-permute-start.1 = (bf16[2,256,256]{2,1,0:T(8,128)(2,1)S(1)}, bf16[2,256,256]{2,1,0:T(8,128)(2,1)S(1)}, u32[]{:S(2)}, u32[]{:S(2)}) collective-permute-start(bf16[2,256,256]{2,1,0:T(8,128)(2,1)S(1)} %bitcast_convert_fusion.refs_0_), channel_id=1, source_target_pairs={{16,0},{24,8},{0,16},{8,24},{17,1},{25,9},{1,17},{9,25},{18,2},{26... | collective-permute-start | bytes 786440 | tf_op jit(solution)/shard_map/ppermute | solution.py:206
  6.2 11.8 %collective-permute-start = (bf16[2,256,256]{2,1,0:T(8,128)(2,1)S(1)}, bf16[2,256,256]{2,1,0:T(8,128)(2,1)S(1)}, u32[]{:S(2)}, u32[]{:S(2)}) collective-permute-start(bf16[2,256,256]{2,1,0:T(8,128)(2,1)S(1)} %bitcast_convert_fusion.refs_0_), channel_id=1, source_target_pairs={{8,0},{0,8},{24,16},{16,24},{9,1},{1,9},{25,17},{17,25},{10,2},{2,... | collective-permute-start | bytes 786440 | tf_op jit(solution)/shard_map/ppermute | solution.py:206
  10.8 1.6 %copy-start.1 = (bf16[2,8,256,256]{3,2,1,0:T(8,128)(2,1)S(1)}, bf16[2,8,256,256]{3,2,1,0:T(8,128)(2,1)}, u32[]{:S(2)}) copy-start(bf16[2,8,256,256]{3,2,1,0:T(8,128)(2,1)} %k_ref.1) | copy-start | bytes 6291460
  12.4 0.7 copy-start.3
  13.1 0.7 copy-start.4
  18.8 26.5 %copy-start.2 = (f32[2,1,256,256]{3,2,1,0:T(8,128)S(1)}, f32[2,1,256,256]{3,2,1,0:T(8,128)}, u32[]{:S(2)}) copy-start(f32[2,1,256,256]{3,2,1,0:T(8,128)} %param.8) | copy-start | bytes 1572868
  18.8 8.7 %collective-permute-start.9 = (bf16[2,256,256]{2,1,0:T(8,128)(2,1)S(1)}, bf16[2,256,256]{2,1,0:T(8,128)(2,1)S(1)}, u32[]{:S(2)}, u32[]{:S(2)}) collective-permute-start(bf16[2,256,256]{2,1,0:T(8,128)(2,1)S(1)} %shard_map.86.refs_1_.refs_0_), channel_id=1, source_target_pairs={{24,0},{16,8},{8,16},{0,24},{25,1},{17,9},{9,17},{1,25},{26,2},{18... | collective-permute-start | bytes 786440 | tf_op jit(solution)/shard_map/ppermute | solution.py:206
  20.5 7.0 %collective-permute-start.6 = (bf16[2,256,256]{2,1,0:T(8,128)(2,1)S(1)}, bf16[2,256,256]{2,1,0:T(8,128)(2,1)S(1)}, u32[]{:S(2)}, u32[]{:S(2)}) collective-permute-start(bf16[2,256,256]{2,1,0:T(8,128)(2,1)S(1)} %shard_map.87.refs_2_), channel_id=1, source_target_pairs={{2,0},{3,1},{0,2},{1,3},{6,4},{7,5},{4,6},{5,7},{10,8},{11,9},{8,1... | collective-permute-start | bytes 786440 | tf_op jit(solution)/shard_map/ppermute | solution.py:215
  20.7 14.2 %collective-permute-start.8 = (bf16[2,256,256]{2,1,0:T(8,128)(2,1)S(1)}, bf16[2,256,256]{2,1,0:T(8,128)(2,1)S(1)}, u32[]{:S(2)}, u32[]{:S(2)}) collective-permute-start(bf16[2,256,256]{2,1,0:T(8,128)(2,1)S(1)} %shard_map.86.refs_1_.refs_0_), channel_id=1, source_target_pairs={{16,0},{24,8},{0,16},{8,24},{17,1},{25,9},{1,17},{9,25},{18,2},{26... | collective-permute-start | bytes 786440 | tf_op jit(solution)/shard_map/ppermute | solution.py:206
  21.9 13.0 %collective-permute-start.7 = (bf16[2,256,256]{2,1,0:T(8,128)(2,1)S(1)}, bf16[2,256,256]{2,1,0:T(8,128)(2,1)S(1)}, u32[]{:S(2)}, u32[]{:S(2)}) collective-permute-start(bf16[2,256,256]{2,1,0:T(8,128)(2,1)S(1)} %shard_map.86.refs_1_.refs_0_), channel_id=1, source_target_pairs={{8,0},{0,8},{24,16},{16,24},{9,1},{1,9},{25,17},{17,25},{10,2},{2,... | collective-permute-start | bytes 786440 | tf_op jit(solution)/shard_map/ppermute | solution.py:206
  21.9 16.3 %collective-permute-start.3 = (bf16[2,256,256]{2,1,0:T(8,128)(2,1)S(1)}, bf16[2,256,256]{2,1,0:T(8,128)(2,1)S(1)}, u32[]{:S(2)}, u32[]{:S(2)}) collective-permute-start(bf16[2,256,256]{2,1,0:T(8,128)(2,1)S(1)} %shard_map.86.refs_1_.refs_0_), channel_id=1, source_target_pairs={{0,0},{1,1},{2,2},{3,3},{4,16},{5,17},{6,18},{7,19},{8,8},{9,9},{1... | collective-permute-start | bytes 786440 | tf_op jit(solution)/shard_map/ppermute | solution.py:223
  38.9 6.4 %collective-permute-start.12 = (bf16[8,256,256]{2,1,0:T(8,128)(2,1)S(1)}, bf16[8,256,256]{2,1,0:T(8,128)(2,1)S(1)}, u32[]{:S(2)}, u32[]{:S(2)}) collective-permute-start(bf16[8,256,256]{2,1,0:T(8,128)(2,1)S(1)} %get-tuple-element.20.own_ref), channel_id=1, source_target_pairs={{1,0},{0,1},{3,2},{2,3},{5,4},{4,5},{7,6},{6,7},{9,8},{8,9},{11,10... | collective-permute-start | bytes 3145736 | tf_op jit(solution)/shard_map/ppermute | solution.py:212
  40.8 7.9 %collective-permute-start.10 = (bf16[256,256]{1,0:T(8,128)(2,1)S(1)}, bf16[256,256]{1,0:T(8,128)(2,1)S(1)}, u32[]{:S(2)}, u32[]{:S(2)}) collective-permute-start(bf16[256,256]{1,0:T(8,128)(2,1)S(1)} %get-tuple-element.18), channel_id=1, source_target_pairs={{0,0},{1,1},{2,8},{3,9},{4,4},{5,5},{6,12},{7,13},{8,2},{9,3},{10,... | collective-permute-start | bytes 393224 | tf_op jit(solution)/shard_map/ppermute | solution.py:223
  44.0 7.6 %collective-permute-start.11 = (bf16[256,256]{1,0:T(8,128)(2,1)S(1)}, bf16[256,256]{1,0:T(8,128)(2,1)S(1)}, u32[]{:S(2)}, u32[]{:S(2)}) collective-permute-start(bf16[256,256]{1,0:T(8,128)(2,1)S(1)} %get-tuple-element.19), channel_id=1, source_target_pairs={{0,1},{1,0},{2,9},{3,8},{4,5},{5,4},{6,13},{7,12},{8,3},{9,2},{10,... | collective-permute-start | bytes 393224 | tf_op jit(solution)/shard_map/ppermute | solution.py:223
  52.3 8.6 %collective-permute-start.15 = (bf16[2,256,256]{2,1,0:T(8,128)(2,1)S(1)}, bf16[2,256,256]{2,1,0:T(8,128)(2,1)S(1)}, u32[]{:S(2)}, u32[]{:S(2)}) collective-permute-start(bf16[2,256,256]{2,1,0:T(8,128)(2,1)S(1)} %get-tuple-element.23.refs_0_), channel_id=1, source_target_pairs={{24,0},{16,8},{8,16},{0,24},{25,1},{17,9},{9,17},{1,25},{26,2},{18... | collective-permute-start | bytes 786440 | tf_op jit(solution)/shard_map/ppermute | solution.py:206
  52.4 13.3 %collective-permute-start.14 = (bf16[2,256,256]{2,1,0:T(8,128)(2,1)S(1)}, bf16[2,256,256]{2,1,0:T(8,128)(2,1)S(1)}, u32[]{:S(2)}, u32[]{:S(2)}) collective-permute-start(bf16[2,256,256]{2,1,0:T(8,128)(2,1)S(1)} %get-tuple-element.23.refs_0_), channel_id=1, source_target_pairs={{16,0},{24,8},{0,16},{8,24},{17,1},{25,9},{1,17},{9,25},{18,2},{26... | collective-permute-start | bytes 786440 | tf_op jit(solution)/shard_map/ppermute | solution.py:206
  52.5 13.2 %collective-permute-start.13 = (bf16[2,256,256]{2,1,0:T(8,128)(2,1)S(1)}, bf16[2,256,256]{2,1,0:T(8,128)(2,1)S(1)}, u32[]{:S(2)}, u32[]{:S(2)}) collective-permute-start(bf16[2,256,256]{2,1,0:T(8,128)(2,1)S(1)} %get-tuple-element.23.refs_0_), channel_id=1, source_target_pairs={{8,0},{0,8},{24,16},{16,24},{9,1},{1,9},{25,17},{17,25},{10,2},{2,... | collective-permute-start | bytes 786440 | tf_op jit(solution)/shard_map/ppermute | solution.py:206
  55.0 14.6 %collective-permute-start.18 = (bf16[2,256,256]{2,1,0:T(8,128)(2,1)S(1)}, bf16[2,256,256]{2,1,0:T(8,128)(2,1)S(1)}, u32[]{:S(2)}, u32[]{:S(2)}) collective-permute-start(bf16[2,256,256]{2,1,0:T(8,128)(2,1)S(1)} %get-tuple-element.23.refs_0_), channel_id=1, source_target_pairs={{4,0},{5,1},{6,2},{7,3},{0,4},{1,5},{2,6},{3,7},{12,8},{13,9},{14,... | collective-permute-start | bytes 786440 | tf_op jit(solution)/shard_map/ppermute | solution.py:215
  55.1 14.7 %collective-permute-start.17 = (bf16[2,256,256]{2,1,0:T(8,128)(2,1)S(1)}, bf16[2,256,256]{2,1,0:T(8,128)(2,1)S(1)}, u32[]{:S(2)}, u32[]{:S(2)}) collective-permute-start(bf16[2,256,256]{2,1,0:T(8,128)(2,1)S(1)} %get-tuple-element.23.refs_0_), channel_id=1, source_target_pairs={{2,0},{3,1},{0,2},{1,3},{6,4},{7,5},{4,6},{5,7},{10,8},{11,9},{8,1... | collective-permute-start | bytes 786440 | tf_op jit(solution)/shard_map/ppermute | solution.py:215
  66.4 10.6 %collective-permute-start.22 = (bf16[2,256,256]{2,1,0:T(8,128)(2,1)S(1)}, bf16[2,256,256]{2,1,0:T(8,128)(2,1)S(1)}, u32[]{:S(2)}, u32[]{:S(2)}) collective-permute-start(bf16[2,256,256]{2,1,0:T(8,128)(2,1)S(1)} %shard_map.91.refs_1_.refs_0_), channel_id=1, source_target_pairs={{24,0},{16,8},{8,16},{0,24},{25,1},{17,9},{9,17},{1,25},{26,2},{18... | collective-permute-start | bytes 786440 | tf_op jit(solution)/shard_map/ppermute | solution.py:206
  69.6 7.4 %collective-permute-start.19 = (bf16[2,256,256]{2,1,0:T(8,128)(2,1)S(1)}, bf16[2,256,256]{2,1,0:T(8,128)(2,1)S(1)}, u32[]{:S(2)}, u32[]{:S(2)}) collective-permute-start(bf16[2,256,256]{2,1,0:T(8,128)(2,1)S(1)} %shard_map.92.refs_2_), channel_id=1, source_target_pairs={{2,0},{3,1},{0,2},{1,3},{6,4},{7,5},{4,6},{5,7},{10,8},{11,9},{8,1... | collective-permute-start | bytes 786440 | tf_op jit(solution)/shard_map/ppermute | solution.py:215
  69.6 12.8 %collective-permute-start.21 = (bf16[2,256,256]{2,1,0:T(8,128)(2,1)S(1)}, bf16[2,256,256]{2,1,0:T(8,128)(2,1)S(1)}, u32[]{:S(2)}, u32[]{:S(2)}) collective-permute-start(bf16[2,256,256]{2,1,0:T(8,128)(2,1)S(1)} %shard_map.91.refs_1_.refs_0_), channel_id=1, source_target_pairs={{16,0},{24,8},{0,16},{8,24},{17,1},{25,9},{1,17},{9,25},{18,2},{26... | collective-permute-start | bytes 786440 | tf_op jit(solution)/shard_map/ppermute | solution.py:206
  69.6 12.8 %collective-permute-start.20 = (bf16[2,256,256]{2,1,0:T(8,128)(2,1)S(1)}, bf16[2,256,256]{2,1,0:T(8,128)(2,1)S(1)}, u32[]{:S(2)}, u32[]{:S(2)}) collective-permute-start(bf16[2,256,256]{2,1,0:T(8,128)(2,1)S(1)} %shard_map.91.refs_1_.refs_0_), channel_id=1, source_target_pairs={{8,0},{0,8},{24,16},{16,24},{9,1},{1,9},{25,17},{17,25},{10,2},{2,... | collective-permute-start | bytes 786440 | tf_op jit(solution)/shard_map/ppermute | solution.py:206
  69.7 16.5 %collective-permute-start.16 = (bf16[2,256,256]{2,1,0:T(8,128)(2,1)S(1)}, bf16[2,256,256]{2,1,0:T(8,128)(2,1)S(1)}, u32[]{:S(2)}, u32[]{:S(2)}) collective-permute-start(bf16[2,256,256]{2,1,0:T(8,128)(2,1)S(1)} %shard_map.91.refs_1_.refs_0_), channel_id=1, source_target_pairs={{0,0},{1,1},{2,2},{3,3},{4,16},{5,17},{6,18},{7,19},{8,8},{9,9},{1... | collective-permute-start | bytes 786440 | tf_op jit(solution)/shard_map/ppermute | solution.py:223
  86.9 6.2 %collective-permute-start.25 = (bf16[8,256,256]{2,1,0:T(8,128)(2,1)S(1)}, bf16[8,256,256]{2,1,0:T(8,128)(2,1)S(1)}, u32[]{:S(2)}, u32[]{:S(2)}) collective-permute-start(bf16[8,256,256]{2,1,0:T(8,128)(2,1)S(1)} %get-tuple-element.26.own_ref), channel_id=1, source_target_pairs={{1,0},{0,1},{3,2},{2,3},{5,4},{4,5},{7,6},{6,7},{9,8},{8,9},{11,10... | collective-permute-start | bytes 3145736 | tf_op jit(solution)/shard_map/ppermute | solution.py:212
  88.6 7.9 %collective-permute-start.23 = (bf16[256,256]{1,0:T(8,128)(2,1)S(1)}, bf16[256,256]{1,0:T(8,128)(2,1)S(1)}, u32[]{:S(2)}, u32[]{:S(2)}) collective-permute-start(bf16[256,256]{1,0:T(8,128)(2,1)S(1)} %get-tuple-element.24), channel_id=1, source_target_pairs={{0,0},{1,1},{2,8},{3,9},{4,4},{5,5},{6,12},{7,13},{8,2},{9,3},{10,... | collective-permute-start | bytes 393224 | tf_op jit(solution)/shard_map/ppermute | solution.py:223
  91.4 8.0 %collective-permute-start.24 = (bf16[256,256]{1,0:T(8,128)(2,1)S(1)}, bf16[256,256]{1,0:T(8,128)(2,1)S(1)}, u32[]{:S(2)}, u32[]{:S(2)}) collective-permute-start(bf16[256,256]{1,0:T(8,128)(2,1)S(1)} %get-tuple-element.25), channel_id=1, source_target_pairs={{0,1},{1,0},{2,9},{3,8},{4,5},{5,4},{6,13},{7,12},{8,3},{9,2},{10,... | collective-permute-start | bytes 393224 | tf_op jit(solution)/shard_map/ppermute | solution.py:223
where the time goes:
time: 101 us
  waiting for transfers between devices  49.9 us (49%)
  starting transfers between devices  34.6 us (34%)
  Pallas kernels  8.86 us (9%)
  local copies, waits for them, and re-layouts  4.6 us (5%)
  other arithmetic  2.77 us (3%)
    ppermute x12, waiting for transfers between devices, from_row(): return lax.ppermute(x, 'row', [(r ^ step, r) for r in range(rows)])  26.4 us
    ppermute x6, starting transfers between devices, crossing(): return lax.ppermute(x, ('row', 'col'), pairs)  16.9 us
    ppermute x6, waiting for transfers between devices, crossing(): return lax.ppermute(x, ('row', 'col'), pairs)  16.9 us
    ppermute x12, starting transfers between devices, from_row(): return lax.ppermute(x, 'row', [(r ^ step, r) for r in range(rows)])  9.88 us
    pallas_call x9, Pallas kernels, call(): pl.pallas_call(body, out_shape=out_shape, in_specs=in_specs, out_specs=VM...  8.86 us
    ppermute x6, waiting for transfers between devices, from_chip(): return lax.ppermute(x, 'col', [(c ^ 2 * step, c) for c in range(cols)])  6.66 us
    ppermute x6, starting transfers between devices, from_chip(): return lax.ppermute(x, 'col', [(c ^ 2 * step, c) for c in range(cols)])  4.29 us
    ppermute x2, starting transfers between devices, swapped(): return lax.ppermute(x, 'col', [(c ^ 1, c) for c in range(cols)])  3.54 us
  transfers between devices with their start and end apart: 26, of which 14 were waited for; matrix products, arithmetic and copies ran while one was open for 3% of the time, Pallas kernels for 5%

commit v1 on v0

--- a/solution.py
+++ b/solution.py
@@ -60,56 +60,44 @@
     )
 
 
-def piece_blocks(refs, rows):
-    found, refs, size = [], list(refs), refs[0].shape[0]
-    for step in range(rows):
-        blocks = []
-        while len(blocks) < size:
-            ref = refs.pop(0)
-            blocks += [(ref, at) for at in range(ref.shape[0])]
-        found.append(blocks)
-    return found
-
-
-def coupled_body(rows, k_ref, *refs):
-    out_ref = refs[-1]
+def coupled_body(rows, meta, k_ref, *refs):
+    out_ref, same_ref, other_ref = refs[-3:]
     orb_rows, virt, _ = out_ref.shape
-    blocks = piece_blocks(refs[:-1], rows)
+    side = meta[2 * orb_rows, 1] % 2
     total = None
     for step in range(rows):
         for t in range(orb_rows):
-            ref, at = blocks[step][t]
             left = k_ref[step, :, t * virt : (t + 1) * virt]
-            part = jnp.dot(left, ref[at], preferred_element_type=jnp.float32)
+            part = jnp.dot(left, refs[step][t], preferred_element_type=jnp.float32)
             total = part if total is None else total + part
     out_ref[...] = total.astype(out_ref.dtype).reshape(out_ref.shape)
-
-
-def coupled_blocks(rows, kept, pieces):
+    same_ref[...] = out_ref[side]
+    other_ref[...] = out_ref[1 - side]
+
+
+def coupled_blocks(rows, meta, kept, pieces):
     orb_rows, virt, _ = pieces[0].shape
     count = rows * orb_rows
-    shape = jax.ShapeDtypeStruct((orb_rows, virt, virt), jnp.bfloat16)
+    block = jax.ShapeDtypeStruct((virt, virt), jnp.bfloat16)
+    shape = (jax.ShapeDtypeStruct((orb_rows, virt, virt), jnp.bfloat16), block, block)
     body = functools.partial(coupled_body, rows)
     flops, moved = 2 * orb_rows * count * virt**3, 2 * (orb_rows + 1) * count * virt**2
-    return call(body, shape, [VMEM] * (1 + len(pieces)), flops, moved, kept, *pieces)
-
-
-def column_body(meta, crossing_ref, *refs):
-    out_ref, same_ref, other_ref = refs[-3:]
-    orb_rows = crossing_ref.shape[0]
-    my_col = meta[2 * orb_rows, 1]
+    return call(body, shape, [SMEM] + [VMEM] * (1 + len(pieces)), flops, moved, meta, kept, *pieces)
+
+
+def column_body(meta, *refs):
+    out_ref = refs[-1]
+    orb_rows = refs[0].shape[0]
+    my_place = meta[2 * orb_rows, 1] // 2
     for step in range(out_ref.shape[0] // orb_rows):
-        out_ref[pl.ds((my_col // 2 ^ step) * orb_rows, orb_rows)] = refs[step][...]
-    same_ref[...] = crossing_ref[my_col % 2]
-    other_ref[...] = crossing_ref[1 - my_col % 2]
-
-
-def whole_column(meta, pieces, crossing, others):
-    orb_rows, virt, _ = crossing.shape
-    block = jax.ShapeDtypeStruct((virt, virt), jnp.bfloat16)
-    shape = (jax.ShapeDtypeStruct((orb_rows * len(pieces), virt, virt), jnp.bfloat16), block, block)
-    operands = [crossing, *pieces, *others]
-    moved = 4 * orb_rows * (len(pieces) + 1) * virt**2
+        out_ref[pl.ds((my_place ^ step) * orb_rows, orb_rows)] = refs[step][...]
+
+
+def whole_column(meta, pieces, others):
+    orb_rows, virt, _ = pieces[0].shape
+    shape = jax.ShapeDtypeStruct((orb_rows * len(pieces), virt, virt), jnp.bfloat16)
+    operands = [*pieces, *others]
+    moved = 4 * orb_rows * len(pieces) * virt**2
     return call(column_body, shape, [SMEM] + [VMEM] * len(operands), 0, moved, meta, *operands)
 
 
@@ -141,7 +129,6 @@
 def first_body(rows, meta, own_ref, other_ref, *refs):
     state_ref, coulomb_ref, inverse_ref, out_ref = refs[-4:]
     orb_rows = out_ref.shape[0]
-    blocks = piece_blocks(refs[:-4], rows)
     my_row, side = meta[2 * orb_rows, 0], meta[2 * orb_rows, 1] % 2
     total = None
     for step in range(rows):
@@ -150,9 +137,8 @@
             left = [
                 jnp.where(side == t, own_ref[at * orb_rows + i], other_ref[at * orb_rows + i]) for i in range(orb_rows)
             ]
-            ref, place = blocks[step][t]
             left = masked_pair(meta, at * orb_rows + t, left)
-            part = jnp.dot(left, ref[place], preferred_element_type=jnp.float32)
+            part = jnp.dot(left, refs[step][t], preferred_element_type=jnp.float32)
             total = part if total is None else total + part
     linear = coulomb_ref[...].astype(jnp.float32) + coupling * refs[0][...].astype(jnp.float32)
     residual = linear + coupling * coupling * total.reshape(out_ref.shape)
@@ -253,15 +239,19 @@
         column = {0: half, 1: from_chip(half, 1)}
         for step in range(2, halves, 2):
             column[step] = from_chip(half, step)
-        coupled = coupled_blocks(rows, kept, a_pieces)
-        c_pieces = row_gathered(coupled)
-        half_way = crossing(coupled, high_parts)
+        coupled, same, other = coupled_blocks(rows, meta, kept, a_pieces)
+        c_pieces = {0: coupled, 1: from_row(coupled, 1)}
+        for step in range(2, rows, 2):
+            c_pieces[step] = from_row(coupled, step)
+            c_pieces[step + 1] = from_row(c_pieces[step], 1)
+        c_pieces = [c_pieces[step] for step in range(rows)]
+        same, other = crossing(same, high_parts), crossing(other, last_bits)
         for step in range(2, halves, 2):
             column[step] = tied(column[step], coupled)
             column[step + 1] = from_chip(column[step], 1)
         column = [column[step] for step in range(halves)]
-        own, same, other = whole_column(meta, column, half_way, c_pieces[1:])
-        same, other = crossing(same, last_bits), crossing(other, last_bits, 1)
+        own = whole_column(meta, column, [c_pieces[1], c_pieces[2], same, other])
+        same, other = crossing(same, last_bits), crossing(other, high_parts, 1)
         part = first_update(rows, meta, own, swapped(own), c_pieces, state, coulomb_own, inverse)
         state, half = second_update(meta, same, other, part, inverse)
     return state[:, None]

time: 101 us -> 95.8 us (0.949)
  waiting for transfers between devices: 49.9 us -> 34.2 us
  starting transfers between devices: 34.6 us -> 43.3 us
  Pallas kernels: 8.86 us -> 10.1 us
    ppermute x6 -> x8, waiting for transfers between devices: 16.9 us -> 9.89 us  [crossing(): return lax.ppermute(x, ('row', 'col'), pairs)]
    ppermute x6 -> x8, starting transfers between devices: 16.9 us -> 23.6 us  [crossing(): return lax.ppermute(x, ('row', 'col'), pairs)]
    ppermute x12, waiting for transfers between devices: 26.4 us -> 21.7 us  [from_row(): return lax.ppermute(x, 'row', [(r ^ step, r) for r in range(rows)])]
    ppermute x6, waiting for transfers between devices: 6.66 us -> 2.59 us  [from_chip(): return lax.ppermute(x, 'col', [(c ^ 2 * step, c) for c in range(cols)])]
    ppermute x6, starting transfers between devices: 4.29 us -> 5.96 us  [from_chip(): return lax.ppermute(x, 'col', [(c ^ 2 * step, c) for c in range(cols)])]
    pallas_call x9, Pallas kernels: 8.86 us -> 10.1 us  [call(): pl.pallas_call(body, out_shape=out_shape, in_specs=in_specs, out_specs=VM...]
  transfers between devices with their start and end apart: 26 -> 28, of which waited for: 14 -> 10; matrix products, arithmetic and copies ran while one was open for 3% -> 4% of each run, Pallas kernels for 5% -> 7%
where the time goes in v1:
time: 95.8 us; the launch traced here: 95.2 us
  starting transfers between devices  43.3 us (45%)
  waiting for transfers between devices  34.2 us (36%)
  Pallas kernels  10.1 us (11%)
  local copies, waits for them, and re-layouts  4.6 us (5%)
  other arithmetic  2.77 us (3%)
    ppermute x8, starting transfers between devices, crossing(): return lax.ppermute(x, ('row', 'col'), pairs)  23.6 us
    ppermute x12, waiting for transfers between devices, from_row(): return lax.ppermute(x, 'row', [(r ^ step, r) for r in range(rows)])  21.7 us
    pallas_call x9, Pallas kernels, call(): pl.pallas_call(body, out_shape=out_shape, in_specs=in_specs, out_specs=VM...  10.1 us
    ppermute x8, waiting for transfers between devices, crossing(): return lax.ppermute(x, ('row', 'col'), pairs)  9.89 us
    ppermute x12, starting transfers between devices, from_row(): return lax.ppermute(x, 'row', [(r ^ step, r) for r in range(rows)])  9.54 us
    ppermute x6, starting transfers between devices, from_chip(): return lax.ppermute(x, 'col', [(c ^ 2 * step, c) for c in range(cols)])  5.96 us
    ppermute x2, starting transfers between devices, swapped(): return lax.ppermute(x, 'col', [(c ^ 1, c) for c in range(cols)])  4.23 us
    unnamed x10, local copies, waits for them, and re-layouts  2.93 us
  transfers between devices with their start and end apart: 28, of which 10 were waited for; matrix products, arithmetic and copies ran while one was open for 4% of the time, Pallas kernels for 7%

profile of v1, /device:TPU:7, one launch (start us, length us, event | category | flops | bytes accessed | tf_op | source)
XLA Modules:
  0.0 95.2 jit_solution(13649182521397705579)
XLA Ops:
  1.1 2.4 %collective-permute-start.8 = (bf16[2,256,256]{2,1,0:T(8,128)(2,1)S(1)}, bf16[2,256,256]{2,1,0:T(8,128)(2,1)S(1)}, u32[]{:S(2)}, u32[]{:S(2)}) collective-permute-start(bf16[2,256,256]{2,1,0:T(8,128)(2,1)S(1)} %bitcast_convert_fusion.refs_0_), channel_id=1, source_target_pairs={{4,0},{5,1},{6,2},{7,3},{0,4},{1,5},{2,6},{3,7},{12,8},{13,9},{14,... | collective-permute-start | bytes 786440 | tf_op jit(solution)/shard_map/ppermute | solution.py:201
  3.5 1.3 %collective-permute-start.7 = (bf16[2,256,256]{2,1,0:T(8,128)(2,1)S(1)}, bf16[2,256,256]{2,1,0:T(8,128)(2,1)S(1)}, u32[]{:S(2)}, u32[]{:S(2)}) collective-permute-start(bf16[2,256,256]{2,1,0:T(8,128)(2,1)S(1)} %bitcast_convert_fusion.refs_0_), channel_id=1, source_target_pairs={{2,0},{3,1},{0,2},{1,3},{6,4},{7,5},{4,6},{5,7},{10,8},{11,9},{8,1... | collective-permute-start | bytes 786440 | tf_op jit(solution)/shard_map/ppermute | solution.py:201
  5.0 1.2 %collective-permute-start.1 = (bf16[2,256,256]{2,1,0:T(8,128)(2,1)S(1)}, bf16[2,256,256]{2,1,0:T(8,128)(2,1)S(1)}, u32[]{:S(2)}, u32[]{:S(2)}) collective-permute-start(bf16[2,256,256]{2,1,0:T(8,128)(2,1)S(1)} %bitcast_convert_fusion.refs_0_), channel_id=1, source_target_pairs={{16,0},{24,8},{0,16},{8,24},{17,1},{25,9},{1,17},{9,25},{18,2},{26... | collective-permute-start | bytes 786440 | tf_op jit(solution)/shard_map/ppermute | solution.py:192
  6.2 1.2 %collective-permute-start = (bf16[2,256,256]{2,1,0:T(8,128)(2,1)S(1)}, bf16[2,256,256]{2,1,0:T(8,128)(2,1)S(1)}, u32[]{:S(2)}, u32[]{:S(2)}) collective-permute-start(bf16[2,256,256]{2,1,0:T(8,128)(2,1)S(1)} %bitcast_convert_fusion.refs_0_), channel_id=1, source_target_pairs={{8,0},{0,8},{24,16},{16,24},{9,1},{1,9},{25,17},{17,25},{10,2},{2,... | collective-permute-start | bytes 786440 | tf_op jit(solution)/shard_map/ppermute | solution.py:192
  10.8 1.6 %copy-done.1 = bf16[2,8,256,256]{3,2,1,0:T(8,128)(2,1)S(1)} copy-done((bf16[2,8,256,256]{3,2,1,0:T(8,128)(2,1)S(1)}, bf16[2,8,256,256]{3,2,1,0:T(8,128)(2,1)}, u32[]{:S(2)}) %copy-start.1) | copy-done | bytes 2097176
  14.7 3.3 %collective-permute-done.1.refs_2_ = bf16[2,256,256]{2,1,0:T(8,128)(2,1)S(1)} collective-permute-done((bf16[2,256,256]{2,1,0:T(8,128)(2,1)S(1)}, bf16[2,256,256]{2,1,0:T(8,128)(2,1)S(1)}, u32[]{:S(2)}, u32[]{:S(2)}) %collective-permute-start.1) | collective-permute-done | bytes 262176 | tf_op jit(solution)/shard_map/ppermute | solution.py:192
  18.0 1.4 %shard_map.86 = (bf16[2,256,256]{2,1,0:T(8,128)(2,1)S(1)}, bf16[256,256]{1,0:T(8,128)(2,1)S(1)}, bf16[256,256]{1,0:T(8,128)(2,1)S(1)}) custom-call(s32[5,8]{1,0:T(8,128)S(1)} %pad_add_fusion.meta, bf16[4,512,512]{2,1,0:T(8,128)(2,1)S(1)} %get-tuple-element.17.k_ref, bf16[2,256,256]{2,1,0:T(8,128)(2,1)S(1)} %bitcast_convert_fusion.refs_0_, ...), custom_call_target="tpu_custom_call" | custom-call | flops 536870912 | bytes 3145728 | tf_op jit(solution)/shard_map/pallas_call | solution.py:23
  19.7 1.7 %collective-permute-start.11 = (bf16[2,256,256]{2,1,0:T(8,128)(2,1)S(1)}, bf16[2,256,256]{2,1,0:T(8,128)(2,1)S(1)}, u32[]{:S(2)}, u32[]{:S(2)}) collective-permute-start(bf16[2,256,256]{2,1,0:T(8,128)(2,1)S(1)} %get-tuple-element.20.refs_1_.refs_0_), channel_id=1, source_target_pairs={{16,0},{24,8},{0,16},{8,24},{17,1},{25,9},{1,17},{9,25},{18,2},{26... | collective-permute-start | bytes 786440 | tf_op jit(solution)/shard_map/ppermute | solution.py:192
  21.6 2.9 %collective-permute-start.3 = (bf16[256,256]{1,0:T(8,128)(2,1)S(1)}, bf16[256,256]{1,0:T(8,128)(2,1)S(1)}, u32[]{:S(2)}, u32[]{:S(2)}) collective-permute-start(bf16[256,256]{1,0:T(8,128)(2,1)S(1)} %get-tuple-element.18), channel_id=1, source_target_pairs={{0,0},{1,1},{2,2},{3,3},{4,16},{5,17},{6,18},{7,19},{8,8},{9,9},{1... | collective-permute-start | bytes 393224 | tf_op jit(solution)/shard_map/ppermute | solution.py:209
  24.6 3.1 %collective-permute-start.5 = (bf16[256,256]{1,0:T(8,128)(2,1)S(1)}, bf16[256,256]{1,0:T(8,128)(2,1)S(1)}, u32[]{:S(2)}, u32[]{:S(2)}) collective-permute-start(bf16[256,256]{1,0:T(8,128)(2,1)S(1)} %get-tuple-element.19), channel_id=1, source_target_pairs={{0,0},{1,1},{2,8},{3,9},{4,4},{5,5},{6,12},{7,13},{8,2},{9,3},{10,... | collective-permute-start | bytes 393224 | tf_op jit(solution)/shard_map/ppermute | solution.py:209
  27.7 4.8 %collective-permute-done.3.refs_6_ = bf16[256,256]{1,0:T(8,128)(2,1)S(1)} collective-permute-done((bf16[256,256]{1,0:T(8,128)(2,1)S(1)}, bf16[256,256]{1,0:T(8,128)(2,1)S(1)}, u32[]{:S(2)}, u32[]{:S(2)}) %collective-permute-start.3) | collective-permute-done | bytes 131104 | tf_op jit(solution)/shard_map/ppermute | solution.py:209
  33.2 1.6 %collective-permute-start.12 = (bf16[8,256,256]{2,1,0:T(8,128)(2,1)S(1)}, bf16[8,256,256]{2,1,0:T(8,128)(2,1)S(1)}, u32[]{:S(2)}, u32[]{:S(2)}) collective-permute-start(bf16[8,256,256]{2,1,0:T(8,128)(2,1)S(1)} %shard_map.88.own_ref), channel_id=1, source_target_pairs={{1,0},{0,1},{3,2},{2,3},{5,4},{4,5},{7,6},{6,7},{9,8},{8,9},{11,10... | collective-permute-start | bytes 3145736 | tf_op jit(solution)/shard_map/ppermute | solution.py:198
  34.8 1.2 %collective-permute-start.13 = (bf16[2,256,256]{2,1,0:T(8,128)(2,1)S(1)}, bf16[2,256,256]{2,1,0:T(8,128)(2,1)S(1)}, u32[]{:S(2)}, u32[]{:S(2)}) collective-permute-start(bf16[2,256,256]{2,1,0:T(8,128)(2,1)S(1)} %collective-permute-done.11.refs_5_.refs_2_), channel_id=1, source_target_pairs={{8,0},{0,8},{24,16},{16,24},{9,1},{1,9},{25,17},{17,25},{10,2},{2,... | collective-permute-start | bytes 786440 | tf_op jit(solution)/shard_map/ppermute | solution.py:192
  36.1 2.1 %collective-permute-start.4 = (bf16[256,256]{1,0:T(8,128)(2,1)S(1)}, bf16[256,256]{1,0:T(8,128)(2,1)S(1)}, u32[]{:S(2)}, u32[]{:S(2)}) collective-permute-start(bf16[256,256]{1,0:T(8,128)(2,1)S(1)} %collective-permute-done.3.refs_6_), channel_id=1, source_target_pairs={{0,0},{1,1},{2,8},{3,9},{4,4},{5,5},{6,12},{7,13},{8,2},{9,3},{10,... | collective-permute-start | bytes 393224 | tf_op jit(solution)/shard_map/ppermute | solution.py:209
  38.2 3.3 %collective-permute-start.6 = (bf16[256,256]{1,0:T(8,128)(2,1)S(1)}, bf16[256,256]{1,0:T(8,128)(2,1)S(1)}, u32[]{:S(2)}, u32[]{:S(2)}) collective-permute-start(bf16[256,256]{1,0:T(8,128)(2,1)S(1)} %collective-permute-done.5.refs_7_), channel_id=1, source_target_pairs={{0,1},{1,0},{2,3},{3,2},{4,17},{5,16},{6,19},{7,18},{8,9},{9,8},{1... | collective-permute-start | bytes 393224 | tf_op jit(solution)/shard_map/ppermute | solution.py:209
  41.5 4.0 %collective-permute-done.13.refs_3_ = bf16[2,256,256]{2,1,0:T(8,128)(2,1)S(1)} collective-permute-done((bf16[2,256,256]{2,1,0:T(8,128)(2,1)S(1)}, bf16[2,256,256]{2,1,0:T(8,128)(2,1)S(1)}, u32[]{:S(2)}, u32[]{:S(2)}) %collective-permute-start.13) | collective-permute-done | bytes 262176 | tf_op jit(solution)/shard_map/ppermute | solution.py:192
  45.5 1.4 %shard_map.89.part_ref = f32[2,256,256]{2,1,0:T(8,128)S(1)} custom-call(s32[5,8]{1,0:T(8,128)S(1)} %pad_add_fusion.meta, bf16[8,256,256]{2,1,0:T(8,128)(2,1)S(1)} %shard_map.88.own_ref, bf16[8,256,256]{2,1,0:T(8,128)(2,1)S(1)} %collective-permute-done.12.other_ref, bf16[2,256,256]{2,1,0:T(8,128)(2,1)S(1)} %get-tuple-element.20.refs_1_.refs_0_, ...), custom_call_target="tpu_custom_call" | custom-call | flops 536870912 | bytes 6291456 | tf_op jit(solution)/shard_map/pallas_call | solution.py:23
  48.2 2.6 %collective-permute-start.14 = (bf16[2,256,256]{2,1,0:T(8,128)(2,1)S(1)}, bf16[2,256,256]{2,1,0:T(8,128)(2,1)S(1)}, u32[]{:S(2)}, u32[]{:S(2)}) collective-permute-start(bf16[2,256,256]{2,1,0:T(8,128)(2,1)S(1)} %get-tuple-element.23.refs_0_), channel_id=1, source_target_pairs={{8,0},{0,8},{24,16},{16,24},{9,1},{1,9},{25,17},{17,25},{10,2},{2,... | collective-permute-start | bytes 786440 | tf_op jit(solution)/shard_map/ppermute | solution.py:192
  50.8 1.1 %collective-permute-start.22 = (bf16[2,256,256]{2,1,0:T(8,128)(2,1)S(1)}, bf16[2,256,256]{2,1,0:T(8,128)(2,1)S(1)}, u32[]{:S(2)}, u32[]{:S(2)}) collective-permute-start(bf16[2,256,256]{2,1,0:T(8,128)(2,1)S(1)} %get-tuple-element.23.refs_0_), channel_id=1, source_target_pairs={{4,0},{5,1},{6,2},{7,3},{0,4},{1,5},{2,6},{3,7},{12,8},{13,9},{14,... | collective-permute-start | bytes 786440 | tf_op jit(solution)/shard_map/ppermute | solution.py:201
  52.8 3.6 %collective-permute-done.16.refs_3_ = bf16[2,256,256]{2,1,0:T(8,128)(2,1)S(1)} collective-permute-done((bf16[2,256,256]{2,1,0:T(8,128)(2,1)S(1)}, bf16[2,256,256]{2,1,0:T(8,128)(2,1)S(1)}, u32[]{:S(2)}, u32[]{:S(2)}) %collective-permute-start.16) | collective-permute-done | bytes 262176 | tf_op jit(solution)/shard_map/ppermute | solution.py:192
  56.4 4.8 %collective-permute-done.15.refs_2_ = bf16[2,256,256]{2,1,0:T(8,128)(2,1)S(1)} collective-permute-done((bf16[2,256,256]{2,1,0:T(8,128)(2,1)S(1)}, bf16[2,256,256]{2,1,0:T(8,128)(2,1)S(1)}, u32[]{:S(2)}, u32[]{:S(2)}) %collective-permute-start.15) | collective-permute-done | bytes 262176 | tf_op jit(solution)/shard_map/ppermute | solution.py:192
  61.2 1.4 %shard_map.91 = (bf16[2,256,256]{2,1,0:T(8,128)(2,1)S(1)}, bf16[256,256]{1,0:T(8,128)(2,1)S(1)}, bf16[256,256]{1,0:T(8,128)(2,1)S(1)}) custom-call(s32[5,8]{1,0:T(8,128)S(1)} %pad_add_fusion.meta, bf16[4,512,512]{2,1,0:T(8,128)(2,1)S(1)} %get-tuple-element.17.k_ref, bf16[2,256,256]{2,1,0:T(8,128)(2,1)S(1)} %get-tuple-element.23.refs_0_, ...), custom_call_target="tpu_custom_call" | custom-call | flops 536870912 | bytes 3145728 | tf_op jit(solution)/shard_map/pallas_call | solution.py:23
  62.6 2.6 %collective-permute-done.22.refs_0_ = bf16[2,256,256]{2,1,0:T(8,128)(2,1)S(1)} collective-permute-done((bf16[2,256,256]{2,1,0:T(8,128)(2,1)S(1)}, bf16[2,256,256]{2,1,0:T(8,128)(2,1)S(1)}, u32[]{:S(2)}, u32[]{:S(2)}) %collective-permute-start.22) | collective-permute-done | bytes 262176 | tf_op jit(solution)/shard_map/ppermute | solution.py:201
  66.2 5.1 %collective-permute-start.17 = (bf16[256,256]{1,0:T(8,128)(2,1)S(1)}, bf16[256,256]{1,0:T(8,128)(2,1)S(1)}, u32[]{:S(2)}, u32[]{:S(2)}) collective-permute-start(bf16[256,256]{1,0:T(8,128)(2,1)S(1)} %get-tuple-element.24), channel_id=1, source_target_pairs={{0,0},{1,1},{2,2},{3,3},{4,16},{5,17},{6,18},{7,19},{8,8},{9,9},{1... | collective-permute-start | bytes 393224 | tf_op jit(solution)/shard_map/ppermute | solution.py:209
  71.3 2.2 %collective-permute-start.19 = (bf16[256,256]{1,0:T(8,128)(2,1)S(1)}, bf16[256,256]{1,0:T(8,128)(2,1)S(1)}, u32[]{:S(2)}, u32[]{:S(2)}) collective-permute-start(bf16[256,256]{1,0:T(8,128)(2,1)S(1)} %get-tuple-element.25), channel_id=1, source_target_pairs={{0,0},{1,1},{2,8},{3,9},{4,4},{5,5},{6,12},{7,13},{8,2},{9,3},{10,... | collective-permute-start | bytes 393224 | tf_op jit(solution)/shard_map/ppermute | solution.py:209
  74.5 3.7 %collective-permute-done.19.refs_7_ = bf16[256,256]{1,0:T(8,128)(2,1)S(1)} collective-permute-done((bf16[256,256]{1,0:T(8,128)(2,1)S(1)}, bf16[256,256]{1,0:T(8,128)(2,1)S(1)}, u32[]{:S(2)}, u32[]{:S(2)}) %collective-permute-start.19) | collective-permute-done | bytes 131104 | tf_op jit(solution)/shard_map/ppermute | solution.py:209
  78.9 2.6 %collective-permute-start.26 = (bf16[8,256,256]{2,1,0:T(8,128)(2,1)S(1)}, bf16[8,256,256]{2,1,0:T(8,128)(2,1)S(1)}, u32[]{:S(2)}, u32[]{:S(2)}) collective-permute-start(bf16[8,256,256]{2,1,0:T(8,128)(2,1)S(1)} %shard_map.93.own_ref), channel_id=1, source_target_pairs={{1,0},{0,1},{3,2},{2,3},{5,4},{4,5},{7,6},{6,7},{9,8},{8,9},{11,10... | collective-permute-start | bytes 3145736 | tf_op jit(solution)/shard_map/ppermute | solution.py:198
  81.5 2.5 %collective-permute-start.18 = (bf16[256,256]{1,0:T(8,128)(2,1)S(1)}, bf16[256,256]{1,0:T(8,128)(2,1)S(1)}, u32[]{:S(2)}, u32[]{:S(2)}) collective-permute-start(bf16[256,256]{1,0:T(8,128)(2,1)S(1)} %collective-permute-done.17.refs_6_), channel_id=1, source_target_pairs={{0,0},{1,1},{2,8},{3,9},{4,4},{5,5},{6,12},{7,13},{8,2},{9,3},{10,... | collective-permute-start | bytes 393224 | tf_op jit(solution)/shard_map/ppermute | solution.py:209
  84.0 2.3 %collective-permute-start.20 = (bf16[256,256]{1,0:T(8,128)(2,1)S(1)}, bf16[256,256]{1,0:T(8,128)(2,1)S(1)}, u32[]{:S(2)}, u32[]{:S(2)}) collective-permute-start(bf16[256,256]{1,0:T(8,128)(2,1)S(1)} %collective-permute-done.19.refs_7_), channel_id=1, source_target_pairs={{0,1},{1,0},{2,3},{3,2},{4,17},{5,16},{6,19},{7,18},{8,9},{9,8},{1... | collective-permute-start | bytes 393224 | tf_op jit(solution)/shard_map/ppermute | solution.py:209
  86.3 5.9 %collective-permute-done.27.refs_3_ = bf16[2,256,256]{2,1,0:T(8,128)(2,1)S(1)} collective-permute-done((bf16[2,256,256]{2,1,0:T(8,128)(2,1)S(1)}, bf16[2,256,256]{2,1,0:T(8,128)(2,1)S(1)}, u32[]{:S(2)}, u32[]{:S(2)}) %collective-permute-start.27) | collective-permute-done | bytes 262176 | tf_op jit(solution)/shard_map/ppermute | solution.py:192
  92.2 1.3 %shard_map.94.part_ref = f32[2,256,256]{2,1,0:T(8,128)S(1)} custom-call(s32[5,8]{1,0:T(8,128)S(1)} %pad_add_fusion.meta, bf16[8,256,256]{2,1,0:T(8,128)(2,1)S(1)} %shard_map.93.own_ref, bf16[8,256,256]{2,1,0:T(8,128)(2,1)S(1)} %collective-permute-done.26.other_ref, bf16[2,256,256]{2,1,0:T(8,128)(2,1)S(1)} %get-tuple-element.26.refs_1_.refs_0_, ...), custom_call_target="tpu_custom_call" | custom-call | flops 536870912 | bytes 6291456 | tf_op jit(solution)/shard_map/pallas_call | solution.py:23
  93.6 1.6 %shard_map.95 = (f32[2,256,256]{2,1,0:T(8,128)}, bf16[2,256,256]{2,1,0:T(8,128)(2,1)}) custom-call(s32[5,8]{1,0:T(8,128)S(1)} %pad_add_fusion.meta, bf16[256,256]{1,0:T(8,128)(2,1)S(1)} %collective-permute-done.18.same_ref, bf16[256,256]{1,0:T(8,128)(2,1)S(1)} %collective-permute-done.20.other_ref, f32[2,256,256]{2,1,0:T(8,128)S(1)} %shard_map.94.part_ref, ...), custom_call_target="tpu_custom_call" | custom-call | bytes 2097152 | tf_op jit(solution)/shard_map/pallas_call | solution.py:23
  (57 shorter events, 13.1 us)
Async XLA Ops:
  0.0 9.1 %copy-start = (s32[2,8,8]{2,1,0:T(8,128)S(1)}, s32[2,8,8]{2,1,0:T(8,128)}, u32[]{:S(2)}) copy-start(s32[2,8,8]{2,1,0:T(8,128)} %param.12) | copy-start | bytes 1540
  1.1 18.3 %collective-permute-start.8 = (bf16[2,256,256]{2,1,0:T(8,128)(2,1)S(1)}, bf16[2,256,256]{2,1,0:T(8,128)(2,1)S(1)}, u32[]{:S(2)}, u32[]{:S(2)}) collective-permute-start(bf16[2,256,256]{2,1,0:T(8,128)(2,1)S(1)} %bitcast_convert_fusion.refs_0_), channel_id=1, source_target_pairs={{4,0},{5,1},{6,2},{7,3},{0,4},{1,5},{2,6},{3,7},{12,8},{13,9},{14,... | collective-permute-start | bytes 786440 | tf_op jit(solution)/shard_map/ppermute | solution.py:201
  3.5 21.1 %collective-permute-start.7 = (bf16[2,256,256]{2,1,0:T(8,128)(2,1)S(1)}, bf16[2,256,256]{2,1,0:T(8,128)(2,1)S(1)}, u32[]{:S(2)}, u32[]{:S(2)}) collective-permute-start(bf16[2,256,256]{2,1,0:T(8,128)(2,1)S(1)} %bitcast_convert_fusion.refs_0_), channel_id=1, source_target_pairs={{2,0},{3,1},{0,2},{1,3},{6,4},{7,5},{4,6},{5,7},{10,8},{11,9},{8,1... | collective-permute-start | bytes 786440 | tf_op jit(solution)/shard_map/ppermute | solution.py:201
  4.8 9.9 %collective-permute-start.2 = (bf16[2,256,256]{2,1,0:T(8,128)(2,1)S(1)}, bf16[2,256,256]{2,1,0:T(8,128)(2,1)S(1)}, u32[]{:S(2)}, u32[]{:S(2)}) collective-permute-start(bf16[2,256,256]{2,1,0:T(8,128)(2,1)S(1)} %bitcast_convert_fusion.refs_0_), channel_id=1, source_target_pairs={{24,0},{16,8},{8,16},{0,24},{25,1},{17,9},{9,17},{1,25},{26,2},{18... | collective-permute-start | bytes 786440 | tf_op jit(solution)/shard_map/ppermute | solution.py:192
  5.0 13.1 %collective-permute-start.1 = (bf16[2,256,256]{2,1,0:T(8,128)(2,1)S(1)}, bf16[2,256,256]{2,1,0:T(8,128)(2,1)S(1)}, u32[]{:S(2)}, u32[]{:S(2)}) collective-permute-start(bf16[2,256,256]{2,1,0:T(8,128)(2,1)S(1)} %bitcast_convert_fusion.refs_0_), channel_id=1, source_target_pairs={{16,0},{24,8},{0,16},{8,24},{17,1},{25,9},{1,17},{9,25},{18,2},{26... | collective-permute-start | bytes 786440 | tf_op jit(solution)/shard_map/ppermute | solution.py:192
  6.2 11.8 %collective-permute-start = (bf16[2,256,256]{2,1,0:T(8,128)(2,1)S(1)}, bf16[2,256,256]{2,1,0:T(8,128)(2,1)S(1)}, u32[]{:S(2)}, u32[]{:S(2)}) collective-permute-start(bf16[2,256,256]{2,1,0:T(8,128)(2,1)S(1)} %bitcast_convert_fusion.refs_0_), channel_id=1, source_target_pairs={{8,0},{0,8},{24,16},{16,24},{9,1},{1,9},{25,17},{17,25},{10,2},{2,... | collective-permute-start | bytes 786440 | tf_op jit(solution)/shard_map/ppermute | solution.py:192
  10.8 1.6 %copy-start.1 = (bf16[2,8,256,256]{3,2,1,0:T(8,128)(2,1)S(1)}, bf16[2,8,256,256]{3,2,1,0:T(8,128)(2,1)}, u32[]{:S(2)}) copy-start(bf16[2,8,256,256]{3,2,1,0:T(8,128)(2,1)} %k_ref.1) | copy-start | bytes 6291460
  12.4 0.7 copy-start.3
  19.4 26.1 %copy-start.2 = (f32[2,1,256,256]{3,2,1,0:T(8,128)S(1)}, f32[2,1,256,256]{3,2,1,0:T(8,128)}, u32[]{:S(2)}) copy-start(f32[2,1,256,256]{3,2,1,0:T(8,128)} %param.8) | copy-start | bytes 1572868
  19.4 13.1 %collective-permute-start.9 = (bf16[2,256,256]{2,1,0:T(8,128)(2,1)S(1)}, bf16[2,256,256]{2,1,0:T(8,128)(2,1)S(1)}, u32[]{:S(2)}, u32[]{:S(2)}) collective-permute-start(bf16[2,256,256]{2,1,0:T(8,128)(2,1)S(1)} %shard_map.87.refs_2_), channel_id=1, source_target_pairs={{2,0},{3,1},{0,2},{1,3},{6,4},{7,5},{4,6},{5,7},{10,8},{11,9},{8,1... | collective-permute-start | bytes 786440 | tf_op jit(solution)/shard_map/ppermute | solution.py:201
  19.7 12.9 %collective-permute-start.11 = (bf16[2,256,256]{2,1,0:T(8,128)(2,1)S(1)}, bf16[2,256,256]{2,1,0:T(8,128)(2,1)S(1)}, u32[]{:S(2)}, u32[]{:S(2)}) collective-permute-start(bf16[2,256,256]{2,1,0:T(8,128)(2,1)S(1)} %get-tuple-element.20.refs_1_.refs_0_), channel_id=1, source_target_pairs={{16,0},{24,8},{0,16},{8,24},{17,1},{25,9},{1,17},{9,25},{18,2},{26... | collective-permute-start | bytes 786440 | tf_op jit(solution)/shard_map/ppermute | solution.py:192
  21.4 11.2 %collective-permute-start.10 = (bf16[2,256,256]{2,1,0:T(8,128)(2,1)S(1)}, bf16[2,256,256]{2,1,0:T(8,128)(2,1)S(1)}, u32[]{:S(2)}, u32[]{:S(2)}) collective-permute-start(bf16[2,256,256]{2,1,0:T(8,128)(2,1)S(1)} %get-tuple-element.20.refs_1_.refs_0_), channel_id=1, source_target_pairs={{8,0},{0,8},{24,16},{16,24},{9,1},{1,9},{25,17},{17,25},{10,2},{2,... | collective-permute-start | bytes 786440 | tf_op jit(solution)/shard_map/ppermute | solution.py:192
  21.6 10.9 %collective-permute-start.3 = (bf16[256,256]{1,0:T(8,128)(2,1)S(1)}, bf16[256,256]{1,0:T(8,128)(2,1)S(1)}, u32[]{:S(2)}, u32[]{:S(2)}) collective-permute-start(bf16[256,256]{1,0:T(8,128)(2,1)S(1)} %get-tuple-element.18), channel_id=1, source_target_pairs={{0,0},{1,1},{2,2},{3,3},{4,16},{5,17},{6,18},{7,19},{8,8},{9,9},{1... | collective-permute-start | bytes 393224 | tf_op jit(solution)/shard_map/ppermute | solution.py:209
  24.6 8.0 %collective-permute-start.5 = (bf16[256,256]{1,0:T(8,128)(2,1)S(1)}, bf16[256,256]{1,0:T(8,128)(2,1)S(1)}, u32[]{:S(2)}, u32[]{:S(2)}) collective-permute-start(bf16[256,256]{1,0:T(8,128)(2,1)S(1)} %get-tuple-element.19), channel_id=1, source_target_pairs={{0,0},{1,1},{2,8},{3,9},{4,4},{5,5},{6,12},{7,13},{8,2},{9,3},{10,... | collective-permute-start | bytes 393224 | tf_op jit(solution)/shard_map/ppermute | solution.py:209
  33.2 12.3 %collective-permute-start.12 = (bf16[8,256,256]{2,1,0:T(8,128)(2,1)S(1)}, bf16[8,256,256]{2,1,0:T(8,128)(2,1)S(1)}, u32[]{:S(2)}, u32[]{:S(2)}) collective-permute-start(bf16[8,256,256]{2,1,0:T(8,128)(2,1)S(1)} %shard_map.88.own_ref), channel_id=1, source_target_pairs={{1,0},{0,1},{3,2},{2,3},{5,4},{4,5},{7,6},{6,7},{9,8},{8,9},{11,10... | collective-permute-start | bytes 3145736 | tf_op jit(solution)/shard_map/ppermute | solution.py:198
  34.8 10.7 %collective-permute-start.13 = (bf16[2,256,256]{2,1,0:T(8,128)(2,1)S(1)}, bf16[2,256,256]{2,1,0:T(8,128)(2,1)S(1)}, u32[]{:S(2)}, u32[]{:S(2)}) collective-permute-start(bf16[2,256,256]{2,1,0:T(8,128)(2,1)S(1)} %collective-permute-done.11.refs_5_.refs_2_), channel_id=1, source_target_pairs={{8,0},{0,8},{24,16},{16,24},{9,1},{1,9},{25,17},{17,25},{10,2},{2,... | collective-permute-start | bytes 786440 | tf_op jit(solution)/shard_map/ppermute | solution.py:192
  36.1 10.9 %collective-permute-start.4 = (bf16[256,256]{1,0:T(8,128)(2,1)S(1)}, bf16[256,256]{1,0:T(8,128)(2,1)S(1)}, u32[]{:S(2)}, u32[]{:S(2)}) collective-permute-start(bf16[256,256]{1,0:T(8,128)(2,1)S(1)} %collective-permute-done.3.refs_6_), channel_id=1, source_target_pairs={{0,0},{1,1},{2,8},{3,9},{4,4},{5,5},{6,12},{7,13},{8,2},{9,3},{10,... | collective-permute-start | bytes 393224 | tf_op jit(solution)/shard_map/ppermute | solution.py:209
  38.2 9.1 %collective-permute-start.6 = (bf16[256,256]{1,0:T(8,128)(2,1)S(1)}, bf16[256,256]{1,0:T(8,128)(2,1)S(1)}, u32[]{:S(2)}, u32[]{:S(2)}) collective-permute-start(bf16[256,256]{1,0:T(8,128)(2,1)S(1)} %collective-permute-done.5.refs_7_), channel_id=1, source_target_pairs={{0,1},{1,0},{2,3},{3,2},{4,17},{5,16},{6,19},{7,18},{8,9},{9,8},{1... | collective-permute-start | bytes 393224 | tf_op jit(solution)/shard_map/ppermute | solution.py:209
  48.1 8.4 %collective-permute-start.16 = (bf16[2,256,256]{2,1,0:T(8,128)(2,1)S(1)}, bf16[2,256,256]{2,1,0:T(8,128)(2,1)S(1)}, u32[]{:S(2)}, u32[]{:S(2)}) collective-permute-start(bf16[2,256,256]{2,1,0:T(8,128)(2,1)S(1)} %get-tuple-element.23.refs_0_), channel_id=1, source_target_pairs={{24,0},{16,8},{8,16},{0,24},{25,1},{17,9},{9,17},{1,25},{26,2},{18... | collective-permute-start | bytes 786440 | tf_op jit(solution)/shard_map/ppermute | solution.py:192
  48.1 13.1 %collective-permute-start.15 = (bf16[2,256,256]{2,1,0:T(8,128)(2,1)S(1)}, bf16[2,256,256]{2,1,0:T(8,128)(2,1)S(1)}, u32[]{:S(2)}, u32[]{:S(2)}) collective-permute-start(bf16[2,256,256]{2,1,0:T(8,128)(2,1)S(1)} %get-tuple-element.23.refs_0_), channel_id=1, source_target_pairs={{16,0},{24,8},{0,16},{8,24},{17,1},{25,9},{1,17},{9,25},{18,2},{26... | collective-permute-start | bytes 786440 | tf_op jit(solution)/shard_map/ppermute | solution.py:192
  48.2 13.0 %collective-permute-start.14 = (bf16[2,256,256]{2,1,0:T(8,128)(2,1)S(1)}, bf16[2,256,256]{2,1,0:T(8,128)(2,1)S(1)}, u32[]{:S(2)}, u32[]{:S(2)}) collective-permute-start(bf16[2,256,256]{2,1,0:T(8,128)(2,1)S(1)} %get-tuple-element.23.refs_0_), channel_id=1, source_target_pairs={{8,0},{0,8},{24,16},{16,24},{9,1},{1,9},{25,17},{17,25},{10,2},{2,... | collective-permute-start | bytes 786440 | tf_op jit(solution)/shard_map/ppermute | solution.py:192
  50.8 14.4 %collective-permute-start.22 = (bf16[2,256,256]{2,1,0:T(8,128)(2,1)S(1)}, bf16[2,256,256]{2,1,0:T(8,128)(2,1)S(1)}, u32[]{:S(2)}, u32[]{:S(2)}) collective-permute-start(bf16[2,256,256]{2,1,0:T(8,128)(2,1)S(1)} %get-tuple-element.23.refs_0_), channel_id=1, source_target_pairs={{4,0},{5,1},{6,2},{7,3},{0,4},{1,5},{2,6},{3,7},{12,8},{13,9},{14,... | collective-permute-start | bytes 786440 | tf_op jit(solution)/shard_map/ppermute | solution.py:201
  51.9 19.4 %collective-permute-start.21 = (bf16[2,256,256]{2,1,0:T(8,128)(2,1)S(1)}, bf16[2,256,256]{2,1,0:T(8,128)(2,1)S(1)}, u32[]{:S(2)}, u32[]{:S(2)}) collective-permute-start(bf16[2,256,256]{2,1,0:T(8,128)(2,1)S(1)} %get-tuple-element.23.refs_0_), channel_id=1, source_target_pairs={{2,0},{3,1},{0,2},{1,3},{6,4},{7,5},{4,6},{5,7},{10,8},{11,9},{8,1... | collective-permute-start | bytes 786440 | tf_op jit(solution)/shard_map/ppermute | solution.py:201
  65.2 13.0 %collective-permute-start.23 = (bf16[2,256,256]{2,1,0:T(8,128)(2,1)S(1)}, bf16[2,256,256]{2,1,0:T(8,128)(2,1)S(1)}, u32[]{:S(2)}, u32[]{:S(2)}) collective-permute-start(bf16[2,256,256]{2,1,0:T(8,128)(2,1)S(1)} %shard_map.92.refs_2_), channel_id=1, source_target_pairs={{2,0},{3,1},{0,2},{1,3},{6,4},{7,5},{4,6},{5,7},{10,8},{11,9},{8,1... | collective-permute-start | bytes 786440 | tf_op jit(solution)/shard_map/ppermute | solution.py:201
  65.2 13.0 %collective-permute-start.25 = (bf16[2,256,256]{2,1,0:T(8,128)(2,1)S(1)}, bf16[2,256,256]{2,1,0:T(8,128)(2,1)S(1)}, u32[]{:S(2)}, u32[]{:S(2)}) collective-permute-start(bf16[2,256,256]{2,1,0:T(8,128)(2,1)S(1)} %get-tuple-element.26.refs_1_.refs_0_), channel_id=1, source_target_pairs={{16,0},{24,8},{0,16},{8,24},{17,1},{25,9},{1,17},{9,25},{18,2},{26... | collective-permute-start | bytes 786440 | tf_op jit(solution)/shard_map/ppermute | solution.py:192
  65.3 12.9 %collective-permute-start.24 = (bf16[2,256,256]{2,1,0:T(8,128)(2,1)S(1)}, bf16[2,256,256]{2,1,0:T(8,128)(2,1)S(1)}, u32[]{:S(2)}, u32[]{:S(2)}) collective-permute-start(bf16[2,256,256]{2,1,0:T(8,128)(2,1)S(1)} %get-tuple-element.26.refs_1_.refs_0_), channel_id=1, source_target_pairs={{8,0},{0,8},{24,16},{16,24},{9,1},{1,9},{25,17},{17,25},{10,2},{2,... | collective-permute-start | bytes 786440 | tf_op jit(solution)/shard_map/ppermute | solution.py:192
  66.2 8.4 %collective-permute-start.17 = (bf16[256,256]{1,0:T(8,128)(2,1)S(1)}, bf16[256,256]{1,0:T(8,128)(2,1)S(1)}, u32[]{:S(2)}, u32[]{:S(2)}) collective-permute-start(bf16[256,256]{1,0:T(8,128)(2,1)S(1)} %get-tuple-element.24), channel_id=1, source_target_pairs={{0,0},{1,1},{2,2},{3,3},{4,16},{5,17},{6,18},{7,19},{8,8},{9,9},{1... | collective-permute-start | bytes 393224 | tf_op jit(solution)/shard_map/ppermute | solution.py:209
  71.3 6.9 %collective-permute-start.19 = (bf16[256,256]{1,0:T(8,128)(2,1)S(1)}, bf16[256,256]{1,0:T(8,128)(2,1)S(1)}, u32[]{:S(2)}, u32[]{:S(2)}) collective-permute-start(bf16[256,256]{1,0:T(8,128)(2,1)S(1)} %get-tuple-element.25), channel_id=1, source_target_pairs={{0,0},{1,1},{2,8},{3,9},{4,4},{5,5},{6,12},{7,13},{8,2},{9,3},{10,... | collective-permute-start | bytes 393224 | tf_op jit(solution)/shard_map/ppermute | solution.py:209
  78.9 13.3 %collective-permute-start.26 = (bf16[8,256,256]{2,1,0:T(8,128)(2,1)S(1)}, bf16[8,256,256]{2,1,0:T(8,128)(2,1)S(1)}, u32[]{:S(2)}, u32[]{:S(2)}) collective-permute-start(bf16[8,256,256]{2,1,0:T(8,128)(2,1)S(1)} %shard_map.93.own_ref), channel_id=1, source_target_pairs={{1,0},{0,1},{3,2},{2,3},{5,4},{4,5},{7,6},{6,7},{9,8},{8,9},{11,10... | collective-permute-start | bytes 3145736 | tf_op jit(solution)/shard_map/ppermute | solution.py:198
  81.5 10.7 %collective-permute-start.27 = (bf16[2,256,256]{2,1,0:T(8,128)(2,1)S(1)}, bf16[2,256,256]{2,1,0:T(8,128)(2,1)S(1)}, u32[]{:S(2)}, u32[]{:S(2)}) collective-permute-start(bf16[2,256,256]{2,1,0:T(8,128)(2,1)S(1)} %collective-permute-done.25.refs_5_.refs_2_), channel_id=1, source_target_pairs={{8,0},{0,8},{24,16},{16,24},{9,1},{1,9},{25,17},{17,25},{10,2},{2,... | collective-permute-start | bytes 786440 | tf_op jit(solution)/shard_map/ppermute | solution.py:192
  81.5 12.0 %collective-permute-start.18 = (bf16[256,256]{1,0:T(8,128)(2,1)S(1)}, bf16[256,256]{1,0:T(8,128)(2,1)S(1)}, u32[]{:S(2)}, u32[]{:S(2)}) collective-permute-start(bf16[256,256]{1,0:T(8,128)(2,1)S(1)} %collective-permute-done.17.refs_6_), channel_id=1, source_target_pairs={{0,0},{1,1},{2,8},{3,9},{4,4},{5,5},{6,12},{7,13},{8,2},{9,3},{10,... | collective-permute-start | bytes 393224 | tf_op jit(solution)/shard_map/ppermute | solution.py:209
  84.0 9.5 %collective-permute-start.20 = (bf16[256,256]{1,0:T(8,128)(2,1)S(1)}, bf16[256,256]{1,0:T(8,128)(2,1)S(1)}, u32[]{:S(2)}, u32[]{:S(2)}) collective-permute-start(bf16[256,256]{1,0:T(8,128)(2,1)S(1)} %collective-permute-done.19.refs_7_), channel_id=1, source_target_pairs={{0,1},{1,0},{2,3},{3,2},{4,17},{5,16},{6,19},{7,18},{8,9},{9,8},{1... | collective-permute-start | bytes 393224 | tf_op jit(solution)/shard_map/ppermute | solution.py:209
  (1 other events, 0.7 us)

commit v2 on v1

--- a/solution.py
+++ b/solution.py
@@ -60,6 +60,17 @@
     )
 
 
+def piece_blocks(refs, rows):
+    found, refs, size = [], list(refs), refs[0].shape[0]
+    for step in range(rows):
+        blocks = []
+        while len(blocks) < size:
+            ref = refs.pop(0)
+            blocks += [(ref, at) for at in range(ref.shape[0])]
+        found.append(blocks)
+    return found
+
+
 def coupled_body(rows, meta, k_ref, *refs):
     out_ref, same_ref, other_ref = refs[-3:]
     orb_rows, virt, _ = out_ref.shape
@@ -70,19 +81,20 @@
             left = k_ref[step, :, t * virt : (t + 1) * virt]
             part = jnp.dot(left, refs[step][t], preferred_element_type=jnp.float32)
             total = part if total is None else total + part
-    out_ref[...] = total.astype(out_ref.dtype).reshape(out_ref.shape)
-    same_ref[...] = out_ref[side]
-    other_ref[...] = out_ref[1 - side]
-
-
-def coupled_blocks(rows, meta, kept, pieces):
+    first, second = total[:virt].astype(out_ref.dtype), total[virt:].astype(out_ref.dtype)
+    out_ref[0], out_ref[1] = first, second
+    same_ref[...] = jnp.where(side == 0, first, second)
+    other_ref[...] = jnp.where(side == 0, second, first)
+
+
+def coupled_blocks(rows, meta, kept, pieces, other):
     orb_rows, virt, _ = pieces[0].shape
     count = rows * orb_rows
     block = jax.ShapeDtypeStruct((virt, virt), jnp.bfloat16)
     shape = (jax.ShapeDtypeStruct((orb_rows, virt, virt), jnp.bfloat16), block, block)
     body = functools.partial(coupled_body, rows)
     flops, moved = 2 * orb_rows * count * virt**3, 2 * (orb_rows + 1) * count * virt**2
-    return call(body, shape, [SMEM] + [VMEM] * (1 + len(pieces)), flops, moved, meta, kept, *pieces)
+    return call(body, shape, [SMEM] + [VMEM] * (2 + len(pieces)), flops, moved, meta, kept, *pieces, other)
 
 
 def column_body(meta, *refs):
@@ -129,6 +141,7 @@
 def first_body(rows, meta, own_ref, other_ref, *refs):
     state_ref, coulomb_ref, inverse_ref, out_ref = refs[-4:]
     orb_rows = out_ref.shape[0]
+    blocks = piece_blocks(refs[:-4], rows)
     my_row, side = meta[2 * orb_rows, 0], meta[2 * orb_rows, 1] % 2
     total = None
     for step in range(rows):
@@ -138,19 +151,21 @@
                 jnp.where(side == t, own_ref[at * orb_rows + i], other_ref[at * orb_rows + i]) for i in range(orb_rows)
             ]
             left = masked_pair(meta, at * orb_rows + t, left)
-            part = jnp.dot(left, refs[step][t], preferred_element_type=jnp.float32)
+            ref, place = blocks[step][t]
+            part = jnp.dot(left, ref[place], preferred_element_type=jnp.float32)
             total = part if total is None else total + part
     linear = coulomb_ref[...].astype(jnp.float32) + coupling * refs[0][...].astype(jnp.float32)
     residual = linear + coupling * coupling * total.reshape(out_ref.shape)
     out_ref[...] = damping * state_ref[...] - residual * inverse_ref[...]
 
 
-def second_body(meta, same_ref, other_ref, part_ref, inverse_ref, out_ref, half_ref):
+def second_body(meta, same_ref, other_ref, part_ref, inverse_ref, out_ref, *half_refs):
     side = meta[2 * out_ref.shape[0], 1] % 2
     for ref, at in ((same_ref, side), (other_ref, 1 - side)):
         state = part_ref[at] - coupling * turned(ref[...]) * inverse_ref[at]
         out_ref[at] = state
-        half_ref[at] = state.astype(half_ref.dtype)
+        for half_ref in half_refs:
+            half_ref[at] = state.astype(half_ref.dtype)
 
 
 def first_update(rows, meta, own, other, c_pieces, state, coulomb_own, inverse):
@@ -163,8 +178,9 @@
     )
 
 
-def second_update(meta, same, other, part, inverse):
+def second_update(meta, same, other, part, inverse, with_half):
     shape = (jax.ShapeDtypeStruct(part.shape, jnp.float32), jax.ShapeDtypeStruct(part.shape, jnp.bfloat16))
+    shape = shape if with_half else shape[:1]
     return call(second_body, shape, [SMEM] + [VMEM] * 4, 0, 16 * part.size, meta, same, other, part, inverse)
 
 
@@ -239,21 +255,23 @@
         column = {0: half, 1: from_chip(half, 1)}
         for step in range(2, halves, 2):
             column[step] = from_chip(half, step)
-        coupled, same, other = coupled_blocks(rows, meta, kept, a_pieces)
-        c_pieces = {0: coupled, 1: from_row(coupled, 1)}
+        coupled, same, other = coupled_blocks(rows, meta, kept, a_pieces, column[1])
+        near = from_row(coupled, 1)
+        c_pieces, far = [coupled, near], []
         for step in range(2, rows, 2):
-            c_pieces[step] = from_row(coupled, step)
-            c_pieces[step + 1] = from_row(c_pieces[step], 1)
-        c_pieces = [c_pieces[step] for step in range(rows)]
+            piece = from_row(coupled, step)
+            far += [from_row(piece[0:1], 1), from_row(near[1:2], step)]
+            c_pieces += [piece, *far[-2:]]
         same, other = crossing(same, high_parts), crossing(other, last_bits)
         for step in range(2, halves, 2):
             column[step] = tied(column[step], coupled)
             column[step + 1] = from_chip(column[step], 1)
         column = [column[step] for step in range(halves)]
-        own = whole_column(meta, column, [c_pieces[1], c_pieces[2], same, other])
+        own = whole_column(meta, column, [*far, same, other])
         same, other = crossing(same, last_bits), crossing(other, high_parts, 1)
         part = first_update(rows, meta, own, swapped(own), c_pieces, state, coulomb_own, inverse)
-        state, half = second_update(meta, same, other, part, inverse)
+        state, *halves_out = second_update(meta, same, other, part, inverse, sweep_index < ITERS - 1)
+        half = halves_out[0] if halves_out else None
     return state[:, None]
 
 

time: 95.8 us -> 97.7 us (1.020); the launches traced: 95.2 us -> 96 us
    ppermute x12 -> x14, waiting for transfers between devices: 21.7 us -> 17.1 us  [from_row(): return lax.ppermute(x, 'row', [(r ^ step, r) for r in range(rows)])]
    ppermute x8, waiting for transfers between devices: 9.89 us -> 14.1 us  [crossing(): return lax.ppermute(x, ('row', 'col'), pairs)]
    ppermute x12 -> x14, starting transfers between devices: 9.54 us -> 12.4 us  [from_row(): return lax.ppermute(x, 'row', [(r ^ step, r) for r in range(rows)])]
    ppermute x8, starting transfers between devices: 23.6 us -> 21.5 us  [crossing(): return lax.ppermute(x, ('row', 'col'), pairs)]
    ppermute x6, starting transfers between devices: 5.96 us -> 4.59 us  [from_chip(): return lax.ppermute(x, 'col', [(c ^ 2 * step, c) for c in range(cols)])]
    ppermute x6, waiting for transfers between devices: 2.59 us -> 3.7 us  [from_chip(): return lax.ppermute(x, 'col', [(c ^ 2 * step, c) for c in range(cols)])]
  transfers between devices with their start and end apart: 28 -> 30, of which waited for: 10 -> 16; matrix products, arithmetic and copies ran while one was open for 4% -> 4% of each run, Pallas kernels for 7% -> 7%
where the time goes in v2:
time: 97.7 us; the launch traced here: 96 us
  starting transfers between devices  43.5 us (45%)
  waiting for transfers between devices  34.9 us (36%)
  Pallas kernels  9.93 us (10%)
  local copies, waits for them, and re-layouts  4.64 us (5%)
  other arithmetic  2.77 us (3%)
    ppermute x8, starting transfers between devices, crossing(): return lax.ppermute(x, ('row', 'col'), pairs)  21.5 us
    ppermute x14, waiting for transfers between devices, from_row(): return lax.ppermute(x, 'row', [(r ^ step, r) for r in range(rows)])  17.1 us
    ppermute x8, waiting for transfers between devices, crossing(): return lax.ppermute(x, ('row', 'col'), pairs)  14.1 us
    ppermute x14, starting transfers between devices, from_row(): return lax.ppermute(x, 'row', [(r ^ step, r) for r in range(rows)])  12.4 us
    pallas_call x9, Pallas kernels, call(): pl.pallas_call(body, out_shape=out_shape, in_specs=in_specs, out_specs=VM...  9.93 us
    ppermute x2, starting transfers between devices, swapped(): return lax.ppermute(x, 'col', [(c ^ 1, c) for c in range(cols)])  4.97 us
    ppermute x6, starting transfers between devices, from_chip(): return lax.ppermute(x, 'col', [(c ^ 2 * step, c) for c in range(cols)])  4.59 us
    ppermute x6, waiting for transfers between devices, from_chip(): return lax.ppermute(x, 'col', [(c ^ 2 * step, c) for c in range(cols)])  3.7 us
  transfers between devices with their start and end apart: 30, of which 16 were waited for; matrix products, arithmetic and copies ran while one was open for 4% of the time, Pallas kernels for 7%

profile of v2, /device:TPU:7, one launch (start us, length us, event | category | flops | bytes accessed | tf_op | source)
XLA Modules:
  0.0 96.0 jit_solution(318166516610606353)
XLA Ops:
  1.1 2.4 %collective-permute-start.8 = (bf16[2,256,256]{2,1,0:T(8,128)(2,1)S(1)}, bf16[2,256,256]{2,1,0:T(8,128)(2,1)S(1)}, u32[]{:S(2)}, u32[]{:S(2)}) collective-permute-start(bf16[2,256,256]{2,1,0:T(8,128)(2,1)S(1)} %bitcast_convert_fusion.refs_0_), channel_id=1, source_target_pairs={{4,0},{5,1},{6,2},{7,3},{0,4},{1,5},{2,6},{3,7},{12,8},{13,9},{14,... | collective-permute-start | bytes 786440 | tf_op jit(solution)/shard_map/ppermute | solution.py:217
  3.5 1.3 %collective-permute-start.3 = (bf16[2,256,256]{2,1,0:T(8,128)(2,1)S(1)}, bf16[2,256,256]{2,1,0:T(8,128)(2,1)S(1)}, u32[]{:S(2)}, u32[]{:S(2)}) collective-permute-start(bf16[2,256,256]{2,1,0:T(8,128)(2,1)S(1)} %bitcast_convert_fusion.refs_0_), channel_id=1, source_target_pairs={{2,0},{3,1},{0,2},{1,3},{6,4},{7,5},{4,6},{5,7},{10,8},{11,9},{8,1... | collective-permute-start | bytes 786440 | tf_op jit(solution)/shard_map/ppermute | solution.py:217
  5.0 1.2 %collective-permute-start.1 = (bf16[2,256,256]{2,1,0:T(8,128)(2,1)S(1)}, bf16[2,256,256]{2,1,0:T(8,128)(2,1)S(1)}, u32[]{:S(2)}, u32[]{:S(2)}) collective-permute-start(bf16[2,256,256]{2,1,0:T(8,128)(2,1)S(1)} %bitcast_convert_fusion.refs_0_), channel_id=1, source_target_pairs={{16,0},{24,8},{0,16},{8,24},{17,1},{25,9},{1,17},{9,25},{18,2},{26... | collective-permute-start | bytes 786440 | tf_op jit(solution)/shard_map/ppermute | solution.py:208
  10.8 1.6 %copy-done.1 = bf16[2,8,256,256]{3,2,1,0:T(8,128)(2,1)S(1)} copy-done((bf16[2,8,256,256]{3,2,1,0:T(8,128)(2,1)S(1)}, bf16[2,8,256,256]{3,2,1,0:T(8,128)(2,1)}, u32[]{:S(2)}) %copy-start.1) | copy-done | bytes 2097176
  14.7 3.3 %collective-permute-done.1.refs_2_ = bf16[2,256,256]{2,1,0:T(8,128)(2,1)S(1)} collective-permute-done((bf16[2,256,256]{2,1,0:T(8,128)(2,1)S(1)}, bf16[2,256,256]{2,1,0:T(8,128)(2,1)S(1)}, u32[]{:S(2)}, u32[]{:S(2)}) %collective-permute-start.1) | collective-permute-done | bytes 262176 | tf_op jit(solution)/shard_map/ppermute | solution.py:208
  18.0 1.3 %shard_map.86 = (bf16[2,256,256]{2,1,0:T(8,128)(2,1)S(1)}, bf16[256,256]{1,0:T(8,128)(2,1)S(1)}, bf16[256,256]{1,0:T(8,128)(2,1)S(1)}) custom-call(s32[5,8]{1,0:T(8,128)S(1)} %pad_add_fusion.meta, bf16[4,512,512]{2,1,0:T(8,128)(2,1)S(1)} %get-tuple-element.16.k_ref, bf16[2,256,256]{2,1,0:T(8,128)(2,1)S(1)} %bitcast_convert_fusion.refs_0_, ...), custom_call_target="tpu_custom_call" | custom-call | flops 536870912 | bytes 3145728 | tf_op jit(solution)/shard_map/pallas_call | solution.py:23
  19.4 1.8 %collective-permute-start.12 = (bf16[2,256,256]{2,1,0:T(8,128)(2,1)S(1)}, bf16[2,256,256]{2,1,0:T(8,128)(2,1)S(1)}, u32[]{:S(2)}, u32[]{:S(2)}) collective-permute-start(bf16[2,256,256]{2,1,0:T(8,128)(2,1)S(1)} %get-tuple-element.19.refs_1_.refs_0_), channel_id=1, source_target_pairs={{8,0},{0,8},{24,16},{16,24},{9,1},{1,9},{25,17},{17,25},{10,2},{2,... | collective-permute-start | bytes 786440 | tf_op jit(solution)/shard_map/ppermute | solution.py:208
  21.6 2.9 %collective-permute-start.4 = (bf16[256,256]{1,0:T(8,128)(2,1)S(1)}, bf16[256,256]{1,0:T(8,128)(2,1)S(1)}, u32[]{:S(2)}, u32[]{:S(2)}) collective-permute-start(bf16[256,256]{1,0:T(8,128)(2,1)S(1)} %get-tuple-element.17), channel_id=1, source_target_pairs={{0,0},{1,1},{2,2},{3,3},{4,16},{5,17},{6,18},{7,19},{8,8},{9,9},{1... | collective-permute-start | bytes 393224 | tf_op jit(solution)/shard_map/ppermute | solution.py:225
  24.5 3.1 %collective-permute-start.6 = (bf16[256,256]{1,0:T(8,128)(2,1)S(1)}, bf16[256,256]{1,0:T(8,128)(2,1)S(1)}, u32[]{:S(2)}, u32[]{:S(2)}) collective-permute-start(bf16[256,256]{1,0:T(8,128)(2,1)S(1)} %get-tuple-element.18), channel_id=1, source_target_pairs={{0,0},{1,1},{2,8},{3,9},{4,4},{5,5},{6,12},{7,13},{8,2},{9,3},{10,... | collective-permute-start | bytes 393224 | tf_op jit(solution)/shard_map/ppermute | solution.py:225
  29.6 2.5 %collective-permute-done.6.refs_7_ = bf16[256,256]{1,0:T(8,128)(2,1)S(1)} collective-permute-done((bf16[256,256]{1,0:T(8,128)(2,1)S(1)}, bf16[256,256]{1,0:T(8,128)(2,1)S(1)}, u32[]{:S(2)}, u32[]{:S(2)}) %collective-permute-start.6) | collective-permute-done | bytes 131104 | tf_op jit(solution)/shard_map/ppermute | solution.py:225
  32.0 1.9 %collective-permute-done.13.refs_5_.refs_4_ = bf16[1,256,256]{2,1,0:T(8,128)(2,1)S(1)} collective-permute-done((bf16[1,256,256]{2,1,0:T(8,128)(2,1)S(1)}, bf16[1,256,256]{2,1,0:T(8,128)(2,1)S(1)}, u32[]{:S(2)}, u32[]{:S(2)}) %collective-permute-start.13) | collective-permute-done | bytes 131104 | tf_op jit(solution)/shard_map/ppermute | solution.py:208
  35.6 3.3 %collective-permute-start.14 = (bf16[8,256,256]{2,1,0:T(8,128)(2,1)S(1)}, bf16[8,256,256]{2,1,0:T(8,128)(2,1)S(1)}, u32[]{:S(2)}, u32[]{:S(2)}) collective-permute-start(bf16[8,256,256]{2,1,0:T(8,128)(2,1)S(1)} %shard_map.88.own_ref), channel_id=1, source_target_pairs={{1,0},{0,1},{3,2},{2,3},{5,4},{4,5},{7,6},{6,7},{9,8},{8,9},{11,10... | collective-permute-start | bytes 3145736 | tf_op jit(solution)/shard_map/ppermute | solution.py:214
  38.9 1.9 %collective-permute-start.5 = (bf16[256,256]{1,0:T(8,128)(2,1)S(1)}, bf16[256,256]{1,0:T(8,128)(2,1)S(1)}, u32[]{:S(2)}, u32[]{:S(2)}) collective-permute-start(bf16[256,256]{1,0:T(8,128)(2,1)S(1)} %collective-permute-done.4.refs_6_), channel_id=1, source_target_pairs={{0,0},{1,1},{2,8},{3,9},{4,4},{5,5},{6,12},{7,13},{8,2},{9,3},{10,... | collective-permute-start | bytes 393224 | tf_op jit(solution)/shard_map/ppermute | solution.py:225
  40.8 2.0 %collective-permute-start.7 = (bf16[256,256]{1,0:T(8,128)(2,1)S(1)}, bf16[256,256]{1,0:T(8,128)(2,1)S(1)}, u32[]{:S(2)}, u32[]{:S(2)}) collective-permute-start(bf16[256,256]{1,0:T(8,128)(2,1)S(1)} %collective-permute-done.6.refs_7_), channel_id=1, source_target_pairs={{0,1},{1,0},{2,3},{3,2},{4,17},{5,16},{6,19},{7,18},{8,9},{9,8},{1... | collective-permute-start | bytes 393224 | tf_op jit(solution)/shard_map/ppermute | solution.py:225
  42.8 1.4 %shard_map.89.part_ref = f32[2,256,256]{2,1,0:T(8,128)S(1)} custom-call(s32[5,8]{1,0:T(8,128)S(1)} %pad_add_fusion.meta, bf16[8,256,256]{2,1,0:T(8,128)(2,1)S(1)} %shard_map.88.own_ref, bf16[8,256,256]{2,1,0:T(8,128)(2,1)S(1)} %collective-permute-done.14.other_ref, bf16[2,256,256]{2,1,0:T(8,128)(2,1)S(1)} %get-tuple-element.19.refs_1_.refs_0_, ...), custom_call_target="tpu_custom_call" | custom-call | flops 536870912 | bytes 6291456 | tf_op jit(solution)/shard_map/pallas_call | solution.py:23
  44.2 2.6 %collective-permute-done.5.same_ref = bf16[256,256]{1,0:T(8,128)(2,1)S(1)} collective-permute-done((bf16[256,256]{1,0:T(8,128)(2,1)S(1)}, bf16[256,256]{1,0:T(8,128)(2,1)S(1)}, u32[]{:S(2)}, u32[]{:S(2)}) %collective-permute-start.5) | collective-permute-done | bytes 131104 | tf_op jit(solution)/shard_map/ppermute | solution.py:225
  49.4 3.5 %collective-permute-start.16 = (bf16[2,256,256]{2,1,0:T(8,128)(2,1)S(1)}, bf16[2,256,256]{2,1,0:T(8,128)(2,1)S(1)}, u32[]{:S(2)}, u32[]{:S(2)}) collective-permute-start(bf16[2,256,256]{2,1,0:T(8,128)(2,1)S(1)} %get-tuple-element.22.refs_0_), channel_id=1, source_target_pairs={{16,0},{24,8},{0,16},{8,24},{17,1},{25,9},{1,17},{9,25},{18,2},{26... | collective-permute-start | bytes 786440 | tf_op jit(solution)/shard_map/ppermute | solution.py:208
  53.1 3.4 %collective-permute-done.18.refs_4_.refs_1_ = bf16[2,256,256]{2,1,0:T(8,128)(2,1)S(1)} collective-permute-done((bf16[2,256,256]{2,1,0:T(8,128)(2,1)S(1)}, bf16[2,256,256]{2,1,0:T(8,128)(2,1)S(1)}, u32[]{:S(2)}, u32[]{:S(2)}) %collective-permute-start.18) | collective-permute-done | bytes 262176 | tf_op jit(solution)/shard_map/ppermute | solution.py:217
  57.5 5.9 %collective-permute-done.16.refs_2_ = bf16[2,256,256]{2,1,0:T(8,128)(2,1)S(1)} collective-permute-done((bf16[2,256,256]{2,1,0:T(8,128)(2,1)S(1)}, bf16[2,256,256]{2,1,0:T(8,128)(2,1)S(1)}, u32[]{:S(2)}, u32[]{:S(2)}) %collective-permute-start.16) | collective-permute-done | bytes 262176 | tf_op jit(solution)/shard_map/ppermute | solution.py:208
  63.5 1.3 %shard_map.91 = (bf16[2,256,256]{2,1,0:T(8,128)(2,1)S(1)}, bf16[256,256]{1,0:T(8,128)(2,1)S(1)}, bf16[256,256]{1,0:T(8,128)(2,1)S(1)}) custom-call(s32[5,8]{1,0:T(8,128)S(1)} %pad_add_fusion.meta, bf16[4,512,512]{2,1,0:T(8,128)(2,1)S(1)} %get-tuple-element.16.k_ref, bf16[2,256,256]{2,1,0:T(8,128)(2,1)S(1)} %get-tuple-element.22.refs_0_, ...), custom_call_target="tpu_custom_call" | custom-call | flops 536870912 | bytes 3145728 | tf_op jit(solution)/shard_map/pallas_call | solution.py:23
  64.8 1.2 %collective-permute-start.27 = (bf16[2,256,256]{2,1,0:T(8,128)(2,1)S(1)}, bf16[2,256,256]{2,1,0:T(8,128)(2,1)S(1)}, u32[]{:S(2)}, u32[]{:S(2)}) collective-permute-start(bf16[2,256,256]{2,1,0:T(8,128)(2,1)S(1)} %get-tuple-element.25.refs_1_.refs_0_), channel_id=1, source_target_pairs={{8,0},{0,8},{24,16},{16,24},{9,1},{1,9},{25,17},{17,25},{10,2},{2,... | collective-permute-start | bytes 786440 | tf_op jit(solution)/shard_map/ppermute | solution.py:208
  67.9 3.4 %collective-permute-start.19 = (bf16[256,256]{1,0:T(8,128)(2,1)S(1)}, bf16[256,256]{1,0:T(8,128)(2,1)S(1)}, u32[]{:S(2)}, u32[]{:S(2)}) collective-permute-start(bf16[256,256]{1,0:T(8,128)(2,1)S(1)} %get-tuple-element.23), channel_id=1, source_target_pairs={{0,0},{1,1},{2,2},{3,3},{4,16},{5,17},{6,18},{7,19},{8,8},{9,9},{1... | collective-permute-start | bytes 393224 | tf_op jit(solution)/shard_map/ppermute | solution.py:225
  71.3 2.6 %collective-permute-start.21 = (bf16[256,256]{1,0:T(8,128)(2,1)S(1)}, bf16[256,256]{1,0:T(8,128)(2,1)S(1)}, u32[]{:S(2)}, u32[]{:S(2)}) collective-permute-start(bf16[256,256]{1,0:T(8,128)(2,1)S(1)} %get-tuple-element.24), channel_id=1, source_target_pairs={{0,0},{1,1},{2,8},{3,9},{4,4},{5,5},{6,12},{7,13},{8,2},{9,3},{10,... | collective-permute-start | bytes 393224 | tf_op jit(solution)/shard_map/ppermute | solution.py:225
  74.2 1.9 %collective-permute-done.19.refs_6_ = bf16[256,256]{1,0:T(8,128)(2,1)S(1)} collective-permute-done((bf16[256,256]{1,0:T(8,128)(2,1)S(1)}, bf16[256,256]{1,0:T(8,128)(2,1)S(1)}, u32[]{:S(2)}, u32[]{:S(2)}) %collective-permute-start.19) | collective-permute-done | bytes 131104 | tf_op jit(solution)/shard_map/ppermute | solution.py:225
  76.1 2.3 %collective-permute-done.21.refs_7_ = bf16[256,256]{1,0:T(8,128)(2,1)S(1)} collective-permute-done((bf16[256,256]{1,0:T(8,128)(2,1)S(1)}, bf16[256,256]{1,0:T(8,128)(2,1)S(1)}, u32[]{:S(2)}, u32[]{:S(2)}) %collective-permute-start.21) | collective-permute-done | bytes 131104 | tf_op jit(solution)/shard_map/ppermute | solution.py:225
  78.4 2.9 %collective-permute-done.26.refs_4_.refs_3_ = bf16[1,256,256]{2,1,0:T(8,128)(2,1)S(1)} collective-permute-done((bf16[1,256,256]{2,1,0:T(8,128)(2,1)S(1)}, bf16[1,256,256]{2,1,0:T(8,128)(2,1)S(1)}, u32[]{:S(2)}, u32[]{:S(2)}) %collective-permute-start.26) | collective-permute-done | bytes 131104 | tf_op jit(solution)/shard_map/ppermute | solution.py:208
  82.0 1.6 %collective-permute-start.29 = (bf16[8,256,256]{2,1,0:T(8,128)(2,1)S(1)}, bf16[8,256,256]{2,1,0:T(8,128)(2,1)S(1)}, u32[]{:S(2)}, u32[]{:S(2)}) collective-permute-start(bf16[8,256,256]{2,1,0:T(8,128)(2,1)S(1)} %shard_map.93.own_ref), channel_id=1, source_target_pairs={{1,0},{0,1},{3,2},{2,3},{5,4},{4,5},{7,6},{6,7},{9,8},{8,9},{11,10... | collective-permute-start | bytes 3145736 | tf_op jit(solution)/shard_map/ppermute | solution.py:214
  83.7 3.5 %collective-permute-start.20 = (bf16[256,256]{1,0:T(8,128)(2,1)S(1)}, bf16[256,256]{1,0:T(8,128)(2,1)S(1)}, u32[]{:S(2)}, u32[]{:S(2)}) collective-permute-start(bf16[256,256]{1,0:T(8,128)(2,1)S(1)} %collective-permute-done.19.refs_6_), channel_id=1, source_target_pairs={{0,0},{1,1},{2,8},{3,9},{4,4},{5,5},{6,12},{7,13},{8,2},{9,3},{10,... | collective-permute-start | bytes 393224 | tf_op jit(solution)/shard_map/ppermute | solution.py:225
  87.2 2.1 %collective-permute-start.22 = (bf16[256,256]{1,0:T(8,128)(2,1)S(1)}, bf16[256,256]{1,0:T(8,128)(2,1)S(1)}, u32[]{:S(2)}, u32[]{:S(2)}) collective-permute-start(bf16[256,256]{1,0:T(8,128)(2,1)S(1)} %collective-permute-done.21.refs_7_), channel_id=1, source_target_pairs={{0,1},{1,0},{2,3},{3,2},{4,17},{5,16},{6,19},{7,18},{8,9},{9,8},{1... | collective-permute-start | bytes 393224 | tf_op jit(solution)/shard_map/ppermute | solution.py:225
  89.2 1.3 %shard_map.94.part_ref = f32[2,256,256]{2,1,0:T(8,128)S(1)} custom-call(s32[5,8]{1,0:T(8,128)S(1)} %pad_add_fusion.meta, bf16[8,256,256]{2,1,0:T(8,128)(2,1)S(1)} %shard_map.93.own_ref, bf16[8,256,256]{2,1,0:T(8,128)(2,1)S(1)} %collective-permute-done.29.other_ref, bf16[2,256,256]{2,1,0:T(8,128)(2,1)S(1)} %get-tuple-element.25.refs_1_.refs_0_, ...), custom_call_target="tpu_custom_call" | custom-call | flops 536870912 | bytes 6291456 | tf_op jit(solution)/shard_map/pallas_call | solution.py:23
  91.6 2.9 %collective-permute-done.22.other_ref = bf16[256,256]{1,0:T(8,128)(2,1)S(1)} collective-permute-done((bf16[256,256]{1,0:T(8,128)(2,1)S(1)}, bf16[256,256]{1,0:T(8,128)(2,1)S(1)}, u32[]{:S(2)}, u32[]{:S(2)}) %collective-permute-start.22) | collective-permute-done | bytes 131104 | tf_op jit(solution)/shard_map/ppermute | solution.py:225
  94.4 1.5 %shard_map.95 = f32[2,256,256]{2,1,0:T(8,128)} custom-call(s32[5,8]{1,0:T(8,128)S(1)} %pad_add_fusion.meta, bf16[256,256]{1,0:T(8,128)(2,1)S(1)} %collective-permute-done.20.same_ref, bf16[256,256]{1,0:T(8,128)(2,1)S(1)} %collective-permute-done.22.other_ref, f32[2,256,256]{2,1,0:T(8,128)S(1)} %shard_map.94.part_ref, ...), custom_call_target="tpu_custom_call" | custom-call | bytes 2097152 | tf_op jit(solution)/shard_map/pallas_call | solution.py:23
  (65 shorter events, 19.8 us)
Async XLA Ops:
  0.0 9.1 %copy-start = (s32[2,8,8]{2,1,0:T(8,128)S(1)}, s32[2,8,8]{2,1,0:T(8,128)}, u32[]{:S(2)}) copy-start(s32[2,8,8]{2,1,0:T(8,128)} %param.12) | copy-start | bytes 1540
  1.1 20.3 %collective-permute-start.8 = (bf16[2,256,256]{2,1,0:T(8,128)(2,1)S(1)}, bf16[2,256,256]{2,1,0:T(8,128)(2,1)S(1)}, u32[]{:S(2)}, u32[]{:S(2)}) collective-permute-start(bf16[2,256,256]{2,1,0:T(8,128)(2,1)S(1)} %bitcast_convert_fusion.refs_0_), channel_id=1, source_target_pairs={{4,0},{5,1},{6,2},{7,3},{0,4},{1,5},{2,6},{3,7},{12,8},{13,9},{14,... | collective-permute-start | bytes 786440 | tf_op jit(solution)/shard_map/ppermute | solution.py:217
  3.5 11.2 %collective-permute-start.3 = (bf16[2,256,256]{2,1,0:T(8,128)(2,1)S(1)}, bf16[2,256,256]{2,1,0:T(8,128)(2,1)S(1)}, u32[]{:S(2)}, u32[]{:S(2)}) collective-permute-start(bf16[2,256,256]{2,1,0:T(8,128)(2,1)S(1)} %bitcast_convert_fusion.refs_0_), channel_id=1, source_target_pairs={{2,0},{3,1},{0,2},{1,3},{6,4},{7,5},{4,6},{5,7},{10,8},{11,9},{8,1... | collective-permute-start | bytes 786440 | tf_op jit(solution)/shard_map/ppermute | solution.py:217
  4.8 9.9 %collective-permute-start.2 = (bf16[2,256,256]{2,1,0:T(8,128)(2,1)S(1)}, bf16[2,256,256]{2,1,0:T(8,128)(2,1)S(1)}, u32[]{:S(2)}, u32[]{:S(2)}) collective-permute-start(bf16[2,256,256]{2,1,0:T(8,128)(2,1)S(1)} %bitcast_convert_fusion.refs_0_), channel_id=1, source_target_pairs={{24,0},{16,8},{8,16},{0,24},{25,1},{17,9},{9,17},{1,25},{26,2},{18... | collective-permute-start | bytes 786440 | tf_op jit(solution)/shard_map/ppermute | solution.py:208
  5.0 13.1 %collective-permute-start.1 = (bf16[2,256,256]{2,1,0:T(8,128)(2,1)S(1)}, bf16[2,256,256]{2,1,0:T(8,128)(2,1)S(1)}, u32[]{:S(2)}, u32[]{:S(2)}) collective-permute-start(bf16[2,256,256]{2,1,0:T(8,128)(2,1)S(1)} %bitcast_convert_fusion.refs_0_), channel_id=1, source_target_pairs={{16,0},{24,8},{0,16},{8,24},{17,1},{25,9},{1,17},{9,25},{18,2},{26... | collective-permute-start | bytes 786440 | tf_op jit(solution)/shard_map/ppermute | solution.py:208
  6.2 11.8 %collective-permute-start = (bf16[2,256,256]{2,1,0:T(8,128)(2,1)S(1)}, bf16[2,256,256]{2,1,0:T(8,128)(2,1)S(1)}, u32[]{:S(2)}, u32[]{:S(2)}) collective-permute-start(bf16[2,256,256]{2,1,0:T(8,128)(2,1)S(1)} %bitcast_convert_fusion.refs_0_), channel_id=1, source_target_pairs={{8,0},{0,8},{24,16},{16,24},{9,1},{1,9},{25,17},{17,25},{10,2},{2,... | collective-permute-start | bytes 786440 | tf_op jit(solution)/shard_map/ppermute | solution.py:208
  19.4 23.5 %copy-start.2 = (f32[2,1,256,256]{3,2,1,0:T(8,128)S(1)}, f32[2,1,256,256]{3,2,1,0:T(8,128)}, u32[]{:S(2)}) copy-start(f32[2,1,256,256]{3,2,1,0:T(8,128)} %param.8) | copy-start | bytes 1572868
  19.4 8.2 %collective-permute-start.12 = (bf16[2,256,256]{2,1,0:T(8,128)(2,1)S(1)}, bf16[2,256,256]{2,1,0:T(8,128)(2,1)S(1)}, u32[]{:S(2)}, u32[]{:S(2)}) collective-permute-start(bf16[2,256,256]{2,1,0:T(8,128)(2,1)S(1)} %get-tuple-element.19.refs_1_.refs_0_), channel_id=1, source_target_pairs={{8,0},{0,8},{24,16},{16,24},{9,1},{1,9},{25,17},{17,25},{10,2},{2,... | collective-permute-start | bytes 786440 | tf_op jit(solution)/shard_map/ppermute | solution.py:208
  21.2 8.3 %collective-permute-start.10 = (bf16[2,256,256]{2,1,0:T(8,128)(2,1)S(1)}, bf16[2,256,256]{2,1,0:T(8,128)(2,1)S(1)}, u32[]{:S(2)}, u32[]{:S(2)}) collective-permute-start(bf16[2,256,256]{2,1,0:T(8,128)(2,1)S(1)} %get-tuple-element.19.refs_1_.refs_0_), channel_id=1, source_target_pairs={{16,0},{24,8},{0,16},{8,24},{17,1},{25,9},{1,17},{9,25},{18,2},{26... | collective-permute-start | bytes 786440 | tf_op jit(solution)/shard_map/ppermute | solution.py:208
  21.4 10.7 %collective-permute-start.9 = (bf16[2,256,256]{2,1,0:T(8,128)(2,1)S(1)}, bf16[2,256,256]{2,1,0:T(8,128)(2,1)S(1)}, u32[]{:S(2)}, u32[]{:S(2)}) collective-permute-start(bf16[2,256,256]{2,1,0:T(8,128)(2,1)S(1)} %shard_map.87.refs_2_), channel_id=1, source_target_pairs={{2,0},{3,1},{0,2},{1,3},{6,4},{7,5},{4,6},{5,7},{10,8},{11,9},{8,1... | collective-permute-start | bytes 786440 | tf_op jit(solution)/shard_map/ppermute | solution.py:217
  21.6 8.0 %collective-permute-start.4 = (bf16[256,256]{1,0:T(8,128)(2,1)S(1)}, bf16[256,256]{1,0:T(8,128)(2,1)S(1)}, u32[]{:S(2)}, u32[]{:S(2)}) collective-permute-start(bf16[256,256]{1,0:T(8,128)(2,1)S(1)} %get-tuple-element.17), channel_id=1, source_target_pairs={{0,0},{1,1},{2,2},{3,3},{4,16},{5,17},{6,18},{7,19},{8,8},{9,9},{1... | collective-permute-start | bytes 393224 | tf_op jit(solution)/shard_map/ppermute | solution.py:225
  24.5 7.5 %collective-permute-start.6 = (bf16[256,256]{1,0:T(8,128)(2,1)S(1)}, bf16[256,256]{1,0:T(8,128)(2,1)S(1)}, u32[]{:S(2)}, u32[]{:S(2)}) collective-permute-start(bf16[256,256]{1,0:T(8,128)(2,1)S(1)} %get-tuple-element.18), channel_id=1, source_target_pairs={{0,0},{1,1},{2,8},{3,9},{4,4},{5,5},{6,12},{7,13},{8,2},{9,3},{10,... | collective-permute-start | bytes 393224 | tf_op jit(solution)/shard_map/ppermute | solution.py:225
  27.6 6.3 %collective-permute-start.13 = (bf16[1,256,256]{2,1,0:T(8,128)(2,1)S(1)}, bf16[1,256,256]{2,1,0:T(8,128)(2,1)S(1)}, u32[]{:S(2)}, u32[]{:S(2)}) collective-permute-start(bf16[1,256,256]{2,1,0:T(8,128)(2,1)S(1)} %slice.17), channel_id=1, source_target_pairs={{16,0},{24,8},{0,16},{8,24},{17,1},{25,9},{1,17},{9,25},{18,2},{26... | collective-permute-start | bytes 393224 | tf_op jit(solution)/shard_map/ppermute | solution.py:208
  29.5 5.4 %collective-permute-start.11 = (bf16[1,256,256]{2,1,0:T(8,128)(2,1)S(1)}, bf16[1,256,256]{2,1,0:T(8,128)(2,1)S(1)}, u32[]{:S(2)}, u32[]{:S(2)}) collective-permute-start(bf16[1,256,256]{2,1,0:T(8,128)(2,1)S(1)} %slice.16), channel_id=1, source_target_pairs={{8,0},{0,8},{24,16},{16,24},{9,1},{1,9},{25,17},{17,25},{10,2},{2,... | collective-permute-start | bytes 393224 | tf_op jit(solution)/shard_map/ppermute | solution.py:208
  35.6 7.3 %collective-permute-start.14 = (bf16[8,256,256]{2,1,0:T(8,128)(2,1)S(1)}, bf16[8,256,256]{2,1,0:T(8,128)(2,1)S(1)}, u32[]{:S(2)}, u32[]{:S(2)}) collective-permute-start(bf16[8,256,256]{2,1,0:T(8,128)(2,1)S(1)} %shard_map.88.own_ref), channel_id=1, source_target_pairs={{1,0},{0,1},{3,2},{2,3},{5,4},{4,5},{7,6},{6,7},{9,8},{8,9},{11,10... | collective-permute-start | bytes 3145736 | tf_op jit(solution)/shard_map/ppermute | solution.py:214
  38.9 7.9 %collective-permute-start.5 = (bf16[256,256]{1,0:T(8,128)(2,1)S(1)}, bf16[256,256]{1,0:T(8,128)(2,1)S(1)}, u32[]{:S(2)}, u32[]{:S(2)}) collective-permute-start(bf16[256,256]{1,0:T(8,128)(2,1)S(1)} %collective-permute-done.4.refs_6_), channel_id=1, source_target_pairs={{0,0},{1,1},{2,8},{3,9},{4,4},{5,5},{6,12},{7,13},{8,2},{9,3},{10,... | collective-permute-start | bytes 393224 | tf_op jit(solution)/shard_map/ppermute | solution.py:225
  40.8 7.0 %collective-permute-start.7 = (bf16[256,256]{1,0:T(8,128)(2,1)S(1)}, bf16[256,256]{1,0:T(8,128)(2,1)S(1)}, u32[]{:S(2)}, u32[]{:S(2)}) collective-permute-start(bf16[256,256]{1,0:T(8,128)(2,1)S(1)} %collective-permute-done.6.refs_7_), channel_id=1, source_target_pairs={{0,1},{1,0},{2,3},{3,2},{4,17},{5,16},{6,19},{7,18},{8,9},{9,8},{1... | collective-permute-start | bytes 393224 | tf_op jit(solution)/shard_map/ppermute | solution.py:225
  48.6 7.9 %collective-permute-start.18 = (bf16[2,256,256]{2,1,0:T(8,128)(2,1)S(1)}, bf16[2,256,256]{2,1,0:T(8,128)(2,1)S(1)}, u32[]{:S(2)}, u32[]{:S(2)}) collective-permute-start(bf16[2,256,256]{2,1,0:T(8,128)(2,1)S(1)} %get-tuple-element.22.refs_0_), channel_id=1, source_target_pairs={{2,0},{3,1},{0,2},{1,3},{6,4},{7,5},{4,6},{5,7},{10,8},{11,9},{8,1... | collective-permute-start | bytes 786440 | tf_op jit(solution)/shard_map/ppermute | solution.py:217
  48.7 8.9 %collective-permute-start.17 = (bf16[2,256,256]{2,1,0:T(8,128)(2,1)S(1)}, bf16[2,256,256]{2,1,0:T(8,128)(2,1)S(1)}, u32[]{:S(2)}, u32[]{:S(2)}) collective-permute-start(bf16[2,256,256]{2,1,0:T(8,128)(2,1)S(1)} %get-tuple-element.22.refs_0_), channel_id=1, source_target_pairs={{24,0},{16,8},{8,16},{0,24},{25,1},{17,9},{9,17},{1,25},{26,2},{18... | collective-permute-start | bytes 786440 | tf_op jit(solution)/shard_map/ppermute | solution.py:208
  49.4 14.0 %collective-permute-start.16 = (bf16[2,256,256]{2,1,0:T(8,128)(2,1)S(1)}, bf16[2,256,256]{2,1,0:T(8,128)(2,1)S(1)}, u32[]{:S(2)}, u32[]{:S(2)}) collective-permute-start(bf16[2,256,256]{2,1,0:T(8,128)(2,1)S(1)} %get-tuple-element.22.refs_0_), channel_id=1, source_target_pairs={{16,0},{24,8},{0,16},{8,24},{17,1},{25,9},{1,17},{9,25},{18,2},{26... | collective-permute-start | bytes 786440 | tf_op jit(solution)/shard_map/ppermute | solution.py:208
  52.9 10.6 %collective-permute-start.15 = (bf16[2,256,256]{2,1,0:T(8,128)(2,1)S(1)}, bf16[2,256,256]{2,1,0:T(8,128)(2,1)S(1)}, u32[]{:S(2)}, u32[]{:S(2)}) collective-permute-start(bf16[2,256,256]{2,1,0:T(8,128)(2,1)S(1)} %get-tuple-element.22.refs_0_), channel_id=1, source_target_pairs={{8,0},{0,8},{24,16},{16,24},{9,1},{1,9},{25,17},{17,25},{10,2},{2,... | collective-permute-start | bytes 786440 | tf_op jit(solution)/shard_map/ppermute | solution.py:208
  52.9 14.5 %collective-permute-start.23 = (bf16[2,256,256]{2,1,0:T(8,128)(2,1)S(1)}, bf16[2,256,256]{2,1,0:T(8,128)(2,1)S(1)}, u32[]{:S(2)}, u32[]{:S(2)}) collective-permute-start(bf16[2,256,256]{2,1,0:T(8,128)(2,1)S(1)} %get-tuple-element.22.refs_0_), channel_id=1, source_target_pairs={{4,0},{5,1},{6,2},{7,3},{0,4},{1,5},{2,6},{3,7},{12,8},{13,9},{14,... | collective-permute-start | bytes 786440 | tf_op jit(solution)/shard_map/ppermute | solution.py:217
  64.8 9.1 %collective-permute-start.27 = (bf16[2,256,256]{2,1,0:T(8,128)(2,1)S(1)}, bf16[2,256,256]{2,1,0:T(8,128)(2,1)S(1)}, u32[]{:S(2)}, u32[]{:S(2)}) collective-permute-start(bf16[2,256,256]{2,1,0:T(8,128)(2,1)S(1)} %get-tuple-element.25.refs_1_.refs_0_), channel_id=1, source_target_pairs={{8,0},{0,8},{24,16},{16,24},{9,1},{1,9},{25,17},{17,25},{10,2},{2,... | collective-permute-start | bytes 786440 | tf_op jit(solution)/shard_map/ppermute | solution.py:208
  66.0 8.1 %collective-permute-start.25 = (bf16[2,256,256]{2,1,0:T(8,128)(2,1)S(1)}, bf16[2,256,256]{2,1,0:T(8,128)(2,1)S(1)}, u32[]{:S(2)}, u32[]{:S(2)}) collective-permute-start(bf16[2,256,256]{2,1,0:T(8,128)(2,1)S(1)} %get-tuple-element.25.refs_1_.refs_0_), channel_id=1, source_target_pairs={{16,0},{24,8},{0,16},{8,24},{17,1},{25,9},{1,17},{9,25},{18,2},{26... | collective-permute-start | bytes 786440 | tf_op jit(solution)/shard_map/ppermute | solution.py:208
  67.4 11.0 %collective-permute-start.24 = (bf16[2,256,256]{2,1,0:T(8,128)(2,1)S(1)}, bf16[2,256,256]{2,1,0:T(8,128)(2,1)S(1)}, u32[]{:S(2)}, u32[]{:S(2)}) collective-permute-start(bf16[2,256,256]{2,1,0:T(8,128)(2,1)S(1)} %shard_map.92.refs_2_), channel_id=1, source_target_pairs={{2,0},{3,1},{0,2},{1,3},{6,4},{7,5},{4,6},{5,7},{10,8},{11,9},{8,1... | collective-permute-start | bytes 786440 | tf_op jit(solution)/shard_map/ppermute | solution.py:217
  67.9 8.1 %collective-permute-start.19 = (bf16[256,256]{1,0:T(8,128)(2,1)S(1)}, bf16[256,256]{1,0:T(8,128)(2,1)S(1)}, u32[]{:S(2)}, u32[]{:S(2)}) collective-permute-start(bf16[256,256]{1,0:T(8,128)(2,1)S(1)} %get-tuple-element.23), channel_id=1, source_target_pairs={{0,0},{1,1},{2,2},{3,3},{4,16},{5,17},{6,18},{7,19},{8,8},{9,9},{1... | collective-permute-start | bytes 393224 | tf_op jit(solution)/shard_map/ppermute | solution.py:225
  71.3 7.1 %collective-permute-start.21 = (bf16[256,256]{1,0:T(8,128)(2,1)S(1)}, bf16[256,256]{1,0:T(8,128)(2,1)S(1)}, u32[]{:S(2)}, u32[]{:S(2)}) collective-permute-start(bf16[256,256]{1,0:T(8,128)(2,1)S(1)} %get-tuple-element.24), channel_id=1, source_target_pairs={{0,0},{1,1},{2,8},{3,9},{4,4},{5,5},{6,12},{7,13},{8,2},{9,3},{10,... | collective-permute-start | bytes 393224 | tf_op jit(solution)/shard_map/ppermute | solution.py:225
  74.0 4.5 %collective-permute-start.28 = (bf16[1,256,256]{2,1,0:T(8,128)(2,1)S(1)}, bf16[1,256,256]{2,1,0:T(8,128)(2,1)S(1)}, u32[]{:S(2)}, u32[]{:S(2)}) collective-permute-start(bf16[1,256,256]{2,1,0:T(8,128)(2,1)S(1)} %slice.19), channel_id=1, source_target_pairs={{16,0},{24,8},{0,16},{8,24},{17,1},{25,9},{1,17},{9,25},{18,2},{26... | collective-permute-start | bytes 393224 | tf_op jit(solution)/shard_map/ppermute | solution.py:208
  74.1 7.2 %collective-permute-start.26 = (bf16[1,256,256]{2,1,0:T(8,128)(2,1)S(1)}, bf16[1,256,256]{2,1,0:T(8,128)(2,1)S(1)}, u32[]{:S(2)}, u32[]{:S(2)}) collective-permute-start(bf16[1,256,256]{2,1,0:T(8,128)(2,1)S(1)} %slice.18), channel_id=1, source_target_pairs={{8,0},{0,8},{24,16},{16,24},{9,1},{1,9},{25,17},{17,25},{10,2},{2,... | collective-permute-start | bytes 393224 | tf_op jit(solution)/shard_map/ppermute | solution.py:208
  82.0 7.2 %collective-permute-start.29 = (bf16[8,256,256]{2,1,0:T(8,128)(2,1)S(1)}, bf16[8,256,256]{2,1,0:T(8,128)(2,1)S(1)}, u32[]{:S(2)}, u32[]{:S(2)}) collective-permute-start(bf16[8,256,256]{2,1,0:T(8,128)(2,1)S(1)} %shard_map.93.own_ref), channel_id=1, source_target_pairs={{1,0},{0,1},{3,2},{2,3},{5,4},{4,5},{7,6},{6,7},{9,8},{8,9},{11,10... | collective-permute-start | bytes 3145736 | tf_op jit(solution)/shard_map/ppermute | solution.py:214
  83.7 7.9 %collective-permute-start.20 = (bf16[256,256]{1,0:T(8,128)(2,1)S(1)}, bf16[256,256]{1,0:T(8,128)(2,1)S(1)}, u32[]{:S(2)}, u32[]{:S(2)}) collective-permute-start(bf16[256,256]{1,0:T(8,128)(2,1)S(1)} %collective-permute-done.19.refs_6_), channel_id=1, source_target_pairs={{0,0},{1,1},{2,8},{3,9},{4,4},{5,5},{6,12},{7,13},{8,2},{9,3},{10,... | collective-permute-start | bytes 393224 | tf_op jit(solution)/shard_map/ppermute | solution.py:225
  87.2 7.3 %collective-permute-start.22 = (bf16[256,256]{1,0:T(8,128)(2,1)S(1)}, bf16[256,256]{1,0:T(8,128)(2,1)S(1)}, u32[]{:S(2)}, u32[]{:S(2)}) collective-permute-start(bf16[256,256]{1,0:T(8,128)(2,1)S(1)} %collective-permute-done.21.refs_7_), channel_id=1, source_target_pairs={{0,1},{1,0},{2,3},{3,2},{4,17},{5,16},{6,19},{7,18},{8,9},{9,8},{1... | collective-permute-start | bytes 393224 | tf_op jit(solution)/shard_map/ppermute | solution.py:225
  (3 other events, 2.9 us)

commit v3 on v2

--- a/solution.py
+++ b/solution.py
@@ -87,14 +87,14 @@
     other_ref[...] = jnp.where(side == 0, second, first)
 
 
-def coupled_blocks(rows, meta, kept, pieces, other):
+def coupled_blocks(rows, meta, kept, pieces):
     orb_rows, virt, _ = pieces[0].shape
     count = rows * orb_rows
     block = jax.ShapeDtypeStruct((virt, virt), jnp.bfloat16)
     shape = (jax.ShapeDtypeStruct((orb_rows, virt, virt), jnp.bfloat16), block, block)
     body = functools.partial(coupled_body, rows)
     flops, moved = 2 * orb_rows * count * virt**3, 2 * (orb_rows + 1) * count * virt**2
-    return call(body, shape, [SMEM] + [VMEM] * (2 + len(pieces)), flops, moved, meta, kept, *pieces, other)
+    return call(body, shape, [SMEM] + [VMEM] * (1 + len(pieces)), flops, moved, meta, kept, *pieces)
 
 
 def column_body(meta, *refs):
@@ -255,7 +255,7 @@
         column = {0: half, 1: from_chip(half, 1)}
         for step in range(2, halves, 2):
             column[step] = from_chip(half, step)
-        coupled, same, other = coupled_blocks(rows, meta, kept, a_pieces, column[1])
+        coupled, same, other = coupled_blocks(rows, meta, kept, a_pieces)
         near = from_row(coupled, 1)
         c_pieces, far = [coupled, near], []
         for step in range(2, rows, 2):
@@ -264,7 +264,7 @@
             c_pieces += [piece, *far[-2:]]
         same, other = crossing(same, high_parts), crossing(other, last_bits)
         for step in range(2, halves, 2):
-            column[step] = tied(column[step], coupled)
+            column[step] = tied(column[step], column[1], coupled)
             column[step + 1] = from_chip(column[step], 1)
         column = [column[step] for step in range(halves)]
         own = whole_column(meta, column, [*far, same, other])

time: 97.7 us -> 96.2 us (0.985)
  waiting for transfers between devices: 34.9 us -> 32.3 us
  starting transfers between devices: 43.5 us -> 45 us
    ppermute x6, waiting for transfers between devices: 3.7 us -> 0.02 us  [from_chip(): return lax.ppermute(x, 'col', [(c ^ 2 * step, c) for c in range(cols)])]
    ppermute x6, starting transfers between devices: 4.59 us -> 7.81 us  [from_chip(): return lax.ppermute(x, 'col', [(c ^ 2 * step, c) for c in range(cols)])]
    ppermute x14, starting transfers between devices: 12.4 us -> 9.3 us  [from_row(): return lax.ppermute(x, 'row', [(r ^ step, r) for r in range(rows)])]
    ppermute x14, waiting for transfers between devices: 17.1 us -> 18.6 us  [from_row(): return lax.ppermute(x, 'row', [(r ^ step, r) for r in range(rows)])]
    ppermute x2, starting transfers between devices: 4.97 us -> 6.4 us  [swapped(): return lax.ppermute(x, 'col', [(c ^ 1, c) for c in range(cols)])]
  transfers between devices with their start and end apart: 30 -> 30, of which waited for: 16 -> 15; matrix products, arithmetic and copies ran while one was open for 4% -> 4% of each run, Pallas kernels for 7% -> 7%
where the time goes in v3:
time: 96.2 us; the launch traced here: 95 us
  starting transfers between devices  45 us (47%)
  waiting for transfers between devices  32.3 us (34%)
  Pallas kernels  9.93 us (10%)
  local copies, waits for them, and re-layouts  4.65 us (5%)
  other arithmetic  2.77 us (3%)
    ppermute x8, starting transfers between devices, crossing(): return lax.ppermute(x, ('row', 'col'), pairs)  21.5 us
    ppermute x14, waiting for transfers between devices, from_row(): return lax.ppermute(x, 'row', [(r ^ step, r) for r in range(rows)])  18.6 us
    ppermute x8, waiting for transfers between devices, crossing(): return lax.ppermute(x, ('row', 'col'), pairs)  13.7 us
    pallas_call x9, Pallas kernels, call(): pl.pallas_call(body, out_shape=out_shape, in_specs=in_specs, out_specs=VM...  9.92 us
    ppermute x14, starting transfers between devices, from_row(): return lax.ppermute(x, 'row', [(r ^ step, r) for r in range(rows)])  9.3 us
    ppermute x6, starting transfers between devices, from_chip(): return lax.ppermute(x, 'col', [(c ^ 2 * step, c) for c in range(cols)])  7.81 us
    ppermute x2, starting transfers between devices, swapped(): return lax.ppermute(x, 'col', [(c ^ 1, c) for c in range(cols)])  6.4 us
    unnamed x10, local copies, waits for them, and re-layouts  2.93 us
  transfers between devices with their start and end apart: 30, of which 15 were waited for; matrix products, arithmetic and copies ran while one was open for 4% of the time, Pallas kernels for 7%

profile of v3, /device:TPU:7, one launch (start us, length us, event | category | flops | bytes accessed | tf_op | source)
XLA Modules:
  0.0 95.0 jit_solution(12457672997657804274)
XLA Ops:
  1.1 2.4 %collective-permute-start.8 = (bf16[2,256,256]{2,1,0:T(8,128)(2,1)S(1)}, bf16[2,256,256]{2,1,0:T(8,128)(2,1)S(1)}, u32[]{:S(2)}, u32[]{:S(2)}) collective-permute-start(bf16[2,256,256]{2,1,0:T(8,128)(2,1)S(1)} %bitcast_convert_fusion.refs_0_), channel_id=1, source_target_pairs={{4,0},{5,1},{6,2},{7,3},{0,4},{1,5},{2,6},{3,7},{12,8},{13,9},{14,... | collective-permute-start | bytes 786440 | tf_op jit(solution)/shard_map/ppermute | solution.py:217
  3.5 1.3 %collective-permute-start.7 = (bf16[2,256,256]{2,1,0:T(8,128)(2,1)S(1)}, bf16[2,256,256]{2,1,0:T(8,128)(2,1)S(1)}, u32[]{:S(2)}, u32[]{:S(2)}) collective-permute-start(bf16[2,256,256]{2,1,0:T(8,128)(2,1)S(1)} %bitcast_convert_fusion.refs_0_), channel_id=1, source_target_pairs={{2,0},{3,1},{0,2},{1,3},{6,4},{7,5},{4,6},{5,7},{10,8},{11,9},{8,1... | collective-permute-start | bytes 786440 | tf_op jit(solution)/shard_map/ppermute | solution.py:217
  10.8 1.6 %copy-done.1 = bf16[2,8,256,256]{3,2,1,0:T(8,128)(2,1)S(1)} copy-done((bf16[2,8,256,256]{3,2,1,0:T(8,128)(2,1)S(1)}, bf16[2,8,256,256]{3,2,1,0:T(8,128)(2,1)}, u32[]{:S(2)}) %copy-start.1) | copy-done | bytes 2097176
  14.7 3.3 %collective-permute-done.1.refs_2_ = bf16[2,256,256]{2,1,0:T(8,128)(2,1)S(1)} collective-permute-done((bf16[2,256,256]{2,1,0:T(8,128)(2,1)S(1)}, bf16[2,256,256]{2,1,0:T(8,128)(2,1)S(1)}, u32[]{:S(2)}, u32[]{:S(2)}) %collective-permute-start.1) | collective-permute-done | bytes 262176 | tf_op jit(solution)/shard_map/ppermute | solution.py:208
  18.0 1.3 %shard_map.86 = (bf16[2,256,256]{2,1,0:T(8,128)(2,1)S(1)}, bf16[256,256]{1,0:T(8,128)(2,1)S(1)}, bf16[256,256]{1,0:T(8,128)(2,1)S(1)}) custom-call(s32[5,8]{1,0:T(8,128)S(1)} %pad_add_fusion.meta, bf16[4,512,512]{2,1,0:T(8,128)(2,1)S(1)} %get-tuple-element.16.k_ref, bf16[2,256,256]{2,1,0:T(8,128)(2,1)S(1)} %bitcast_convert_fusion.refs_0_, ...), custom_call_target="tpu_custom_call" | custom-call | flops 536870912 | bytes 3145728 | tf_op jit(solution)/shard_map/pallas_call | solution.py:23
  19.4 1.8 %collective-permute-start.12 = (bf16[2,256,256]{2,1,0:T(8,128)(2,1)S(1)}, bf16[2,256,256]{2,1,0:T(8,128)(2,1)S(1)}, u32[]{:S(2)}, u32[]{:S(2)}) collective-permute-start(bf16[2,256,256]{2,1,0:T(8,128)(2,1)S(1)} %get-tuple-element.19.refs_2_.refs_0_), channel_id=1, source_target_pairs={{8,0},{0,8},{24,16},{16,24},{9,1},{1,9},{25,17},{17,25},{10,2},{2,... | collective-permute-start | bytes 786440 | tf_op jit(solution)/shard_map/ppermute | solution.py:208
  21.6 2.9 %collective-permute-start.3 = (bf16[256,256]{1,0:T(8,128)(2,1)S(1)}, bf16[256,256]{1,0:T(8,128)(2,1)S(1)}, u32[]{:S(2)}, u32[]{:S(2)}) collective-permute-start(bf16[256,256]{1,0:T(8,128)(2,1)S(1)} %get-tuple-element.17), channel_id=1, source_target_pairs={{0,0},{1,1},{2,2},{3,3},{4,16},{5,17},{6,18},{7,19},{8,8},{9,9},{1... | collective-permute-start | bytes 393224 | tf_op jit(solution)/shard_map/ppermute | solution.py:225
  24.5 3.1 %collective-permute-start.5 = (bf16[256,256]{1,0:T(8,128)(2,1)S(1)}, bf16[256,256]{1,0:T(8,128)(2,1)S(1)}, u32[]{:S(2)}, u32[]{:S(2)}) collective-permute-start(bf16[256,256]{1,0:T(8,128)(2,1)S(1)} %get-tuple-element.18), channel_id=1, source_target_pairs={{0,0},{1,1},{2,8},{3,9},{4,4},{5,5},{6,12},{7,13},{8,2},{9,3},{10,... | collective-permute-start | bytes 393224 | tf_op jit(solution)/shard_map/ppermute | solution.py:225
  29.6 2.5 %collective-permute-done.5.refs_7_ = bf16[256,256]{1,0:T(8,128)(2,1)S(1)} collective-permute-done((bf16[256,256]{1,0:T(8,128)(2,1)S(1)}, bf16[256,256]{1,0:T(8,128)(2,1)S(1)}, u32[]{:S(2)}, u32[]{:S(2)}) %collective-permute-start.5) | collective-permute-done | bytes 131104 | tf_op jit(solution)/shard_map/ppermute | solution.py:225
  32.1 1.9 %collective-permute-done.13.refs_5_.refs_4_ = bf16[1,256,256]{2,1,0:T(8,128)(2,1)S(1)} collective-permute-done((bf16[1,256,256]{2,1,0:T(8,128)(2,1)S(1)}, bf16[1,256,256]{2,1,0:T(8,128)(2,1)S(1)}, u32[]{:S(2)}, u32[]{:S(2)}) %collective-permute-start.13) | collective-permute-done | bytes 131104 | tf_op jit(solution)/shard_map/ppermute | solution.py:208
  35.6 3.3 %collective-permute-start.14 = (bf16[8,256,256]{2,1,0:T(8,128)(2,1)S(1)}, bf16[8,256,256]{2,1,0:T(8,128)(2,1)S(1)}, u32[]{:S(2)}, u32[]{:S(2)}) collective-permute-start(bf16[8,256,256]{2,1,0:T(8,128)(2,1)S(1)} %shard_map.88.own_ref), channel_id=1, source_target_pairs={{1,0},{0,1},{3,2},{2,3},{5,4},{4,5},{7,6},{6,7},{9,8},{8,9},{11,10... | collective-permute-start | bytes 3145736 | tf_op jit(solution)/shard_map/ppermute | solution.py:214
  38.9 1.9 %collective-permute-start.4 = (bf16[256,256]{1,0:T(8,128)(2,1)S(1)}, bf16[256,256]{1,0:T(8,128)(2,1)S(1)}, u32[]{:S(2)}, u32[]{:S(2)}) collective-permute-start(bf16[256,256]{1,0:T(8,128)(2,1)S(1)} %collective-permute-done.3.refs_6_), channel_id=1, source_target_pairs={{0,0},{1,1},{2,8},{3,9},{4,4},{5,5},{6,12},{7,13},{8,2},{9,3},{10,... | collective-permute-start | bytes 393224 | tf_op jit(solution)/shard_map/ppermute | solution.py:225
  40.8 2.0 %collective-permute-start.6 = (bf16[256,256]{1,0:T(8,128)(2,1)S(1)}, bf16[256,256]{1,0:T(8,128)(2,1)S(1)}, u32[]{:S(2)}, u32[]{:S(2)}) collective-permute-start(bf16[256,256]{1,0:T(8,128)(2,1)S(1)} %collective-permute-done.5.refs_7_), channel_id=1, source_target_pairs={{0,1},{1,0},{2,3},{3,2},{4,17},{5,16},{6,19},{7,18},{8,9},{9,8},{1... | collective-permute-start | bytes 393224 | tf_op jit(solution)/shard_map/ppermute | solution.py:225
  42.9 1.4 %shard_map.89.part_ref = f32[2,256,256]{2,1,0:T(8,128)S(1)} custom-call(s32[5,8]{1,0:T(8,128)S(1)} %pad_add_fusion.meta, bf16[8,256,256]{2,1,0:T(8,128)(2,1)S(1)} %shard_map.88.own_ref, bf16[8,256,256]{2,1,0:T(8,128)(2,1)S(1)} %collective-permute-done.14.other_ref, bf16[2,256,256]{2,1,0:T(8,128)(2,1)S(1)} %get-tuple-element.19.refs_2_.refs_0_, ...), custom_call_target="tpu_custom_call" | custom-call | flops 536870912 | bytes 6291456 | tf_op jit(solution)/shard_map/pallas_call | solution.py:23
  44.2 2.5 %collective-permute-done.4.same_ref = bf16[256,256]{1,0:T(8,128)(2,1)S(1)} collective-permute-done((bf16[256,256]{1,0:T(8,128)(2,1)S(1)}, bf16[256,256]{1,0:T(8,128)(2,1)S(1)}, u32[]{:S(2)}, u32[]{:S(2)}) %collective-permute-start.4) | collective-permute-done | bytes 131104 | tf_op jit(solution)/shard_map/ppermute | solution.py:225
  48.6 1.6 %collective-permute-start.16 = (bf16[2,256,256]{2,1,0:T(8,128)(2,1)S(1)}, bf16[2,256,256]{2,1,0:T(8,128)(2,1)S(1)}, u32[]{:S(2)}, u32[]{:S(2)}) collective-permute-start(bf16[2,256,256]{2,1,0:T(8,128)(2,1)S(1)} %get-tuple-element.22.refs_0_), channel_id=1, source_target_pairs={{16,0},{24,8},{0,16},{8,24},{17,1},{25,9},{1,17},{9,25},{18,2},{26... | collective-permute-start | bytes 786440 | tf_op jit(solution)/shard_map/ppermute | solution.py:208
  51.4 1.6 %collective-permute-start.23 = (bf16[2,256,256]{2,1,0:T(8,128)(2,1)S(1)}, bf16[2,256,256]{2,1,0:T(8,128)(2,1)S(1)}, u32[]{:S(2)}, u32[]{:S(2)}) collective-permute-start(bf16[2,256,256]{2,1,0:T(8,128)(2,1)S(1)} %get-tuple-element.22.refs_0_), channel_id=1, source_target_pairs={{4,0},{5,1},{6,2},{7,3},{0,4},{1,5},{2,6},{3,7},{12,8},{13,9},{14,... | collective-permute-start | bytes 786440 | tf_op jit(solution)/shard_map/ppermute | solution.py:217
  53.0 4.4 %collective-permute-done.17.refs_3_ = bf16[2,256,256]{2,1,0:T(8,128)(2,1)S(1)} collective-permute-done((bf16[2,256,256]{2,1,0:T(8,128)(2,1)S(1)}, bf16[2,256,256]{2,1,0:T(8,128)(2,1)S(1)}, u32[]{:S(2)}, u32[]{:S(2)}) %collective-permute-start.17) | collective-permute-done | bytes 262176 | tf_op jit(solution)/shard_map/ppermute | solution.py:208
  57.4 4.7 %collective-permute-done.16.refs_2_ = bf16[2,256,256]{2,1,0:T(8,128)(2,1)S(1)} collective-permute-done((bf16[2,256,256]{2,1,0:T(8,128)(2,1)S(1)}, bf16[2,256,256]{2,1,0:T(8,128)(2,1)S(1)}, u32[]{:S(2)}, u32[]{:S(2)}) %collective-permute-start.16) | collective-permute-done | bytes 262176 | tf_op jit(solution)/shard_map/ppermute | solution.py:208
  63.0 1.3 %shard_map.91 = (bf16[2,256,256]{2,1,0:T(8,128)(2,1)S(1)}, bf16[256,256]{1,0:T(8,128)(2,1)S(1)}, bf16[256,256]{1,0:T(8,128)(2,1)S(1)}) custom-call(s32[5,8]{1,0:T(8,128)S(1)} %pad_add_fusion.meta, bf16[4,512,512]{2,1,0:T(8,128)(2,1)S(1)} %get-tuple-element.16.k_ref, bf16[2,256,256]{2,1,0:T(8,128)(2,1)S(1)} %get-tuple-element.22.refs_0_, ...), custom_call_target="tpu_custom_call" | custom-call | flops 536870912 | bytes 3145728 | tf_op jit(solution)/shard_map/pallas_call | solution.py:23
  65.1 2.3 %collective-permute-start.24 = (bf16[2,256,256]{2,1,0:T(8,128)(2,1)S(1)}, bf16[2,256,256]{2,1,0:T(8,128)(2,1)S(1)}, u32[]{:S(2)}, u32[]{:S(2)}) collective-permute-start(bf16[2,256,256]{2,1,0:T(8,128)(2,1)S(1)} %shard_map.92.refs_2_), channel_id=1, source_target_pairs={{2,0},{3,1},{0,2},{1,3},{6,4},{7,5},{4,6},{5,7},{10,8},{11,9},{8,1... | collective-permute-start | bytes 786440 | tf_op jit(solution)/shard_map/ppermute | solution.py:217
  67.5 2.6 %collective-permute-start.18 = (bf16[256,256]{1,0:T(8,128)(2,1)S(1)}, bf16[256,256]{1,0:T(8,128)(2,1)S(1)}, u32[]{:S(2)}, u32[]{:S(2)}) collective-permute-start(bf16[256,256]{1,0:T(8,128)(2,1)S(1)} %get-tuple-element.23), channel_id=1, source_target_pairs={{0,0},{1,1},{2,2},{3,3},{4,16},{5,17},{6,18},{7,19},{8,8},{9,9},{1... | collective-permute-start | bytes 393224 | tf_op jit(solution)/shard_map/ppermute | solution.py:225
  70.1 3.7 %collective-permute-start.20 = (bf16[256,256]{1,0:T(8,128)(2,1)S(1)}, bf16[256,256]{1,0:T(8,128)(2,1)S(1)}, u32[]{:S(2)}, u32[]{:S(2)}) collective-permute-start(bf16[256,256]{1,0:T(8,128)(2,1)S(1)} %get-tuple-element.24), channel_id=1, source_target_pairs={{0,0},{1,1},{2,8},{3,9},{4,4},{5,5},{6,12},{7,13},{8,2},{9,3},{10,... | collective-permute-start | bytes 393224 | tf_op jit(solution)/shard_map/ppermute | solution.py:225
  73.9 1.9 %collective-permute-done.18.refs_6_ = bf16[256,256]{1,0:T(8,128)(2,1)S(1)} collective-permute-done((bf16[256,256]{1,0:T(8,128)(2,1)S(1)}, bf16[256,256]{1,0:T(8,128)(2,1)S(1)}, u32[]{:S(2)}, u32[]{:S(2)}) %collective-permute-start.18) | collective-permute-done | bytes 131104 | tf_op jit(solution)/shard_map/ppermute | solution.py:225
  75.8 1.3 %collective-permute-done.20.refs_7_ = bf16[256,256]{1,0:T(8,128)(2,1)S(1)} collective-permute-done((bf16[256,256]{1,0:T(8,128)(2,1)S(1)}, bf16[256,256]{1,0:T(8,128)(2,1)S(1)}, u32[]{:S(2)}, u32[]{:S(2)}) %collective-permute-start.20) | collective-permute-done | bytes 131104 | tf_op jit(solution)/shard_map/ppermute | solution.py:225
  77.1 1.5 %collective-permute-done.28.refs_5_.refs_4_ = bf16[1,256,256]{2,1,0:T(8,128)(2,1)S(1)} collective-permute-done((bf16[1,256,256]{2,1,0:T(8,128)(2,1)S(1)}, bf16[1,256,256]{2,1,0:T(8,128)(2,1)S(1)}, u32[]{:S(2)}, u32[]{:S(2)}) %collective-permute-start.28) | collective-permute-done | bytes 131104 | tf_op jit(solution)/shard_map/ppermute | solution.py:208
  79.3 3.1 %collective-permute-start.29 = (bf16[8,256,256]{2,1,0:T(8,128)(2,1)S(1)}, bf16[8,256,256]{2,1,0:T(8,128)(2,1)S(1)}, u32[]{:S(2)}, u32[]{:S(2)}) collective-permute-start(bf16[8,256,256]{2,1,0:T(8,128)(2,1)S(1)} %shard_map.93.own_ref), channel_id=1, source_target_pairs={{1,0},{0,1},{3,2},{2,3},{5,4},{4,5},{7,6},{6,7},{9,8},{8,9},{11,10... | collective-permute-start | bytes 3145736 | tf_op jit(solution)/shard_map/ppermute | solution.py:214
  82.3 3.9 %collective-permute-start.19 = (bf16[256,256]{1,0:T(8,128)(2,1)S(1)}, bf16[256,256]{1,0:T(8,128)(2,1)S(1)}, u32[]{:S(2)}, u32[]{:S(2)}) collective-permute-start(bf16[256,256]{1,0:T(8,128)(2,1)S(1)} %collective-permute-done.18.refs_6_), channel_id=1, source_target_pairs={{0,0},{1,1},{2,8},{3,9},{4,4},{5,5},{6,12},{7,13},{8,2},{9,3},{10,... | collective-permute-start | bytes 393224 | tf_op jit(solution)/shard_map/ppermute | solution.py:225
  86.2 1.4 %collective-permute-start.21 = (bf16[256,256]{1,0:T(8,128)(2,1)S(1)}, bf16[256,256]{1,0:T(8,128)(2,1)S(1)}, u32[]{:S(2)}, u32[]{:S(2)}) collective-permute-start(bf16[256,256]{1,0:T(8,128)(2,1)S(1)} %collective-permute-done.20.refs_7_), channel_id=1, source_target_pairs={{0,1},{1,0},{2,3},{3,2},{4,17},{5,16},{6,19},{7,18},{8,9},{9,8},{1... | collective-permute-start | bytes 393224 | tf_op jit(solution)/shard_map/ppermute | solution.py:225
  87.6 1.3 %shard_map.94.part_ref = f32[2,256,256]{2,1,0:T(8,128)S(1)} custom-call(s32[5,8]{1,0:T(8,128)S(1)} %pad_add_fusion.meta, bf16[8,256,256]{2,1,0:T(8,128)(2,1)S(1)} %shard_map.93.own_ref, bf16[8,256,256]{2,1,0:T(8,128)(2,1)S(1)} %collective-permute-done.29.other_ref, bf16[2,256,256]{2,1,0:T(8,128)(2,1)S(1)} %get-tuple-element.25.refs_2_.refs_0_, ...), custom_call_target="tpu_custom_call" | custom-call | flops 536870912 | bytes 6291456 | tf_op jit(solution)/shard_map/pallas_call | solution.py:23
  90.2 3.3 %collective-permute-done.21.other_ref = bf16[256,256]{1,0:T(8,128)(2,1)S(1)} collective-permute-done((bf16[256,256]{1,0:T(8,128)(2,1)S(1)}, bf16[256,256]{1,0:T(8,128)(2,1)S(1)}, u32[]{:S(2)}, u32[]{:S(2)}) %collective-permute-start.21) | collective-permute-done | bytes 131104 | tf_op jit(solution)/shard_map/ppermute | solution.py:225
  93.5 1.5 %shard_map.95 = f32[2,256,256]{2,1,0:T(8,128)} custom-call(s32[5,8]{1,0:T(8,128)S(1)} %pad_add_fusion.meta, bf16[256,256]{1,0:T(8,128)(2,1)S(1)} %collective-permute-done.19.same_ref, bf16[256,256]{1,0:T(8,128)(2,1)S(1)} %collective-permute-done.21.other_ref, f32[2,256,256]{2,1,0:T(8,128)S(1)} %shard_map.94.part_ref, ...), custom_call_target="tpu_custom_call" | custom-call | bytes 2097152 | tf_op jit(solution)/shard_map/pallas_call | solution.py:23
  (65 shorter events, 20.0 us)
Async XLA Ops:
  0.0 9.1 %copy-start = (s32[2,8,8]{2,1,0:T(8,128)S(1)}, s32[2,8,8]{2,1,0:T(8,128)}, u32[]{:S(2)}) copy-start(s32[2,8,8]{2,1,0:T(8,128)} %param.12) | copy-start | bytes 1540
  1.1 20.3 %collective-permute-start.8 = (bf16[2,256,256]{2,1,0:T(8,128)(2,1)S(1)}, bf16[2,256,256]{2,1,0:T(8,128)(2,1)S(1)}, u32[]{:S(2)}, u32[]{:S(2)}) collective-permute-start(bf16[2,256,256]{2,1,0:T(8,128)(2,1)S(1)} %bitcast_convert_fusion.refs_0_), channel_id=1, source_target_pairs={{4,0},{5,1},{6,2},{7,3},{0,4},{1,5},{2,6},{3,7},{12,8},{13,9},{14,... | collective-permute-start | bytes 786440 | tf_op jit(solution)/shard_map/ppermute | solution.py:217
  3.5 17.9 %collective-permute-start.7 = (bf16[2,256,256]{2,1,0:T(8,128)(2,1)S(1)}, bf16[2,256,256]{2,1,0:T(8,128)(2,1)S(1)}, u32[]{:S(2)}, u32[]{:S(2)}) collective-permute-start(bf16[2,256,256]{2,1,0:T(8,128)(2,1)S(1)} %bitcast_convert_fusion.refs_0_), channel_id=1, source_target_pairs={{2,0},{3,1},{0,2},{1,3},{6,4},{7,5},{4,6},{5,7},{10,8},{11,9},{8,1... | collective-permute-start | bytes 786440 | tf_op jit(solution)/shard_map/ppermute | solution.py:217
  4.8 9.9 %collective-permute-start.2 = (bf16[2,256,256]{2,1,0:T(8,128)(2,1)S(1)}, bf16[2,256,256]{2,1,0:T(8,128)(2,1)S(1)}, u32[]{:S(2)}, u32[]{:S(2)}) collective-permute-start(bf16[2,256,256]{2,1,0:T(8,128)(2,1)S(1)} %bitcast_convert_fusion.refs_0_), channel_id=1, source_target_pairs={{24,0},{16,8},{8,16},{0,24},{25,1},{17,9},{9,17},{1,25},{26,2},{18... | collective-permute-start | bytes 786440 | tf_op jit(solution)/shard_map/ppermute | solution.py:208
  5.0 13.1 %collective-permute-start.1 = (bf16[2,256,256]{2,1,0:T(8,128)(2,1)S(1)}, bf16[2,256,256]{2,1,0:T(8,128)(2,1)S(1)}, u32[]{:S(2)}, u32[]{:S(2)}) collective-permute-start(bf16[2,256,256]{2,1,0:T(8,128)(2,1)S(1)} %bitcast_convert_fusion.refs_0_), channel_id=1, source_target_pairs={{16,0},{24,8},{0,16},{8,24},{17,1},{25,9},{1,17},{9,25},{18,2},{26... | collective-permute-start | bytes 786440 | tf_op jit(solution)/shard_map/ppermute | solution.py:208
  6.2 11.8 %collective-permute-start = (bf16[2,256,256]{2,1,0:T(8,128)(2,1)S(1)}, bf16[2,256,256]{2,1,0:T(8,128)(2,1)S(1)}, u32[]{:S(2)}, u32[]{:S(2)}) collective-permute-start(bf16[2,256,256]{2,1,0:T(8,128)(2,1)S(1)} %bitcast_convert_fusion.refs_0_), channel_id=1, source_target_pairs={{8,0},{0,8},{24,16},{16,24},{9,1},{1,9},{25,17},{17,25},{10,2},{2,... | collective-permute-start | bytes 786440 | tf_op jit(solution)/shard_map/ppermute | solution.py:208
  19.4 23.5 %copy-start.2 = (f32[2,1,256,256]{3,2,1,0:T(8,128)S(1)}, f32[2,1,256,256]{3,2,1,0:T(8,128)}, u32[]{:S(2)}) copy-start(f32[2,1,256,256]{3,2,1,0:T(8,128)} %param.8) | copy-start | bytes 1572868
  19.4 8.3 %collective-permute-start.12 = (bf16[2,256,256]{2,1,0:T(8,128)(2,1)S(1)}, bf16[2,256,256]{2,1,0:T(8,128)(2,1)S(1)}, u32[]{:S(2)}, u32[]{:S(2)}) collective-permute-start(bf16[2,256,256]{2,1,0:T(8,128)(2,1)S(1)} %get-tuple-element.19.refs_2_.refs_0_), channel_id=1, source_target_pairs={{8,0},{0,8},{24,16},{16,24},{9,1},{1,9},{25,17},{17,25},{10,2},{2,... | collective-permute-start | bytes 786440 | tf_op jit(solution)/shard_map/ppermute | solution.py:208
  21.2 8.3 %collective-permute-start.10 = (bf16[2,256,256]{2,1,0:T(8,128)(2,1)S(1)}, bf16[2,256,256]{2,1,0:T(8,128)(2,1)S(1)}, u32[]{:S(2)}, u32[]{:S(2)}) collective-permute-start(bf16[2,256,256]{2,1,0:T(8,128)(2,1)S(1)} %get-tuple-element.19.refs_2_.refs_0_), channel_id=1, source_target_pairs={{16,0},{24,8},{0,16},{8,24},{17,1},{25,9},{1,17},{9,25},{18,2},{26... | collective-permute-start | bytes 786440 | tf_op jit(solution)/shard_map/ppermute | solution.py:208
  21.4 10.7 %collective-permute-start.9 = (bf16[2,256,256]{2,1,0:T(8,128)(2,1)S(1)}, bf16[2,256,256]{2,1,0:T(8,128)(2,1)S(1)}, u32[]{:S(2)}, u32[]{:S(2)}) collective-permute-start(bf16[2,256,256]{2,1,0:T(8,128)(2,1)S(1)} %shard_map.87.refs_2_), channel_id=1, source_target_pairs={{2,0},{3,1},{0,2},{1,3},{6,4},{7,5},{4,6},{5,7},{10,8},{11,9},{8,1... | collective-permute-start | bytes 786440 | tf_op jit(solution)/shard_map/ppermute | solution.py:217
  21.6 8.0 %collective-permute-start.3 = (bf16[256,256]{1,0:T(8,128)(2,1)S(1)}, bf16[256,256]{1,0:T(8,128)(2,1)S(1)}, u32[]{:S(2)}, u32[]{:S(2)}) collective-permute-start(bf16[256,256]{1,0:T(8,128)(2,1)S(1)} %get-tuple-element.17), channel_id=1, source_target_pairs={{0,0},{1,1},{2,2},{3,3},{4,16},{5,17},{6,18},{7,19},{8,8},{9,9},{1... | collective-permute-start | bytes 393224 | tf_op jit(solution)/shard_map/ppermute | solution.py:225
  24.5 7.5 %collective-permute-start.5 = (bf16[256,256]{1,0:T(8,128)(2,1)S(1)}, bf16[256,256]{1,0:T(8,128)(2,1)S(1)}, u32[]{:S(2)}, u32[]{:S(2)}) collective-permute-start(bf16[256,256]{1,0:T(8,128)(2,1)S(1)} %get-tuple-element.18), channel_id=1, source_target_pairs={{0,0},{1,1},{2,8},{3,9},{4,4},{5,5},{6,12},{7,13},{8,2},{9,3},{10,... | collective-permute-start | bytes 393224 | tf_op jit(solution)/shard_map/ppermute | solution.py:225
  27.6 6.3 %collective-permute-start.13 = (bf16[1,256,256]{2,1,0:T(8,128)(2,1)S(1)}, bf16[1,256,256]{2,1,0:T(8,128)(2,1)S(1)}, u32[]{:S(2)}, u32[]{:S(2)}) collective-permute-start(bf16[1,256,256]{2,1,0:T(8,128)(2,1)S(1)} %slice.17), channel_id=1, source_target_pairs={{16,0},{24,8},{0,16},{8,24},{17,1},{25,9},{1,17},{9,25},{18,2},{26... | collective-permute-start | bytes 393224 | tf_op jit(solution)/shard_map/ppermute | solution.py:208
  29.5 5.4 %collective-permute-start.11 = (bf16[1,256,256]{2,1,0:T(8,128)(2,1)S(1)}, bf16[1,256,256]{2,1,0:T(8,128)(2,1)S(1)}, u32[]{:S(2)}, u32[]{:S(2)}) collective-permute-start(bf16[1,256,256]{2,1,0:T(8,128)(2,1)S(1)} %slice.16), channel_id=1, source_target_pairs={{8,0},{0,8},{24,16},{16,24},{9,1},{1,9},{25,17},{17,25},{10,2},{2,... | collective-permute-start | bytes 393224 | tf_op jit(solution)/shard_map/ppermute | solution.py:208
  35.6 7.3 %collective-permute-start.14 = (bf16[8,256,256]{2,1,0:T(8,128)(2,1)S(1)}, bf16[8,256,256]{2,1,0:T(8,128)(2,1)S(1)}, u32[]{:S(2)}, u32[]{:S(2)}) collective-permute-start(bf16[8,256,256]{2,1,0:T(8,128)(2,1)S(1)} %shard_map.88.own_ref), channel_id=1, source_target_pairs={{1,0},{0,1},{3,2},{2,3},{5,4},{4,5},{7,6},{6,7},{9,8},{8,9},{11,10... | collective-permute-start | bytes 3145736 | tf_op jit(solution)/shard_map/ppermute | solution.py:214
  38.9 7.9 %collective-permute-start.4 = (bf16[256,256]{1,0:T(8,128)(2,1)S(1)}, bf16[256,256]{1,0:T(8,128)(2,1)S(1)}, u32[]{:S(2)}, u32[]{:S(2)}) collective-permute-start(bf16[256,256]{1,0:T(8,128)(2,1)S(1)} %collective-permute-done.3.refs_6_), channel_id=1, source_target_pairs={{0,0},{1,1},{2,8},{3,9},{4,4},{5,5},{6,12},{7,13},{8,2},{9,3},{10,... | collective-permute-start | bytes 393224 | tf_op jit(solution)/shard_map/ppermute | solution.py:225
  40.8 7.0 %collective-permute-start.6 = (bf16[256,256]{1,0:T(8,128)(2,1)S(1)}, bf16[256,256]{1,0:T(8,128)(2,1)S(1)}, u32[]{:S(2)}, u32[]{:S(2)}) collective-permute-start(bf16[256,256]{1,0:T(8,128)(2,1)S(1)} %collective-permute-done.5.refs_7_), channel_id=1, source_target_pairs={{0,1},{1,0},{2,3},{3,2},{4,17},{5,16},{6,19},{7,18},{8,9},{9,8},{1... | collective-permute-start | bytes 393224 | tf_op jit(solution)/shard_map/ppermute | solution.py:225
  48.6 8.9 %collective-permute-start.17 = (bf16[2,256,256]{2,1,0:T(8,128)(2,1)S(1)}, bf16[2,256,256]{2,1,0:T(8,128)(2,1)S(1)}, u32[]{:S(2)}, u32[]{:S(2)}) collective-permute-start(bf16[2,256,256]{2,1,0:T(8,128)(2,1)S(1)} %get-tuple-element.22.refs_0_), channel_id=1, source_target_pairs={{24,0},{16,8},{8,16},{0,24},{25,1},{17,9},{9,17},{1,25},{26,2},{18... | collective-permute-start | bytes 786440 | tf_op jit(solution)/shard_map/ppermute | solution.py:208
  48.6 13.5 %collective-permute-start.16 = (bf16[2,256,256]{2,1,0:T(8,128)(2,1)S(1)}, bf16[2,256,256]{2,1,0:T(8,128)(2,1)S(1)}, u32[]{:S(2)}, u32[]{:S(2)}) collective-permute-start(bf16[2,256,256]{2,1,0:T(8,128)(2,1)S(1)} %get-tuple-element.22.refs_0_), channel_id=1, source_target_pairs={{16,0},{24,8},{0,16},{8,24},{17,1},{25,9},{1,17},{9,25},{18,2},{26... | collective-permute-start | bytes 786440 | tf_op jit(solution)/shard_map/ppermute | solution.py:208
  50.3 12.7 %collective-permute-start.15 = (bf16[2,256,256]{2,1,0:T(8,128)(2,1)S(1)}, bf16[2,256,256]{2,1,0:T(8,128)(2,1)S(1)}, u32[]{:S(2)}, u32[]{:S(2)}) collective-permute-start(bf16[2,256,256]{2,1,0:T(8,128)(2,1)S(1)} %get-tuple-element.22.refs_0_), channel_id=1, source_target_pairs={{8,0},{0,8},{24,16},{16,24},{9,1},{1,9},{25,17},{17,25},{10,2},{2,... | collective-permute-start | bytes 786440 | tf_op jit(solution)/shard_map/ppermute | solution.py:208
  51.4 13.8 %collective-permute-start.23 = (bf16[2,256,256]{2,1,0:T(8,128)(2,1)S(1)}, bf16[2,256,256]{2,1,0:T(8,128)(2,1)S(1)}, u32[]{:S(2)}, u32[]{:S(2)}) collective-permute-start(bf16[2,256,256]{2,1,0:T(8,128)(2,1)S(1)} %get-tuple-element.22.refs_0_), channel_id=1, source_target_pairs={{4,0},{5,1},{6,2},{7,3},{0,4},{1,5},{2,6},{3,7},{12,8},{13,9},{14,... | collective-permute-start | bytes 786440 | tf_op jit(solution)/shard_map/ppermute | solution.py:217
  53.0 12.1 %collective-permute-start.22 = (bf16[2,256,256]{2,1,0:T(8,128)(2,1)S(1)}, bf16[2,256,256]{2,1,0:T(8,128)(2,1)S(1)}, u32[]{:S(2)}, u32[]{:S(2)}) collective-permute-start(bf16[2,256,256]{2,1,0:T(8,128)(2,1)S(1)} %get-tuple-element.22.refs_0_), channel_id=1, source_target_pairs={{2,0},{3,1},{0,2},{1,3},{6,4},{7,5},{4,6},{5,7},{10,8},{11,9},{8,1... | collective-permute-start | bytes 786440 | tf_op jit(solution)/shard_map/ppermute | solution.py:217
  64.3 9.4 %collective-permute-start.27 = (bf16[2,256,256]{2,1,0:T(8,128)(2,1)S(1)}, bf16[2,256,256]{2,1,0:T(8,128)(2,1)S(1)}, u32[]{:S(2)}, u32[]{:S(2)}) collective-permute-start(bf16[2,256,256]{2,1,0:T(8,128)(2,1)S(1)} %get-tuple-element.25.refs_2_.refs_0_), channel_id=1, source_target_pairs={{8,0},{0,8},{24,16},{16,24},{9,1},{1,9},{25,17},{17,25},{10,2},{2,... | collective-permute-start | bytes 786440 | tf_op jit(solution)/shard_map/ppermute | solution.py:208
  65.1 8.7 %collective-permute-start.25 = (bf16[2,256,256]{2,1,0:T(8,128)(2,1)S(1)}, bf16[2,256,256]{2,1,0:T(8,128)(2,1)S(1)}, u32[]{:S(2)}, u32[]{:S(2)}) collective-permute-start(bf16[2,256,256]{2,1,0:T(8,128)(2,1)S(1)} %get-tuple-element.25.refs_2_.refs_0_), channel_id=1, source_target_pairs={{16,0},{24,8},{0,16},{8,24},{17,1},{25,9},{1,17},{9,25},{18,2},{26... | collective-permute-start | bytes 786440 | tf_op jit(solution)/shard_map/ppermute | solution.py:208
  65.1 11.9 %collective-permute-start.24 = (bf16[2,256,256]{2,1,0:T(8,128)(2,1)S(1)}, bf16[2,256,256]{2,1,0:T(8,128)(2,1)S(1)}, u32[]{:S(2)}, u32[]{:S(2)}) collective-permute-start(bf16[2,256,256]{2,1,0:T(8,128)(2,1)S(1)} %shard_map.92.refs_2_), channel_id=1, source_target_pairs={{2,0},{3,1},{0,2},{1,3},{6,4},{7,5},{4,6},{5,7},{10,8},{11,9},{8,1... | collective-permute-start | bytes 786440 | tf_op jit(solution)/shard_map/ppermute | solution.py:217
  67.5 8.3 %collective-permute-start.18 = (bf16[256,256]{1,0:T(8,128)(2,1)S(1)}, bf16[256,256]{1,0:T(8,128)(2,1)S(1)}, u32[]{:S(2)}, u32[]{:S(2)}) collective-permute-start(bf16[256,256]{1,0:T(8,128)(2,1)S(1)} %get-tuple-element.23), channel_id=1, source_target_pairs={{0,0},{1,1},{2,2},{3,3},{4,16},{5,17},{6,18},{7,19},{8,8},{9,9},{1... | collective-permute-start | bytes 393224 | tf_op jit(solution)/shard_map/ppermute | solution.py:225
  70.1 7.0 %collective-permute-start.20 = (bf16[256,256]{1,0:T(8,128)(2,1)S(1)}, bf16[256,256]{1,0:T(8,128)(2,1)S(1)}, u32[]{:S(2)}, u32[]{:S(2)}) collective-permute-start(bf16[256,256]{1,0:T(8,128)(2,1)S(1)} %get-tuple-element.24), channel_id=1, source_target_pairs={{0,0},{1,1},{2,8},{3,9},{4,4},{5,5},{6,12},{7,13},{8,2},{9,3},{10,... | collective-permute-start | bytes 393224 | tf_op jit(solution)/shard_map/ppermute | solution.py:225
  73.8 4.8 %collective-permute-start.28 = (bf16[1,256,256]{2,1,0:T(8,128)(2,1)S(1)}, bf16[1,256,256]{2,1,0:T(8,128)(2,1)S(1)}, u32[]{:S(2)}, u32[]{:S(2)}) collective-permute-start(bf16[1,256,256]{2,1,0:T(8,128)(2,1)S(1)} %slice.19), channel_id=1, source_target_pairs={{16,0},{24,8},{0,16},{8,24},{17,1},{25,9},{1,17},{9,25},{18,2},{26... | collective-permute-start | bytes 393224 | tf_op jit(solution)/shard_map/ppermute | solution.py:208
  73.9 4.7 %collective-permute-start.26 = (bf16[1,256,256]{2,1,0:T(8,128)(2,1)S(1)}, bf16[1,256,256]{2,1,0:T(8,128)(2,1)S(1)}, u32[]{:S(2)}, u32[]{:S(2)}) collective-permute-start(bf16[1,256,256]{2,1,0:T(8,128)(2,1)S(1)} %slice.18), channel_id=1, source_target_pairs={{8,0},{0,8},{24,16},{16,24},{9,1},{1,9},{25,17},{17,25},{10,2},{2,... | collective-permute-start | bytes 393224 | tf_op jit(solution)/shard_map/ppermute | solution.py:208
  79.3 8.4 %collective-permute-start.29 = (bf16[8,256,256]{2,1,0:T(8,128)(2,1)S(1)}, bf16[8,256,256]{2,1,0:T(8,128)(2,1)S(1)}, u32[]{:S(2)}, u32[]{:S(2)}) collective-permute-start(bf16[8,256,256]{2,1,0:T(8,128)(2,1)S(1)} %shard_map.93.own_ref), channel_id=1, source_target_pairs={{1,0},{0,1},{3,2},{2,3},{5,4},{4,5},{7,6},{6,7},{9,8},{8,9},{11,10... | collective-permute-start | bytes 3145736 | tf_op jit(solution)/shard_map/ppermute | solution.py:214
  82.3 7.9 %collective-permute-start.19 = (bf16[256,256]{1,0:T(8,128)(2,1)S(1)}, bf16[256,256]{1,0:T(8,128)(2,1)S(1)}, u32[]{:S(2)}, u32[]{:S(2)}) collective-permute-start(bf16[256,256]{1,0:T(8,128)(2,1)S(1)} %collective-permute-done.18.refs_6_), channel_id=1, source_target_pairs={{0,0},{1,1},{2,8},{3,9},{4,4},{5,5},{6,12},{7,13},{8,2},{9,3},{10,... | collective-permute-start | bytes 393224 | tf_op jit(solution)/shard_map/ppermute | solution.py:225
  86.2 7.3 %collective-permute-start.21 = (bf16[256,256]{1,0:T(8,128)(2,1)S(1)}, bf16[256,256]{1,0:T(8,128)(2,1)S(1)}, u32[]{:S(2)}, u32[]{:S(2)}) collective-permute-start(bf16[256,256]{1,0:T(8,128)(2,1)S(1)} %collective-permute-done.20.refs_7_), channel_id=1, source_target_pairs={{0,1},{1,0},{2,3},{3,2},{4,17},{5,16},{6,19},{7,18},{8,9},{9,8},{1... | collective-permute-start | bytes 393224 | tf_op jit(solution)/shard_map/ppermute | solution.py:225
  (3 other events, 2.9 us)

commit v4 on v3

--- a/solution.py
+++ b/solution.py
@@ -71,10 +71,10 @@
     return found
 
 
-def coupled_body(rows, meta, k_ref, *refs):
+def coupled_body(rows, k_ref, *refs):
     out_ref, same_ref, other_ref = refs[-3:]
     orb_rows, virt, _ = out_ref.shape
-    side = meta[2 * orb_rows, 1] % 2
+    side = lax.rem(lax.axis_index("col"), 2)
     total = None
     for step in range(rows):
         for t in range(orb_rows):
@@ -83,34 +83,40 @@
             total = part if total is None else total + part
     first, second = total[:virt].astype(out_ref.dtype), total[virt:].astype(out_ref.dtype)
     out_ref[0], out_ref[1] = first, second
-    same_ref[...] = jnp.where(side == 0, first, second)
-    other_ref[...] = jnp.where(side == 0, second, first)
-
-
-def coupled_blocks(rows, meta, kept, pieces):
+
+    @pl.when(side == 0)
+    def _():
+        same_ref[...], other_ref[...] = first, second
+
+    @pl.when(side == 1)
+    def _():
+        same_ref[...], other_ref[...] = second, first
+
+
+def coupled_blocks(rows, kept, pieces):
     orb_rows, virt, _ = pieces[0].shape
     count = rows * orb_rows
     block = jax.ShapeDtypeStruct((virt, virt), jnp.bfloat16)
     shape = (jax.ShapeDtypeStruct((orb_rows, virt, virt), jnp.bfloat16), block, block)
     body = functools.partial(coupled_body, rows)
     flops, moved = 2 * orb_rows * count * virt**3, 2 * (orb_rows + 1) * count * virt**2
-    return call(body, shape, [SMEM] + [VMEM] * (1 + len(pieces)), flops, moved, meta, kept, *pieces)
-
-
-def column_body(meta, *refs):
+    return call(body, shape, [VMEM] * (1 + len(pieces)), flops, moved, kept, *pieces)
+
+
+def column_body(*refs):
     out_ref = refs[-1]
     orb_rows = refs[0].shape[0]
-    my_place = meta[2 * orb_rows, 1] // 2
+    my_place = lax.div(lax.axis_index("col"), 2)
     for step in range(out_ref.shape[0] // orb_rows):
         out_ref[pl.ds((my_place ^ step) * orb_rows, orb_rows)] = refs[step][...]
 
 
-def whole_column(meta, pieces, others):
+def whole_column(pieces, others):
     orb_rows, virt, _ = pieces[0].shape
     shape = jax.ShapeDtypeStruct((orb_rows * len(pieces), virt, virt), jnp.bfloat16)
     operands = [*pieces, *others]
     moved = 4 * orb_rows * len(pieces) * virt**2
-    return call(column_body, shape, [SMEM] + [VMEM] * len(operands), 0, moved, meta, *operands)
+    return call(column_body, shape, [VMEM] * len(operands), 0, moved, *operands)
 
 
 def tied_body(*refs):
@@ -159,8 +165,8 @@
     out_ref[...] = damping * state_ref[...] - residual * inverse_ref[...]
 
 
-def second_body(meta, same_ref, other_ref, part_ref, inverse_ref, out_ref, *half_refs):
-    side = meta[2 * out_ref.shape[0], 1] % 2
+def second_body(same_ref, other_ref, part_ref, inverse_ref, out_ref, *half_refs):
+    side = lax.rem(lax.axis_index("col"), 2)
     for ref, at in ((same_ref, side), (other_ref, 1 - side)):
         state = part_ref[at] - coupling * turned(ref[...]) * inverse_ref[at]
         out_ref[at] = state
@@ -178,10 +184,10 @@
     )
 
 
-def second_update(meta, same, other, part, inverse, with_half):
+def second_update(same, other, part, inverse, with_half):
     shape = (jax.ShapeDtypeStruct(part.shape, jnp.float32), jax.ShapeDtypeStruct(part.shape, jnp.bfloat16))
     shape = shape if with_half else shape[:1]
-    return call(second_body, shape, [SMEM] + [VMEM] * 4, 0, 16 * part.size, meta, same, other, part, inverse)
+    return call(second_body, shape, [VMEM] * 4, 0, 16 * part.size, same, other, part, inverse)
 
 
 def on_device(
@@ -255,7 +261,7 @@
         column = {0: half, 1: from_chip(half, 1)}
         for step in range(2, halves, 2):
             column[step] = from_chip(half, step)
-        coupled, same, other = coupled_blocks(rows, meta, kept, a_pieces)
+        coupled, same, other = coupled_blocks(rows, kept, a_pieces)
         near = from_row(coupled, 1)
         c_pieces, far = [coupled, near], []
         for step in range(2, rows, 2):
@@ -267,10 +273,10 @@
             column[step] = tied(column[step], column[1], coupled)
             column[step + 1] = from_chip(column[step], 1)
         column = [column[step] for step in range(halves)]
-        own = whole_column(meta, column, [*far, same, other])
+        own = whole_column(column, [*far, same, other])
         same, other = crossing(same, last_bits), crossing(other, high_parts, 1)
         part = first_update(rows, meta, own, swapped(own), c_pieces, state, coulomb_own, inverse)
-        state, *halves_out = second_update(meta, same, other, part, inverse, sweep_index < ITERS - 1)
+        state, *halves_out = second_update(same, other, part, inverse, sweep_index < ITERS - 1)
         half = halves_out[0] if halves_out else None
     return state[:, None]
 

time: 96.2 us -> 92.6 us (0.963)
  Pallas kernels: 9.93 us -> 6.36 us
    pallas_call x9, Pallas kernels: 9.92 us -> 6.36 us  [call(): pl.pallas_call(body, out_shape=out_shape, in_specs=in_specs, out_specs=VM...]
  transfers between devices with their start and end apart: 30 -> 30, of which waited for: 15 -> 16; matrix products, arithmetic and copies ran while one was open for 4% -> 4% of each run, Pallas kernels for 7% -> 6%
where the time goes in v4:
time: 92.6 us; the launch traced here: 91.4 us
  starting transfers between devices  44.8 us (48%)
  waiting for transfers between devices  32.5 us (35%)
  Pallas kernels  6.36 us (7%)
  local copies, waits for them, and re-layouts  4.65 us (5%)
  other arithmetic  2.77 us (3%)
    ppermute x8, starting transfers between devices, crossing(): return lax.ppermute(x, ('row', 'col'), pairs)  21.5 us
    ppermute x14, waiting for transfers between devices, from_row(): return lax.ppermute(x, 'row', [(r ^ step, r) for r in range(rows)])  18.6 us
    ppermute x8, waiting for transfers between devices, crossing(): return lax.ppermute(x, ('row', 'col'), pairs)  13.7 us
    ppermute x14, starting transfers between devices, from_row(): return lax.ppermute(x, 'row', [(r ^ step, r) for r in range(rows)])  9.31 us
    ppermute x6, starting transfers between devices, from_chip(): return lax.ppermute(x, 'col', [(c ^ 2 * step, c) for c in range(cols)])  7.58 us
    ppermute x2, starting transfers between devices, swapped(): return lax.ppermute(x, 'col', [(c ^ 1, c) for c in range(cols)])  6.42 us
    pallas_call x9, Pallas kernels, call(): pl.pallas_call(body, out_shape=out_shape, in_specs=in_specs, out_specs=VM...  6.36 us
    unnamed x10, local copies, waits for them, and re-layouts  2.93 us
  transfers between devices with their start and end apart: 30, of which 16 were waited for; matrix products, arithmetic and copies ran while one was open for 4% of the time, Pallas kernels for 6%

profile of v4, /device:TPU:7, one launch (start us, length us, event | category | flops | bytes accessed | tf_op | source)
XLA Modules:
  0.0 91.4 jit_solution(332191240414653142)
XLA Ops:
  1.1 2.4 %collective-permute-start.8 = (bf16[2,256,256]{2,1,0:T(8,128)(2,1)S(1)}, bf16[2,256,256]{2,1,0:T(8,128)(2,1)S(1)}, u32[]{:S(2)}, u32[]{:S(2)}) collective-permute-start(bf16[2,256,256]{2,1,0:T(8,128)(2,1)S(1)} %bitcast_convert_fusion.refs_0_), channel_id=1, source_target_pairs={{4,0},{5,1},{6,2},{7,3},{0,4},{1,5},{2,6},{3,7},{12,8},{13,9},{14,... | collective-permute-start | bytes 786440 | tf_op jit(solution)/shard_map/ppermute | solution.py:223
  3.5 1.3 %collective-permute-start.7 = (bf16[2,256,256]{2,1,0:T(8,128)(2,1)S(1)}, bf16[2,256,256]{2,1,0:T(8,128)(2,1)S(1)}, u32[]{:S(2)}, u32[]{:S(2)}) collective-permute-start(bf16[2,256,256]{2,1,0:T(8,128)(2,1)S(1)} %bitcast_convert_fusion.refs_0_), channel_id=1, source_target_pairs={{2,0},{3,1},{0,2},{1,3},{6,4},{7,5},{4,6},{5,7},{10,8},{11,9},{8,1... | collective-permute-start | bytes 786440 | tf_op jit(solution)/shard_map/ppermute | solution.py:223
  5.0 1.2 %collective-permute-start.1 = (bf16[2,256,256]{2,1,0:T(8,128)(2,1)S(1)}, bf16[2,256,256]{2,1,0:T(8,128)(2,1)S(1)}, u32[]{:S(2)}, u32[]{:S(2)}) collective-permute-start(bf16[2,256,256]{2,1,0:T(8,128)(2,1)S(1)} %bitcast_convert_fusion.refs_0_), channel_id=1, source_target_pairs={{16,0},{24,8},{0,16},{8,24},{17,1},{25,9},{1,17},{9,25},{18,2},{26... | collective-permute-start | bytes 786440 | tf_op jit(solution)/shard_map/ppermute | solution.py:214
  6.2 1.2 %collective-permute-start = (bf16[2,256,256]{2,1,0:T(8,128)(2,1)S(1)}, bf16[2,256,256]{2,1,0:T(8,128)(2,1)S(1)}, u32[]{:S(2)}, u32[]{:S(2)}) collective-permute-start(bf16[2,256,256]{2,1,0:T(8,128)(2,1)S(1)} %bitcast_convert_fusion.refs_0_), channel_id=1, source_target_pairs={{8,0},{0,8},{24,16},{16,24},{9,1},{1,9},{25,17},{17,25},{10,2},{2,... | collective-permute-start | bytes 786440 | tf_op jit(solution)/shard_map/ppermute | solution.py:214
  10.8 1.6 %copy-done.1 = bf16[2,8,256,256]{3,2,1,0:T(8,128)(2,1)S(1)} copy-done((bf16[2,8,256,256]{3,2,1,0:T(8,128)(2,1)S(1)}, bf16[2,8,256,256]{3,2,1,0:T(8,128)(2,1)}, u32[]{:S(2)}) %copy-start.1) | copy-done | bytes 2097176
  14.7 3.3 %collective-permute-done.1.refs_2_ = bf16[2,256,256]{2,1,0:T(8,128)(2,1)S(1)} collective-permute-done((bf16[2,256,256]{2,1,0:T(8,128)(2,1)S(1)}, bf16[2,256,256]{2,1,0:T(8,128)(2,1)S(1)}, u32[]{:S(2)}, u32[]{:S(2)}) %collective-permute-start.1) | collective-permute-done | bytes 262176 | tf_op jit(solution)/shard_map/ppermute | solution.py:214
  18.8 1.8 %collective-permute-start.12 = (bf16[2,256,256]{2,1,0:T(8,128)(2,1)S(1)}, bf16[2,256,256]{2,1,0:T(8,128)(2,1)S(1)}, u32[]{:S(2)}, u32[]{:S(2)}) collective-permute-start(bf16[2,256,256]{2,1,0:T(8,128)(2,1)S(1)} %get-tuple-element.19.refs_2_.refs_0_), channel_id=1, source_target_pairs={{8,0},{0,8},{24,16},{16,24},{9,1},{1,9},{25,17},{17,25},{10,2},{2,... | collective-permute-start | bytes 786440 | tf_op jit(solution)/shard_map/ppermute | solution.py:214
  21.0 2.9 %collective-permute-start.3 = (bf16[256,256]{1,0:T(8,128)(2,1)S(1)}, bf16[256,256]{1,0:T(8,128)(2,1)S(1)}, u32[]{:S(2)}, u32[]{:S(2)}) collective-permute-start(bf16[256,256]{1,0:T(8,128)(2,1)S(1)} %get-tuple-element.17), channel_id=1, source_target_pairs={{0,0},{1,1},{2,2},{3,3},{4,16},{5,17},{6,18},{7,19},{8,8},{9,9},{1... | collective-permute-start | bytes 393224 | tf_op jit(solution)/shard_map/ppermute | solution.py:231
  23.9 3.1 %collective-permute-start.5 = (bf16[256,256]{1,0:T(8,128)(2,1)S(1)}, bf16[256,256]{1,0:T(8,128)(2,1)S(1)}, u32[]{:S(2)}, u32[]{:S(2)}) collective-permute-start(bf16[256,256]{1,0:T(8,128)(2,1)S(1)} %get-tuple-element.18), channel_id=1, source_target_pairs={{0,0},{1,1},{2,8},{3,9},{4,4},{5,5},{6,12},{7,13},{8,2},{9,3},{10,... | collective-permute-start | bytes 393224 | tf_op jit(solution)/shard_map/ppermute | solution.py:231
  29.0 2.5 %collective-permute-done.5.refs_7_ = bf16[256,256]{1,0:T(8,128)(2,1)S(1)} collective-permute-done((bf16[256,256]{1,0:T(8,128)(2,1)S(1)}, bf16[256,256]{1,0:T(8,128)(2,1)S(1)}, u32[]{:S(2)}, u32[]{:S(2)}) %collective-permute-start.5) | collective-permute-done | bytes 131104 | tf_op jit(solution)/shard_map/ppermute | solution.py:231
  31.5 1.9 %collective-permute-done.13.refs_5_.refs_4_ = bf16[1,256,256]{2,1,0:T(8,128)(2,1)S(1)} collective-permute-done((bf16[1,256,256]{2,1,0:T(8,128)(2,1)S(1)}, bf16[1,256,256]{2,1,0:T(8,128)(2,1)S(1)}, u32[]{:S(2)}, u32[]{:S(2)}) %collective-permute-start.13) | collective-permute-done | bytes 131104 | tf_op jit(solution)/shard_map/ppermute | solution.py:214
  34.4 3.3 %collective-permute-start.14 = (bf16[8,256,256]{2,1,0:T(8,128)(2,1)S(1)}, bf16[8,256,256]{2,1,0:T(8,128)(2,1)S(1)}, u32[]{:S(2)}, u32[]{:S(2)}) collective-permute-start(bf16[8,256,256]{2,1,0:T(8,128)(2,1)S(1)} %shard_map.88.own_ref), channel_id=1, source_target_pairs={{1,0},{0,1},{3,2},{2,3},{5,4},{4,5},{7,6},{6,7},{9,8},{8,9},{11,10... | collective-permute-start | bytes 3145736 | tf_op jit(solution)/shard_map/ppermute | solution.py:220
  37.7 1.9 %collective-permute-start.4 = (bf16[256,256]{1,0:T(8,128)(2,1)S(1)}, bf16[256,256]{1,0:T(8,128)(2,1)S(1)}, u32[]{:S(2)}, u32[]{:S(2)}) collective-permute-start(bf16[256,256]{1,0:T(8,128)(2,1)S(1)} %collective-permute-done.3.refs_6_), channel_id=1, source_target_pairs={{0,0},{1,1},{2,8},{3,9},{4,4},{5,5},{6,12},{7,13},{8,2},{9,3},{10,... | collective-permute-start | bytes 393224 | tf_op jit(solution)/shard_map/ppermute | solution.py:231
  39.6 2.0 %collective-permute-start.6 = (bf16[256,256]{1,0:T(8,128)(2,1)S(1)}, bf16[256,256]{1,0:T(8,128)(2,1)S(1)}, u32[]{:S(2)}, u32[]{:S(2)}) collective-permute-start(bf16[256,256]{1,0:T(8,128)(2,1)S(1)} %collective-permute-done.5.refs_7_), channel_id=1, source_target_pairs={{0,1},{1,0},{2,3},{3,2},{4,17},{5,16},{6,19},{7,18},{8,9},{9,8},{1... | collective-permute-start | bytes 393224 | tf_op jit(solution)/shard_map/ppermute | solution.py:231
  41.7 1.4 %shard_map.89.part_ref = f32[2,256,256]{2,1,0:T(8,128)S(1)} custom-call(s32[5,8]{1,0:T(8,128)S(1)} %pad_add_fusion.meta, bf16[8,256,256]{2,1,0:T(8,128)(2,1)S(1)} %shard_map.88.own_ref, bf16[8,256,256]{2,1,0:T(8,128)(2,1)S(1)} %collective-permute-done.14.other_ref, bf16[2,256,256]{2,1,0:T(8,128)(2,1)S(1)} %get-tuple-element.19.refs_2_.refs_0_, ...), custom_call_target="tpu_custom_call" | custom-call | flops 536870912 | bytes 6291456 | tf_op jit(solution)/shard_map/pallas_call | solution.py:23
  43.1 2.6 %collective-permute-done.4.same_ref = bf16[256,256]{1,0:T(8,128)(2,1)S(1)} collective-permute-done((bf16[256,256]{1,0:T(8,128)(2,1)S(1)}, bf16[256,256]{1,0:T(8,128)(2,1)S(1)}, u32[]{:S(2)}, u32[]{:S(2)}) %collective-permute-start.4) | collective-permute-done | bytes 131104 | tf_op jit(solution)/shard_map/ppermute | solution.py:231
  46.9 1.6 %collective-permute-start.16 = (bf16[2,256,256]{2,1,0:T(8,128)(2,1)S(1)}, bf16[2,256,256]{2,1,0:T(8,128)(2,1)S(1)}, u32[]{:S(2)}, u32[]{:S(2)}) collective-permute-start(bf16[2,256,256]{2,1,0:T(8,128)(2,1)S(1)} %get-tuple-element.22.refs_0_), channel_id=1, source_target_pairs={{16,0},{24,8},{0,16},{8,24},{17,1},{25,9},{1,17},{9,25},{18,2},{26... | collective-permute-start | bytes 786440 | tf_op jit(solution)/shard_map/ppermute | solution.py:214
  49.6 1.6 %collective-permute-start.23 = (bf16[2,256,256]{2,1,0:T(8,128)(2,1)S(1)}, bf16[2,256,256]{2,1,0:T(8,128)(2,1)S(1)}, u32[]{:S(2)}, u32[]{:S(2)}) collective-permute-start(bf16[2,256,256]{2,1,0:T(8,128)(2,1)S(1)} %get-tuple-element.22.refs_0_), channel_id=1, source_target_pairs={{4,0},{5,1},{6,2},{7,3},{0,4},{1,5},{2,6},{3,7},{12,8},{13,9},{14,... | collective-permute-start | bytes 786440 | tf_op jit(solution)/shard_map/ppermute | solution.py:223
  51.2 4.4 %collective-permute-done.17.refs_3_ = bf16[2,256,256]{2,1,0:T(8,128)(2,1)S(1)} collective-permute-done((bf16[2,256,256]{2,1,0:T(8,128)(2,1)S(1)}, bf16[2,256,256]{2,1,0:T(8,128)(2,1)S(1)}, u32[]{:S(2)}, u32[]{:S(2)}) %collective-permute-start.17) | collective-permute-done | bytes 262176 | tf_op jit(solution)/shard_map/ppermute | solution.py:214
  55.7 4.7 %collective-permute-done.16.refs_2_ = bf16[2,256,256]{2,1,0:T(8,128)(2,1)S(1)} collective-permute-done((bf16[2,256,256]{2,1,0:T(8,128)(2,1)S(1)}, bf16[2,256,256]{2,1,0:T(8,128)(2,1)S(1)}, u32[]{:S(2)}, u32[]{:S(2)}) %collective-permute-start.16) | collective-permute-done | bytes 262176 | tf_op jit(solution)/shard_map/ppermute | solution.py:214
  63.0 2.1 %collective-permute-start.24 = (bf16[2,256,256]{2,1,0:T(8,128)(2,1)S(1)}, bf16[2,256,256]{2,1,0:T(8,128)(2,1)S(1)}, u32[]{:S(2)}, u32[]{:S(2)}) collective-permute-start(bf16[2,256,256]{2,1,0:T(8,128)(2,1)S(1)} %shard_map.92.refs_2_), channel_id=1, source_target_pairs={{2,0},{3,1},{0,2},{1,3},{6,4},{7,5},{4,6},{5,7},{10,8},{11,9},{8,1... | collective-permute-start | bytes 786440 | tf_op jit(solution)/shard_map/ppermute | solution.py:223
  65.1 2.6 %collective-permute-start.18 = (bf16[256,256]{1,0:T(8,128)(2,1)S(1)}, bf16[256,256]{1,0:T(8,128)(2,1)S(1)}, u32[]{:S(2)}, u32[]{:S(2)}) collective-permute-start(bf16[256,256]{1,0:T(8,128)(2,1)S(1)} %get-tuple-element.23), channel_id=1, source_target_pairs={{0,0},{1,1},{2,2},{3,3},{4,16},{5,17},{6,18},{7,19},{8,8},{9,9},{1... | collective-permute-start | bytes 393224 | tf_op jit(solution)/shard_map/ppermute | solution.py:231
  67.7 3.7 %collective-permute-start.20 = (bf16[256,256]{1,0:T(8,128)(2,1)S(1)}, bf16[256,256]{1,0:T(8,128)(2,1)S(1)}, u32[]{:S(2)}, u32[]{:S(2)}) collective-permute-start(bf16[256,256]{1,0:T(8,128)(2,1)S(1)} %get-tuple-element.24), channel_id=1, source_target_pairs={{0,0},{1,1},{2,8},{3,9},{4,4},{5,5},{6,12},{7,13},{8,2},{9,3},{10,... | collective-permute-start | bytes 393224 | tf_op jit(solution)/shard_map/ppermute | solution.py:231
  71.6 1.8 %collective-permute-done.18.refs_6_ = bf16[256,256]{1,0:T(8,128)(2,1)S(1)} collective-permute-done((bf16[256,256]{1,0:T(8,128)(2,1)S(1)}, bf16[256,256]{1,0:T(8,128)(2,1)S(1)}, u32[]{:S(2)}, u32[]{:S(2)}) %collective-permute-start.18) | collective-permute-done | bytes 131104 | tf_op jit(solution)/shard_map/ppermute | solution.py:231
  73.4 1.3 %collective-permute-done.20.refs_7_ = bf16[256,256]{1,0:T(8,128)(2,1)S(1)} collective-permute-done((bf16[256,256]{1,0:T(8,128)(2,1)S(1)}, bf16[256,256]{1,0:T(8,128)(2,1)S(1)}, u32[]{:S(2)}, u32[]{:S(2)}) %collective-permute-start.20) | collective-permute-done | bytes 131104 | tf_op jit(solution)/shard_map/ppermute | solution.py:231
  74.7 1.5 %collective-permute-done.28.refs_5_.refs_4_ = bf16[1,256,256]{2,1,0:T(8,128)(2,1)S(1)} collective-permute-done((bf16[1,256,256]{2,1,0:T(8,128)(2,1)S(1)}, bf16[1,256,256]{2,1,0:T(8,128)(2,1)S(1)}, u32[]{:S(2)}, u32[]{:S(2)}) %collective-permute-start.28) | collective-permute-done | bytes 131104 | tf_op jit(solution)/shard_map/ppermute | solution.py:214
  76.3 3.1 %collective-permute-start.29 = (bf16[8,256,256]{2,1,0:T(8,128)(2,1)S(1)}, bf16[8,256,256]{2,1,0:T(8,128)(2,1)S(1)}, u32[]{:S(2)}, u32[]{:S(2)}) collective-permute-start(bf16[8,256,256]{2,1,0:T(8,128)(2,1)S(1)} %shard_map.93.own_ref), channel_id=1, source_target_pairs={{1,0},{0,1},{3,2},{2,3},{5,4},{4,5},{7,6},{6,7},{9,8},{8,9},{11,10... | collective-permute-start | bytes 3145736 | tf_op jit(solution)/shard_map/ppermute | solution.py:220
  79.4 3.8 %collective-permute-start.19 = (bf16[256,256]{1,0:T(8,128)(2,1)S(1)}, bf16[256,256]{1,0:T(8,128)(2,1)S(1)}, u32[]{:S(2)}, u32[]{:S(2)}) collective-permute-start(bf16[256,256]{1,0:T(8,128)(2,1)S(1)} %collective-permute-done.18.refs_6_), channel_id=1, source_target_pairs={{0,0},{1,1},{2,8},{3,9},{4,4},{5,5},{6,12},{7,13},{8,2},{9,3},{10,... | collective-permute-start | bytes 393224 | tf_op jit(solution)/shard_map/ppermute | solution.py:231
  83.2 1.4 %collective-permute-start.21 = (bf16[256,256]{1,0:T(8,128)(2,1)S(1)}, bf16[256,256]{1,0:T(8,128)(2,1)S(1)}, u32[]{:S(2)}, u32[]{:S(2)}) collective-permute-start(bf16[256,256]{1,0:T(8,128)(2,1)S(1)} %collective-permute-done.20.refs_7_), channel_id=1, source_target_pairs={{0,1},{1,0},{2,3},{3,2},{4,17},{5,16},{6,19},{7,18},{8,9},{9,8},{1... | collective-permute-start | bytes 393224 | tf_op jit(solution)/shard_map/ppermute | solution.py:231
  84.6 1.3 %shard_map.94.part_ref = f32[2,256,256]{2,1,0:T(8,128)S(1)} custom-call(s32[5,8]{1,0:T(8,128)S(1)} %pad_add_fusion.meta, bf16[8,256,256]{2,1,0:T(8,128)(2,1)S(1)} %shard_map.93.own_ref, bf16[8,256,256]{2,1,0:T(8,128)(2,1)S(1)} %collective-permute-done.29.other_ref, bf16[2,256,256]{2,1,0:T(8,128)(2,1)S(1)} %get-tuple-element.25.refs_2_.refs_0_, ...), custom_call_target="tpu_custom_call" | custom-call | flops 536870912 | bytes 6291456 | tf_op jit(solution)/shard_map/pallas_call | solution.py:23
  86.0 1.3 %collective-permute-done.19.same_ref = bf16[256,256]{1,0:T(8,128)(2,1)S(1)} collective-permute-done((bf16[256,256]{1,0:T(8,128)(2,1)S(1)}, bf16[256,256]{1,0:T(8,128)(2,1)S(1)}, u32[]{:S(2)}, u32[]{:S(2)}) %collective-permute-start.19) | collective-permute-done | bytes 131104 | tf_op jit(solution)/shard_map/ppermute | solution.py:231
  87.2 3.2 %collective-permute-done.21.other_ref = bf16[256,256]{1,0:T(8,128)(2,1)S(1)} collective-permute-done((bf16[256,256]{1,0:T(8,128)(2,1)S(1)}, bf16[256,256]{1,0:T(8,128)(2,1)S(1)}, u32[]{:S(2)}, u32[]{:S(2)}) %collective-permute-start.21) | collective-permute-done | bytes 131104 | tf_op jit(solution)/shard_map/ppermute | solution.py:231
  (65 shorter events, 17.1 us)
Async XLA Ops:
  0.0 9.1 %copy-start = (s32[2,8,8]{2,1,0:T(8,128)S(1)}, s32[2,8,8]{2,1,0:T(8,128)}, u32[]{:S(2)}) copy-start(s32[2,8,8]{2,1,0:T(8,128)} %param.12) | copy-start | bytes 1540
  1.1 19.7 %collective-permute-start.8 = (bf16[2,256,256]{2,1,0:T(8,128)(2,1)S(1)}, bf16[2,256,256]{2,1,0:T(8,128)(2,1)S(1)}, u32[]{:S(2)}, u32[]{:S(2)}) collective-permute-start(bf16[2,256,256]{2,1,0:T(8,128)(2,1)S(1)} %bitcast_convert_fusion.refs_0_), channel_id=1, source_target_pairs={{4,0},{5,1},{6,2},{7,3},{0,4},{1,5},{2,6},{3,7},{12,8},{13,9},{14,... | collective-permute-start | bytes 786440 | tf_op jit(solution)/shard_map/ppermute | solution.py:223
  3.5 17.3 %collective-permute-start.7 = (bf16[2,256,256]{2,1,0:T(8,128)(2,1)S(1)}, bf16[2,256,256]{2,1,0:T(8,128)(2,1)S(1)}, u32[]{:S(2)}, u32[]{:S(2)}) collective-permute-start(bf16[2,256,256]{2,1,0:T(8,128)(2,1)S(1)} %bitcast_convert_fusion.refs_0_), channel_id=1, source_target_pairs={{2,0},{3,1},{0,2},{1,3},{6,4},{7,5},{4,6},{5,7},{10,8},{11,9},{8,1... | collective-permute-start | bytes 786440 | tf_op jit(solution)/shard_map/ppermute | solution.py:223
  4.8 9.9 %collective-permute-start.2 = (bf16[2,256,256]{2,1,0:T(8,128)(2,1)S(1)}, bf16[2,256,256]{2,1,0:T(8,128)(2,1)S(1)}, u32[]{:S(2)}, u32[]{:S(2)}) collective-permute-start(bf16[2,256,256]{2,1,0:T(8,128)(2,1)S(1)} %bitcast_convert_fusion.refs_0_), channel_id=1, source_target_pairs={{24,0},{16,8},{8,16},{0,24},{25,1},{17,9},{9,17},{1,25},{26,2},{18... | collective-permute-start | bytes 786440 | tf_op jit(solution)/shard_map/ppermute | solution.py:214
  5.0 13.1 %collective-permute-start.1 = (bf16[2,256,256]{2,1,0:T(8,128)(2,1)S(1)}, bf16[2,256,256]{2,1,0:T(8,128)(2,1)S(1)}, u32[]{:S(2)}, u32[]{:S(2)}) collective-permute-start(bf16[2,256,256]{2,1,0:T(8,128)(2,1)S(1)} %bitcast_convert_fusion.refs_0_), channel_id=1, source_target_pairs={{16,0},{24,8},{0,16},{8,24},{17,1},{25,9},{1,17},{9,25},{18,2},{26... | collective-permute-start | bytes 786440 | tf_op jit(solution)/shard_map/ppermute | solution.py:214
  6.2 11.8 %collective-permute-start = (bf16[2,256,256]{2,1,0:T(8,128)(2,1)S(1)}, bf16[2,256,256]{2,1,0:T(8,128)(2,1)S(1)}, u32[]{:S(2)}, u32[]{:S(2)}) collective-permute-start(bf16[2,256,256]{2,1,0:T(8,128)(2,1)S(1)} %bitcast_convert_fusion.refs_0_), channel_id=1, source_target_pairs={{8,0},{0,8},{24,16},{16,24},{9,1},{1,9},{25,17},{17,25},{10,2},{2,... | collective-permute-start | bytes 786440 | tf_op jit(solution)/shard_map/ppermute | solution.py:214
  18.8 22.9 %copy-start.2 = (f32[2,1,256,256]{3,2,1,0:T(8,128)S(1)}, f32[2,1,256,256]{3,2,1,0:T(8,128)}, u32[]{:S(2)}) copy-start(f32[2,1,256,256]{3,2,1,0:T(8,128)} %param.8) | copy-start | bytes 1572868
  18.8 8.3 %collective-permute-start.12 = (bf16[2,256,256]{2,1,0:T(8,128)(2,1)S(1)}, bf16[2,256,256]{2,1,0:T(8,128)(2,1)S(1)}, u32[]{:S(2)}, u32[]{:S(2)}) collective-permute-start(bf16[2,256,256]{2,1,0:T(8,128)(2,1)S(1)} %get-tuple-element.19.refs_2_.refs_0_), channel_id=1, source_target_pairs={{8,0},{0,8},{24,16},{16,24},{9,1},{1,9},{25,17},{17,25},{10,2},{2,... | collective-permute-start | bytes 786440 | tf_op jit(solution)/shard_map/ppermute | solution.py:214
  20.6 8.3 %collective-permute-start.10 = (bf16[2,256,256]{2,1,0:T(8,128)(2,1)S(1)}, bf16[2,256,256]{2,1,0:T(8,128)(2,1)S(1)}, u32[]{:S(2)}, u32[]{:S(2)}) collective-permute-start(bf16[2,256,256]{2,1,0:T(8,128)(2,1)S(1)} %get-tuple-element.19.refs_2_.refs_0_), channel_id=1, source_target_pairs={{16,0},{24,8},{0,16},{8,24},{17,1},{25,9},{1,17},{9,25},{18,2},{26... | collective-permute-start | bytes 786440 | tf_op jit(solution)/shard_map/ppermute | solution.py:214
  20.8 10.7 %collective-permute-start.9 = (bf16[2,256,256]{2,1,0:T(8,128)(2,1)S(1)}, bf16[2,256,256]{2,1,0:T(8,128)(2,1)S(1)}, u32[]{:S(2)}, u32[]{:S(2)}) collective-permute-start(bf16[2,256,256]{2,1,0:T(8,128)(2,1)S(1)} %shard_map.87.refs_2_), channel_id=1, source_target_pairs={{2,0},{3,1},{0,2},{1,3},{6,4},{7,5},{4,6},{5,7},{10,8},{11,9},{8,1... | collective-permute-start | bytes 786440 | tf_op jit(solution)/shard_map/ppermute | solution.py:223
  21.0 8.0 %collective-permute-start.3 = (bf16[256,256]{1,0:T(8,128)(2,1)S(1)}, bf16[256,256]{1,0:T(8,128)(2,1)S(1)}, u32[]{:S(2)}, u32[]{:S(2)}) collective-permute-start(bf16[256,256]{1,0:T(8,128)(2,1)S(1)} %get-tuple-element.17), channel_id=1, source_target_pairs={{0,0},{1,1},{2,2},{3,3},{4,16},{5,17},{6,18},{7,19},{8,8},{9,9},{1... | collective-permute-start | bytes 393224 | tf_op jit(solution)/shard_map/ppermute | solution.py:231
  23.9 7.5 %collective-permute-start.5 = (bf16[256,256]{1,0:T(8,128)(2,1)S(1)}, bf16[256,256]{1,0:T(8,128)(2,1)S(1)}, u32[]{:S(2)}, u32[]{:S(2)}) collective-permute-start(bf16[256,256]{1,0:T(8,128)(2,1)S(1)} %get-tuple-element.18), channel_id=1, source_target_pairs={{0,0},{1,1},{2,8},{3,9},{4,4},{5,5},{6,12},{7,13},{8,2},{9,3},{10,... | collective-permute-start | bytes 393224 | tf_op jit(solution)/shard_map/ppermute | solution.py:231
  27.1 6.3 %collective-permute-start.13 = (bf16[1,256,256]{2,1,0:T(8,128)(2,1)S(1)}, bf16[1,256,256]{2,1,0:T(8,128)(2,1)S(1)}, u32[]{:S(2)}, u32[]{:S(2)}) collective-permute-start(bf16[1,256,256]{2,1,0:T(8,128)(2,1)S(1)} %slice.17), channel_id=1, source_target_pairs={{16,0},{24,8},{0,16},{8,24},{17,1},{25,9},{1,17},{9,25},{18,2},{26... | collective-permute-start | bytes 393224 | tf_op jit(solution)/shard_map/ppermute | solution.py:214
  28.9 5.4 %collective-permute-start.11 = (bf16[1,256,256]{2,1,0:T(8,128)(2,1)S(1)}, bf16[1,256,256]{2,1,0:T(8,128)(2,1)S(1)}, u32[]{:S(2)}, u32[]{:S(2)}) collective-permute-start(bf16[1,256,256]{2,1,0:T(8,128)(2,1)S(1)} %slice.16), channel_id=1, source_target_pairs={{8,0},{0,8},{24,16},{16,24},{9,1},{1,9},{25,17},{17,25},{10,2},{2,... | collective-permute-start | bytes 393224 | tf_op jit(solution)/shard_map/ppermute | solution.py:214
  34.4 7.3 %collective-permute-start.14 = (bf16[8,256,256]{2,1,0:T(8,128)(2,1)S(1)}, bf16[8,256,256]{2,1,0:T(8,128)(2,1)S(1)}, u32[]{:S(2)}, u32[]{:S(2)}) collective-permute-start(bf16[8,256,256]{2,1,0:T(8,128)(2,1)S(1)} %shard_map.88.own_ref), channel_id=1, source_target_pairs={{1,0},{0,1},{3,2},{2,3},{5,4},{4,5},{7,6},{6,7},{9,8},{8,9},{11,10... | collective-permute-start | bytes 3145736 | tf_op jit(solution)/shard_map/ppermute | solution.py:220
  37.7 7.9 %collective-permute-start.4 = (bf16[256,256]{1,0:T(8,128)(2,1)S(1)}, bf16[256,256]{1,0:T(8,128)(2,1)S(1)}, u32[]{:S(2)}, u32[]{:S(2)}) collective-permute-start(bf16[256,256]{1,0:T(8,128)(2,1)S(1)} %collective-permute-done.3.refs_6_), channel_id=1, source_target_pairs={{0,0},{1,1},{2,8},{3,9},{4,4},{5,5},{6,12},{7,13},{8,2},{9,3},{10,... | collective-permute-start | bytes 393224 | tf_op jit(solution)/shard_map/ppermute | solution.py:231
  39.6 7.0 %collective-permute-start.6 = (bf16[256,256]{1,0:T(8,128)(2,1)S(1)}, bf16[256,256]{1,0:T(8,128)(2,1)S(1)}, u32[]{:S(2)}, u32[]{:S(2)}) collective-permute-start(bf16[256,256]{1,0:T(8,128)(2,1)S(1)} %collective-permute-done.5.refs_7_), channel_id=1, source_target_pairs={{0,1},{1,0},{2,3},{3,2},{4,17},{5,16},{6,19},{7,18},{8,9},{9,8},{1... | collective-permute-start | bytes 393224 | tf_op jit(solution)/shard_map/ppermute | solution.py:231
  46.8 8.9 %collective-permute-start.17 = (bf16[2,256,256]{2,1,0:T(8,128)(2,1)S(1)}, bf16[2,256,256]{2,1,0:T(8,128)(2,1)S(1)}, u32[]{:S(2)}, u32[]{:S(2)}) collective-permute-start(bf16[2,256,256]{2,1,0:T(8,128)(2,1)S(1)} %get-tuple-element.22.refs_0_), channel_id=1, source_target_pairs={{24,0},{16,8},{8,16},{0,24},{25,1},{17,9},{9,17},{1,25},{26,2},{18... | collective-permute-start | bytes 786440 | tf_op jit(solution)/shard_map/ppermute | solution.py:214
  46.9 13.5 %collective-permute-start.16 = (bf16[2,256,256]{2,1,0:T(8,128)(2,1)S(1)}, bf16[2,256,256]{2,1,0:T(8,128)(2,1)S(1)}, u32[]{:S(2)}, u32[]{:S(2)}) collective-permute-start(bf16[2,256,256]{2,1,0:T(8,128)(2,1)S(1)} %get-tuple-element.22.refs_0_), channel_id=1, source_target_pairs={{16,0},{24,8},{0,16},{8,24},{17,1},{25,9},{1,17},{9,25},{18,2},{26... | collective-permute-start | bytes 786440 | tf_op jit(solution)/shard_map/ppermute | solution.py:214
  48.5 12.7 %collective-permute-start.15 = (bf16[2,256,256]{2,1,0:T(8,128)(2,1)S(1)}, bf16[2,256,256]{2,1,0:T(8,128)(2,1)S(1)}, u32[]{:S(2)}, u32[]{:S(2)}) collective-permute-start(bf16[2,256,256]{2,1,0:T(8,128)(2,1)S(1)} %get-tuple-element.22.refs_0_), channel_id=1, source_target_pairs={{8,0},{0,8},{24,16},{16,24},{9,1},{1,9},{25,17},{17,25},{10,2},{2,... | collective-permute-start | bytes 786440 | tf_op jit(solution)/shard_map/ppermute | solution.py:214
  49.6 13.4 %collective-permute-start.23 = (bf16[2,256,256]{2,1,0:T(8,128)(2,1)S(1)}, bf16[2,256,256]{2,1,0:T(8,128)(2,1)S(1)}, u32[]{:S(2)}, u32[]{:S(2)}) collective-permute-start(bf16[2,256,256]{2,1,0:T(8,128)(2,1)S(1)} %get-tuple-element.22.refs_0_), channel_id=1, source_target_pairs={{4,0},{5,1},{6,2},{7,3},{0,4},{1,5},{2,6},{3,7},{12,8},{13,9},{14,... | collective-permute-start | bytes 786440 | tf_op jit(solution)/shard_map/ppermute | solution.py:223
  51.2 11.8 %collective-permute-start.22 = (bf16[2,256,256]{2,1,0:T(8,128)(2,1)S(1)}, bf16[2,256,256]{2,1,0:T(8,128)(2,1)S(1)}, u32[]{:S(2)}, u32[]{:S(2)}) collective-permute-start(bf16[2,256,256]{2,1,0:T(8,128)(2,1)S(1)} %get-tuple-element.22.refs_0_), channel_id=1, source_target_pairs={{2,0},{3,1},{0,2},{1,3},{6,4},{7,5},{4,6},{5,7},{10,8},{11,9},{8,1... | collective-permute-start | bytes 786440 | tf_op jit(solution)/shard_map/ppermute | solution.py:223
  62.0 9.4 %collective-permute-start.27 = (bf16[2,256,256]{2,1,0:T(8,128)(2,1)S(1)}, bf16[2,256,256]{2,1,0:T(8,128)(2,1)S(1)}, u32[]{:S(2)}, u32[]{:S(2)}) collective-permute-start(bf16[2,256,256]{2,1,0:T(8,128)(2,1)S(1)} %get-tuple-element.25.refs_2_.refs_0_), channel_id=1, source_target_pairs={{8,0},{0,8},{24,16},{16,24},{9,1},{1,9},{25,17},{17,25},{10,2},{2,... | collective-permute-start | bytes 786440 | tf_op jit(solution)/shard_map/ppermute | solution.py:214
  62.8 8.7 %collective-permute-start.25 = (bf16[2,256,256]{2,1,0:T(8,128)(2,1)S(1)}, bf16[2,256,256]{2,1,0:T(8,128)(2,1)S(1)}, u32[]{:S(2)}, u32[]{:S(2)}) collective-permute-start(bf16[2,256,256]{2,1,0:T(8,128)(2,1)S(1)} %get-tuple-element.25.refs_2_.refs_0_), channel_id=1, source_target_pairs={{16,0},{24,8},{0,16},{8,24},{17,1},{25,9},{1,17},{9,25},{18,2},{26... | collective-permute-start | bytes 786440 | tf_op jit(solution)/shard_map/ppermute | solution.py:214
  63.0 11.7 %collective-permute-start.24 = (bf16[2,256,256]{2,1,0:T(8,128)(2,1)S(1)}, bf16[2,256,256]{2,1,0:T(8,128)(2,1)S(1)}, u32[]{:S(2)}, u32[]{:S(2)}) collective-permute-start(bf16[2,256,256]{2,1,0:T(8,128)(2,1)S(1)} %shard_map.92.refs_2_), channel_id=1, source_target_pairs={{2,0},{3,1},{0,2},{1,3},{6,4},{7,5},{4,6},{5,7},{10,8},{11,9},{8,1... | collective-permute-start | bytes 786440 | tf_op jit(solution)/shard_map/ppermute | solution.py:223
  65.1 8.3 %collective-permute-start.18 = (bf16[256,256]{1,0:T(8,128)(2,1)S(1)}, bf16[256,256]{1,0:T(8,128)(2,1)S(1)}, u32[]{:S(2)}, u32[]{:S(2)}) collective-permute-start(bf16[256,256]{1,0:T(8,128)(2,1)S(1)} %get-tuple-element.23), channel_id=1, source_target_pairs={{0,0},{1,1},{2,2},{3,3},{4,16},{5,17},{6,18},{7,19},{8,8},{9,9},{1... | collective-permute-start | bytes 393224 | tf_op jit(solution)/shard_map/ppermute | solution.py:231
  67.7 7.0 %collective-permute-start.20 = (bf16[256,256]{1,0:T(8,128)(2,1)S(1)}, bf16[256,256]{1,0:T(8,128)(2,1)S(1)}, u32[]{:S(2)}, u32[]{:S(2)}) collective-permute-start(bf16[256,256]{1,0:T(8,128)(2,1)S(1)} %get-tuple-element.24), channel_id=1, source_target_pairs={{0,0},{1,1},{2,8},{3,9},{4,4},{5,5},{6,12},{7,13},{8,2},{9,3},{10,... | collective-permute-start | bytes 393224 | tf_op jit(solution)/shard_map/ppermute | solution.py:231
  71.4 4.8 %collective-permute-start.28 = (bf16[1,256,256]{2,1,0:T(8,128)(2,1)S(1)}, bf16[1,256,256]{2,1,0:T(8,128)(2,1)S(1)}, u32[]{:S(2)}, u32[]{:S(2)}) collective-permute-start(bf16[1,256,256]{2,1,0:T(8,128)(2,1)S(1)} %slice.19), channel_id=1, source_target_pairs={{16,0},{24,8},{0,16},{8,24},{17,1},{25,9},{1,17},{9,25},{18,2},{26... | collective-permute-start | bytes 393224 | tf_op jit(solution)/shard_map/ppermute | solution.py:214
  71.5 4.7 %collective-permute-start.26 = (bf16[1,256,256]{2,1,0:T(8,128)(2,1)S(1)}, bf16[1,256,256]{2,1,0:T(8,128)(2,1)S(1)}, u32[]{:S(2)}, u32[]{:S(2)}) collective-permute-start(bf16[1,256,256]{2,1,0:T(8,128)(2,1)S(1)} %slice.18), channel_id=1, source_target_pairs={{8,0},{0,8},{24,16},{16,24},{9,1},{1,9},{25,17},{17,25},{10,2},{2,... | collective-permute-start | bytes 393224 | tf_op jit(solution)/shard_map/ppermute | solution.py:214
  76.3 8.4 %collective-permute-start.29 = (bf16[8,256,256]{2,1,0:T(8,128)(2,1)S(1)}, bf16[8,256,256]{2,1,0:T(8,128)(2,1)S(1)}, u32[]{:S(2)}, u32[]{:S(2)}) collective-permute-start(bf16[8,256,256]{2,1,0:T(8,128)(2,1)S(1)} %shard_map.93.own_ref), channel_id=1, source_target_pairs={{1,0},{0,1},{3,2},{2,3},{5,4},{4,5},{7,6},{6,7},{9,8},{8,9},{11,10... | collective-permute-start | bytes 3145736 | tf_op jit(solution)/shard_map/ppermute | solution.py:220
  79.4 7.9 %collective-permute-start.19 = (bf16[256,256]{1,0:T(8,128)(2,1)S(1)}, bf16[256,256]{1,0:T(8,128)(2,1)S(1)}, u32[]{:S(2)}, u32[]{:S(2)}) collective-permute-start(bf16[256,256]{1,0:T(8,128)(2,1)S(1)} %collective-permute-done.18.refs_6_), channel_id=1, source_target_pairs={{0,0},{1,1},{2,8},{3,9},{4,4},{5,5},{6,12},{7,13},{8,2},{9,3},{10,... | collective-permute-start | bytes 393224 | tf_op jit(solution)/shard_map/ppermute | solution.py:231
  83.2 7.3 %collective-permute-start.21 = (bf16[256,256]{1,0:T(8,128)(2,1)S(1)}, bf16[256,256]{1,0:T(8,128)(2,1)S(1)}, u32[]{:S(2)}, u32[]{:S(2)}) collective-permute-start(bf16[256,256]{1,0:T(8,128)(2,1)S(1)} %collective-permute-done.20.refs_7_), channel_id=1, source_target_pairs={{0,1},{1,0},{2,3},{3,2},{4,17},{5,16},{6,19},{7,18},{8,9},{9,8},{1... | collective-permute-start | bytes 393224 | tf_op jit(solution)/shard_map/ppermute | solution.py:231
  (3 other events, 2.9 us)

commit v5 on v4

--- a/solution.py
+++ b/solution.py
@@ -270,11 +270,11 @@
             c_pieces += [piece, *far[-2:]]
         same, other = crossing(same, high_parts), crossing(other, last_bits)
         for step in range(2, halves, 2):
-            column[step] = tied(column[step], column[1], coupled)
+            column[step] = tied(column[step], column[1], same, other)
             column[step + 1] = from_chip(column[step], 1)
         column = [column[step] for step in range(halves)]
+        same, other = crossing(same, last_bits), crossing(other, high_parts, 1)
         own = whole_column(column, [*far, same, other])
-        same, other = crossing(same, last_bits), crossing(other, high_parts, 1)
         part = first_update(rows, meta, own, swapped(own), c_pieces, state, coulomb_own, inverse)
         state, *halves_out = second_update(same, other, part, inverse, sweep_index < ITERS - 1)
         half = halves_out[0] if halves_out else None

time: 92.6 us -> 95.8 us (1.035)
  waiting for transfers between devices: 32.5 us -> 43.7 us
  starting transfers between devices: 44.8 us -> 37.6 us
    ppermute x8, waiting for transfers between devices: 13.7 us -> 25 us  [crossing(): return lax.ppermute(x, ('row', 'col'), pairs)]
    ppermute x2, starting transfers between devices: 6.42 us -> 1.16 us  [swapped(): return lax.ppermute(x, 'col', [(c ^ 1, c) for c in range(cols)])]
    ppermute x2, waiting for transfers between devices: 0.01 us -> 4.57 us  [swapped(): return lax.ppermute(x, 'col', [(c ^ 1, c) for c in range(cols)])]
    ppermute x14, waiting for transfers between devices: 18.6 us -> 14.1 us  [from_row(): return lax.ppermute(x, 'row', [(r ^ step, r) for r in range(rows)])]
    ppermute x8, starting transfers between devices: 21.5 us -> 25.1 us  [crossing(): return lax.ppermute(x, ('row', 'col'), pairs)]
    ppermute x14, starting transfers between devices: 9.31 us -> 6.44 us  [from_row(): return lax.ppermute(x, 'row', [(r ^ step, r) for r in range(rows)])]
    ppermute x6, starting transfers between devices: 7.58 us -> 4.93 us  [from_chip(): return lax.ppermute(x, 'col', [(c ^ 2 * step, c) for c in range(cols)])]
  transfers between devices with their start and end apart: 30 -> 30, of which waited for: 16 -> 14; matrix products, arithmetic and copies ran while one was open for 4% -> 4% of each run, Pallas kernels for 6% -> 3%
where the time goes in v5:
time: 95.8 us; the launch traced here: 95.4 us
  waiting for transfers between devices  43.7 us (46%)
  starting transfers between devices  37.6 us (39%)
  Pallas kernels  6.4 us (7%)
  local copies, waits for them, and re-layouts  4.64 us (5%)
  other arithmetic  2.77 us (3%)
    ppermute x8, starting transfers between devices, crossing(): return lax.ppermute(x, ('row', 'col'), pairs)  25.1 us
    ppermute x8, waiting for transfers between devices, crossing(): return lax.ppermute(x, ('row', 'col'), pairs)  25 us
    ppermute x14, waiting for transfers between devices, from_row(): return lax.ppermute(x, 'row', [(r ^ step, r) for r in range(rows)])  14.1 us
    ppermute x14, starting transfers between devices, from_row(): return lax.ppermute(x, 'row', [(r ^ step, r) for r in range(rows)])  6.44 us
    pallas_call x9, Pallas kernels, call(): pl.pallas_call(body, out_shape=out_shape, in_specs=in_specs, out_specs=VM...  6.4 us
    ppermute x6, starting transfers between devices, from_chip(): return lax.ppermute(x, 'col', [(c ^ 2 * step, c) for c in range(cols)])  4.93 us
    ppermute x2, waiting for transfers between devices, swapped(): return lax.ppermute(x, 'col', [(c ^ 1, c) for c in range(cols)])  4.57 us
    unnamed x10, local copies, waits for them, and re-layouts  2.93 us
  transfers between devices with their start and end apart: 30, of which 14 were waited for; matrix products, arithmetic and copies ran while one was open for 4% of the time, Pallas kernels for 3%

profile of v5, /device:TPU:7, one launch (start us, length us, event | category | flops | bytes accessed | tf_op | source)
XLA Modules:
  0.0 95.4 jit_solution(12916328855188934449)
XLA Ops:
  0.0 1.1 %bitcast_convert_fusion.refs_0_ = bf16[2,256,256]{2,1,0:T(8,128)(2,1)S(1)} fusion(f32[2,1,256,256]{3,2,1,0:T(8,128)} %param.8), kind=kLoop, calls=%fused_computation.12 | loop fusion | flops 131072 | bytes 786432 | tf_op jit(solution)/shard_map/convert_element_type | solution.py:240
  1.1 2.4 %collective-permute-start.8 = (bf16[2,256,256]{2,1,0:T(8,128)(2,1)S(1)}, bf16[2,256,256]{2,1,0:T(8,128)(2,1)S(1)}, u32[]{:S(2)}, u32[]{:S(2)}) collective-permute-start(bf16[2,256,256]{2,1,0:T(8,128)(2,1)S(1)} %bitcast_convert_fusion.refs_0_), channel_id=1, source_target_pairs={{4,0},{5,1},{6,2},{7,3},{0,4},{1,5},{2,6},{3,7},{12,8},{13,9},{14,... | collective-permute-start | bytes 786440 | tf_op jit(solution)/shard_map/ppermute | solution.py:223
  3.5 1.3 %collective-permute-start.7 = (bf16[2,256,256]{2,1,0:T(8,128)(2,1)S(1)}, bf16[2,256,256]{2,1,0:T(8,128)(2,1)S(1)}, u32[]{:S(2)}, u32[]{:S(2)}) collective-permute-start(bf16[2,256,256]{2,1,0:T(8,128)(2,1)S(1)} %bitcast_convert_fusion.refs_0_), channel_id=1, source_target_pairs={{2,0},{3,1},{0,2},{1,3},{6,4},{7,5},{4,6},{5,7},{10,8},{11,9},{8,1... | collective-permute-start | bytes 786440 | tf_op jit(solution)/shard_map/ppermute | solution.py:223
  5.0 1.2 %collective-permute-start.1 = (bf16[2,256,256]{2,1,0:T(8,128)(2,1)S(1)}, bf16[2,256,256]{2,1,0:T(8,128)(2,1)S(1)}, u32[]{:S(2)}, u32[]{:S(2)}) collective-permute-start(bf16[2,256,256]{2,1,0:T(8,128)(2,1)S(1)} %bitcast_convert_fusion.refs_0_), channel_id=1, source_target_pairs={{16,0},{24,8},{0,16},{8,24},{17,1},{25,9},{1,17},{9,25},{18,2},{26... | collective-permute-start | bytes 786440 | tf_op jit(solution)/shard_map/ppermute | solution.py:214
  6.2 1.2 %collective-permute-start = (bf16[2,256,256]{2,1,0:T(8,128)(2,1)S(1)}, bf16[2,256,256]{2,1,0:T(8,128)(2,1)S(1)}, u32[]{:S(2)}, u32[]{:S(2)}) collective-permute-start(bf16[2,256,256]{2,1,0:T(8,128)(2,1)S(1)} %bitcast_convert_fusion.refs_0_), channel_id=1, source_target_pairs={{8,0},{0,8},{24,16},{16,24},{9,1},{1,9},{25,17},{17,25},{10,2},{2,... | collective-permute-start | bytes 786440 | tf_op jit(solution)/shard_map/ppermute | solution.py:214
  10.8 1.6 %copy-done.1 = bf16[2,8,256,256]{3,2,1,0:T(8,128)(2,1)S(1)} copy-done((bf16[2,8,256,256]{3,2,1,0:T(8,128)(2,1)S(1)}, bf16[2,8,256,256]{3,2,1,0:T(8,128)(2,1)}, u32[]{:S(2)}) %copy-start.1) | copy-done | bytes 2097176
  13.7 0.9 shard_map.85
  14.7 3.3 %collective-permute-done.1.refs_2_ = bf16[2,256,256]{2,1,0:T(8,128)(2,1)S(1)} collective-permute-done((bf16[2,256,256]{2,1,0:T(8,128)(2,1)S(1)}, bf16[2,256,256]{2,1,0:T(8,128)(2,1)S(1)}, u32[]{:S(2)}, u32[]{:S(2)}) %collective-permute-start.1) | collective-permute-done | bytes 262176 | tf_op jit(solution)/shard_map/ppermute | solution.py:214
  18.8 3.4 %collective-permute-start.3 = (bf16[256,256]{1,0:T(8,128)(2,1)S(1)}, bf16[256,256]{1,0:T(8,128)(2,1)S(1)}, u32[]{:S(2)}, u32[]{:S(2)}) collective-permute-start(bf16[256,256]{1,0:T(8,128)(2,1)S(1)} %get-tuple-element.17), channel_id=1, source_target_pairs={{0,0},{1,1},{2,2},{3,3},{4,16},{5,17},{6,18},{7,19},{8,8},{9,9},{1... | collective-permute-start | bytes 393224 | tf_op jit(solution)/shard_map/ppermute | solution.py:231
  22.5 3.1 %collective-permute-start.5 = (bf16[256,256]{1,0:T(8,128)(2,1)S(1)}, bf16[256,256]{1,0:T(8,128)(2,1)S(1)}, u32[]{:S(2)}, u32[]{:S(2)}) collective-permute-start(bf16[256,256]{1,0:T(8,128)(2,1)S(1)} %get-tuple-element.18), channel_id=1, source_target_pairs={{0,0},{1,1},{2,8},{3,9},{4,4},{5,5},{6,12},{7,13},{8,2},{9,3},{10,... | collective-permute-start | bytes 393224 | tf_op jit(solution)/shard_map/ppermute | solution.py:231
  25.7 4.6 %collective-permute-done.3.refs_2_ = bf16[256,256]{1,0:T(8,128)(2,1)S(1)} collective-permute-done((bf16[256,256]{1,0:T(8,128)(2,1)S(1)}, bf16[256,256]{1,0:T(8,128)(2,1)S(1)}, u32[]{:S(2)}, u32[]{:S(2)}) %collective-permute-start.3) | collective-permute-done | bytes 131104 | tf_op jit(solution)/shard_map/ppermute | solution.py:231
  30.4 5.1 %collective-permute-start.4 = (bf16[256,256]{1,0:T(8,128)(2,1)S(1)}, bf16[256,256]{1,0:T(8,128)(2,1)S(1)}, u32[]{:S(2)}, u32[]{:S(2)}) collective-permute-start(bf16[256,256]{1,0:T(8,128)(2,1)S(1)} %collective-permute-done.3.refs_2_), channel_id=1, source_target_pairs={{0,0},{1,1},{2,8},{3,9},{4,4},{5,5},{6,12},{7,13},{8,2},{9,3},{10,... | collective-permute-start | bytes 393224 | tf_op jit(solution)/shard_map/ppermute | solution.py:231
  35.4 1.8 %collective-permute-start.6 = (bf16[256,256]{1,0:T(8,128)(2,1)S(1)}, bf16[256,256]{1,0:T(8,128)(2,1)S(1)}, u32[]{:S(2)}, u32[]{:S(2)}) collective-permute-start(bf16[256,256]{1,0:T(8,128)(2,1)S(1)} %collective-permute-done.5.refs_3_), channel_id=1, source_target_pairs={{0,1},{1,0},{2,3},{3,2},{4,17},{5,16},{6,19},{7,18},{8,9},{9,8},{1... | collective-permute-start | bytes 393224 | tf_op jit(solution)/shard_map/ppermute | solution.py:231
  37.5 4.7 %collective-permute-done.4.refs_6_.same_ref = bf16[256,256]{1,0:T(8,128)(2,1)S(1)} collective-permute-done((bf16[256,256]{1,0:T(8,128)(2,1)S(1)}, bf16[256,256]{1,0:T(8,128)(2,1)S(1)}, u32[]{:S(2)}, u32[]{:S(2)}) %collective-permute-start.4) | collective-permute-done | bytes 131104 | tf_op jit(solution)/shard_map/ppermute | solution.py:231
  42.1 2.5 %collective-permute-done.6.refs_7_.other_ref = bf16[256,256]{1,0:T(8,128)(2,1)S(1)} collective-permute-done((bf16[256,256]{1,0:T(8,128)(2,1)S(1)}, bf16[256,256]{1,0:T(8,128)(2,1)S(1)}, u32[]{:S(2)}, u32[]{:S(2)}) %collective-permute-start.6) | collective-permute-done | bytes 131104 | tf_op jit(solution)/shard_map/ppermute | solution.py:231
  46.0 2.3 %collective-permute-done.14.other_ref = bf16[8,256,256]{2,1,0:T(8,128)(2,1)S(1)} collective-permute-done((bf16[8,256,256]{2,1,0:T(8,128)(2,1)S(1)}, bf16[8,256,256]{2,1,0:T(8,128)(2,1)S(1)}, u32[]{:S(2)}, u32[]{:S(2)}) %collective-permute-start.14) | collective-permute-done | bytes 1048608 | tf_op jit(solution)/shard_map/ppermute | solution.py:220
  48.3 1.4 %shard_map.89.part_ref = f32[2,256,256]{2,1,0:T(8,128)S(1)} custom-call(s32[5,8]{1,0:T(8,128)S(1)} %pad_add_fusion.meta, bf16[8,256,256]{2,1,0:T(8,128)(2,1)S(1)} %shard_map.88.own_ref, bf16[8,256,256]{2,1,0:T(8,128)(2,1)S(1)} %collective-permute-done.14.other_ref, bf16[2,256,256]{2,1,0:T(8,128)(2,1)S(1)} %get-tuple-element.19.refs_0_, ...), custom_call_target="tpu_custom_call" | custom-call | flops 536870912 | bytes 6291456 | tf_op jit(solution)/shard_map/pallas_call | solution.py:23
  49.9 1.0 %collective-permute-start.16 = (bf16[2,256,256]{2,1,0:T(8,128)(2,1)S(1)}, bf16[2,256,256]{2,1,0:T(8,128)(2,1)S(1)}, u32[]{:S(2)}, u32[]{:S(2)}) collective-permute-start(bf16[2,256,256]{2,1,0:T(8,128)(2,1)S(1)} %get-tuple-element.22.refs_0_), channel_id=1, source_target_pairs={{16,0},{24,8},{0,16},{8,24},{17,1},{25,9},{1,17},{9,25},{18,2},{26... | collective-permute-start | bytes 786440 | tf_op jit(solution)/shard_map/ppermute | solution.py:214
  50.9 1.7 %collective-permute-start.15 = (bf16[2,256,256]{2,1,0:T(8,128)(2,1)S(1)}, bf16[2,256,256]{2,1,0:T(8,128)(2,1)S(1)}, u32[]{:S(2)}, u32[]{:S(2)}) collective-permute-start(bf16[2,256,256]{2,1,0:T(8,128)(2,1)S(1)} %get-tuple-element.22.refs_0_), channel_id=1, source_target_pairs={{8,0},{0,8},{24,16},{16,24},{9,1},{1,9},{25,17},{17,25},{10,2},{2,... | collective-permute-start | bytes 786440 | tf_op jit(solution)/shard_map/ppermute | solution.py:214
  52.6 1.3 %collective-permute-start.23 = (bf16[2,256,256]{2,1,0:T(8,128)(2,1)S(1)}, bf16[2,256,256]{2,1,0:T(8,128)(2,1)S(1)}, u32[]{:S(2)}, u32[]{:S(2)}) collective-permute-start(bf16[2,256,256]{2,1,0:T(8,128)(2,1)S(1)} %get-tuple-element.22.refs_0_), channel_id=1, source_target_pairs={{4,0},{5,1},{6,2},{7,3},{0,4},{1,5},{2,6},{3,7},{12,8},{13,9},{14,... | collective-permute-start | bytes 786440 | tf_op jit(solution)/shard_map/ppermute | solution.py:223
  53.8 4.6 %collective-permute-done.17.refs_3_ = bf16[2,256,256]{2,1,0:T(8,128)(2,1)S(1)} collective-permute-done((bf16[2,256,256]{2,1,0:T(8,128)(2,1)S(1)}, bf16[2,256,256]{2,1,0:T(8,128)(2,1)S(1)}, u32[]{:S(2)}, u32[]{:S(2)}) %collective-permute-start.17) | collective-permute-done | bytes 262176 | tf_op jit(solution)/shard_map/ppermute | solution.py:214
  58.4 4.7 %collective-permute-done.16.refs_2_ = bf16[2,256,256]{2,1,0:T(8,128)(2,1)S(1)} collective-permute-done((bf16[2,256,256]{2,1,0:T(8,128)(2,1)S(1)}, bf16[2,256,256]{2,1,0:T(8,128)(2,1)S(1)}, u32[]{:S(2)}, u32[]{:S(2)}) %collective-permute-start.16) | collective-permute-done | bytes 262176 | tf_op jit(solution)/shard_map/ppermute | solution.py:214
  64.5 3.7 %collective-permute-start.18 = (bf16[256,256]{1,0:T(8,128)(2,1)S(1)}, bf16[256,256]{1,0:T(8,128)(2,1)S(1)}, u32[]{:S(2)}, u32[]{:S(2)}) collective-permute-start(bf16[256,256]{1,0:T(8,128)(2,1)S(1)} %get-tuple-element.23), channel_id=1, source_target_pairs={{0,0},{1,1},{2,2},{3,3},{4,16},{5,17},{6,18},{7,19},{8,8},{9,9},{1... | collective-permute-start | bytes 393224 | tf_op jit(solution)/shard_map/ppermute | solution.py:231
  68.6 2.0 %collective-permute-start.20 = (bf16[256,256]{1,0:T(8,128)(2,1)S(1)}, bf16[256,256]{1,0:T(8,128)(2,1)S(1)}, u32[]{:S(2)}, u32[]{:S(2)}) collective-permute-start(bf16[256,256]{1,0:T(8,128)(2,1)S(1)} %get-tuple-element.24), channel_id=1, source_target_pairs={{0,0},{1,1},{2,8},{3,9},{4,4},{5,5},{6,12},{7,13},{8,2},{9,3},{10,... | collective-permute-start | bytes 393224 | tf_op jit(solution)/shard_map/ppermute | solution.py:231
  70.7 4.6 %collective-permute-done.18.refs_2_ = bf16[256,256]{1,0:T(8,128)(2,1)S(1)} collective-permute-done((bf16[256,256]{1,0:T(8,128)(2,1)S(1)}, bf16[256,256]{1,0:T(8,128)(2,1)S(1)}, u32[]{:S(2)}, u32[]{:S(2)}) %collective-permute-start.18) | collective-permute-done | bytes 131104 | tf_op jit(solution)/shard_map/ppermute | solution.py:231
  75.4 4.1 %collective-permute-start.19 = (bf16[256,256]{1,0:T(8,128)(2,1)S(1)}, bf16[256,256]{1,0:T(8,128)(2,1)S(1)}, u32[]{:S(2)}, u32[]{:S(2)}) collective-permute-start(bf16[256,256]{1,0:T(8,128)(2,1)S(1)} %collective-permute-done.18.refs_2_), channel_id=1, source_target_pairs={{0,0},{1,1},{2,8},{3,9},{4,4},{5,5},{6,12},{7,13},{8,2},{9,3},{10,... | collective-permute-start | bytes 393224 | tf_op jit(solution)/shard_map/ppermute | solution.py:231
  79.6 1.7 %collective-permute-start.21 = (bf16[256,256]{1,0:T(8,128)(2,1)S(1)}, bf16[256,256]{1,0:T(8,128)(2,1)S(1)}, u32[]{:S(2)}, u32[]{:S(2)}) collective-permute-start(bf16[256,256]{1,0:T(8,128)(2,1)S(1)} %collective-permute-done.20.refs_3_), channel_id=1, source_target_pairs={{0,1},{1,0},{2,3},{3,2},{4,17},{5,16},{6,19},{7,18},{8,9},{9,8},{1... | collective-permute-start | bytes 393224 | tf_op jit(solution)/shard_map/ppermute | solution.py:231
  81.5 4.7 %collective-permute-done.19.refs_6_.same_ref = bf16[256,256]{1,0:T(8,128)(2,1)S(1)} collective-permute-done((bf16[256,256]{1,0:T(8,128)(2,1)S(1)}, bf16[256,256]{1,0:T(8,128)(2,1)S(1)}, u32[]{:S(2)}, u32[]{:S(2)}) %collective-permute-start.19) | collective-permute-done | bytes 131104 | tf_op jit(solution)/shard_map/ppermute | solution.py:231
  86.3 3.7 %collective-permute-done.21.refs_7_.other_ref = bf16[256,256]{1,0:T(8,128)(2,1)S(1)} collective-permute-done((bf16[256,256]{1,0:T(8,128)(2,1)S(1)}, bf16[256,256]{1,0:T(8,128)(2,1)S(1)}, u32[]{:S(2)}, u32[]{:S(2)}) %collective-permute-start.21) | collective-permute-done | bytes 131104 | tf_op jit(solution)/shard_map/ppermute | solution.py:231
  90.8 2.3 %collective-permute-done.29.other_ref = bf16[8,256,256]{2,1,0:T(8,128)(2,1)S(1)} collective-permute-done((bf16[8,256,256]{2,1,0:T(8,128)(2,1)S(1)}, bf16[8,256,256]{2,1,0:T(8,128)(2,1)S(1)}, u32[]{:S(2)}, u32[]{:S(2)}) %collective-permute-start.29) | collective-permute-done | bytes 1048608 | tf_op jit(solution)/shard_map/ppermute | solution.py:220
  93.1 1.4 %shard_map.94.part_ref = f32[2,256,256]{2,1,0:T(8,128)S(1)} custom-call(s32[5,8]{1,0:T(8,128)S(1)} %pad_add_fusion.meta, bf16[8,256,256]{2,1,0:T(8,128)(2,1)S(1)} %shard_map.93.own_ref, bf16[8,256,256]{2,1,0:T(8,128)(2,1)S(1)} %collective-permute-done.29.other_ref, bf16[2,256,256]{2,1,0:T(8,128)(2,1)S(1)} %get-tuple-element.25.refs_0_, ...), custom_call_target="tpu_custom_call" | custom-call | flops 536870912 | bytes 6291456 | tf_op jit(solution)/shard_map/pallas_call | solution.py:23
  94.4 0.9 shard_map.95
  (65 shorter events, 10.7 us)
Async XLA Ops:
  0.0 9.1 %copy-start = (s32[2,8,8]{2,1,0:T(8,128)S(1)}, s32[2,8,8]{2,1,0:T(8,128)}, u32[]{:S(2)}) copy-start(s32[2,8,8]{2,1,0:T(8,128)} %param.12) | copy-start | bytes 1540
  1.1 24.5 %collective-permute-start.8 = (bf16[2,256,256]{2,1,0:T(8,128)(2,1)S(1)}, bf16[2,256,256]{2,1,0:T(8,128)(2,1)S(1)}, u32[]{:S(2)}, u32[]{:S(2)}) collective-permute-start(bf16[2,256,256]{2,1,0:T(8,128)(2,1)S(1)} %bitcast_convert_fusion.refs_0_), channel_id=1, source_target_pairs={{4,0},{5,1},{6,2},{7,3},{0,4},{1,5},{2,6},{3,7},{12,8},{13,9},{14,... | collective-permute-start | bytes 786440 | tf_op jit(solution)/shard_map/ppermute | solution.py:223
  3.5 22.3 %collective-permute-start.7 = (bf16[2,256,256]{2,1,0:T(8,128)(2,1)S(1)}, bf16[2,256,256]{2,1,0:T(8,128)(2,1)S(1)}, u32[]{:S(2)}, u32[]{:S(2)}) collective-permute-start(bf16[2,256,256]{2,1,0:T(8,128)(2,1)S(1)} %bitcast_convert_fusion.refs_0_), channel_id=1, source_target_pairs={{2,0},{3,1},{0,2},{1,3},{6,4},{7,5},{4,6},{5,7},{10,8},{11,9},{8,1... | collective-permute-start | bytes 786440 | tf_op jit(solution)/shard_map/ppermute | solution.py:223
  4.8 9.9 %collective-permute-start.2 = (bf16[2,256,256]{2,1,0:T(8,128)(2,1)S(1)}, bf16[2,256,256]{2,1,0:T(8,128)(2,1)S(1)}, u32[]{:S(2)}, u32[]{:S(2)}) collective-permute-start(bf16[2,256,256]{2,1,0:T(8,128)(2,1)S(1)} %bitcast_convert_fusion.refs_0_), channel_id=1, source_target_pairs={{24,0},{16,8},{8,16},{0,24},{25,1},{17,9},{9,17},{1,25},{26,2},{18... | collective-permute-start | bytes 786440 | tf_op jit(solution)/shard_map/ppermute | solution.py:214
  5.0 13.1 %collective-permute-start.1 = (bf16[2,256,256]{2,1,0:T(8,128)(2,1)S(1)}, bf16[2,256,256]{2,1,0:T(8,128)(2,1)S(1)}, u32[]{:S(2)}, u32[]{:S(2)}) collective-permute-start(bf16[2,256,256]{2,1,0:T(8,128)(2,1)S(1)} %bitcast_convert_fusion.refs_0_), channel_id=1, source_target_pairs={{16,0},{24,8},{0,16},{8,24},{17,1},{25,9},{1,17},{9,25},{18,2},{26... | collective-permute-start | bytes 786440 | tf_op jit(solution)/shard_map/ppermute | solution.py:214
  6.2 11.8 %collective-permute-start = (bf16[2,256,256]{2,1,0:T(8,128)(2,1)S(1)}, bf16[2,256,256]{2,1,0:T(8,128)(2,1)S(1)}, u32[]{:S(2)}, u32[]{:S(2)}) collective-permute-start(bf16[2,256,256]{2,1,0:T(8,128)(2,1)S(1)} %bitcast_convert_fusion.refs_0_), channel_id=1, source_target_pairs={{8,0},{0,8},{24,16},{16,24},{9,1},{1,9},{25,17},{17,25},{10,2},{2,... | collective-permute-start | bytes 786440 | tf_op jit(solution)/shard_map/ppermute | solution.py:214
  18.8 11.6 %collective-permute-start.3 = (bf16[256,256]{1,0:T(8,128)(2,1)S(1)}, bf16[256,256]{1,0:T(8,128)(2,1)S(1)}, u32[]{:S(2)}, u32[]{:S(2)}) collective-permute-start(bf16[256,256]{1,0:T(8,128)(2,1)S(1)} %get-tuple-element.17), channel_id=1, source_target_pairs={{0,0},{1,1},{2,2},{3,3},{4,16},{5,17},{6,18},{7,19},{8,8},{9,9},{1... | collective-permute-start | bytes 393224 | tf_op jit(solution)/shard_map/ppermute | solution.py:231
  22.2 15.1 %collective-permute-start.12 = (bf16[2,256,256]{2,1,0:T(8,128)(2,1)S(1)}, bf16[2,256,256]{2,1,0:T(8,128)(2,1)S(1)}, u32[]{:S(2)}, u32[]{:S(2)}) collective-permute-start(bf16[2,256,256]{2,1,0:T(8,128)(2,1)S(1)} %get-tuple-element.19.refs_0_), channel_id=1, source_target_pairs={{8,0},{0,8},{24,16},{16,24},{9,1},{1,9},{25,17},{17,25},{10,2},{2,... | collective-permute-start | bytes 786440 | tf_op jit(solution)/shard_map/ppermute | solution.py:214
  22.5 25.8 %copy-start.2 = (f32[2,1,256,256]{3,2,1,0:T(8,128)S(1)}, f32[2,1,256,256]{3,2,1,0:T(8,128)}, u32[]{:S(2)}) copy-start(f32[2,1,256,256]{3,2,1,0:T(8,128)} %param.8) | copy-start | bytes 1572868
  22.5 7.9 %collective-permute-start.5 = (bf16[256,256]{1,0:T(8,128)(2,1)S(1)}, bf16[256,256]{1,0:T(8,128)(2,1)S(1)}, u32[]{:S(2)}, u32[]{:S(2)}) collective-permute-start(bf16[256,256]{1,0:T(8,128)(2,1)S(1)} %get-tuple-element.18), channel_id=1, source_target_pairs={{0,0},{1,1},{2,8},{3,9},{4,4},{5,5},{6,12},{7,13},{8,2},{9,3},{10,... | collective-permute-start | bytes 393224 | tf_op jit(solution)/shard_map/ppermute | solution.py:231
  25.6 11.7 %collective-permute-start.10 = (bf16[2,256,256]{2,1,0:T(8,128)(2,1)S(1)}, bf16[2,256,256]{2,1,0:T(8,128)(2,1)S(1)}, u32[]{:S(2)}, u32[]{:S(2)}) collective-permute-start(bf16[2,256,256]{2,1,0:T(8,128)(2,1)S(1)} %get-tuple-element.19.refs_0_), channel_id=1, source_target_pairs={{16,0},{24,8},{0,16},{8,24},{17,1},{25,9},{1,17},{9,25},{18,2},{26... | collective-permute-start | bytes 786440 | tf_op jit(solution)/shard_map/ppermute | solution.py:214
  30.4 14.3 %collective-permute-start.9 = (bf16[2,256,256]{2,1,0:T(8,128)(2,1)S(1)}, bf16[2,256,256]{2,1,0:T(8,128)(2,1)S(1)}, u32[]{:S(2)}, u32[]{:S(2)}) collective-permute-start(bf16[2,256,256]{2,1,0:T(8,128)(2,1)S(1)} %shard_map.87.refs_2_), channel_id=1, source_target_pairs={{2,0},{3,1},{0,2},{1,3},{6,4},{7,5},{4,6},{5,7},{10,8},{11,9},{8,1... | collective-permute-start | bytes 786440 | tf_op jit(solution)/shard_map/ppermute | solution.py:223
  30.4 11.8 %collective-permute-start.4 = (bf16[256,256]{1,0:T(8,128)(2,1)S(1)}, bf16[256,256]{1,0:T(8,128)(2,1)S(1)}, u32[]{:S(2)}, u32[]{:S(2)}) collective-permute-start(bf16[256,256]{1,0:T(8,128)(2,1)S(1)} %collective-permute-done.3.refs_2_), channel_id=1, source_target_pairs={{0,0},{1,1},{2,8},{3,9},{4,4},{5,5},{6,12},{7,13},{8,2},{9,3},{10,... | collective-permute-start | bytes 393224 | tf_op jit(solution)/shard_map/ppermute | solution.py:231
  35.4 9.2 %collective-permute-start.6 = (bf16[256,256]{1,0:T(8,128)(2,1)S(1)}, bf16[256,256]{1,0:T(8,128)(2,1)S(1)}, u32[]{:S(2)}, u32[]{:S(2)}) collective-permute-start(bf16[256,256]{1,0:T(8,128)(2,1)S(1)} %collective-permute-done.5.refs_3_), channel_id=1, source_target_pairs={{0,1},{1,0},{2,3},{3,2},{4,17},{5,16},{6,19},{7,18},{8,9},{9,8},{1... | collective-permute-start | bytes 393224 | tf_op jit(solution)/shard_map/ppermute | solution.py:231
  37.3 8.2 %collective-permute-start.13 = (bf16[1,256,256]{2,1,0:T(8,128)(2,1)S(1)}, bf16[1,256,256]{2,1,0:T(8,128)(2,1)S(1)}, u32[]{:S(2)}, u32[]{:S(2)}) collective-permute-start(bf16[1,256,256]{2,1,0:T(8,128)(2,1)S(1)} %slice.17), channel_id=1, source_target_pairs={{16,0},{24,8},{0,16},{8,24},{17,1},{25,9},{1,17},{9,25},{18,2},{26... | collective-permute-start | bytes 393224 | tf_op jit(solution)/shard_map/ppermute | solution.py:214
  37.4 8.1 %collective-permute-start.11 = (bf16[1,256,256]{2,1,0:T(8,128)(2,1)S(1)}, bf16[1,256,256]{2,1,0:T(8,128)(2,1)S(1)}, u32[]{:S(2)}, u32[]{:S(2)}) collective-permute-start(bf16[1,256,256]{2,1,0:T(8,128)(2,1)S(1)} %slice.16), channel_id=1, source_target_pairs={{8,0},{0,8},{24,16},{16,24},{9,1},{1,9},{25,17},{17,25},{10,2},{2,... | collective-permute-start | bytes 393224 | tf_op jit(solution)/shard_map/ppermute | solution.py:214
  45.6 2.7 %collective-permute-start.14 = (bf16[8,256,256]{2,1,0:T(8,128)(2,1)S(1)}, bf16[8,256,256]{2,1,0:T(8,128)(2,1)S(1)}, u32[]{:S(2)}, u32[]{:S(2)}) collective-permute-start(bf16[8,256,256]{2,1,0:T(8,128)(2,1)S(1)} %shard_map.88.own_ref), channel_id=1, source_target_pairs={{1,0},{0,1},{3,2},{2,3},{5,4},{4,5},{7,6},{6,7},{9,8},{8,9},{11,10... | collective-permute-start | bytes 3145736 | tf_op jit(solution)/shard_map/ppermute | solution.py:220
  49.9 8.5 %collective-permute-start.17 = (bf16[2,256,256]{2,1,0:T(8,128)(2,1)S(1)}, bf16[2,256,256]{2,1,0:T(8,128)(2,1)S(1)}, u32[]{:S(2)}, u32[]{:S(2)}) collective-permute-start(bf16[2,256,256]{2,1,0:T(8,128)(2,1)S(1)} %get-tuple-element.22.refs_0_), channel_id=1, source_target_pairs={{24,0},{16,8},{8,16},{0,24},{25,1},{17,9},{9,17},{1,25},{26,2},{18... | collective-permute-start | bytes 786440 | tf_op jit(solution)/shard_map/ppermute | solution.py:214
  49.9 13.1 %collective-permute-start.16 = (bf16[2,256,256]{2,1,0:T(8,128)(2,1)S(1)}, bf16[2,256,256]{2,1,0:T(8,128)(2,1)S(1)}, u32[]{:S(2)}, u32[]{:S(2)}) collective-permute-start(bf16[2,256,256]{2,1,0:T(8,128)(2,1)S(1)} %get-tuple-element.22.refs_0_), channel_id=1, source_target_pairs={{16,0},{24,8},{0,16},{8,24},{17,1},{25,9},{1,17},{9,25},{18,2},{26... | collective-permute-start | bytes 786440 | tf_op jit(solution)/shard_map/ppermute | solution.py:214
  50.9 12.8 %collective-permute-start.15 = (bf16[2,256,256]{2,1,0:T(8,128)(2,1)S(1)}, bf16[2,256,256]{2,1,0:T(8,128)(2,1)S(1)}, u32[]{:S(2)}, u32[]{:S(2)}) collective-permute-start(bf16[2,256,256]{2,1,0:T(8,128)(2,1)S(1)} %get-tuple-element.22.refs_0_), channel_id=1, source_target_pairs={{8,0},{0,8},{24,16},{16,24},{9,1},{1,9},{25,17},{17,25},{10,2},{2,... | collective-permute-start | bytes 786440 | tf_op jit(solution)/shard_map/ppermute | solution.py:214
  52.6 18.0 %collective-permute-start.23 = (bf16[2,256,256]{2,1,0:T(8,128)(2,1)S(1)}, bf16[2,256,256]{2,1,0:T(8,128)(2,1)S(1)}, u32[]{:S(2)}, u32[]{:S(2)}) collective-permute-start(bf16[2,256,256]{2,1,0:T(8,128)(2,1)S(1)} %get-tuple-element.22.refs_0_), channel_id=1, source_target_pairs={{4,0},{5,1},{6,2},{7,3},{0,4},{1,5},{2,6},{3,7},{12,8},{13,9},{14,... | collective-permute-start | bytes 786440 | tf_op jit(solution)/shard_map/ppermute | solution.py:223
  53.8 16.9 %collective-permute-start.22 = (bf16[2,256,256]{2,1,0:T(8,128)(2,1)S(1)}, bf16[2,256,256]{2,1,0:T(8,128)(2,1)S(1)}, u32[]{:S(2)}, u32[]{:S(2)}) collective-permute-start(bf16[2,256,256]{2,1,0:T(8,128)(2,1)S(1)} %get-tuple-element.22.refs_0_), channel_id=1, source_target_pairs={{2,0},{3,1},{0,2},{1,3},{6,4},{7,5},{4,6},{5,7},{10,8},{11,9},{8,1... | collective-permute-start | bytes 786440 | tf_op jit(solution)/shard_map/ppermute | solution.py:223
  64.5 10.9 %collective-permute-start.18 = (bf16[256,256]{1,0:T(8,128)(2,1)S(1)}, bf16[256,256]{1,0:T(8,128)(2,1)S(1)}, u32[]{:S(2)}, u32[]{:S(2)}) collective-permute-start(bf16[256,256]{1,0:T(8,128)(2,1)S(1)} %get-tuple-element.23), channel_id=1, source_target_pairs={{0,0},{1,1},{2,2},{3,3},{4,16},{5,17},{6,18},{7,19},{8,8},{9,9},{1... | collective-permute-start | bytes 393224 | tf_op jit(solution)/shard_map/ppermute | solution.py:231
  68.2 13.1 %collective-permute-start.27 = (bf16[2,256,256]{2,1,0:T(8,128)(2,1)S(1)}, bf16[2,256,256]{2,1,0:T(8,128)(2,1)S(1)}, u32[]{:S(2)}, u32[]{:S(2)}) collective-permute-start(bf16[2,256,256]{2,1,0:T(8,128)(2,1)S(1)} %get-tuple-element.25.refs_0_), channel_id=1, source_target_pairs={{8,0},{0,8},{24,16},{16,24},{9,1},{1,9},{25,17},{17,25},{10,2},{2,... | collective-permute-start | bytes 786440 | tf_op jit(solution)/shard_map/ppermute | solution.py:214
  68.6 6.9 %collective-permute-start.20 = (bf16[256,256]{1,0:T(8,128)(2,1)S(1)}, bf16[256,256]{1,0:T(8,128)(2,1)S(1)}, u32[]{:S(2)}, u32[]{:S(2)}) collective-permute-start(bf16[256,256]{1,0:T(8,128)(2,1)S(1)} %get-tuple-element.24), channel_id=1, source_target_pairs={{0,0},{1,1},{2,8},{3,9},{4,4},{5,5},{6,12},{7,13},{8,2},{9,3},{10,... | collective-permute-start | bytes 393224 | tf_op jit(solution)/shard_map/ppermute | solution.py:231
  70.6 10.8 %collective-permute-start.25 = (bf16[2,256,256]{2,1,0:T(8,128)(2,1)S(1)}, bf16[2,256,256]{2,1,0:T(8,128)(2,1)S(1)}, u32[]{:S(2)}, u32[]{:S(2)}) collective-permute-start(bf16[2,256,256]{2,1,0:T(8,128)(2,1)S(1)} %get-tuple-element.25.refs_0_), channel_id=1, source_target_pairs={{16,0},{24,8},{0,16},{8,24},{17,1},{25,9},{1,17},{9,25},{18,2},{26... | collective-permute-start | bytes 786440 | tf_op jit(solution)/shard_map/ppermute | solution.py:214
  75.4 14.5 %collective-permute-start.24 = (bf16[2,256,256]{2,1,0:T(8,128)(2,1)S(1)}, bf16[2,256,256]{2,1,0:T(8,128)(2,1)S(1)}, u32[]{:S(2)}, u32[]{:S(2)}) collective-permute-start(bf16[2,256,256]{2,1,0:T(8,128)(2,1)S(1)} %shard_map.92.refs_2_), channel_id=1, source_target_pairs={{2,0},{3,1},{0,2},{1,3},{6,4},{7,5},{4,6},{5,7},{10,8},{11,9},{8,1... | collective-permute-start | bytes 786440 | tf_op jit(solution)/shard_map/ppermute | solution.py:223
  75.4 10.8 %collective-permute-start.19 = (bf16[256,256]{1,0:T(8,128)(2,1)S(1)}, bf16[256,256]{1,0:T(8,128)(2,1)S(1)}, u32[]{:S(2)}, u32[]{:S(2)}) collective-permute-start(bf16[256,256]{1,0:T(8,128)(2,1)S(1)} %collective-permute-done.18.refs_2_), channel_id=1, source_target_pairs={{0,0},{1,1},{2,8},{3,9},{4,4},{5,5},{6,12},{7,13},{8,2},{9,3},{10,... | collective-permute-start | bytes 393224 | tf_op jit(solution)/shard_map/ppermute | solution.py:231
  79.6 10.4 %collective-permute-start.21 = (bf16[256,256]{1,0:T(8,128)(2,1)S(1)}, bf16[256,256]{1,0:T(8,128)(2,1)S(1)}, u32[]{:S(2)}, u32[]{:S(2)}) collective-permute-start(bf16[256,256]{1,0:T(8,128)(2,1)S(1)} %collective-permute-done.20.refs_3_), channel_id=1, source_target_pairs={{0,1},{1,0},{2,3},{3,2},{4,17},{5,16},{6,19},{7,18},{8,9},{9,8},{1... | collective-permute-start | bytes 393224 | tf_op jit(solution)/shard_map/ppermute | solution.py:231
  81.3 8.6 %collective-permute-start.28 = (bf16[1,256,256]{2,1,0:T(8,128)(2,1)S(1)}, bf16[1,256,256]{2,1,0:T(8,128)(2,1)S(1)}, u32[]{:S(2)}, u32[]{:S(2)}) collective-permute-start(bf16[1,256,256]{2,1,0:T(8,128)(2,1)S(1)} %slice.19), channel_id=1, source_target_pairs={{16,0},{24,8},{0,16},{8,24},{17,1},{25,9},{1,17},{9,25},{18,2},{26... | collective-permute-start | bytes 393224 | tf_op jit(solution)/shard_map/ppermute | solution.py:214
  81.5 8.5 %collective-permute-start.26 = (bf16[1,256,256]{2,1,0:T(8,128)(2,1)S(1)}, bf16[1,256,256]{2,1,0:T(8,128)(2,1)S(1)}, u32[]{:S(2)}, u32[]{:S(2)}) collective-permute-start(bf16[1,256,256]{2,1,0:T(8,128)(2,1)S(1)} %slice.18), channel_id=1, source_target_pairs={{8,0},{0,8},{24,16},{16,24},{9,1},{1,9},{25,17},{17,25},{10,2},{2,... | collective-permute-start | bytes 393224 | tf_op jit(solution)/shard_map/ppermute | solution.py:214
  90.1 3.0 %collective-permute-start.29 = (bf16[8,256,256]{2,1,0:T(8,128)(2,1)S(1)}, bf16[8,256,256]{2,1,0:T(8,128)(2,1)S(1)}, u32[]{:S(2)}, u32[]{:S(2)}) collective-permute-start(bf16[8,256,256]{2,1,0:T(8,128)(2,1)S(1)} %shard_map.93.own_ref), channel_id=1, source_target_pairs={{1,0},{0,1},{3,2},{2,3},{5,4},{4,5},{7,6},{6,7},{9,8},{8,9},{11,10... | collective-permute-start | bytes 3145736 | tf_op jit(solution)/shard_map/ppermute | solution.py:220
  (3 other events, 2.9 us)

commit v6 on v4

--- a/solution.py
+++ b/solution.py
@@ -265,9 +265,8 @@
         near = from_row(coupled, 1)
         c_pieces, far = [coupled, near], []
         for step in range(2, rows, 2):
-            piece = from_row(coupled, step)
-            far += [from_row(piece[0:1], 1), from_row(near[1:2], step)]
-            c_pieces += [piece, *far[-2:]]
+            far.append(from_row(near, step))
+            c_pieces += [from_row(coupled, step), far[-1]]
         same, other = crossing(same, high_parts), crossing(other, last_bits)
         for step in range(2, halves, 2):
             column[step] = tied(column[step], column[1], coupled)

time: 92.6 us -> 103 us (1.11)
  waiting for transfers between devices: 32.5 us -> 45 us
  starting transfers between devices: 44.8 us -> 43.1 us
    ppermute x14 -> x12, waiting for transfers between devices: 18.6 us -> 32.9 us  [from_row(): return lax.ppermute(x, 'row', [(r ^ step, r) for r in range(rows)])]
    ppermute x8, waiting for transfers between devices: 13.7 us -> 10.5 us  [crossing(): return lax.ppermute(x, ('row', 'col'), pairs)]
    ppermute x6, starting transfers between devices: 7.58 us -> 5.3 us  [from_chip(): return lax.ppermute(x, 'col', [(c ^ 2 * step, c) for c in range(cols)])]
    ppermute x14 -> x12, starting transfers between devices: 9.31 us -> 11 us  [from_row(): return lax.ppermute(x, 'row', [(r ^ step, r) for r in range(rows)])]
    ppermute x6, waiting for transfers between devices: 0.24 us -> 1.55 us  [from_chip(): return lax.ppermute(x, 'col', [(c ^ 2 * step, c) for c in range(cols)])]
    ppermute x2, starting transfers between devices: 6.42 us -> 5.24 us  [swapped(): return lax.ppermute(x, 'col', [(c ^ 1, c) for c in range(cols)])]
  transfers between devices with their start and end apart: 30 -> 28, of which waited for: 16 -> 11; matrix products, arithmetic and copies ran while one was open for 4% -> 3% of each run, Pallas kernels for 6% -> 5%
where the time goes in v6:
time: 103 us; the launch traced here: 102 us
  waiting for transfers between devices  45 us (44%)
  starting transfers between devices  43.1 us (42%)
  Pallas kernels  6.38 us (6%)
  local copies, waits for them, and re-layouts  4.6 us (4%)
  other arithmetic  2.77 us (3%)
    ppermute x12, waiting for transfers between devices, from_row(): return lax.ppermute(x, 'row', [(r ^ step, r) for r in range(rows)])  32.9 us
    ppermute x8, starting transfers between devices, crossing(): return lax.ppermute(x, ('row', 'col'), pairs)  21.5 us
    ppermute x12, starting transfers between devices, from_row(): return lax.ppermute(x, 'row', [(r ^ step, r) for r in range(rows)])  11 us
    ppermute x8, waiting for transfers between devices, crossing(): return lax.ppermute(x, ('row', 'col'), pairs)  10.5 us
    pallas_call x9, Pallas kernels, call(): pl.pallas_call(body, out_shape=out_shape, in_specs=in_specs, out_specs=VM...  6.38 us
    ppermute x6, starting transfers between devices, from_chip(): return lax.ppermute(x, 'col', [(c ^ 2 * step, c) for c in range(cols)])  5.3 us
    ppermute x2, starting transfers between devices, swapped(): return lax.ppermute(x, 'col', [(c ^ 1, c) for c in range(cols)])  5.24 us
    unnamed x10, local copies, waits for them, and re-layouts  2.93 us
  transfers between devices with their start and end apart: 28, of which 11 were waited for; matrix products, arithmetic and copies ran while one was open for 3% of the time, Pallas kernels for 5%

profile of v6, /device:TPU:7, one launch (start us, length us, event | category | flops | bytes accessed | tf_op | source)
XLA Modules:
  0.0 102.0 jit_solution(15480922384085615099)
XLA Ops:
  1.1 2.4 %collective-permute-start.8 = (bf16[2,256,256]{2,1,0:T(8,128)(2,1)S(1)}, bf16[2,256,256]{2,1,0:T(8,128)(2,1)S(1)}, u32[]{:S(2)}, u32[]{:S(2)}) collective-permute-start(bf16[2,256,256]{2,1,0:T(8,128)(2,1)S(1)} %bitcast_convert_fusion.refs_0_), channel_id=1, source_target_pairs={{4,0},{5,1},{6,2},{7,3},{0,4},{1,5},{2,6},{3,7},{12,8},{13,9},{14,... | collective-permute-start | bytes 786440 | tf_op jit(solution)/shard_map/ppermute | solution.py:223
  3.5 1.3 %collective-permute-start.7 = (bf16[2,256,256]{2,1,0:T(8,128)(2,1)S(1)}, bf16[2,256,256]{2,1,0:T(8,128)(2,1)S(1)}, u32[]{:S(2)}, u32[]{:S(2)}) collective-permute-start(bf16[2,256,256]{2,1,0:T(8,128)(2,1)S(1)} %bitcast_convert_fusion.refs_0_), channel_id=1, source_target_pairs={{2,0},{3,1},{0,2},{1,3},{6,4},{7,5},{4,6},{5,7},{10,8},{11,9},{8,1... | collective-permute-start | bytes 786440 | tf_op jit(solution)/shard_map/ppermute | solution.py:223
  5.0 1.2 %collective-permute-start.1 = (bf16[2,256,256]{2,1,0:T(8,128)(2,1)S(1)}, bf16[2,256,256]{2,1,0:T(8,128)(2,1)S(1)}, u32[]{:S(2)}, u32[]{:S(2)}) collective-permute-start(bf16[2,256,256]{2,1,0:T(8,128)(2,1)S(1)} %bitcast_convert_fusion.refs_0_), channel_id=1, source_target_pairs={{16,0},{24,8},{0,16},{8,24},{17,1},{25,9},{1,17},{9,25},{18,2},{26... | collective-permute-start | bytes 786440 | tf_op jit(solution)/shard_map/ppermute | solution.py:214
  6.2 1.2 %collective-permute-start = (bf16[2,256,256]{2,1,0:T(8,128)(2,1)S(1)}, bf16[2,256,256]{2,1,0:T(8,128)(2,1)S(1)}, u32[]{:S(2)}, u32[]{:S(2)}) collective-permute-start(bf16[2,256,256]{2,1,0:T(8,128)(2,1)S(1)} %bitcast_convert_fusion.refs_0_), channel_id=1, source_target_pairs={{8,0},{0,8},{24,16},{16,24},{9,1},{1,9},{25,17},{17,25},{10,2},{2,... | collective-permute-start | bytes 786440 | tf_op jit(solution)/shard_map/ppermute | solution.py:214
  10.8 1.6 %copy-done.1 = bf16[2,8,256,256]{3,2,1,0:T(8,128)(2,1)S(1)} copy-done((bf16[2,8,256,256]{3,2,1,0:T(8,128)(2,1)S(1)}, bf16[2,8,256,256]{3,2,1,0:T(8,128)(2,1)}, u32[]{:S(2)}) %copy-start.1) | copy-done | bytes 2097176
  14.7 3.3 %collective-permute-done.1.refs_2_ = bf16[2,256,256]{2,1,0:T(8,128)(2,1)S(1)} collective-permute-done((bf16[2,256,256]{2,1,0:T(8,128)(2,1)S(1)}, bf16[2,256,256]{2,1,0:T(8,128)(2,1)S(1)}, u32[]{:S(2)}, u32[]{:S(2)}) %collective-permute-start.1) | collective-permute-done | bytes 262176 | tf_op jit(solution)/shard_map/ppermute | solution.py:214
  18.8 1.8 %collective-permute-start.10 = (bf16[2,256,256]{2,1,0:T(8,128)(2,1)S(1)}, bf16[2,256,256]{2,1,0:T(8,128)(2,1)S(1)}, u32[]{:S(2)}, u32[]{:S(2)}) collective-permute-start(bf16[2,256,256]{2,1,0:T(8,128)(2,1)S(1)} %get-tuple-element.19.refs_2_.refs_0_), channel_id=1, source_target_pairs={{8,0},{0,8},{24,16},{16,24},{9,1},{1,9},{25,17},{17,25},{10,2},{2,... | collective-permute-start | bytes 786440 | tf_op jit(solution)/shard_map/ppermute | solution.py:214
  20.8 5.2 %collective-permute-done.10.refs_1_ = bf16[2,256,256]{2,1,0:T(8,128)(2,1)S(1)} collective-permute-done((bf16[2,256,256]{2,1,0:T(8,128)(2,1)S(1)}, bf16[2,256,256]{2,1,0:T(8,128)(2,1)S(1)}, u32[]{:S(2)}, u32[]{:S(2)}) %collective-permute-start.10) | collective-permute-done | bytes 262176 | tf_op jit(solution)/shard_map/ppermute | solution.py:214
  25.9 1.9 %collective-permute-start.11 = (bf16[2,256,256]{2,1,0:T(8,128)(2,1)S(1)}, bf16[2,256,256]{2,1,0:T(8,128)(2,1)S(1)}, u32[]{:S(2)}, u32[]{:S(2)}) collective-permute-start(bf16[2,256,256]{2,1,0:T(8,128)(2,1)S(1)} %collective-permute-done.10.refs_1_), channel_id=1, source_target_pairs={{16,0},{24,8},{0,16},{8,24},{17,1},{25,9},{1,17},{9,25},{18,2},{26... | collective-permute-start | bytes 786440 | tf_op jit(solution)/shard_map/ppermute | solution.py:214
  27.8 1.9 %collective-permute-start.3 = (bf16[256,256]{1,0:T(8,128)(2,1)S(1)}, bf16[256,256]{1,0:T(8,128)(2,1)S(1)}, u32[]{:S(2)}, u32[]{:S(2)}) collective-permute-start(bf16[256,256]{1,0:T(8,128)(2,1)S(1)} %get-tuple-element.17), channel_id=1, source_target_pairs={{0,0},{1,1},{2,2},{3,3},{4,16},{5,17},{6,18},{7,19},{8,8},{9,9},{1... | collective-permute-start | bytes 393224 | tf_op jit(solution)/shard_map/ppermute | solution.py:231
  29.7 3.2 %collective-permute-start.5 = (bf16[256,256]{1,0:T(8,128)(2,1)S(1)}, bf16[256,256]{1,0:T(8,128)(2,1)S(1)}, u32[]{:S(2)}, u32[]{:S(2)}) collective-permute-start(bf16[256,256]{1,0:T(8,128)(2,1)S(1)} %get-tuple-element.18), channel_id=1, source_target_pairs={{0,0},{1,1},{2,8},{3,9},{4,4},{5,5},{6,12},{7,13},{8,2},{9,3},{10,... | collective-permute-start | bytes 393224 | tf_op jit(solution)/shard_map/ppermute | solution.py:231
  32.9 5.8 %collective-permute-done.3.refs_5_ = bf16[256,256]{1,0:T(8,128)(2,1)S(1)} collective-permute-done((bf16[256,256]{1,0:T(8,128)(2,1)S(1)}, bf16[256,256]{1,0:T(8,128)(2,1)S(1)}, u32[]{:S(2)}, u32[]{:S(2)}) %collective-permute-start.3) | collective-permute-done | bytes 131104 | tf_op jit(solution)/shard_map/ppermute | solution.py:231
  38.9 1.4 %collective-permute-start.12 = (bf16[8,256,256]{2,1,0:T(8,128)(2,1)S(1)}, bf16[8,256,256]{2,1,0:T(8,128)(2,1)S(1)}, u32[]{:S(2)}, u32[]{:S(2)}) collective-permute-start(bf16[8,256,256]{2,1,0:T(8,128)(2,1)S(1)} %shard_map.88.own_ref), channel_id=1, source_target_pairs={{1,0},{0,1},{3,2},{2,3},{5,4},{4,5},{7,6},{6,7},{9,8},{8,9},{11,10... | collective-permute-start | bytes 3145736 | tf_op jit(solution)/shard_map/ppermute | solution.py:220
  40.3 2.5 %collective-permute-start.4 = (bf16[256,256]{1,0:T(8,128)(2,1)S(1)}, bf16[256,256]{1,0:T(8,128)(2,1)S(1)}, u32[]{:S(2)}, u32[]{:S(2)}) collective-permute-start(bf16[256,256]{1,0:T(8,128)(2,1)S(1)} %collective-permute-done.3.refs_5_), channel_id=1, source_target_pairs={{0,0},{1,1},{2,8},{3,9},{4,4},{5,5},{6,12},{7,13},{8,2},{9,3},{10,... | collective-permute-start | bytes 393224 | tf_op jit(solution)/shard_map/ppermute | solution.py:231
  42.8 2.5 %collective-permute-start.6 = (bf16[256,256]{1,0:T(8,128)(2,1)S(1)}, bf16[256,256]{1,0:T(8,128)(2,1)S(1)}, u32[]{:S(2)}, u32[]{:S(2)}) collective-permute-start(bf16[256,256]{1,0:T(8,128)(2,1)S(1)} %collective-permute-done.5.refs_6_), channel_id=1, source_target_pairs={{0,1},{1,0},{2,3},{3,2},{4,17},{5,16},{6,19},{7,18},{8,9},{9,8},{1... | collective-permute-start | bytes 393224 | tf_op jit(solution)/shard_map/ppermute | solution.py:231
  45.3 5.7 %collective-permute-done.13.refs_2_ = bf16[2,256,256]{2,1,0:T(8,128)(2,1)S(1)} collective-permute-done((bf16[2,256,256]{2,1,0:T(8,128)(2,1)S(1)}, bf16[2,256,256]{2,1,0:T(8,128)(2,1)S(1)}, u32[]{:S(2)}, u32[]{:S(2)}) %collective-permute-start.13) | collective-permute-done | bytes 262176 | tf_op jit(solution)/shard_map/ppermute | solution.py:214
  51.0 1.4 %shard_map.89.part_ref = f32[2,256,256]{2,1,0:T(8,128)S(1)} custom-call(s32[5,8]{1,0:T(8,128)S(1)} %pad_add_fusion.meta, bf16[8,256,256]{2,1,0:T(8,128)(2,1)S(1)} %shard_map.88.own_ref, bf16[8,256,256]{2,1,0:T(8,128)(2,1)S(1)} %collective-permute-done.12.other_ref, bf16[2,256,256]{2,1,0:T(8,128)(2,1)S(1)} %get-tuple-element.19.refs_2_.refs_0_, ...), custom_call_target="tpu_custom_call" | custom-call | flops 536870912 | bytes 6291456 | tf_op jit(solution)/shard_map/pallas_call | solution.py:23
  52.6 1.4 %collective-permute-start.15 = (bf16[2,256,256]{2,1,0:T(8,128)(2,1)S(1)}, bf16[2,256,256]{2,1,0:T(8,128)(2,1)S(1)}, u32[]{:S(2)}, u32[]{:S(2)}) collective-permute-start(bf16[2,256,256]{2,1,0:T(8,128)(2,1)S(1)} %get-tuple-element.22.refs_0_), channel_id=1, source_target_pairs={{16,0},{24,8},{0,16},{8,24},{17,1},{25,9},{1,17},{9,25},{18,2},{26... | collective-permute-start | bytes 786440 | tf_op jit(solution)/shard_map/ppermute | solution.py:214
  55.3 1.5 %collective-permute-start.22 = (bf16[2,256,256]{2,1,0:T(8,128)(2,1)S(1)}, bf16[2,256,256]{2,1,0:T(8,128)(2,1)S(1)}, u32[]{:S(2)}, u32[]{:S(2)}) collective-permute-start(bf16[2,256,256]{2,1,0:T(8,128)(2,1)S(1)} %get-tuple-element.22.refs_0_), channel_id=1, source_target_pairs={{4,0},{5,1},{6,2},{7,3},{0,4},{1,5},{2,6},{3,7},{12,8},{13,9},{14,... | collective-permute-start | bytes 786440 | tf_op jit(solution)/shard_map/ppermute | solution.py:223
  56.7 3.9 %collective-permute-done.16.refs_3_ = bf16[2,256,256]{2,1,0:T(8,128)(2,1)S(1)} collective-permute-done((bf16[2,256,256]{2,1,0:T(8,128)(2,1)S(1)}, bf16[2,256,256]{2,1,0:T(8,128)(2,1)S(1)}, u32[]{:S(2)}, u32[]{:S(2)}) %collective-permute-start.16) | collective-permute-done | bytes 262176 | tf_op jit(solution)/shard_map/ppermute | solution.py:214
  60.6 5.1 %collective-permute-done.15.refs_2_ = bf16[2,256,256]{2,1,0:T(8,128)(2,1)S(1)} collective-permute-done((bf16[2,256,256]{2,1,0:T(8,128)(2,1)S(1)}, bf16[2,256,256]{2,1,0:T(8,128)(2,1)S(1)}, u32[]{:S(2)}, u32[]{:S(2)}) %collective-permute-start.15) | collective-permute-done | bytes 262176 | tf_op jit(solution)/shard_map/ppermute | solution.py:214
  66.4 2.0 %collective-permute-start.24 = (bf16[2,256,256]{2,1,0:T(8,128)(2,1)S(1)}, bf16[2,256,256]{2,1,0:T(8,128)(2,1)S(1)}, u32[]{:S(2)}, u32[]{:S(2)}) collective-permute-start(bf16[2,256,256]{2,1,0:T(8,128)(2,1)S(1)} %get-tuple-element.25.refs_2_.refs_0_), channel_id=1, source_target_pairs={{8,0},{0,8},{24,16},{16,24},{9,1},{1,9},{25,17},{17,25},{10,2},{2,... | collective-permute-start | bytes 786440 | tf_op jit(solution)/shard_map/ppermute | solution.py:214
  68.4 1.5 %collective-permute-done.22.refs_0_ = bf16[2,256,256]{2,1,0:T(8,128)(2,1)S(1)} collective-permute-done((bf16[2,256,256]{2,1,0:T(8,128)(2,1)S(1)}, bf16[2,256,256]{2,1,0:T(8,128)(2,1)S(1)}, u32[]{:S(2)}, u32[]{:S(2)}) %collective-permute-start.22) | collective-permute-done | bytes 262176 | tf_op jit(solution)/shard_map/ppermute | solution.py:223
  70.0 3.9 %collective-permute-done.24.refs_1_ = bf16[2,256,256]{2,1,0:T(8,128)(2,1)S(1)} collective-permute-done((bf16[2,256,256]{2,1,0:T(8,128)(2,1)S(1)}, bf16[2,256,256]{2,1,0:T(8,128)(2,1)S(1)}, u32[]{:S(2)}, u32[]{:S(2)}) %collective-permute-start.24) | collective-permute-done | bytes 262176 | tf_op jit(solution)/shard_map/ppermute | solution.py:214
  73.9 4.3 %collective-permute-start.17 = (bf16[256,256]{1,0:T(8,128)(2,1)S(1)}, bf16[256,256]{1,0:T(8,128)(2,1)S(1)}, u32[]{:S(2)}, u32[]{:S(2)}) collective-permute-start(bf16[256,256]{1,0:T(8,128)(2,1)S(1)} %get-tuple-element.23), channel_id=1, source_target_pairs={{0,0},{1,1},{2,2},{3,3},{4,16},{5,17},{6,18},{7,19},{8,8},{9,9},{1... | collective-permute-start | bytes 393224 | tf_op jit(solution)/shard_map/ppermute | solution.py:231
  78.2 2.2 %collective-permute-start.19 = (bf16[256,256]{1,0:T(8,128)(2,1)S(1)}, bf16[256,256]{1,0:T(8,128)(2,1)S(1)}, u32[]{:S(2)}, u32[]{:S(2)}) collective-permute-start(bf16[256,256]{1,0:T(8,128)(2,1)S(1)} %get-tuple-element.24), channel_id=1, source_target_pairs={{0,0},{1,1},{2,8},{3,9},{4,4},{5,5},{6,12},{7,13},{8,2},{9,3},{10,... | collective-permute-start | bytes 393224 | tf_op jit(solution)/shard_map/ppermute | solution.py:231
  81.5 3.6 %collective-permute-done.19.refs_6_ = bf16[256,256]{1,0:T(8,128)(2,1)S(1)} collective-permute-done((bf16[256,256]{1,0:T(8,128)(2,1)S(1)}, bf16[256,256]{1,0:T(8,128)(2,1)S(1)}, u32[]{:S(2)}, u32[]{:S(2)}) %collective-permute-start.19) | collective-permute-done | bytes 131104 | tf_op jit(solution)/shard_map/ppermute | solution.py:231
  85.2 3.8 %collective-permute-start.26 = (bf16[8,256,256]{2,1,0:T(8,128)(2,1)S(1)}, bf16[8,256,256]{2,1,0:T(8,128)(2,1)S(1)}, u32[]{:S(2)}, u32[]{:S(2)}) collective-permute-start(bf16[8,256,256]{2,1,0:T(8,128)(2,1)S(1)} %shard_map.93.own_ref), channel_id=1, source_target_pairs={{1,0},{0,1},{3,2},{2,3},{5,4},{4,5},{7,6},{6,7},{9,8},{8,9},{11,10... | collective-permute-start | bytes 3145736 | tf_op jit(solution)/shard_map/ppermute | solution.py:220
  89.0 1.9 %collective-permute-start.18 = (bf16[256,256]{1,0:T(8,128)(2,1)S(1)}, bf16[256,256]{1,0:T(8,128)(2,1)S(1)}, u32[]{:S(2)}, u32[]{:S(2)}) collective-permute-start(bf16[256,256]{1,0:T(8,128)(2,1)S(1)} %collective-permute-done.17.refs_5_), channel_id=1, source_target_pairs={{0,0},{1,1},{2,8},{3,9},{4,4},{5,5},{6,12},{7,13},{8,2},{9,3},{10,... | collective-permute-start | bytes 393224 | tf_op jit(solution)/shard_map/ppermute | solution.py:231
  91.0 3.0 %collective-permute-start.20 = (bf16[256,256]{1,0:T(8,128)(2,1)S(1)}, bf16[256,256]{1,0:T(8,128)(2,1)S(1)}, u32[]{:S(2)}, u32[]{:S(2)}) collective-permute-start(bf16[256,256]{1,0:T(8,128)(2,1)S(1)} %collective-permute-done.19.refs_6_), channel_id=1, source_target_pairs={{0,1},{1,0},{2,3},{3,2},{4,17},{5,16},{6,19},{7,18},{8,9},{9,8},{1... | collective-permute-start | bytes 393224 | tf_op jit(solution)/shard_map/ppermute | solution.py:231
  93.9 5.8 %collective-permute-done.27.refs_2_ = bf16[2,256,256]{2,1,0:T(8,128)(2,1)S(1)} collective-permute-done((bf16[2,256,256]{2,1,0:T(8,128)(2,1)S(1)}, bf16[2,256,256]{2,1,0:T(8,128)(2,1)S(1)}, u32[]{:S(2)}, u32[]{:S(2)}) %collective-permute-start.27) | collective-permute-done | bytes 262176 | tf_op jit(solution)/shard_map/ppermute | solution.py:214
  99.7 1.4 %shard_map.94.part_ref = f32[2,256,256]{2,1,0:T(8,128)S(1)} custom-call(s32[5,8]{1,0:T(8,128)S(1)} %pad_add_fusion.meta, bf16[8,256,256]{2,1,0:T(8,128)(2,1)S(1)} %shard_map.93.own_ref, bf16[8,256,256]{2,1,0:T(8,128)(2,1)S(1)} %collective-permute-done.26.other_ref, bf16[2,256,256]{2,1,0:T(8,128)(2,1)S(1)} %get-tuple-element.25.refs_2_.refs_0_, ...), custom_call_target="tpu_custom_call" | custom-call | flops 536870912 | bytes 6291456 | tf_op jit(solution)/shard_map/pallas_call | solution.py:23
  (57 shorter events, 12.3 us)
Async XLA Ops:
  0.0 9.1 %copy-start = (s32[2,8,8]{2,1,0:T(8,128)S(1)}, s32[2,8,8]{2,1,0:T(8,128)}, u32[]{:S(2)}) copy-start(s32[2,8,8]{2,1,0:T(8,128)} %param.12) | copy-start | bytes 1540
  1.1 19.5 %collective-permute-start.8 = (bf16[2,256,256]{2,1,0:T(8,128)(2,1)S(1)}, bf16[2,256,256]{2,1,0:T(8,128)(2,1)S(1)}, u32[]{:S(2)}, u32[]{:S(2)}) collective-permute-start(bf16[2,256,256]{2,1,0:T(8,128)(2,1)S(1)} %bitcast_convert_fusion.refs_0_), channel_id=1, source_target_pairs={{4,0},{5,1},{6,2},{7,3},{0,4},{1,5},{2,6},{3,7},{12,8},{13,9},{14,... | collective-permute-start | bytes 786440 | tf_op jit(solution)/shard_map/ppermute | solution.py:223
  3.5 17.1 %collective-permute-start.7 = (bf16[2,256,256]{2,1,0:T(8,128)(2,1)S(1)}, bf16[2,256,256]{2,1,0:T(8,128)(2,1)S(1)}, u32[]{:S(2)}, u32[]{:S(2)}) collective-permute-start(bf16[2,256,256]{2,1,0:T(8,128)(2,1)S(1)} %bitcast_convert_fusion.refs_0_), channel_id=1, source_target_pairs={{2,0},{3,1},{0,2},{1,3},{6,4},{7,5},{4,6},{5,7},{10,8},{11,9},{8,1... | collective-permute-start | bytes 786440 | tf_op jit(solution)/shard_map/ppermute | solution.py:223
  4.8 9.9 %collective-permute-start.2 = (bf16[2,256,256]{2,1,0:T(8,128)(2,1)S(1)}, bf16[2,256,256]{2,1,0:T(8,128)(2,1)S(1)}, u32[]{:S(2)}, u32[]{:S(2)}) collective-permute-start(bf16[2,256,256]{2,1,0:T(8,128)(2,1)S(1)} %bitcast_convert_fusion.refs_0_), channel_id=1, source_target_pairs={{24,0},{16,8},{8,16},{0,24},{25,1},{17,9},{9,17},{1,25},{26,2},{18... | collective-permute-start | bytes 786440 | tf_op jit(solution)/shard_map/ppermute | solution.py:214
  5.0 13.1 %collective-permute-start.1 = (bf16[2,256,256]{2,1,0:T(8,128)(2,1)S(1)}, bf16[2,256,256]{2,1,0:T(8,128)(2,1)S(1)}, u32[]{:S(2)}, u32[]{:S(2)}) collective-permute-start(bf16[2,256,256]{2,1,0:T(8,128)(2,1)S(1)} %bitcast_convert_fusion.refs_0_), channel_id=1, source_target_pairs={{16,0},{24,8},{0,16},{8,24},{17,1},{25,9},{1,17},{9,25},{18,2},{26... | collective-permute-start | bytes 786440 | tf_op jit(solution)/shard_map/ppermute | solution.py:214
  6.2 11.8 %collective-permute-start = (bf16[2,256,256]{2,1,0:T(8,128)(2,1)S(1)}, bf16[2,256,256]{2,1,0:T(8,128)(2,1)S(1)}, u32[]{:S(2)}, u32[]{:S(2)}) collective-permute-start(bf16[2,256,256]{2,1,0:T(8,128)(2,1)S(1)} %bitcast_convert_fusion.refs_0_), channel_id=1, source_target_pairs={{8,0},{0,8},{24,16},{16,24},{9,1},{1,9},{25,17},{17,25},{10,2},{2,... | collective-permute-start | bytes 786440 | tf_op jit(solution)/shard_map/ppermute | solution.py:214
  10.8 1.6 %copy-start.1 = (bf16[2,8,256,256]{3,2,1,0:T(8,128)(2,1)S(1)}, bf16[2,8,256,256]{3,2,1,0:T(8,128)(2,1)}, u32[]{:S(2)}) copy-start(bf16[2,8,256,256]{3,2,1,0:T(8,128)(2,1)} %k_ref.1) | copy-start | bytes 6291460
  12.4 0.7 copy-start.3
  18.8 32.2 %copy-start.2 = (f32[2,1,256,256]{3,2,1,0:T(8,128)S(1)}, f32[2,1,256,256]{3,2,1,0:T(8,128)}, u32[]{:S(2)}) copy-start(f32[2,1,256,256]{3,2,1,0:T(8,128)} %param.8) | copy-start | bytes 1572868
  18.8 7.1 %collective-permute-start.10 = (bf16[2,256,256]{2,1,0:T(8,128)(2,1)S(1)}, bf16[2,256,256]{2,1,0:T(8,128)(2,1)S(1)}, u32[]{:S(2)}, u32[]{:S(2)}) collective-permute-start(bf16[2,256,256]{2,1,0:T(8,128)(2,1)S(1)} %get-tuple-element.19.refs_2_.refs_0_), channel_id=1, source_target_pairs={{8,0},{0,8},{24,16},{16,24},{9,1},{1,9},{25,17},{17,25},{10,2},{2,... | collective-permute-start | bytes 786440 | tf_op jit(solution)/shard_map/ppermute | solution.py:214
  20.6 18.2 %collective-permute-start.9 = (bf16[2,256,256]{2,1,0:T(8,128)(2,1)S(1)}, bf16[2,256,256]{2,1,0:T(8,128)(2,1)S(1)}, u32[]{:S(2)}, u32[]{:S(2)}) collective-permute-start(bf16[2,256,256]{2,1,0:T(8,128)(2,1)S(1)} %shard_map.87.refs_2_), channel_id=1, source_target_pairs={{2,0},{3,1},{0,2},{1,3},{6,4},{7,5},{4,6},{5,7},{10,8},{11,9},{8,1... | collective-permute-start | bytes 786440 | tf_op jit(solution)/shard_map/ppermute | solution.py:223
  25.9 12.8 %collective-permute-start.11 = (bf16[2,256,256]{2,1,0:T(8,128)(2,1)S(1)}, bf16[2,256,256]{2,1,0:T(8,128)(2,1)S(1)}, u32[]{:S(2)}, u32[]{:S(2)}) collective-permute-start(bf16[2,256,256]{2,1,0:T(8,128)(2,1)S(1)} %collective-permute-done.10.refs_1_), channel_id=1, source_target_pairs={{16,0},{24,8},{0,16},{8,24},{17,1},{25,9},{1,17},{9,25},{18,2},{26... | collective-permute-start | bytes 786440 | tf_op jit(solution)/shard_map/ppermute | solution.py:214
  27.8 10.9 %collective-permute-start.3 = (bf16[256,256]{1,0:T(8,128)(2,1)S(1)}, bf16[256,256]{1,0:T(8,128)(2,1)S(1)}, u32[]{:S(2)}, u32[]{:S(2)}) collective-permute-start(bf16[256,256]{1,0:T(8,128)(2,1)S(1)} %get-tuple-element.17), channel_id=1, source_target_pairs={{0,0},{1,1},{2,2},{3,3},{4,16},{5,17},{6,18},{7,19},{8,8},{9,9},{1... | collective-permute-start | bytes 393224 | tf_op jit(solution)/shard_map/ppermute | solution.py:231
  29.7 9.0 %collective-permute-start.5 = (bf16[256,256]{1,0:T(8,128)(2,1)S(1)}, bf16[256,256]{1,0:T(8,128)(2,1)S(1)}, u32[]{:S(2)}, u32[]{:S(2)}) collective-permute-start(bf16[256,256]{1,0:T(8,128)(2,1)S(1)} %get-tuple-element.18), channel_id=1, source_target_pairs={{0,0},{1,1},{2,8},{3,9},{4,4},{5,5},{6,12},{7,13},{8,2},{9,3},{10,... | collective-permute-start | bytes 393224 | tf_op jit(solution)/shard_map/ppermute | solution.py:231
  38.9 12.1 %collective-permute-start.12 = (bf16[8,256,256]{2,1,0:T(8,128)(2,1)S(1)}, bf16[8,256,256]{2,1,0:T(8,128)(2,1)S(1)}, u32[]{:S(2)}, u32[]{:S(2)}) collective-permute-start(bf16[8,256,256]{2,1,0:T(8,128)(2,1)S(1)} %shard_map.88.own_ref), channel_id=1, source_target_pairs={{1,0},{0,1},{3,2},{2,3},{5,4},{4,5},{7,6},{6,7},{9,8},{8,9},{11,10... | collective-permute-start | bytes 3145736 | tf_op jit(solution)/shard_map/ppermute | solution.py:220
  40.3 10.7 %collective-permute-start.13 = (bf16[2,256,256]{2,1,0:T(8,128)(2,1)S(1)}, bf16[2,256,256]{2,1,0:T(8,128)(2,1)S(1)}, u32[]{:S(2)}, u32[]{:S(2)}) collective-permute-start(bf16[2,256,256]{2,1,0:T(8,128)(2,1)S(1)} %get-tuple-element.19.refs_2_.refs_0_), channel_id=1, source_target_pairs={{16,0},{24,8},{0,16},{8,24},{17,1},{25,9},{1,17},{9,25},{18,2},{26... | collective-permute-start | bytes 786440 | tf_op jit(solution)/shard_map/ppermute | solution.py:214
  40.3 12.1 %collective-permute-start.4 = (bf16[256,256]{1,0:T(8,128)(2,1)S(1)}, bf16[256,256]{1,0:T(8,128)(2,1)S(1)}, u32[]{:S(2)}, u32[]{:S(2)}) collective-permute-start(bf16[256,256]{1,0:T(8,128)(2,1)S(1)} %collective-permute-done.3.refs_5_), channel_id=1, source_target_pairs={{0,0},{1,1},{2,8},{3,9},{4,4},{5,5},{6,12},{7,13},{8,2},{9,3},{10,... | collective-permute-start | bytes 393224 | tf_op jit(solution)/shard_map/ppermute | solution.py:231
  42.8 9.6 %collective-permute-start.6 = (bf16[256,256]{1,0:T(8,128)(2,1)S(1)}, bf16[256,256]{1,0:T(8,128)(2,1)S(1)}, u32[]{:S(2)}, u32[]{:S(2)}) collective-permute-start(bf16[256,256]{1,0:T(8,128)(2,1)S(1)} %collective-permute-done.5.refs_6_), channel_id=1, source_target_pairs={{0,1},{1,0},{2,3},{3,2},{4,17},{5,16},{6,19},{7,18},{8,9},{9,8},{1... | collective-permute-start | bytes 393224 | tf_op jit(solution)/shard_map/ppermute | solution.py:231
  52.5 8.0 %collective-permute-start.16 = (bf16[2,256,256]{2,1,0:T(8,128)(2,1)S(1)}, bf16[2,256,256]{2,1,0:T(8,128)(2,1)S(1)}, u32[]{:S(2)}, u32[]{:S(2)}) collective-permute-start(bf16[2,256,256]{2,1,0:T(8,128)(2,1)S(1)} %get-tuple-element.22.refs_0_), channel_id=1, source_target_pairs={{24,0},{16,8},{8,16},{0,24},{25,1},{17,9},{9,17},{1,25},{26,2},{18... | collective-permute-start | bytes 786440 | tf_op jit(solution)/shard_map/ppermute | solution.py:214
  52.6 13.0 %collective-permute-start.15 = (bf16[2,256,256]{2,1,0:T(8,128)(2,1)S(1)}, bf16[2,256,256]{2,1,0:T(8,128)(2,1)S(1)}, u32[]{:S(2)}, u32[]{:S(2)}) collective-permute-start(bf16[2,256,256]{2,1,0:T(8,128)(2,1)S(1)} %get-tuple-element.22.refs_0_), channel_id=1, source_target_pairs={{16,0},{24,8},{0,16},{8,24},{17,1},{25,9},{1,17},{9,25},{18,2},{26... | collective-permute-start | bytes 786440 | tf_op jit(solution)/shard_map/ppermute | solution.py:214
  54.0 11.6 %collective-permute-start.14 = (bf16[2,256,256]{2,1,0:T(8,128)(2,1)S(1)}, bf16[2,256,256]{2,1,0:T(8,128)(2,1)S(1)}, u32[]{:S(2)}, u32[]{:S(2)}) collective-permute-start(bf16[2,256,256]{2,1,0:T(8,128)(2,1)S(1)} %get-tuple-element.22.refs_0_), channel_id=1, source_target_pairs={{8,0},{0,8},{24,16},{16,24},{9,1},{1,9},{25,17},{17,25},{10,2},{2,... | collective-permute-start | bytes 786440 | tf_op jit(solution)/shard_map/ppermute | solution.py:214
  55.3 14.7 %collective-permute-start.22 = (bf16[2,256,256]{2,1,0:T(8,128)(2,1)S(1)}, bf16[2,256,256]{2,1,0:T(8,128)(2,1)S(1)}, u32[]{:S(2)}, u32[]{:S(2)}) collective-permute-start(bf16[2,256,256]{2,1,0:T(8,128)(2,1)S(1)} %get-tuple-element.22.refs_0_), channel_id=1, source_target_pairs={{4,0},{5,1},{6,2},{7,3},{0,4},{1,5},{2,6},{3,7},{12,8},{13,9},{14,... | collective-permute-start | bytes 786440 | tf_op jit(solution)/shard_map/ppermute | solution.py:223
  56.7 13.2 %collective-permute-start.21 = (bf16[2,256,256]{2,1,0:T(8,128)(2,1)S(1)}, bf16[2,256,256]{2,1,0:T(8,128)(2,1)S(1)}, u32[]{:S(2)}, u32[]{:S(2)}) collective-permute-start(bf16[2,256,256]{2,1,0:T(8,128)(2,1)S(1)} %get-tuple-element.22.refs_0_), channel_id=1, source_target_pairs={{2,0},{3,1},{0,2},{1,3},{6,4},{7,5},{4,6},{5,7},{10,8},{11,9},{8,1... | collective-permute-start | bytes 786440 | tf_op jit(solution)/shard_map/ppermute | solution.py:223
  66.4 7.5 %collective-permute-start.24 = (bf16[2,256,256]{2,1,0:T(8,128)(2,1)S(1)}, bf16[2,256,256]{2,1,0:T(8,128)(2,1)S(1)}, u32[]{:S(2)}, u32[]{:S(2)}) collective-permute-start(bf16[2,256,256]{2,1,0:T(8,128)(2,1)S(1)} %get-tuple-element.25.refs_2_.refs_0_), channel_id=1, source_target_pairs={{8,0},{0,8},{24,16},{16,24},{9,1},{1,9},{25,17},{17,25},{10,2},{2,... | collective-permute-start | bytes 786440 | tf_op jit(solution)/shard_map/ppermute | solution.py:214
  69.9 15.1 %collective-permute-start.23 = (bf16[2,256,256]{2,1,0:T(8,128)(2,1)S(1)}, bf16[2,256,256]{2,1,0:T(8,128)(2,1)S(1)}, u32[]{:S(2)}, u32[]{:S(2)}) collective-permute-start(bf16[2,256,256]{2,1,0:T(8,128)(2,1)S(1)} %shard_map.92.refs_2_), channel_id=1, source_target_pairs={{2,0},{3,1},{0,2},{1,3},{6,4},{7,5},{4,6},{5,7},{10,8},{11,9},{8,1... | collective-permute-start | bytes 786440 | tf_op jit(solution)/shard_map/ppermute | solution.py:223
  73.9 11.2 %collective-permute-start.25 = (bf16[2,256,256]{2,1,0:T(8,128)(2,1)S(1)}, bf16[2,256,256]{2,1,0:T(8,128)(2,1)S(1)}, u32[]{:S(2)}, u32[]{:S(2)}) collective-permute-start(bf16[2,256,256]{2,1,0:T(8,128)(2,1)S(1)} %collective-permute-done.24.refs_1_), channel_id=1, source_target_pairs={{16,0},{24,8},{0,16},{8,24},{17,1},{25,9},{1,17},{9,25},{18,2},{26... | collective-permute-start | bytes 786440 | tf_op jit(solution)/shard_map/ppermute | solution.py:214
  73.9 7.6 %collective-permute-start.17 = (bf16[256,256]{1,0:T(8,128)(2,1)S(1)}, bf16[256,256]{1,0:T(8,128)(2,1)S(1)}, u32[]{:S(2)}, u32[]{:S(2)}) collective-permute-start(bf16[256,256]{1,0:T(8,128)(2,1)S(1)} %get-tuple-element.23), channel_id=1, source_target_pairs={{0,0},{1,1},{2,2},{3,3},{4,16},{5,17},{6,18},{7,19},{8,8},{9,9},{1... | collective-permute-start | bytes 393224 | tf_op jit(solution)/shard_map/ppermute | solution.py:231
  78.2 6.9 %collective-permute-start.19 = (bf16[256,256]{1,0:T(8,128)(2,1)S(1)}, bf16[256,256]{1,0:T(8,128)(2,1)S(1)}, u32[]{:S(2)}, u32[]{:S(2)}) collective-permute-start(bf16[256,256]{1,0:T(8,128)(2,1)S(1)} %get-tuple-element.24), channel_id=1, source_target_pairs={{0,0},{1,1},{2,8},{3,9},{4,4},{5,5},{6,12},{7,13},{8,2},{9,3},{10,... | collective-permute-start | bytes 393224 | tf_op jit(solution)/shard_map/ppermute | solution.py:231
  85.2 14.5 %collective-permute-start.26 = (bf16[8,256,256]{2,1,0:T(8,128)(2,1)S(1)}, bf16[8,256,256]{2,1,0:T(8,128)(2,1)S(1)}, u32[]{:S(2)}, u32[]{:S(2)}) collective-permute-start(bf16[8,256,256]{2,1,0:T(8,128)(2,1)S(1)} %shard_map.93.own_ref), channel_id=1, source_target_pairs={{1,0},{0,1},{3,2},{2,3},{5,4},{4,5},{7,6},{6,7},{9,8},{8,9},{11,10... | collective-permute-start | bytes 3145736 | tf_op jit(solution)/shard_map/ppermute | solution.py:220
  89.0 10.7 %collective-permute-start.27 = (bf16[2,256,256]{2,1,0:T(8,128)(2,1)S(1)}, bf16[2,256,256]{2,1,0:T(8,128)(2,1)S(1)}, u32[]{:S(2)}, u32[]{:S(2)}) collective-permute-start(bf16[2,256,256]{2,1,0:T(8,128)(2,1)S(1)} %get-tuple-element.25.refs_2_.refs_0_), channel_id=1, source_target_pairs={{16,0},{24,8},{0,16},{8,24},{17,1},{25,9},{1,17},{9,25},{18,2},{26... | collective-permute-start | bytes 786440 | tf_op jit(solution)/shard_map/ppermute | solution.py:214
  89.0 12.1 %collective-permute-start.18 = (bf16[256,256]{1,0:T(8,128)(2,1)S(1)}, bf16[256,256]{1,0:T(8,128)(2,1)S(1)}, u32[]{:S(2)}, u32[]{:S(2)}) collective-permute-start(bf16[256,256]{1,0:T(8,128)(2,1)S(1)} %collective-permute-done.17.refs_5_), channel_id=1, source_target_pairs={{0,0},{1,1},{2,8},{3,9},{4,4},{5,5},{6,12},{7,13},{8,2},{9,3},{10,... | collective-permute-start | bytes 393224 | tf_op jit(solution)/shard_map/ppermute | solution.py:231
  91.0 10.1 %collective-permute-start.20 = (bf16[256,256]{1,0:T(8,128)(2,1)S(1)}, bf16[256,256]{1,0:T(8,128)(2,1)S(1)}, u32[]{:S(2)}, u32[]{:S(2)}) collective-permute-start(bf16[256,256]{1,0:T(8,128)(2,1)S(1)} %collective-permute-done.19.refs_6_), channel_id=1, source_target_pairs={{0,1},{1,0},{2,3},{3,2},{4,17},{5,16},{6,19},{7,18},{8,9},{9,8},{1... | collective-permute-start | bytes 393224 | tf_op jit(solution)/shard_map/ppermute | solution.py:231
  (1 other events, 0.7 us)

commit v7 on v4

--- a/solution.py
+++ b/solution.py
@@ -273,7 +273,7 @@
             column[step] = tied(column[step], column[1], coupled)
             column[step + 1] = from_chip(column[step], 1)
         column = [column[step] for step in range(halves)]
-        own = whole_column(column, [*far, same, other])
+        own = whole_column(column, [c_pieces[1], c_pieces[2], same, other])
         same, other = crossing(same, last_bits), crossing(other, high_parts, 1)
         part = first_update(rows, meta, own, swapped(own), c_pieces, state, coulomb_own, inverse)
         state, *halves_out = second_update(same, other, part, inverse, sweep_index < ITERS - 1)

time: 92.6 us -> 93.6 us (1.011)
  waiting for transfers between devices: 32.5 us -> 35.2 us
  starting transfers between devices: 44.8 us -> 43 us
    ppermute x8, waiting for transfers between devices: 13.7 us -> 19.5 us  [crossing(): return lax.ppermute(x, ('row', 'col'), pairs)]
    ppermute x14, waiting for transfers between devices: 18.6 us -> 14.1 us  [from_row(): return lax.ppermute(x, 'row', [(r ^ step, r) for r in range(rows)])]
    ppermute x2, starting transfers between devices: 6.42 us -> 4.35 us  [swapped(): return lax.ppermute(x, 'col', [(c ^ 1, c) for c in range(cols)])]
    ppermute x6, starting transfers between devices: 7.58 us -> 5.54 us  [from_chip(): return lax.ppermute(x, 'col', [(c ^ 2 * step, c) for c in range(cols)])]
    ppermute x14, starting transfers between devices: 9.31 us -> 11 us  [from_row(): return lax.ppermute(x, 'row', [(r ^ step, r) for r in range(rows)])]
    ppermute x6, waiting for transfers between devices: 0.24 us -> 1.51 us  [from_chip(): return lax.ppermute(x, 'col', [(c ^ 2 * step, c) for c in range(cols)])]
  transfers between devices with their start and end apart: 30 -> 30, of which waited for: 16 -> 13; matrix products, arithmetic and copies ran while one was open for 4% -> 4% of each run, Pallas kernels for 6% -> 6%
where the time goes in v7:
time: 93.6 us; the launch traced here: 92.3 us
  starting transfers between devices  43 us (46%)
  waiting for transfers between devices  35.2 us (38%)
  Pallas kernels  6.41 us (7%)
  local copies, waits for them, and re-layouts  4.64 us (5%)
  other arithmetic  2.77 us (3%)
    ppermute x8, starting transfers between devices, crossing(): return lax.ppermute(x, ('row', 'col'), pairs)  22.2 us
    ppermute x8, waiting for transfers between devices, crossing(): return lax.ppermute(x, ('row', 'col'), pairs)  19.5 us
    ppermute x14, waiting for transfers between devices, from_row(): return lax.ppermute(x, 'row', [(r ^ step, r) for r in range(rows)])  14.1 us
    ppermute x14, starting transfers between devices, from_row(): return lax.ppermute(x, 'row', [(r ^ step, r) for r in range(rows)])  11 us
    pallas_call x9, Pallas kernels, call(): pl.pallas_call(body, out_shape=out_shape, in_specs=in_specs, out_specs=VM...  6.41 us
    ppermute x6, starting transfers between devices, from_chip(): return lax.ppermute(x, 'col', [(c ^ 2 * step, c) for c in range(cols)])  5.54 us
    ppermute x2, starting transfers between devices, swapped(): return lax.ppermute(x, 'col', [(c ^ 1, c) for c in range(cols)])  4.35 us
    unnamed x10, local copies, waits for them, and re-layouts  2.93 us
  transfers between devices with their start and end apart: 30, of which 13 were waited for; matrix products, arithmetic and copies ran while one was open for 4% of the time, Pallas kernels for 6%

profile of v7, /device:TPU:7, one launch (start us, length us, event | category | flops | bytes accessed | tf_op | source)
XLA Modules:
  0.0 92.3 jit_solution(12715412431777707448)
XLA Ops:
  0.0 1.1 %bitcast_convert_fusion.refs_0_ = bf16[2,256,256]{2,1,0:T(8,128)(2,1)S(1)} fusion(f32[2,1,256,256]{3,2,1,0:T(8,128)} %param.8), kind=kLoop, calls=%fused_computation.12 | loop fusion | flops 131072 | bytes 786432 | tf_op jit(solution)/shard_map/convert_element_type | solution.py:240
  1.1 2.4 %collective-permute-start.8 = (bf16[2,256,256]{2,1,0:T(8,128)(2,1)S(1)}, bf16[2,256,256]{2,1,0:T(8,128)(2,1)S(1)}, u32[]{:S(2)}, u32[]{:S(2)}) collective-permute-start(bf16[2,256,256]{2,1,0:T(8,128)(2,1)S(1)} %bitcast_convert_fusion.refs_0_), channel_id=1, source_target_pairs={{4,0},{5,1},{6,2},{7,3},{0,4},{1,5},{2,6},{3,7},{12,8},{13,9},{14,... | collective-permute-start | bytes 786440 | tf_op jit(solution)/shard_map/ppermute | solution.py:223
  3.5 1.3 %collective-permute-start.7 = (bf16[2,256,256]{2,1,0:T(8,128)(2,1)S(1)}, bf16[2,256,256]{2,1,0:T(8,128)(2,1)S(1)}, u32[]{:S(2)}, u32[]{:S(2)}) collective-permute-start(bf16[2,256,256]{2,1,0:T(8,128)(2,1)S(1)} %bitcast_convert_fusion.refs_0_), channel_id=1, source_target_pairs={{2,0},{3,1},{0,2},{1,3},{6,4},{7,5},{4,6},{5,7},{10,8},{11,9},{8,1... | collective-permute-start | bytes 786440 | tf_op jit(solution)/shard_map/ppermute | solution.py:223
  5.0 1.2 %collective-permute-start.1 = (bf16[2,256,256]{2,1,0:T(8,128)(2,1)S(1)}, bf16[2,256,256]{2,1,0:T(8,128)(2,1)S(1)}, u32[]{:S(2)}, u32[]{:S(2)}) collective-permute-start(bf16[2,256,256]{2,1,0:T(8,128)(2,1)S(1)} %bitcast_convert_fusion.refs_0_), channel_id=1, source_target_pairs={{16,0},{24,8},{0,16},{8,24},{17,1},{25,9},{1,17},{9,25},{18,2},{26... | collective-permute-start | bytes 786440 | tf_op jit(solution)/shard_map/ppermute | solution.py:214
  6.2 1.2 %collective-permute-start = (bf16[2,256,256]{2,1,0:T(8,128)(2,1)S(1)}, bf16[2,256,256]{2,1,0:T(8,128)(2,1)S(1)}, u32[]{:S(2)}, u32[]{:S(2)}) collective-permute-start(bf16[2,256,256]{2,1,0:T(8,128)(2,1)S(1)} %bitcast_convert_fusion.refs_0_), channel_id=1, source_target_pairs={{8,0},{0,8},{24,16},{16,24},{9,1},{1,9},{25,17},{17,25},{10,2},{2,... | collective-permute-start | bytes 786440 | tf_op jit(solution)/shard_map/ppermute | solution.py:214
  10.8 1.6 %copy-done.1 = bf16[2,8,256,256]{3,2,1,0:T(8,128)(2,1)S(1)} copy-done((bf16[2,8,256,256]{3,2,1,0:T(8,128)(2,1)S(1)}, bf16[2,8,256,256]{3,2,1,0:T(8,128)(2,1)}, u32[]{:S(2)}) %copy-start.1) | copy-done | bytes 2097176
  14.7 3.3 %collective-permute-done.1.refs_2_ = bf16[2,256,256]{2,1,0:T(8,128)(2,1)S(1)} collective-permute-done((bf16[2,256,256]{2,1,0:T(8,128)(2,1)S(1)}, bf16[2,256,256]{2,1,0:T(8,128)(2,1)S(1)}, u32[]{:S(2)}, u32[]{:S(2)}) %collective-permute-start.1) | collective-permute-done | bytes 262176 | tf_op jit(solution)/shard_map/ppermute | solution.py:214
  19.1 1.7 %collective-permute-start.11 = (bf16[2,256,256]{2,1,0:T(8,128)(2,1)S(1)}, bf16[2,256,256]{2,1,0:T(8,128)(2,1)S(1)}, u32[]{:S(2)}, u32[]{:S(2)}) collective-permute-start(bf16[2,256,256]{2,1,0:T(8,128)(2,1)S(1)} %get-tuple-element.19.refs_2_.refs_0_), channel_id=1, source_target_pairs={{16,0},{24,8},{0,16},{8,24},{17,1},{25,9},{1,17},{9,25},{18,2},{26... | collective-permute-start | bytes 786440 | tf_op jit(solution)/shard_map/ppermute | solution.py:214
  21.0 2.9 %collective-permute-start.3 = (bf16[256,256]{1,0:T(8,128)(2,1)S(1)}, bf16[256,256]{1,0:T(8,128)(2,1)S(1)}, u32[]{:S(2)}, u32[]{:S(2)}) collective-permute-start(bf16[256,256]{1,0:T(8,128)(2,1)S(1)} %get-tuple-element.17), channel_id=1, source_target_pairs={{0,0},{1,1},{2,2},{3,3},{4,16},{5,17},{6,18},{7,19},{8,8},{9,9},{1... | collective-permute-start | bytes 393224 | tf_op jit(solution)/shard_map/ppermute | solution.py:231
  23.9 3.1 %collective-permute-start.5 = (bf16[256,256]{1,0:T(8,128)(2,1)S(1)}, bf16[256,256]{1,0:T(8,128)(2,1)S(1)}, u32[]{:S(2)}, u32[]{:S(2)}) collective-permute-start(bf16[256,256]{1,0:T(8,128)(2,1)S(1)} %get-tuple-element.18), channel_id=1, source_target_pairs={{0,0},{1,1},{2,8},{3,9},{4,4},{5,5},{6,12},{7,13},{8,2},{9,3},{10,... | collective-permute-start | bytes 393224 | tf_op jit(solution)/shard_map/ppermute | solution.py:231
  27.1 4.9 %collective-permute-done.3.refs_6_ = bf16[256,256]{1,0:T(8,128)(2,1)S(1)} collective-permute-done((bf16[256,256]{1,0:T(8,128)(2,1)S(1)}, bf16[256,256]{1,0:T(8,128)(2,1)S(1)}, u32[]{:S(2)}, u32[]{:S(2)}) %collective-permute-start.3) | collective-permute-done | bytes 131104 | tf_op jit(solution)/shard_map/ppermute | solution.py:231
  32.0 1.6 %collective-permute-start.12 = (bf16[8,256,256]{2,1,0:T(8,128)(2,1)S(1)}, bf16[8,256,256]{2,1,0:T(8,128)(2,1)S(1)}, u32[]{:S(2)}, u32[]{:S(2)}) collective-permute-start(bf16[8,256,256]{2,1,0:T(8,128)(2,1)S(1)} %shard_map.88.own_ref), channel_id=1, source_target_pairs={{1,0},{0,1},{3,2},{2,3},{5,4},{4,5},{7,6},{6,7},{9,8},{8,9},{11,10... | collective-permute-start | bytes 3145736 | tf_op jit(solution)/shard_map/ppermute | solution.py:220
  33.6 1.3 %collective-permute-start.13 = (bf16[1,256,256]{2,1,0:T(8,128)(2,1)S(1)}, bf16[1,256,256]{2,1,0:T(8,128)(2,1)S(1)}, u32[]{:S(2)}, u32[]{:S(2)}) collective-permute-start(bf16[1,256,256]{2,1,0:T(8,128)(2,1)S(1)} %slice.16), channel_id=1, source_target_pairs={{8,0},{0,8},{24,16},{16,24},{9,1},{1,9},{25,17},{17,25},{10,2},{2,... | collective-permute-start | bytes 393224 | tf_op jit(solution)/shard_map/ppermute | solution.py:214
  35.2 1.9 %collective-permute-start.4 = (bf16[256,256]{1,0:T(8,128)(2,1)S(1)}, bf16[256,256]{1,0:T(8,128)(2,1)S(1)}, u32[]{:S(2)}, u32[]{:S(2)}) collective-permute-start(bf16[256,256]{1,0:T(8,128)(2,1)S(1)} %collective-permute-done.3.refs_6_), channel_id=1, source_target_pairs={{0,0},{1,1},{2,8},{3,9},{4,4},{5,5},{6,12},{7,13},{8,2},{9,3},{10,... | collective-permute-start | bytes 393224 | tf_op jit(solution)/shard_map/ppermute | solution.py:231
  37.1 3.2 %collective-permute-start.6 = (bf16[256,256]{1,0:T(8,128)(2,1)S(1)}, bf16[256,256]{1,0:T(8,128)(2,1)S(1)}, u32[]{:S(2)}, u32[]{:S(2)}) collective-permute-start(bf16[256,256]{1,0:T(8,128)(2,1)S(1)} %collective-permute-done.5.refs_7_), channel_id=1, source_target_pairs={{0,1},{1,0},{2,3},{3,2},{4,17},{5,16},{6,19},{7,18},{8,9},{9,8},{1... | collective-permute-start | bytes 393224 | tf_op jit(solution)/shard_map/ppermute | solution.py:231
  40.4 1.4 %shard_map.89.part_ref = f32[2,256,256]{2,1,0:T(8,128)S(1)} custom-call(s32[5,8]{1,0:T(8,128)S(1)} %pad_add_fusion.meta, bf16[8,256,256]{2,1,0:T(8,128)(2,1)S(1)} %shard_map.88.own_ref, bf16[8,256,256]{2,1,0:T(8,128)(2,1)S(1)} %collective-permute-done.12.other_ref, bf16[2,256,256]{2,1,0:T(8,128)(2,1)S(1)} %get-tuple-element.19.refs_2_.refs_0_, ...), custom_call_target="tpu_custom_call" | custom-call | flops 536870912 | bytes 6291456 | tf_op jit(solution)/shard_map/pallas_call | solution.py:23
  42.8 3.6 %collective-permute-done.6.other_ref = bf16[256,256]{1,0:T(8,128)(2,1)S(1)} collective-permute-done((bf16[256,256]{1,0:T(8,128)(2,1)S(1)}, bf16[256,256]{1,0:T(8,128)(2,1)S(1)}, u32[]{:S(2)}, u32[]{:S(2)}) %collective-permute-start.6) | collective-permute-done | bytes 131104 | tf_op jit(solution)/shard_map/ppermute | solution.py:231
  46.6 2.7 %collective-permute-start.16 = (bf16[2,256,256]{2,1,0:T(8,128)(2,1)S(1)}, bf16[2,256,256]{2,1,0:T(8,128)(2,1)S(1)}, u32[]{:S(2)}, u32[]{:S(2)}) collective-permute-start(bf16[2,256,256]{2,1,0:T(8,128)(2,1)S(1)} %get-tuple-element.22.refs_0_), channel_id=1, source_target_pairs={{16,0},{24,8},{0,16},{8,24},{17,1},{25,9},{1,17},{9,25},{18,2},{26... | collective-permute-start | bytes 786440 | tf_op jit(solution)/shard_map/ppermute | solution.py:214
  49.3 1.6 %collective-permute-start.22 = (bf16[2,256,256]{2,1,0:T(8,128)(2,1)S(1)}, bf16[2,256,256]{2,1,0:T(8,128)(2,1)S(1)}, u32[]{:S(2)}, u32[]{:S(2)}) collective-permute-start(bf16[2,256,256]{2,1,0:T(8,128)(2,1)S(1)} %get-tuple-element.22.refs_0_), channel_id=1, source_target_pairs={{2,0},{3,1},{0,2},{1,3},{6,4},{7,5},{4,6},{5,7},{10,8},{11,9},{8,1... | collective-permute-start | bytes 786440 | tf_op jit(solution)/shard_map/ppermute | solution.py:223
  51.0 4.1 %collective-permute-done.17.refs_3_ = bf16[2,256,256]{2,1,0:T(8,128)(2,1)S(1)} collective-permute-done((bf16[2,256,256]{2,1,0:T(8,128)(2,1)S(1)}, bf16[2,256,256]{2,1,0:T(8,128)(2,1)S(1)}, u32[]{:S(2)}, u32[]{:S(2)}) %collective-permute-start.17) | collective-permute-done | bytes 262176 | tf_op jit(solution)/shard_map/ppermute | solution.py:214
  55.0 6.3 %collective-permute-done.16.refs_2_ = bf16[2,256,256]{2,1,0:T(8,128)(2,1)S(1)} collective-permute-done((bf16[2,256,256]{2,1,0:T(8,128)(2,1)S(1)}, bf16[2,256,256]{2,1,0:T(8,128)(2,1)S(1)}, u32[]{:S(2)}, u32[]{:S(2)}) %collective-permute-start.16) | collective-permute-done | bytes 262176 | tf_op jit(solution)/shard_map/ppermute | solution.py:214
  62.1 1.5 %collective-permute-done.23.refs_0_ = bf16[2,256,256]{2,1,0:T(8,128)(2,1)S(1)} collective-permute-done((bf16[2,256,256]{2,1,0:T(8,128)(2,1)S(1)}, bf16[2,256,256]{2,1,0:T(8,128)(2,1)S(1)}, u32[]{:S(2)}, u32[]{:S(2)}) %collective-permute-start.23) | collective-permute-done | bytes 262176 | tf_op jit(solution)/shard_map/ppermute | solution.py:223
  65.5 4.4 %collective-permute-start.18 = (bf16[256,256]{1,0:T(8,128)(2,1)S(1)}, bf16[256,256]{1,0:T(8,128)(2,1)S(1)}, u32[]{:S(2)}, u32[]{:S(2)}) collective-permute-start(bf16[256,256]{1,0:T(8,128)(2,1)S(1)} %get-tuple-element.23), channel_id=1, source_target_pairs={{0,0},{1,1},{2,2},{3,3},{4,16},{5,17},{6,18},{7,19},{8,8},{9,9},{1... | collective-permute-start | bytes 393224 | tf_op jit(solution)/shard_map/ppermute | solution.py:231
  69.9 1.9 %collective-permute-start.20 = (bf16[256,256]{1,0:T(8,128)(2,1)S(1)}, bf16[256,256]{1,0:T(8,128)(2,1)S(1)}, u32[]{:S(2)}, u32[]{:S(2)}) collective-permute-start(bf16[256,256]{1,0:T(8,128)(2,1)S(1)} %get-tuple-element.24), channel_id=1, source_target_pairs={{0,0},{1,1},{2,8},{3,9},{4,4},{5,5},{6,12},{7,13},{8,2},{9,3},{10,... | collective-permute-start | bytes 393224 | tf_op jit(solution)/shard_map/ppermute | solution.py:231
  71.8 3.1 %collective-permute-done.18.refs_6_ = bf16[256,256]{1,0:T(8,128)(2,1)S(1)} collective-permute-done((bf16[256,256]{1,0:T(8,128)(2,1)S(1)}, bf16[256,256]{1,0:T(8,128)(2,1)S(1)}, u32[]{:S(2)}, u32[]{:S(2)}) %collective-permute-start.18) | collective-permute-done | bytes 131104 | tf_op jit(solution)/shard_map/ppermute | solution.py:231
  74.9 1.9 %collective-permute-done.20.refs_7_ = bf16[256,256]{1,0:T(8,128)(2,1)S(1)} collective-permute-done((bf16[256,256]{1,0:T(8,128)(2,1)S(1)}, bf16[256,256]{1,0:T(8,128)(2,1)S(1)}, u32[]{:S(2)}, u32[]{:S(2)}) %collective-permute-start.20) | collective-permute-done | bytes 131104 | tf_op jit(solution)/shard_map/ppermute | solution.py:231
  76.9 2.7 %collective-permute-start.27 = (bf16[8,256,256]{2,1,0:T(8,128)(2,1)S(1)}, bf16[8,256,256]{2,1,0:T(8,128)(2,1)S(1)}, u32[]{:S(2)}, u32[]{:S(2)}) collective-permute-start(bf16[8,256,256]{2,1,0:T(8,128)(2,1)S(1)} %shard_map.93.own_ref), channel_id=1, source_target_pairs={{1,0},{0,1},{3,2},{2,3},{5,4},{4,5},{7,6},{6,7},{9,8},{8,9},{11,10... | collective-permute-start | bytes 3145736 | tf_op jit(solution)/shard_map/ppermute | solution.py:220
  79.8 2.4 %collective-permute-start.19 = (bf16[256,256]{1,0:T(8,128)(2,1)S(1)}, bf16[256,256]{1,0:T(8,128)(2,1)S(1)}, u32[]{:S(2)}, u32[]{:S(2)}) collective-permute-start(bf16[256,256]{1,0:T(8,128)(2,1)S(1)} %collective-permute-done.18.refs_6_), channel_id=1, source_target_pairs={{0,0},{1,1},{2,8},{3,9},{4,4},{5,5},{6,12},{7,13},{8,2},{9,3},{10,... | collective-permute-start | bytes 393224 | tf_op jit(solution)/shard_map/ppermute | solution.py:231
  82.3 2.3 %collective-permute-start.21 = (bf16[256,256]{1,0:T(8,128)(2,1)S(1)}, bf16[256,256]{1,0:T(8,128)(2,1)S(1)}, u32[]{:S(2)}, u32[]{:S(2)}) collective-permute-start(bf16[256,256]{1,0:T(8,128)(2,1)S(1)} %collective-permute-done.20.refs_7_), channel_id=1, source_target_pairs={{0,1},{1,0},{2,3},{3,2},{4,17},{5,16},{6,19},{7,18},{8,9},{9,8},{1... | collective-permute-start | bytes 393224 | tf_op jit(solution)/shard_map/ppermute | solution.py:231
  84.9 1.4 %shard_map.94.part_ref = f32[2,256,256]{2,1,0:T(8,128)S(1)} custom-call(s32[5,8]{1,0:T(8,128)S(1)} %pad_add_fusion.meta, bf16[8,256,256]{2,1,0:T(8,128)(2,1)S(1)} %shard_map.93.own_ref, bf16[8,256,256]{2,1,0:T(8,128)(2,1)S(1)} %collective-permute-done.27.other_ref, bf16[2,256,256]{2,1,0:T(8,128)(2,1)S(1)} %get-tuple-element.25.refs_2_.refs_0_, ...), custom_call_target="tpu_custom_call" | custom-call | flops 536870912 | bytes 6291456 | tf_op jit(solution)/shard_map/pallas_call | solution.py:23
  86.3 1.1 %collective-permute-done.19.same_ref = bf16[256,256]{1,0:T(8,128)(2,1)S(1)} collective-permute-done((bf16[256,256]{1,0:T(8,128)(2,1)S(1)}, bf16[256,256]{1,0:T(8,128)(2,1)S(1)}, u32[]{:S(2)}, u32[]{:S(2)}) %collective-permute-start.19) | collective-permute-done | bytes 131104 | tf_op jit(solution)/shard_map/ppermute | solution.py:231
  87.4 4.0 %collective-permute-done.21.other_ref = bf16[256,256]{1,0:T(8,128)(2,1)S(1)} collective-permute-done((bf16[256,256]{1,0:T(8,128)(2,1)S(1)}, bf16[256,256]{1,0:T(8,128)(2,1)S(1)}, u32[]{:S(2)}, u32[]{:S(2)}) %collective-permute-start.21) | collective-permute-done | bytes 131104 | tf_op jit(solution)/shard_map/ppermute | solution.py:231
  (65 shorter events, 13.0 us)
Async XLA Ops:
  0.0 9.1 %copy-start = (s32[2,8,8]{2,1,0:T(8,128)S(1)}, s32[2,8,8]{2,1,0:T(8,128)}, u32[]{:S(2)}) copy-start(s32[2,8,8]{2,1,0:T(8,128)} %param.12) | copy-start | bytes 1540
  1.1 17.7 %collective-permute-start.8 = (bf16[2,256,256]{2,1,0:T(8,128)(2,1)S(1)}, bf16[2,256,256]{2,1,0:T(8,128)(2,1)S(1)}, u32[]{:S(2)}, u32[]{:S(2)}) collective-permute-start(bf16[2,256,256]{2,1,0:T(8,128)(2,1)S(1)} %bitcast_convert_fusion.refs_0_), channel_id=1, source_target_pairs={{4,0},{5,1},{6,2},{7,3},{0,4},{1,5},{2,6},{3,7},{12,8},{13,9},{14,... | collective-permute-start | bytes 786440 | tf_op jit(solution)/shard_map/ppermute | solution.py:223
  3.5 15.3 %collective-permute-start.7 = (bf16[2,256,256]{2,1,0:T(8,128)(2,1)S(1)}, bf16[2,256,256]{2,1,0:T(8,128)(2,1)S(1)}, u32[]{:S(2)}, u32[]{:S(2)}) collective-permute-start(bf16[2,256,256]{2,1,0:T(8,128)(2,1)S(1)} %bitcast_convert_fusion.refs_0_), channel_id=1, source_target_pairs={{2,0},{3,1},{0,2},{1,3},{6,4},{7,5},{4,6},{5,7},{10,8},{11,9},{8,1... | collective-permute-start | bytes 786440 | tf_op jit(solution)/shard_map/ppermute | solution.py:223
  4.8 9.9 %collective-permute-start.2 = (bf16[2,256,256]{2,1,0:T(8,128)(2,1)S(1)}, bf16[2,256,256]{2,1,0:T(8,128)(2,1)S(1)}, u32[]{:S(2)}, u32[]{:S(2)}) collective-permute-start(bf16[2,256,256]{2,1,0:T(8,128)(2,1)S(1)} %bitcast_convert_fusion.refs_0_), channel_id=1, source_target_pairs={{24,0},{16,8},{8,16},{0,24},{25,1},{17,9},{9,17},{1,25},{26,2},{18... | collective-permute-start | bytes 786440 | tf_op jit(solution)/shard_map/ppermute | solution.py:214
  5.0 13.1 %collective-permute-start.1 = (bf16[2,256,256]{2,1,0:T(8,128)(2,1)S(1)}, bf16[2,256,256]{2,1,0:T(8,128)(2,1)S(1)}, u32[]{:S(2)}, u32[]{:S(2)}) collective-permute-start(bf16[2,256,256]{2,1,0:T(8,128)(2,1)S(1)} %bitcast_convert_fusion.refs_0_), channel_id=1, source_target_pairs={{16,0},{24,8},{0,16},{8,24},{17,1},{25,9},{1,17},{9,25},{18,2},{26... | collective-permute-start | bytes 786440 | tf_op jit(solution)/shard_map/ppermute | solution.py:214
  6.2 11.8 %collective-permute-start = (bf16[2,256,256]{2,1,0:T(8,128)(2,1)S(1)}, bf16[2,256,256]{2,1,0:T(8,128)(2,1)S(1)}, u32[]{:S(2)}, u32[]{:S(2)}) collective-permute-start(bf16[2,256,256]{2,1,0:T(8,128)(2,1)S(1)} %bitcast_convert_fusion.refs_0_), channel_id=1, source_target_pairs={{8,0},{0,8},{24,16},{16,24},{9,1},{1,9},{25,17},{17,25},{10,2},{2,... | collective-permute-start | bytes 786440 | tf_op jit(solution)/shard_map/ppermute | solution.py:214
  18.8 21.6 %copy-start.2 = (f32[2,1,256,256]{3,2,1,0:T(8,128)S(1)}, f32[2,1,256,256]{3,2,1,0:T(8,128)}, u32[]{:S(2)}) copy-start(f32[2,1,256,256]{3,2,1,0:T(8,128)} %param.8) | copy-start | bytes 1572868
  18.8 13.1 %collective-permute-start.9 = (bf16[2,256,256]{2,1,0:T(8,128)(2,1)S(1)}, bf16[2,256,256]{2,1,0:T(8,128)(2,1)S(1)}, u32[]{:S(2)}, u32[]{:S(2)}) collective-permute-start(bf16[2,256,256]{2,1,0:T(8,128)(2,1)S(1)} %shard_map.87.refs_2_), channel_id=1, source_target_pairs={{2,0},{3,1},{0,2},{1,3},{6,4},{7,5},{4,6},{5,7},{10,8},{11,9},{8,1... | collective-permute-start | bytes 786440 | tf_op jit(solution)/shard_map/ppermute | solution.py:223
  19.1 12.9 %collective-permute-start.11 = (bf16[2,256,256]{2,1,0:T(8,128)(2,1)S(1)}, bf16[2,256,256]{2,1,0:T(8,128)(2,1)S(1)}, u32[]{:S(2)}, u32[]{:S(2)}) collective-permute-start(bf16[2,256,256]{2,1,0:T(8,128)(2,1)S(1)} %get-tuple-element.19.refs_2_.refs_0_), channel_id=1, source_target_pairs={{16,0},{24,8},{0,16},{8,24},{17,1},{25,9},{1,17},{9,25},{18,2},{26... | collective-permute-start | bytes 786440 | tf_op jit(solution)/shard_map/ppermute | solution.py:214
  20.7 11.2 %collective-permute-start.10 = (bf16[2,256,256]{2,1,0:T(8,128)(2,1)S(1)}, bf16[2,256,256]{2,1,0:T(8,128)(2,1)S(1)}, u32[]{:S(2)}, u32[]{:S(2)}) collective-permute-start(bf16[2,256,256]{2,1,0:T(8,128)(2,1)S(1)} %get-tuple-element.19.refs_2_.refs_0_), channel_id=1, source_target_pairs={{8,0},{0,8},{24,16},{16,24},{9,1},{1,9},{25,17},{17,25},{10,2},{2,... | collective-permute-start | bytes 786440 | tf_op jit(solution)/shard_map/ppermute | solution.py:214
  21.0 10.9 %collective-permute-start.3 = (bf16[256,256]{1,0:T(8,128)(2,1)S(1)}, bf16[256,256]{1,0:T(8,128)(2,1)S(1)}, u32[]{:S(2)}, u32[]{:S(2)}) collective-permute-start(bf16[256,256]{1,0:T(8,128)(2,1)S(1)} %get-tuple-element.17), channel_id=1, source_target_pairs={{0,0},{1,1},{2,2},{3,3},{4,16},{5,17},{6,18},{7,19},{8,8},{9,9},{1... | collective-permute-start | bytes 393224 | tf_op jit(solution)/shard_map/ppermute | solution.py:231
  23.9 8.0 %collective-permute-start.5 = (bf16[256,256]{1,0:T(8,128)(2,1)S(1)}, bf16[256,256]{1,0:T(8,128)(2,1)S(1)}, u32[]{:S(2)}, u32[]{:S(2)}) collective-permute-start(bf16[256,256]{1,0:T(8,128)(2,1)S(1)} %get-tuple-element.18), channel_id=1, source_target_pairs={{0,0},{1,1},{2,8},{3,9},{4,4},{5,5},{6,12},{7,13},{8,2},{9,3},{10,... | collective-permute-start | bytes 393224 | tf_op jit(solution)/shard_map/ppermute | solution.py:231
  32.0 8.4 %collective-permute-start.12 = (bf16[8,256,256]{2,1,0:T(8,128)(2,1)S(1)}, bf16[8,256,256]{2,1,0:T(8,128)(2,1)S(1)}, u32[]{:S(2)}, u32[]{:S(2)}) collective-permute-start(bf16[8,256,256]{2,1,0:T(8,128)(2,1)S(1)} %shard_map.88.own_ref), channel_id=1, source_target_pairs={{1,0},{0,1},{3,2},{2,3},{5,4},{4,5},{7,6},{6,7},{9,8},{8,9},{11,10... | collective-permute-start | bytes 3145736 | tf_op jit(solution)/shard_map/ppermute | solution.py:220
  33.6 6.7 %collective-permute-start.13 = (bf16[1,256,256]{2,1,0:T(8,128)(2,1)S(1)}, bf16[1,256,256]{2,1,0:T(8,128)(2,1)S(1)}, u32[]{:S(2)}, u32[]{:S(2)}) collective-permute-start(bf16[1,256,256]{2,1,0:T(8,128)(2,1)S(1)} %slice.16), channel_id=1, source_target_pairs={{8,0},{0,8},{24,16},{16,24},{9,1},{1,9},{25,17},{17,25},{10,2},{2,... | collective-permute-start | bytes 393224 | tf_op jit(solution)/shard_map/ppermute | solution.py:214
  34.9 5.5 %collective-permute-start.14 = (bf16[1,256,256]{2,1,0:T(8,128)(2,1)S(1)}, bf16[1,256,256]{2,1,0:T(8,128)(2,1)S(1)}, u32[]{:S(2)}, u32[]{:S(2)}) collective-permute-start(bf16[1,256,256]{2,1,0:T(8,128)(2,1)S(1)} %slice.17), channel_id=1, source_target_pairs={{16,0},{24,8},{0,16},{8,24},{17,1},{25,9},{1,17},{9,25},{18,2},{26... | collective-permute-start | bytes 393224 | tf_op jit(solution)/shard_map/ppermute | solution.py:214
  35.2 7.6 %collective-permute-start.4 = (bf16[256,256]{1,0:T(8,128)(2,1)S(1)}, bf16[256,256]{1,0:T(8,128)(2,1)S(1)}, u32[]{:S(2)}, u32[]{:S(2)}) collective-permute-start(bf16[256,256]{1,0:T(8,128)(2,1)S(1)} %collective-permute-done.3.refs_6_), channel_id=1, source_target_pairs={{0,0},{1,1},{2,8},{3,9},{4,4},{5,5},{6,12},{7,13},{8,2},{9,3},{10,... | collective-permute-start | bytes 393224 | tf_op jit(solution)/shard_map/ppermute | solution.py:231
  37.1 9.2 %collective-permute-start.6 = (bf16[256,256]{1,0:T(8,128)(2,1)S(1)}, bf16[256,256]{1,0:T(8,128)(2,1)S(1)}, u32[]{:S(2)}, u32[]{:S(2)}) collective-permute-start(bf16[256,256]{1,0:T(8,128)(2,1)S(1)} %collective-permute-done.5.refs_7_), channel_id=1, source_target_pairs={{0,1},{1,0},{2,3},{3,2},{4,17},{5,16},{6,19},{7,18},{8,9},{9,8},{1... | collective-permute-start | bytes 393224 | tf_op jit(solution)/shard_map/ppermute | solution.py:231
  46.5 8.5 %collective-permute-start.17 = (bf16[2,256,256]{2,1,0:T(8,128)(2,1)S(1)}, bf16[2,256,256]{2,1,0:T(8,128)(2,1)S(1)}, u32[]{:S(2)}, u32[]{:S(2)}) collective-permute-start(bf16[2,256,256]{2,1,0:T(8,128)(2,1)S(1)} %get-tuple-element.22.refs_0_), channel_id=1, source_target_pairs={{24,0},{16,8},{8,16},{0,24},{25,1},{17,9},{9,17},{1,25},{26,2},{18... | collective-permute-start | bytes 786440 | tf_op jit(solution)/shard_map/ppermute | solution.py:214
  46.6 14.7 %collective-permute-start.16 = (bf16[2,256,256]{2,1,0:T(8,128)(2,1)S(1)}, bf16[2,256,256]{2,1,0:T(8,128)(2,1)S(1)}, u32[]{:S(2)}, u32[]{:S(2)}) collective-permute-start(bf16[2,256,256]{2,1,0:T(8,128)(2,1)S(1)} %get-tuple-element.22.refs_0_), channel_id=1, source_target_pairs={{16,0},{24,8},{0,16},{8,24},{17,1},{25,9},{1,17},{9,25},{18,2},{26... | collective-permute-start | bytes 786440 | tf_op jit(solution)/shard_map/ppermute | solution.py:214
  49.3 12.0 %collective-permute-start.15 = (bf16[2,256,256]{2,1,0:T(8,128)(2,1)S(1)}, bf16[2,256,256]{2,1,0:T(8,128)(2,1)S(1)}, u32[]{:S(2)}, u32[]{:S(2)}) collective-permute-start(bf16[2,256,256]{2,1,0:T(8,128)(2,1)S(1)} %get-tuple-element.22.refs_0_), channel_id=1, source_target_pairs={{8,0},{0,8},{24,16},{16,24},{9,1},{1,9},{25,17},{17,25},{10,2},{2,... | collective-permute-start | bytes 786440 | tf_op jit(solution)/shard_map/ppermute | solution.py:214
  49.3 14.3 %collective-permute-start.23 = (bf16[2,256,256]{2,1,0:T(8,128)(2,1)S(1)}, bf16[2,256,256]{2,1,0:T(8,128)(2,1)S(1)}, u32[]{:S(2)}, u32[]{:S(2)}) collective-permute-start(bf16[2,256,256]{2,1,0:T(8,128)(2,1)S(1)} %get-tuple-element.22.refs_0_), channel_id=1, source_target_pairs={{4,0},{5,1},{6,2},{7,3},{0,4},{1,5},{2,6},{3,7},{12,8},{13,9},{14,... | collective-permute-start | bytes 786440 | tf_op jit(solution)/shard_map/ppermute | solution.py:223
  49.3 14.3 %collective-permute-start.22 = (bf16[2,256,256]{2,1,0:T(8,128)(2,1)S(1)}, bf16[2,256,256]{2,1,0:T(8,128)(2,1)S(1)}, u32[]{:S(2)}, u32[]{:S(2)}) collective-permute-start(bf16[2,256,256]{2,1,0:T(8,128)(2,1)S(1)} %get-tuple-element.22.refs_0_), channel_id=1, source_target_pairs={{2,0},{3,1},{0,2},{1,3},{6,4},{7,5},{4,6},{5,7},{10,8},{11,9},{8,1... | collective-permute-start | bytes 786440 | tf_op jit(solution)/shard_map/ppermute | solution.py:223
  63.6 13.2 %collective-permute-start.24 = (bf16[2,256,256]{2,1,0:T(8,128)(2,1)S(1)}, bf16[2,256,256]{2,1,0:T(8,128)(2,1)S(1)}, u32[]{:S(2)}, u32[]{:S(2)}) collective-permute-start(bf16[2,256,256]{2,1,0:T(8,128)(2,1)S(1)} %shard_map.92.refs_2_), channel_id=1, source_target_pairs={{2,0},{3,1},{0,2},{1,3},{6,4},{7,5},{4,6},{5,7},{10,8},{11,9},{8,1... | collective-permute-start | bytes 786440 | tf_op jit(solution)/shard_map/ppermute | solution.py:223
  63.6 13.2 %collective-permute-start.26 = (bf16[2,256,256]{2,1,0:T(8,128)(2,1)S(1)}, bf16[2,256,256]{2,1,0:T(8,128)(2,1)S(1)}, u32[]{:S(2)}, u32[]{:S(2)}) collective-permute-start(bf16[2,256,256]{2,1,0:T(8,128)(2,1)S(1)} %get-tuple-element.25.refs_2_.refs_0_), channel_id=1, source_target_pairs={{16,0},{24,8},{0,16},{8,24},{17,1},{25,9},{1,17},{9,25},{18,2},{26... | collective-permute-start | bytes 786440 | tf_op jit(solution)/shard_map/ppermute | solution.py:214
  64.5 12.3 %collective-permute-start.25 = (bf16[2,256,256]{2,1,0:T(8,128)(2,1)S(1)}, bf16[2,256,256]{2,1,0:T(8,128)(2,1)S(1)}, u32[]{:S(2)}, u32[]{:S(2)}) collective-permute-start(bf16[2,256,256]{2,1,0:T(8,128)(2,1)S(1)} %get-tuple-element.25.refs_2_.refs_0_), channel_id=1, source_target_pairs={{8,0},{0,8},{24,16},{16,24},{9,1},{1,9},{25,17},{17,25},{10,2},{2,... | collective-permute-start | bytes 786440 | tf_op jit(solution)/shard_map/ppermute | solution.py:214
  65.5 9.4 %collective-permute-start.18 = (bf16[256,256]{1,0:T(8,128)(2,1)S(1)}, bf16[256,256]{1,0:T(8,128)(2,1)S(1)}, u32[]{:S(2)}, u32[]{:S(2)}) collective-permute-start(bf16[256,256]{1,0:T(8,128)(2,1)S(1)} %get-tuple-element.23), channel_id=1, source_target_pairs={{0,0},{1,1},{2,2},{3,3},{4,16},{5,17},{6,18},{7,19},{8,8},{9,9},{1... | collective-permute-start | bytes 393224 | tf_op jit(solution)/shard_map/ppermute | solution.py:231
  69.9 6.9 %collective-permute-start.20 = (bf16[256,256]{1,0:T(8,128)(2,1)S(1)}, bf16[256,256]{1,0:T(8,128)(2,1)S(1)}, u32[]{:S(2)}, u32[]{:S(2)}) collective-permute-start(bf16[256,256]{1,0:T(8,128)(2,1)S(1)} %get-tuple-element.24), channel_id=1, source_target_pairs={{0,0},{1,1},{2,8},{3,9},{4,4},{5,5},{6,12},{7,13},{8,2},{9,3},{10,... | collective-permute-start | bytes 393224 | tf_op jit(solution)/shard_map/ppermute | solution.py:231
  76.9 8.0 %collective-permute-start.27 = (bf16[8,256,256]{2,1,0:T(8,128)(2,1)S(1)}, bf16[8,256,256]{2,1,0:T(8,128)(2,1)S(1)}, u32[]{:S(2)}, u32[]{:S(2)}) collective-permute-start(bf16[8,256,256]{2,1,0:T(8,128)(2,1)S(1)} %shard_map.93.own_ref), channel_id=1, source_target_pairs={{1,0},{0,1},{3,2},{2,3},{5,4},{4,5},{7,6},{6,7},{9,8},{8,9},{11,10... | collective-permute-start | bytes 3145736 | tf_op jit(solution)/shard_map/ppermute | solution.py:220
  79.6 5.2 %collective-permute-start.28 = (bf16[1,256,256]{2,1,0:T(8,128)(2,1)S(1)}, bf16[1,256,256]{2,1,0:T(8,128)(2,1)S(1)}, u32[]{:S(2)}, u32[]{:S(2)}) collective-permute-start(bf16[1,256,256]{2,1,0:T(8,128)(2,1)S(1)} %slice.18), channel_id=1, source_target_pairs={{8,0},{0,8},{24,16},{16,24},{9,1},{1,9},{25,17},{17,25},{10,2},{2,... | collective-permute-start | bytes 393224 | tf_op jit(solution)/shard_map/ppermute | solution.py:214
  79.7 5.2 %collective-permute-start.29 = (bf16[1,256,256]{2,1,0:T(8,128)(2,1)S(1)}, bf16[1,256,256]{2,1,0:T(8,128)(2,1)S(1)}, u32[]{:S(2)}, u32[]{:S(2)}) collective-permute-start(bf16[1,256,256]{2,1,0:T(8,128)(2,1)S(1)} %slice.19), channel_id=1, source_target_pairs={{16,0},{24,8},{0,16},{8,24},{17,1},{25,9},{1,17},{9,25},{18,2},{26... | collective-permute-start | bytes 393224 | tf_op jit(solution)/shard_map/ppermute | solution.py:214
  79.8 7.6 %collective-permute-start.19 = (bf16[256,256]{1,0:T(8,128)(2,1)S(1)}, bf16[256,256]{1,0:T(8,128)(2,1)S(1)}, u32[]{:S(2)}, u32[]{:S(2)}) collective-permute-start(bf16[256,256]{1,0:T(8,128)(2,1)S(1)} %collective-permute-done.18.refs_6_), channel_id=1, source_target_pairs={{0,0},{1,1},{2,8},{3,9},{4,4},{5,5},{6,12},{7,13},{8,2},{9,3},{10,... | collective-permute-start | bytes 393224 | tf_op jit(solution)/shard_map/ppermute | solution.py:231
  82.3 9.1 %collective-permute-start.21 = (bf16[256,256]{1,0:T(8,128)(2,1)S(1)}, bf16[256,256]{1,0:T(8,128)(2,1)S(1)}, u32[]{:S(2)}, u32[]{:S(2)}) collective-permute-start(bf16[256,256]{1,0:T(8,128)(2,1)S(1)} %collective-permute-done.20.refs_7_), channel_id=1, source_target_pairs={{0,1},{1,0},{2,3},{3,2},{4,17},{5,16},{6,19},{7,18},{8,9},{9,8},{1... | collective-permute-start | bytes 393224 | tf_op jit(solution)/shard_map/ppermute | solution.py:231
  (3 other events, 2.9 us)

commit v8 on v7

--- a/solution.py
+++ b/solution.py
@@ -273,7 +273,7 @@
             column[step] = tied(column[step], column[1], coupled)
             column[step + 1] = from_chip(column[step], 1)
         column = [column[step] for step in range(halves)]
-        own = whole_column(column, [c_pieces[1], c_pieces[2], same, other])
+        own = whole_column(column, [*far[1::2], c_pieces[2], same, other])
         same, other = crossing(same, last_bits), crossing(other, high_parts, 1)
         part = first_update(rows, meta, own, swapped(own), c_pieces, state, coulomb_own, inverse)
         state, *halves_out = second_update(same, other, part, inverse, sweep_index < ITERS - 1)

time: 93.6 us -> 93.7 us (level)
  waiting for transfers between devices: 35.2 us -> 36.7 us
    ppermute x14, waiting for transfers between devices: 14.1 us -> 15.8 us  [from_row(): return lax.ppermute(x, 'row', [(r ^ step, r) for r in range(rows)])]
    ppermute x8, waiting for transfers between devices: 19.5 us -> 18.2 us  [crossing(): return lax.ppermute(x, ('row', 'col'), pairs)]
    ppermute x6, waiting for transfers between devices: 1.51 us -> 2.67 us  [from_chip(): return lax.ppermute(x, 'col', [(c ^ 2 * step, c) for c in range(cols)])]
    ppermute x14, starting transfers between devices: 11 us -> 9.9 us  [from_row(): return lax.ppermute(x, 'row', [(r ^ step, r) for r in range(rows)])]
    ppermute x8, starting transfers between devices: 22.2 us -> 23.2 us  [crossing(): return lax.ppermute(x, ('row', 'col'), pairs)]
  transfers between devices with their start and end apart: 30 -> 30, of which waited for: 13 -> 15; matrix products, arithmetic and copies ran while one was open for 4% -> 4% of each run, Pallas kernels for 6% -> 5%
where the time goes in v8:
time: 93.7 us; the launch traced here: 93.2 us
  starting transfers between devices  42.4 us (45%)
  waiting for transfers between devices  36.7 us (39%)
  Pallas kernels  6.37 us (7%)
  local copies, waits for them, and re-layouts  4.64 us (5%)
  other arithmetic  2.77 us (3%)
    ppermute x8, starting transfers between devices, crossing(): return lax.ppermute(x, ('row', 'col'), pairs)  23.2 us
    ppermute x8, waiting for transfers between devices, crossing(): return lax.ppermute(x, ('row', 'col'), pairs)  18.2 us
    ppermute x14, waiting for transfers between devices, from_row(): return lax.ppermute(x, 'row', [(r ^ step, r) for r in range(rows)])  15.8 us
    ppermute x14, starting transfers between devices, from_row(): return lax.ppermute(x, 'row', [(r ^ step, r) for r in range(rows)])  9.9 us
    pallas_call x9, Pallas kernels, call(): pl.pallas_call(body, out_shape=out_shape, in_specs=in_specs, out_specs=VM...  6.37 us
    ppermute x6, starting transfers between devices, from_chip(): return lax.ppermute(x, 'col', [(c ^ 2 * step, c) for c in range(cols)])  5.33 us
    ppermute x2, starting transfers between devices, swapped(): return lax.ppermute(x, 'col', [(c ^ 1, c) for c in range(cols)])  4.05 us
    unnamed x10, local copies, waits for them, and re-layouts  2.93 us
  transfers between devices with their start and end apart: 30, of which 15 were waited for; matrix products, arithmetic and copies ran while one was open for 4% of the time, Pallas kernels for 5%

profile of v8, /device:TPU:7, one launch (start us, length us, event | category | flops | bytes accessed | tf_op | source)
XLA Modules:
  0.0 93.2 jit_solution(8149553903880584360)
XLA Ops:
  0.0 1.1 %bitcast_convert_fusion.refs_0_ = bf16[2,256,256]{2,1,0:T(8,128)(2,1)S(1)} fusion(f32[2,1,256,256]{3,2,1,0:T(8,128)} %param.8), kind=kLoop, calls=%fused_computation.12 | loop fusion | flops 131072 | bytes 786432 | tf_op jit(solution)/shard_map/convert_element_type | solution.py:240
  1.1 2.4 %collective-permute-start.8 = (bf16[2,256,256]{2,1,0:T(8,128)(2,1)S(1)}, bf16[2,256,256]{2,1,0:T(8,128)(2,1)S(1)}, u32[]{:S(2)}, u32[]{:S(2)}) collective-permute-start(bf16[2,256,256]{2,1,0:T(8,128)(2,1)S(1)} %bitcast_convert_fusion.refs_0_), channel_id=1, source_target_pairs={{4,0},{5,1},{6,2},{7,3},{0,4},{1,5},{2,6},{3,7},{12,8},{13,9},{14,... | collective-permute-start | bytes 786440 | tf_op jit(solution)/shard_map/ppermute | solution.py:223
  3.5 1.3 %collective-permute-start.7 = (bf16[2,256,256]{2,1,0:T(8,128)(2,1)S(1)}, bf16[2,256,256]{2,1,0:T(8,128)(2,1)S(1)}, u32[]{:S(2)}, u32[]{:S(2)}) collective-permute-start(bf16[2,256,256]{2,1,0:T(8,128)(2,1)S(1)} %bitcast_convert_fusion.refs_0_), channel_id=1, source_target_pairs={{2,0},{3,1},{0,2},{1,3},{6,4},{7,5},{4,6},{5,7},{10,8},{11,9},{8,1... | collective-permute-start | bytes 786440 | tf_op jit(solution)/shard_map/ppermute | solution.py:223
  5.0 1.2 %collective-permute-start.1 = (bf16[2,256,256]{2,1,0:T(8,128)(2,1)S(1)}, bf16[2,256,256]{2,1,0:T(8,128)(2,1)S(1)}, u32[]{:S(2)}, u32[]{:S(2)}) collective-permute-start(bf16[2,256,256]{2,1,0:T(8,128)(2,1)S(1)} %bitcast_convert_fusion.refs_0_), channel_id=1, source_target_pairs={{16,0},{24,8},{0,16},{8,24},{17,1},{25,9},{1,17},{9,25},{18,2},{26... | collective-permute-start | bytes 786440 | tf_op jit(solution)/shard_map/ppermute | solution.py:214
  6.2 1.2 %collective-permute-start = (bf16[2,256,256]{2,1,0:T(8,128)(2,1)S(1)}, bf16[2,256,256]{2,1,0:T(8,128)(2,1)S(1)}, u32[]{:S(2)}, u32[]{:S(2)}) collective-permute-start(bf16[2,256,256]{2,1,0:T(8,128)(2,1)S(1)} %bitcast_convert_fusion.refs_0_), channel_id=1, source_target_pairs={{8,0},{0,8},{24,16},{16,24},{9,1},{1,9},{25,17},{17,25},{10,2},{2,... | collective-permute-start | bytes 786440 | tf_op jit(solution)/shard_map/ppermute | solution.py:214
  10.8 1.6 %copy-done.1 = bf16[2,8,256,256]{3,2,1,0:T(8,128)(2,1)S(1)} copy-done((bf16[2,8,256,256]{3,2,1,0:T(8,128)(2,1)S(1)}, bf16[2,8,256,256]{3,2,1,0:T(8,128)(2,1)}, u32[]{:S(2)}) %copy-start.1) | copy-done | bytes 2097176
  14.7 3.3 %collective-permute-done.1.refs_2_ = bf16[2,256,256]{2,1,0:T(8,128)(2,1)S(1)} collective-permute-done((bf16[2,256,256]{2,1,0:T(8,128)(2,1)S(1)}, bf16[2,256,256]{2,1,0:T(8,128)(2,1)S(1)}, u32[]{:S(2)}, u32[]{:S(2)}) %collective-permute-start.1) | collective-permute-done | bytes 262176 | tf_op jit(solution)/shard_map/ppermute | solution.py:214
  18.8 1.8 %collective-permute-start.10 = (bf16[2,256,256]{2,1,0:T(8,128)(2,1)S(1)}, bf16[2,256,256]{2,1,0:T(8,128)(2,1)S(1)}, u32[]{:S(2)}, u32[]{:S(2)}) collective-permute-start(bf16[2,256,256]{2,1,0:T(8,128)(2,1)S(1)} %get-tuple-element.19.refs_2_.refs_0_), channel_id=1, source_target_pairs={{8,0},{0,8},{24,16},{16,24},{9,1},{1,9},{25,17},{17,25},{10,2},{2,... | collective-permute-start | bytes 786440 | tf_op jit(solution)/shard_map/ppermute | solution.py:214
  21.0 2.9 %collective-permute-start.3 = (bf16[256,256]{1,0:T(8,128)(2,1)S(1)}, bf16[256,256]{1,0:T(8,128)(2,1)S(1)}, u32[]{:S(2)}, u32[]{:S(2)}) collective-permute-start(bf16[256,256]{1,0:T(8,128)(2,1)S(1)} %get-tuple-element.17), channel_id=1, source_target_pairs={{0,0},{1,1},{2,2},{3,3},{4,16},{5,17},{6,18},{7,19},{8,8},{9,9},{1... | collective-permute-start | bytes 393224 | tf_op jit(solution)/shard_map/ppermute | solution.py:231
  23.9 3.1 %collective-permute-start.5 = (bf16[256,256]{1,0:T(8,128)(2,1)S(1)}, bf16[256,256]{1,0:T(8,128)(2,1)S(1)}, u32[]{:S(2)}, u32[]{:S(2)}) collective-permute-start(bf16[256,256]{1,0:T(8,128)(2,1)S(1)} %get-tuple-element.18), channel_id=1, source_target_pairs={{0,0},{1,1},{2,8},{3,9},{4,4},{5,5},{6,12},{7,13},{8,2},{9,3},{10,... | collective-permute-start | bytes 393224 | tf_op jit(solution)/shard_map/ppermute | solution.py:231
  27.9 2.3 %collective-permute-done.3.refs_6_ = bf16[256,256]{1,0:T(8,128)(2,1)S(1)} collective-permute-done((bf16[256,256]{1,0:T(8,128)(2,1)S(1)}, bf16[256,256]{1,0:T(8,128)(2,1)S(1)}, u32[]{:S(2)}, u32[]{:S(2)}) %collective-permute-start.3) | collective-permute-done | bytes 131104 | tf_op jit(solution)/shard_map/ppermute | solution.py:231
  30.2 1.0 %collective-permute-done.5.refs_7_ = bf16[256,256]{1,0:T(8,128)(2,1)S(1)} collective-permute-done((bf16[256,256]{1,0:T(8,128)(2,1)S(1)}, bf16[256,256]{1,0:T(8,128)(2,1)S(1)}, u32[]{:S(2)}, u32[]{:S(2)}) %collective-permute-start.5) | collective-permute-done | bytes 131104 | tf_op jit(solution)/shard_map/ppermute | solution.py:231
  31.3 2.1 %collective-permute-done.11.refs_4_ = bf16[1,256,256]{2,1,0:T(8,128)(2,1)S(1)} collective-permute-done((bf16[1,256,256]{2,1,0:T(8,128)(2,1)S(1)}, bf16[1,256,256]{2,1,0:T(8,128)(2,1)S(1)}, u32[]{:S(2)}, u32[]{:S(2)}) %collective-permute-start.11) | collective-permute-done | bytes 131104 | tf_op jit(solution)/shard_map/ppermute | solution.py:214
  33.5 1.8 %collective-permute-start.13 = (bf16[8,256,256]{2,1,0:T(8,128)(2,1)S(1)}, bf16[8,256,256]{2,1,0:T(8,128)(2,1)S(1)}, u32[]{:S(2)}, u32[]{:S(2)}) collective-permute-start(bf16[8,256,256]{2,1,0:T(8,128)(2,1)S(1)} %shard_map.88.own_ref), channel_id=1, source_target_pairs={{1,0},{0,1},{3,2},{2,3},{5,4},{4,5},{7,6},{6,7},{9,8},{8,9},{11,10... | collective-permute-start | bytes 3145736 | tf_op jit(solution)/shard_map/ppermute | solution.py:220
  35.7 4.0 %collective-permute-start.4 = (bf16[256,256]{1,0:T(8,128)(2,1)S(1)}, bf16[256,256]{1,0:T(8,128)(2,1)S(1)}, u32[]{:S(2)}, u32[]{:S(2)}) collective-permute-start(bf16[256,256]{1,0:T(8,128)(2,1)S(1)} %collective-permute-done.3.refs_6_), channel_id=1, source_target_pairs={{0,0},{1,1},{2,8},{3,9},{4,4},{5,5},{6,12},{7,13},{8,2},{9,3},{10,... | collective-permute-start | bytes 393224 | tf_op jit(solution)/shard_map/ppermute | solution.py:231
  40.4 1.4 %shard_map.89.part_ref = f32[2,256,256]{2,1,0:T(8,128)S(1)} custom-call(s32[5,8]{1,0:T(8,128)S(1)} %pad_add_fusion.meta, bf16[8,256,256]{2,1,0:T(8,128)(2,1)S(1)} %shard_map.88.own_ref, bf16[8,256,256]{2,1,0:T(8,128)(2,1)S(1)} %collective-permute-done.13.other_ref, bf16[2,256,256]{2,1,0:T(8,128)(2,1)S(1)} %get-tuple-element.19.refs_2_.refs_0_, ...), custom_call_target="tpu_custom_call" | custom-call | flops 536870912 | bytes 6291456 | tf_op jit(solution)/shard_map/pallas_call | solution.py:23
  41.8 1.4 %collective-permute-done.4.same_ref = bf16[256,256]{1,0:T(8,128)(2,1)S(1)} collective-permute-done((bf16[256,256]{1,0:T(8,128)(2,1)S(1)}, bf16[256,256]{1,0:T(8,128)(2,1)S(1)}, u32[]{:S(2)}, u32[]{:S(2)}) %collective-permute-start.4) | collective-permute-done | bytes 131104 | tf_op jit(solution)/shard_map/ppermute | solution.py:231
  43.2 4.2 %collective-permute-done.6.other_ref = bf16[256,256]{1,0:T(8,128)(2,1)S(1)} collective-permute-done((bf16[256,256]{1,0:T(8,128)(2,1)S(1)}, bf16[256,256]{1,0:T(8,128)(2,1)S(1)}, u32[]{:S(2)}, u32[]{:S(2)}) %collective-permute-start.6) | collective-permute-done | bytes 131104 | tf_op jit(solution)/shard_map/ppermute | solution.py:231
  47.7 2.6 %collective-permute-start.15 = (bf16[2,256,256]{2,1,0:T(8,128)(2,1)S(1)}, bf16[2,256,256]{2,1,0:T(8,128)(2,1)S(1)}, u32[]{:S(2)}, u32[]{:S(2)}) collective-permute-start(bf16[2,256,256]{2,1,0:T(8,128)(2,1)S(1)} %get-tuple-element.22.refs_0_), channel_id=1, source_target_pairs={{8,0},{0,8},{24,16},{16,24},{9,1},{1,9},{25,17},{17,25},{10,2},{2,... | collective-permute-start | bytes 786440 | tf_op jit(solution)/shard_map/ppermute | solution.py:214
  51.8 4.3 %collective-permute-done.17.refs_3_ = bf16[2,256,256]{2,1,0:T(8,128)(2,1)S(1)} collective-permute-done((bf16[2,256,256]{2,1,0:T(8,128)(2,1)S(1)}, bf16[2,256,256]{2,1,0:T(8,128)(2,1)S(1)}, u32[]{:S(2)}, u32[]{:S(2)}) %collective-permute-start.17) | collective-permute-done | bytes 262176 | tf_op jit(solution)/shard_map/ppermute | solution.py:214
  56.1 4.8 %collective-permute-done.16.refs_2_ = bf16[2,256,256]{2,1,0:T(8,128)(2,1)S(1)} collective-permute-done((bf16[2,256,256]{2,1,0:T(8,128)(2,1)S(1)}, bf16[2,256,256]{2,1,0:T(8,128)(2,1)S(1)}, u32[]{:S(2)}, u32[]{:S(2)}) %collective-permute-start.16) | collective-permute-done | bytes 262176 | tf_op jit(solution)/shard_map/ppermute | solution.py:214
  61.9 2.7 %collective-permute-done.23.refs_0_ = bf16[2,256,256]{2,1,0:T(8,128)(2,1)S(1)} collective-permute-done((bf16[2,256,256]{2,1,0:T(8,128)(2,1)S(1)}, bf16[2,256,256]{2,1,0:T(8,128)(2,1)S(1)}, u32[]{:S(2)}, u32[]{:S(2)}) %collective-permute-start.23) | collective-permute-done | bytes 262176 | tf_op jit(solution)/shard_map/ppermute | solution.py:223
  65.4 3.6 %collective-permute-start.18 = (bf16[256,256]{1,0:T(8,128)(2,1)S(1)}, bf16[256,256]{1,0:T(8,128)(2,1)S(1)}, u32[]{:S(2)}, u32[]{:S(2)}) collective-permute-start(bf16[256,256]{1,0:T(8,128)(2,1)S(1)} %get-tuple-element.23), channel_id=1, source_target_pairs={{0,0},{1,1},{2,2},{3,3},{4,16},{5,17},{6,18},{7,19},{8,8},{9,9},{1... | collective-permute-start | bytes 393224 | tf_op jit(solution)/shard_map/ppermute | solution.py:231
  69.0 3.3 %collective-permute-start.20 = (bf16[256,256]{1,0:T(8,128)(2,1)S(1)}, bf16[256,256]{1,0:T(8,128)(2,1)S(1)}, u32[]{:S(2)}, u32[]{:S(2)}) collective-permute-start(bf16[256,256]{1,0:T(8,128)(2,1)S(1)} %get-tuple-element.24), channel_id=1, source_target_pairs={{0,0},{1,1},{2,8},{3,9},{4,4},{5,5},{6,12},{7,13},{8,2},{9,3},{10,... | collective-permute-start | bytes 393224 | tf_op jit(solution)/shard_map/ppermute | solution.py:231
  72.4 2.3 %collective-permute-done.18.refs_6_ = bf16[256,256]{1,0:T(8,128)(2,1)S(1)} collective-permute-done((bf16[256,256]{1,0:T(8,128)(2,1)S(1)}, bf16[256,256]{1,0:T(8,128)(2,1)S(1)}, u32[]{:S(2)}, u32[]{:S(2)}) %collective-permute-start.18) | collective-permute-done | bytes 131104 | tf_op jit(solution)/shard_map/ppermute | solution.py:231
  74.7 1.2 %collective-permute-done.20.refs_7_ = bf16[256,256]{1,0:T(8,128)(2,1)S(1)} collective-permute-done((bf16[256,256]{1,0:T(8,128)(2,1)S(1)}, bf16[256,256]{1,0:T(8,128)(2,1)S(1)}, u32[]{:S(2)}, u32[]{:S(2)}) %collective-permute-start.20) | collective-permute-done | bytes 131104 | tf_op jit(solution)/shard_map/ppermute | solution.py:231
  75.9 1.1 %collective-permute-done.26.refs_4_ = bf16[1,256,256]{2,1,0:T(8,128)(2,1)S(1)} collective-permute-done((bf16[1,256,256]{2,1,0:T(8,128)(2,1)S(1)}, bf16[1,256,256]{2,1,0:T(8,128)(2,1)S(1)}, u32[]{:S(2)}, u32[]{:S(2)}) %collective-permute-start.26) | collective-permute-done | bytes 131104 | tf_op jit(solution)/shard_map/ppermute | solution.py:214
  77.1 2.3 %collective-permute-start.28 = (bf16[8,256,256]{2,1,0:T(8,128)(2,1)S(1)}, bf16[8,256,256]{2,1,0:T(8,128)(2,1)S(1)}, u32[]{:S(2)}, u32[]{:S(2)}) collective-permute-start(bf16[8,256,256]{2,1,0:T(8,128)(2,1)S(1)} %shard_map.93.own_ref), channel_id=1, source_target_pairs={{1,0},{0,1},{3,2},{2,3},{5,4},{4,5},{7,6},{6,7},{9,8},{8,9},{11,10... | collective-permute-start | bytes 3145736 | tf_op jit(solution)/shard_map/ppermute | solution.py:220
  79.5 4.3 %collective-permute-start.19 = (bf16[256,256]{1,0:T(8,128)(2,1)S(1)}, bf16[256,256]{1,0:T(8,128)(2,1)S(1)}, u32[]{:S(2)}, u32[]{:S(2)}) collective-permute-start(bf16[256,256]{1,0:T(8,128)(2,1)S(1)} %collective-permute-done.18.refs_6_), channel_id=1, source_target_pairs={{0,0},{1,1},{2,8},{3,9},{4,4},{5,5},{6,12},{7,13},{8,2},{9,3},{10,... | collective-permute-start | bytes 393224 | tf_op jit(solution)/shard_map/ppermute | solution.py:231
  83.7 1.4 %collective-permute-start.21 = (bf16[256,256]{1,0:T(8,128)(2,1)S(1)}, bf16[256,256]{1,0:T(8,128)(2,1)S(1)}, u32[]{:S(2)}, u32[]{:S(2)}) collective-permute-start(bf16[256,256]{1,0:T(8,128)(2,1)S(1)} %collective-permute-done.20.refs_7_), channel_id=1, source_target_pairs={{0,1},{1,0},{2,3},{3,2},{4,17},{5,16},{6,19},{7,18},{8,9},{9,8},{1... | collective-permute-start | bytes 393224 | tf_op jit(solution)/shard_map/ppermute | solution.py:231
  85.1 1.4 %shard_map.94.part_ref = f32[2,256,256]{2,1,0:T(8,128)S(1)} custom-call(s32[5,8]{1,0:T(8,128)S(1)} %pad_add_fusion.meta, bf16[8,256,256]{2,1,0:T(8,128)(2,1)S(1)} %shard_map.93.own_ref, bf16[8,256,256]{2,1,0:T(8,128)(2,1)S(1)} %collective-permute-done.28.other_ref, bf16[2,256,256]{2,1,0:T(8,128)(2,1)S(1)} %get-tuple-element.25.refs_2_.refs_0_, ...), custom_call_target="tpu_custom_call" | custom-call | flops 536870912 | bytes 6291456 | tf_op jit(solution)/shard_map/pallas_call | solution.py:23
  87.3 5.0 %collective-permute-done.21.other_ref = bf16[256,256]{1,0:T(8,128)(2,1)S(1)} collective-permute-done((bf16[256,256]{1,0:T(8,128)(2,1)S(1)}, bf16[256,256]{1,0:T(8,128)(2,1)S(1)}, u32[]{:S(2)}, u32[]{:S(2)}) %collective-permute-start.21) | collective-permute-done | bytes 131104 | tf_op jit(solution)/shard_map/ppermute | solution.py:231
  (65 shorter events, 14.8 us)
Async XLA Ops:
  0.0 9.1 %copy-start = (s32[2,8,8]{2,1,0:T(8,128)S(1)}, s32[2,8,8]{2,1,0:T(8,128)}, u32[]{:S(2)}) copy-start(s32[2,8,8]{2,1,0:T(8,128)} %param.12) | copy-start | bytes 1540
  1.1 19.5 %collective-permute-start.8 = (bf16[2,256,256]{2,1,0:T(8,128)(2,1)S(1)}, bf16[2,256,256]{2,1,0:T(8,128)(2,1)S(1)}, u32[]{:S(2)}, u32[]{:S(2)}) collective-permute-start(bf16[2,256,256]{2,1,0:T(8,128)(2,1)S(1)} %bitcast_convert_fusion.refs_0_), channel_id=1, source_target_pairs={{4,0},{5,1},{6,2},{7,3},{0,4},{1,5},{2,6},{3,7},{12,8},{13,9},{14,... | collective-permute-start | bytes 786440 | tf_op jit(solution)/shard_map/ppermute | solution.py:223
  3.5 17.1 %collective-permute-start.7 = (bf16[2,256,256]{2,1,0:T(8,128)(2,1)S(1)}, bf16[2,256,256]{2,1,0:T(8,128)(2,1)S(1)}, u32[]{:S(2)}, u32[]{:S(2)}) collective-permute-start(bf16[2,256,256]{2,1,0:T(8,128)(2,1)S(1)} %bitcast_convert_fusion.refs_0_), channel_id=1, source_target_pairs={{2,0},{3,1},{0,2},{1,3},{6,4},{7,5},{4,6},{5,7},{10,8},{11,9},{8,1... | collective-permute-start | bytes 786440 | tf_op jit(solution)/shard_map/ppermute | solution.py:223
  4.8 9.9 %collective-permute-start.2 = (bf16[2,256,256]{2,1,0:T(8,128)(2,1)S(1)}, bf16[2,256,256]{2,1,0:T(8,128)(2,1)S(1)}, u32[]{:S(2)}, u32[]{:S(2)}) collective-permute-start(bf16[2,256,256]{2,1,0:T(8,128)(2,1)S(1)} %bitcast_convert_fusion.refs_0_), channel_id=1, source_target_pairs={{24,0},{16,8},{8,16},{0,24},{25,1},{17,9},{9,17},{1,25},{26,2},{18... | collective-permute-start | bytes 786440 | tf_op jit(solution)/shard_map/ppermute | solution.py:214
  5.0 13.1 %collective-permute-start.1 = (bf16[2,256,256]{2,1,0:T(8,128)(2,1)S(1)}, bf16[2,256,256]{2,1,0:T(8,128)(2,1)S(1)}, u32[]{:S(2)}, u32[]{:S(2)}) collective-permute-start(bf16[2,256,256]{2,1,0:T(8,128)(2,1)S(1)} %bitcast_convert_fusion.refs_0_), channel_id=1, source_target_pairs={{16,0},{24,8},{0,16},{8,24},{17,1},{25,9},{1,17},{9,25},{18,2},{26... | collective-permute-start | bytes 786440 | tf_op jit(solution)/shard_map/ppermute | solution.py:214
  6.2 11.8 %collective-permute-start = (bf16[2,256,256]{2,1,0:T(8,128)(2,1)S(1)}, bf16[2,256,256]{2,1,0:T(8,128)(2,1)S(1)}, u32[]{:S(2)}, u32[]{:S(2)}) collective-permute-start(bf16[2,256,256]{2,1,0:T(8,128)(2,1)S(1)} %bitcast_convert_fusion.refs_0_), channel_id=1, source_target_pairs={{8,0},{0,8},{24,16},{16,24},{9,1},{1,9},{25,17},{17,25},{10,2},{2,... | collective-permute-start | bytes 786440 | tf_op jit(solution)/shard_map/ppermute | solution.py:214
  18.8 21.7 %copy-start.2 = (f32[2,1,256,256]{3,2,1,0:T(8,128)S(1)}, f32[2,1,256,256]{3,2,1,0:T(8,128)}, u32[]{:S(2)}) copy-start(f32[2,1,256,256]{3,2,1,0:T(8,128)} %param.8) | copy-start | bytes 1572868
  18.8 8.3 %collective-permute-start.10 = (bf16[2,256,256]{2,1,0:T(8,128)(2,1)S(1)}, bf16[2,256,256]{2,1,0:T(8,128)(2,1)S(1)}, u32[]{:S(2)}, u32[]{:S(2)}) collective-permute-start(bf16[2,256,256]{2,1,0:T(8,128)(2,1)S(1)} %get-tuple-element.19.refs_2_.refs_0_), channel_id=1, source_target_pairs={{8,0},{0,8},{24,16},{16,24},{9,1},{1,9},{25,17},{17,25},{10,2},{2,... | collective-permute-start | bytes 786440 | tf_op jit(solution)/shard_map/ppermute | solution.py:214
  20.6 10.7 %collective-permute-start.9 = (bf16[2,256,256]{2,1,0:T(8,128)(2,1)S(1)}, bf16[2,256,256]{2,1,0:T(8,128)(2,1)S(1)}, u32[]{:S(2)}, u32[]{:S(2)}) collective-permute-start(bf16[2,256,256]{2,1,0:T(8,128)(2,1)S(1)} %shard_map.87.refs_2_), channel_id=1, source_target_pairs={{2,0},{3,1},{0,2},{1,3},{6,4},{7,5},{4,6},{5,7},{10,8},{11,9},{8,1... | collective-permute-start | bytes 786440 | tf_op jit(solution)/shard_map/ppermute | solution.py:223
  20.8 10.5 %collective-permute-start.12 = (bf16[2,256,256]{2,1,0:T(8,128)(2,1)S(1)}, bf16[2,256,256]{2,1,0:T(8,128)(2,1)S(1)}, u32[]{:S(2)}, u32[]{:S(2)}) collective-permute-start(bf16[2,256,256]{2,1,0:T(8,128)(2,1)S(1)} %get-tuple-element.19.refs_2_.refs_0_), channel_id=1, source_target_pairs={{16,0},{24,8},{0,16},{8,24},{17,1},{25,9},{1,17},{9,25},{18,2},{26... | collective-permute-start | bytes 786440 | tf_op jit(solution)/shard_map/ppermute | solution.py:214
  21.0 9.2 %collective-permute-start.3 = (bf16[256,256]{1,0:T(8,128)(2,1)S(1)}, bf16[256,256]{1,0:T(8,128)(2,1)S(1)}, u32[]{:S(2)}, u32[]{:S(2)}) collective-permute-start(bf16[256,256]{1,0:T(8,128)(2,1)S(1)} %get-tuple-element.17), channel_id=1, source_target_pairs={{0,0},{1,1},{2,2},{3,3},{4,16},{5,17},{6,18},{7,19},{8,8},{9,9},{1... | collective-permute-start | bytes 393224 | tf_op jit(solution)/shard_map/ppermute | solution.py:231
  23.9 7.3 %collective-permute-start.5 = (bf16[256,256]{1,0:T(8,128)(2,1)S(1)}, bf16[256,256]{1,0:T(8,128)(2,1)S(1)}, u32[]{:S(2)}, u32[]{:S(2)}) collective-permute-start(bf16[256,256]{1,0:T(8,128)(2,1)S(1)} %get-tuple-element.18), channel_id=1, source_target_pairs={{0,0},{1,1},{2,8},{3,9},{4,4},{5,5},{6,12},{7,13},{8,2},{9,3},{10,... | collective-permute-start | bytes 393224 | tf_op jit(solution)/shard_map/ppermute | solution.py:231
  27.1 6.3 %collective-permute-start.11 = (bf16[1,256,256]{2,1,0:T(8,128)(2,1)S(1)}, bf16[1,256,256]{2,1,0:T(8,128)(2,1)S(1)}, u32[]{:S(2)}, u32[]{:S(2)}) collective-permute-start(bf16[1,256,256]{2,1,0:T(8,128)(2,1)S(1)} %slice.16), channel_id=1, source_target_pairs={{16,0},{24,8},{0,16},{8,24},{17,1},{25,9},{1,17},{9,25},{18,2},{26... | collective-permute-start | bytes 393224 | tf_op jit(solution)/shard_map/ppermute | solution.py:214
  33.5 7.0 %collective-permute-start.13 = (bf16[8,256,256]{2,1,0:T(8,128)(2,1)S(1)}, bf16[8,256,256]{2,1,0:T(8,128)(2,1)S(1)}, u32[]{:S(2)}, u32[]{:S(2)}) collective-permute-start(bf16[8,256,256]{2,1,0:T(8,128)(2,1)S(1)} %shard_map.88.own_ref), channel_id=1, source_target_pairs={{1,0},{0,1},{3,2},{2,3},{5,4},{4,5},{7,6},{6,7},{9,8},{8,9},{11,10... | collective-permute-start | bytes 3145736 | tf_op jit(solution)/shard_map/ppermute | solution.py:220
  35.3 5.2 %collective-permute-start.14 = (bf16[1,256,256]{2,1,0:T(8,128)(2,1)S(1)}, bf16[1,256,256]{2,1,0:T(8,128)(2,1)S(1)}, u32[]{:S(2)}, u32[]{:S(2)}) collective-permute-start(bf16[1,256,256]{2,1,0:T(8,128)(2,1)S(1)} %slice.17), channel_id=1, source_target_pairs={{8,0},{0,8},{24,16},{16,24},{9,1},{1,9},{25,17},{17,25},{10,2},{2,... | collective-permute-start | bytes 393224 | tf_op jit(solution)/shard_map/ppermute | solution.py:214
  35.7 7.6 %collective-permute-start.4 = (bf16[256,256]{1,0:T(8,128)(2,1)S(1)}, bf16[256,256]{1,0:T(8,128)(2,1)S(1)}, u32[]{:S(2)}, u32[]{:S(2)}) collective-permute-start(bf16[256,256]{1,0:T(8,128)(2,1)S(1)} %collective-permute-done.3.refs_6_), channel_id=1, source_target_pairs={{0,0},{1,1},{2,8},{3,9},{4,4},{5,5},{6,12},{7,13},{8,2},{9,3},{10,... | collective-permute-start | bytes 393224 | tf_op jit(solution)/shard_map/ppermute | solution.py:231
  39.7 7.7 %collective-permute-start.6 = (bf16[256,256]{1,0:T(8,128)(2,1)S(1)}, bf16[256,256]{1,0:T(8,128)(2,1)S(1)}, u32[]{:S(2)}, u32[]{:S(2)}) collective-permute-start(bf16[256,256]{1,0:T(8,128)(2,1)S(1)} %collective-permute-done.5.refs_7_), channel_id=1, source_target_pairs={{0,1},{1,0},{2,3},{3,2},{4,17},{5,16},{6,19},{7,18},{8,9},{9,8},{1... | collective-permute-start | bytes 393224 | tf_op jit(solution)/shard_map/ppermute | solution.py:231
  47.6 8.5 %collective-permute-start.17 = (bf16[2,256,256]{2,1,0:T(8,128)(2,1)S(1)}, bf16[2,256,256]{2,1,0:T(8,128)(2,1)S(1)}, u32[]{:S(2)}, u32[]{:S(2)}) collective-permute-start(bf16[2,256,256]{2,1,0:T(8,128)(2,1)S(1)} %get-tuple-element.22.refs_0_), channel_id=1, source_target_pairs={{24,0},{16,8},{8,16},{0,24},{25,1},{17,9},{9,17},{1,25},{26,2},{18... | collective-permute-start | bytes 786440 | tf_op jit(solution)/shard_map/ppermute | solution.py:214
  47.7 13.2 %collective-permute-start.16 = (bf16[2,256,256]{2,1,0:T(8,128)(2,1)S(1)}, bf16[2,256,256]{2,1,0:T(8,128)(2,1)S(1)}, u32[]{:S(2)}, u32[]{:S(2)}) collective-permute-start(bf16[2,256,256]{2,1,0:T(8,128)(2,1)S(1)} %get-tuple-element.22.refs_0_), channel_id=1, source_target_pairs={{16,0},{24,8},{0,16},{8,24},{17,1},{25,9},{1,17},{9,25},{18,2},{26... | collective-permute-start | bytes 786440 | tf_op jit(solution)/shard_map/ppermute | solution.py:214
  47.7 13.1 %collective-permute-start.15 = (bf16[2,256,256]{2,1,0:T(8,128)(2,1)S(1)}, bf16[2,256,256]{2,1,0:T(8,128)(2,1)S(1)}, u32[]{:S(2)}, u32[]{:S(2)}) collective-permute-start(bf16[2,256,256]{2,1,0:T(8,128)(2,1)S(1)} %get-tuple-element.22.refs_0_), channel_id=1, source_target_pairs={{8,0},{0,8},{24,16},{16,24},{9,1},{1,9},{25,17},{17,25},{10,2},{2,... | collective-permute-start | bytes 786440 | tf_op jit(solution)/shard_map/ppermute | solution.py:214
  50.3 14.3 %collective-permute-start.23 = (bf16[2,256,256]{2,1,0:T(8,128)(2,1)S(1)}, bf16[2,256,256]{2,1,0:T(8,128)(2,1)S(1)}, u32[]{:S(2)}, u32[]{:S(2)}) collective-permute-start(bf16[2,256,256]{2,1,0:T(8,128)(2,1)S(1)} %get-tuple-element.22.refs_0_), channel_id=1, source_target_pairs={{4,0},{5,1},{6,2},{7,3},{0,4},{1,5},{2,6},{3,7},{12,8},{13,9},{14,... | collective-permute-start | bytes 786440 | tf_op jit(solution)/shard_map/ppermute | solution.py:223
  51.2 13.4 %collective-permute-start.22 = (bf16[2,256,256]{2,1,0:T(8,128)(2,1)S(1)}, bf16[2,256,256]{2,1,0:T(8,128)(2,1)S(1)}, u32[]{:S(2)}, u32[]{:S(2)}) collective-permute-start(bf16[2,256,256]{2,1,0:T(8,128)(2,1)S(1)} %get-tuple-element.22.refs_0_), channel_id=1, source_target_pairs={{2,0},{3,1},{0,2},{1,3},{6,4},{7,5},{4,6},{5,7},{10,8},{11,9},{8,1... | collective-permute-start | bytes 786440 | tf_op jit(solution)/shard_map/ppermute | solution.py:223
  61.6 10.7 %collective-permute-start.25 = (bf16[2,256,256]{2,1,0:T(8,128)(2,1)S(1)}, bf16[2,256,256]{2,1,0:T(8,128)(2,1)S(1)}, u32[]{:S(2)}, u32[]{:S(2)}) collective-permute-start(bf16[2,256,256]{2,1,0:T(8,128)(2,1)S(1)} %get-tuple-element.25.refs_2_.refs_0_), channel_id=1, source_target_pairs={{8,0},{0,8},{24,16},{16,24},{9,1},{1,9},{25,17},{17,25},{10,2},{2,... | collective-permute-start | bytes 786440 | tf_op jit(solution)/shard_map/ppermute | solution.py:214
  64.6 11.3 %collective-permute-start.24 = (bf16[2,256,256]{2,1,0:T(8,128)(2,1)S(1)}, bf16[2,256,256]{2,1,0:T(8,128)(2,1)S(1)}, u32[]{:S(2)}, u32[]{:S(2)}) collective-permute-start(bf16[2,256,256]{2,1,0:T(8,128)(2,1)S(1)} %shard_map.92.refs_2_), channel_id=1, source_target_pairs={{2,0},{3,1},{0,2},{1,3},{6,4},{7,5},{4,6},{5,7},{10,8},{11,9},{8,1... | collective-permute-start | bytes 786440 | tf_op jit(solution)/shard_map/ppermute | solution.py:223
  64.6 11.3 %collective-permute-start.27 = (bf16[2,256,256]{2,1,0:T(8,128)(2,1)S(1)}, bf16[2,256,256]{2,1,0:T(8,128)(2,1)S(1)}, u32[]{:S(2)}, u32[]{:S(2)}) collective-permute-start(bf16[2,256,256]{2,1,0:T(8,128)(2,1)S(1)} %get-tuple-element.25.refs_2_.refs_0_), channel_id=1, source_target_pairs={{16,0},{24,8},{0,16},{8,24},{17,1},{25,9},{1,17},{9,25},{18,2},{26... | collective-permute-start | bytes 786440 | tf_op jit(solution)/shard_map/ppermute | solution.py:214
  65.4 9.3 %collective-permute-start.18 = (bf16[256,256]{1,0:T(8,128)(2,1)S(1)}, bf16[256,256]{1,0:T(8,128)(2,1)S(1)}, u32[]{:S(2)}, u32[]{:S(2)}) collective-permute-start(bf16[256,256]{1,0:T(8,128)(2,1)S(1)} %get-tuple-element.23), channel_id=1, source_target_pairs={{0,0},{1,1},{2,2},{3,3},{4,16},{5,17},{6,18},{7,19},{8,8},{9,9},{1... | collective-permute-start | bytes 393224 | tf_op jit(solution)/shard_map/ppermute | solution.py:231
  69.0 6.9 %collective-permute-start.20 = (bf16[256,256]{1,0:T(8,128)(2,1)S(1)}, bf16[256,256]{1,0:T(8,128)(2,1)S(1)}, u32[]{:S(2)}, u32[]{:S(2)}) collective-permute-start(bf16[256,256]{1,0:T(8,128)(2,1)S(1)} %get-tuple-element.24), channel_id=1, source_target_pairs={{0,0},{1,1},{2,8},{3,9},{4,4},{5,5},{6,12},{7,13},{8,2},{9,3},{10,... | collective-permute-start | bytes 393224 | tf_op jit(solution)/shard_map/ppermute | solution.py:231
  72.3 4.7 %collective-permute-start.26 = (bf16[1,256,256]{2,1,0:T(8,128)(2,1)S(1)}, bf16[1,256,256]{2,1,0:T(8,128)(2,1)S(1)}, u32[]{:S(2)}, u32[]{:S(2)}) collective-permute-start(bf16[1,256,256]{2,1,0:T(8,128)(2,1)S(1)} %slice.18), channel_id=1, source_target_pairs={{16,0},{24,8},{0,16},{8,24},{17,1},{25,9},{1,17},{9,25},{18,2},{26... | collective-permute-start | bytes 393224 | tf_op jit(solution)/shard_map/ppermute | solution.py:214
  77.1 8.0 %collective-permute-start.28 = (bf16[8,256,256]{2,1,0:T(8,128)(2,1)S(1)}, bf16[8,256,256]{2,1,0:T(8,128)(2,1)S(1)}, u32[]{:S(2)}, u32[]{:S(2)}) collective-permute-start(bf16[8,256,256]{2,1,0:T(8,128)(2,1)S(1)} %shard_map.93.own_ref), channel_id=1, source_target_pairs={{1,0},{0,1},{3,2},{2,3},{5,4},{4,5},{7,6},{6,7},{9,8},{8,9},{11,10... | collective-permute-start | bytes 3145736 | tf_op jit(solution)/shard_map/ppermute | solution.py:220
  79.4 5.7 %collective-permute-start.29 = (bf16[1,256,256]{2,1,0:T(8,128)(2,1)S(1)}, bf16[1,256,256]{2,1,0:T(8,128)(2,1)S(1)}, u32[]{:S(2)}, u32[]{:S(2)}) collective-permute-start(bf16[1,256,256]{2,1,0:T(8,128)(2,1)S(1)} %slice.19), channel_id=1, source_target_pairs={{8,0},{0,8},{24,16},{16,24},{9,1},{1,9},{25,17},{17,25},{10,2},{2,... | collective-permute-start | bytes 393224 | tf_op jit(solution)/shard_map/ppermute | solution.py:214
  79.5 7.9 %collective-permute-start.19 = (bf16[256,256]{1,0:T(8,128)(2,1)S(1)}, bf16[256,256]{1,0:T(8,128)(2,1)S(1)}, u32[]{:S(2)}, u32[]{:S(2)}) collective-permute-start(bf16[256,256]{1,0:T(8,128)(2,1)S(1)} %collective-permute-done.18.refs_6_), channel_id=1, source_target_pairs={{0,0},{1,1},{2,8},{3,9},{4,4},{5,5},{6,12},{7,13},{8,2},{9,3},{10,... | collective-permute-start | bytes 393224 | tf_op jit(solution)/shard_map/ppermute | solution.py:231
  83.7 8.6 %collective-permute-start.21 = (bf16[256,256]{1,0:T(8,128)(2,1)S(1)}, bf16[256,256]{1,0:T(8,128)(2,1)S(1)}, u32[]{:S(2)}, u32[]{:S(2)}) collective-permute-start(bf16[256,256]{1,0:T(8,128)(2,1)S(1)} %collective-permute-done.20.refs_7_), channel_id=1, source_target_pairs={{0,1},{1,0},{2,3},{3,2},{4,17},{5,16},{6,19},{7,18},{8,9},{9,8},{1... | collective-permute-start | bytes 393224 | tf_op jit(solution)/shard_map/ppermute | solution.py:231
  (3 other events, 2.9 us)

commit v9 on v4

--- a/solution.py
+++ b/solution.py
@@ -268,13 +268,13 @@
             piece = from_row(coupled, step)
             far += [from_row(piece[0:1], 1), from_row(near[1:2], step)]
             c_pieces += [piece, *far[-2:]]
-        same, other = crossing(same, high_parts), crossing(other, last_bits)
+        same, other = crossing(same, last_bits), crossing(other, high_parts)
         for step in range(2, halves, 2):
             column[step] = tied(column[step], column[1], coupled)
             column[step + 1] = from_chip(column[step], 1)
         column = [column[step] for step in range(halves)]
         own = whole_column(column, [*far, same, other])
-        same, other = crossing(same, last_bits), crossing(other, high_parts, 1)
+        same, other = crossing(same, high_parts), crossing(other, last_bits, 1)
         part = first_update(rows, meta, own, swapped(own), c_pieces, state, coulomb_own, inverse)
         state, *halves_out = second_update(same, other, part, inverse, sweep_index < ITERS - 1)
         half = halves_out[0] if halves_out else None

time: 92.6 us -> 93 us (level)
  waiting for transfers between devices: 32.5 us -> 34.2 us
  starting transfers between devices: 44.8 us -> 43.7 us
    ppermute x8, waiting for transfers between devices: 13.7 us -> 21.3 us  [crossing(): return lax.ppermute(x, ('row', 'col'), pairs)]
    ppermute x14, waiting for transfers between devices: 18.6 us -> 12.5 us  [from_row(): return lax.ppermute(x, 'row', [(r ^ step, r) for r in range(rows)])]
    ppermute x2, starting transfers between devices: 6.42 us -> 4.73 us  [swapped(): return lax.ppermute(x, 'col', [(c ^ 1, c) for c in range(cols)])]
    ppermute x14, starting transfers between devices: 9.31 us -> 10.6 us  [from_row(): return lax.ppermute(x, 'row', [(r ^ step, r) for r in range(rows)])]
  transfers between devices with their start and end apart: 30 -> 30, of which waited for: 16 -> 11; matrix products, arithmetic and copies ran while one was open for 4% -> 4% of each run, Pallas kernels for 6% -> 6%
where the time goes in v9:
time: 93 us; the launch traced here: 91.9 us
  starting transfers between devices  43.7 us (47%)
  waiting for transfers between devices  34.2 us (37%)
  Pallas kernels  6.37 us (7%)
  local copies, waits for them, and re-layouts  4.65 us (5%)
  other arithmetic  2.77 us (3%)
    ppermute x8, waiting for transfers between devices, crossing(): return lax.ppermute(x, ('row', 'col'), pairs)  21.3 us
    ppermute x8, starting transfers between devices, crossing(): return lax.ppermute(x, ('row', 'col'), pairs)  21.2 us
    ppermute x14, waiting for transfers between devices, from_row(): return lax.ppermute(x, 'row', [(r ^ step, r) for r in range(rows)])  12.5 us
    ppermute x14, starting transfers between devices, from_row(): return lax.ppermute(x, 'row', [(r ^ step, r) for r in range(rows)])  10.6 us
    ppermute x6, starting transfers between devices, from_chip(): return lax.ppermute(x, 'col', [(c ^ 2 * step, c) for c in range(cols)])  7.23 us
    pallas_call x9, Pallas kernels, call(): pl.pallas_call(body, out_shape=out_shape, in_specs=in_specs, out_specs=VM...  6.37 us
    ppermute x2, starting transfers between devices, swapped(): return lax.ppermute(x, 'col', [(c ^ 1, c) for c in range(cols)])  4.73 us
    unnamed x10, local copies, waits for them, and re-layouts  2.93 us
  transfers between devices with their start and end apart: 30, of which 11 were waited for; matrix products, arithmetic and copies ran while one was open for 4% of the time, Pallas kernels for 6%

profile of v9, /device:TPU:7, one launch (start us, length us, event | category | flops | bytes accessed | tf_op | source)
XLA Modules:
  0.0 91.9 jit_solution(10476352931300570687)
XLA Ops:
  0.0 1.1 %bitcast_convert_fusion.refs_0_ = bf16[2,256,256]{2,1,0:T(8,128)(2,1)S(1)} fusion(f32[2,1,256,256]{3,2,1,0:T(8,128)} %param.8), kind=kLoop, calls=%fused_computation.12 | loop fusion | flops 131072 | bytes 786432 | tf_op jit(solution)/shard_map/convert_element_type | solution.py:240
  1.1 2.4 %collective-permute-start.8 = (bf16[2,256,256]{2,1,0:T(8,128)(2,1)S(1)}, bf16[2,256,256]{2,1,0:T(8,128)(2,1)S(1)}, u32[]{:S(2)}, u32[]{:S(2)}) collective-permute-start(bf16[2,256,256]{2,1,0:T(8,128)(2,1)S(1)} %bitcast_convert_fusion.refs_0_), channel_id=1, source_target_pairs={{4,0},{5,1},{6,2},{7,3},{0,4},{1,5},{2,6},{3,7},{12,8},{13,9},{14,... | collective-permute-start | bytes 786440 | tf_op jit(solution)/shard_map/ppermute | solution.py:223
  3.5 1.3 %collective-permute-start.7 = (bf16[2,256,256]{2,1,0:T(8,128)(2,1)S(1)}, bf16[2,256,256]{2,1,0:T(8,128)(2,1)S(1)}, u32[]{:S(2)}, u32[]{:S(2)}) collective-permute-start(bf16[2,256,256]{2,1,0:T(8,128)(2,1)S(1)} %bitcast_convert_fusion.refs_0_), channel_id=1, source_target_pairs={{2,0},{3,1},{0,2},{1,3},{6,4},{7,5},{4,6},{5,7},{10,8},{11,9},{8,1... | collective-permute-start | bytes 786440 | tf_op jit(solution)/shard_map/ppermute | solution.py:223
  5.0 1.2 %collective-permute-start.1 = (bf16[2,256,256]{2,1,0:T(8,128)(2,1)S(1)}, bf16[2,256,256]{2,1,0:T(8,128)(2,1)S(1)}, u32[]{:S(2)}, u32[]{:S(2)}) collective-permute-start(bf16[2,256,256]{2,1,0:T(8,128)(2,1)S(1)} %bitcast_convert_fusion.refs_0_), channel_id=1, source_target_pairs={{16,0},{24,8},{0,16},{8,24},{17,1},{25,9},{1,17},{9,25},{18,2},{26... | collective-permute-start | bytes 786440 | tf_op jit(solution)/shard_map/ppermute | solution.py:214
  6.2 1.2 %collective-permute-start = (bf16[2,256,256]{2,1,0:T(8,128)(2,1)S(1)}, bf16[2,256,256]{2,1,0:T(8,128)(2,1)S(1)}, u32[]{:S(2)}, u32[]{:S(2)}) collective-permute-start(bf16[2,256,256]{2,1,0:T(8,128)(2,1)S(1)} %bitcast_convert_fusion.refs_0_), channel_id=1, source_target_pairs={{8,0},{0,8},{24,16},{16,24},{9,1},{1,9},{25,17},{17,25},{10,2},{2,... | collective-permute-start | bytes 786440 | tf_op jit(solution)/shard_map/ppermute | solution.py:214
  10.8 1.6 %copy-done.1 = bf16[2,8,256,256]{3,2,1,0:T(8,128)(2,1)S(1)} copy-done((bf16[2,8,256,256]{3,2,1,0:T(8,128)(2,1)S(1)}, bf16[2,8,256,256]{3,2,1,0:T(8,128)(2,1)}, u32[]{:S(2)}) %copy-start.1) | copy-done | bytes 2097176
  13.7 0.9 %shard_map.85 = (bf16[4,512,512]{2,1,0:T(8,128)(2,1)S(1)}, bf16[2,256,256]{2,1,0:T(8,128)(2,1)S(1)}, f32[2,256,256]{2,1,0:T(8,128)S(1)}) custom-call(s32[5,8]{1,0:T(8,128)S(1)} %pad_add_fusion.meta, f32[1,8]{1,0:T(1,128)S(1)} %bitcast.14, bf16[2,8,256,256]{3,2,1,0:T(8,128)(2,1)S(1)} %copy-done.1, f32[1,256]{1,0:T(1,128)S(1)} %bitcast.13, ...), custom_call_target="tpu_custom_call" | custom-call | bytes 4194304 | tf_op jit(solution)/shard_map/pallas_call | solution.py:23
  14.7 3.3 %collective-permute-done.1.refs_2_ = bf16[2,256,256]{2,1,0:T(8,128)(2,1)S(1)} collective-permute-done((bf16[2,256,256]{2,1,0:T(8,128)(2,1)S(1)}, bf16[2,256,256]{2,1,0:T(8,128)(2,1)S(1)}, u32[]{:S(2)}, u32[]{:S(2)}) %collective-permute-start.1) | collective-permute-done | bytes 262176 | tf_op jit(solution)/shard_map/ppermute | solution.py:214
  18.8 1.8 %collective-permute-start.12 = (bf16[2,256,256]{2,1,0:T(8,128)(2,1)S(1)}, bf16[2,256,256]{2,1,0:T(8,128)(2,1)S(1)}, u32[]{:S(2)}, u32[]{:S(2)}) collective-permute-start(bf16[2,256,256]{2,1,0:T(8,128)(2,1)S(1)} %get-tuple-element.19.refs_2_.refs_0_), channel_id=1, source_target_pairs={{8,0},{0,8},{24,16},{16,24},{9,1},{1,9},{25,17},{17,25},{10,2},{2,... | collective-permute-start | bytes 786440 | tf_op jit(solution)/shard_map/ppermute | solution.py:214
  21.0 4.1 %collective-permute-start.3 = (bf16[256,256]{1,0:T(8,128)(2,1)S(1)}, bf16[256,256]{1,0:T(8,128)(2,1)S(1)}, u32[]{:S(2)}, u32[]{:S(2)}) collective-permute-start(bf16[256,256]{1,0:T(8,128)(2,1)S(1)} %get-tuple-element.17), channel_id=1, source_target_pairs={{0,0},{1,1},{2,8},{3,9},{4,4},{5,5},{6,12},{7,13},{8,2},{9,3},{10,... | collective-permute-start | bytes 393224 | tf_op jit(solution)/shard_map/ppermute | solution.py:231
  25.1 1.9 %collective-permute-start.5 = (bf16[256,256]{1,0:T(8,128)(2,1)S(1)}, bf16[256,256]{1,0:T(8,128)(2,1)S(1)}, u32[]{:S(2)}, u32[]{:S(2)}) collective-permute-start(bf16[256,256]{1,0:T(8,128)(2,1)S(1)} %get-tuple-element.18), channel_id=1, source_target_pairs={{0,0},{1,1},{2,2},{3,3},{4,16},{5,17},{6,18},{7,19},{8,8},{9,9},{1... | collective-permute-start | bytes 393224 | tf_op jit(solution)/shard_map/ppermute | solution.py:231
  28.2 2.7 %collective-permute-done.3.refs_6_ = bf16[256,256]{1,0:T(8,128)(2,1)S(1)} collective-permute-done((bf16[256,256]{1,0:T(8,128)(2,1)S(1)}, bf16[256,256]{1,0:T(8,128)(2,1)S(1)}, u32[]{:S(2)}, u32[]{:S(2)}) %collective-permute-start.3) | collective-permute-done | bytes 131104 | tf_op jit(solution)/shard_map/ppermute | solution.py:231
  30.9 3.5 %collective-permute-done.5.refs_7_ = bf16[256,256]{1,0:T(8,128)(2,1)S(1)} collective-permute-done((bf16[256,256]{1,0:T(8,128)(2,1)S(1)}, bf16[256,256]{1,0:T(8,128)(2,1)S(1)}, u32[]{:S(2)}, u32[]{:S(2)}) %collective-permute-start.5) | collective-permute-done | bytes 131104 | tf_op jit(solution)/shard_map/ppermute | solution.py:231
  34.6 2.6 %collective-permute-start.14 = (bf16[8,256,256]{2,1,0:T(8,128)(2,1)S(1)}, bf16[8,256,256]{2,1,0:T(8,128)(2,1)S(1)}, u32[]{:S(2)}, u32[]{:S(2)}) collective-permute-start(bf16[8,256,256]{2,1,0:T(8,128)(2,1)S(1)} %shard_map.88.own_ref), channel_id=1, source_target_pairs={{1,0},{0,1},{3,2},{2,3},{5,4},{4,5},{7,6},{6,7},{9,8},{8,9},{11,10... | collective-permute-start | bytes 3145736 | tf_op jit(solution)/shard_map/ppermute | solution.py:220
  37.2 3.7 %collective-permute-start.4 = (bf16[256,256]{1,0:T(8,128)(2,1)S(1)}, bf16[256,256]{1,0:T(8,128)(2,1)S(1)}, u32[]{:S(2)}, u32[]{:S(2)}) collective-permute-start(bf16[256,256]{1,0:T(8,128)(2,1)S(1)} %collective-permute-done.3.refs_6_), channel_id=1, source_target_pairs={{0,0},{1,1},{2,2},{3,3},{4,16},{5,17},{6,18},{7,19},{8,8},{9,9},{1... | collective-permute-start | bytes 393224 | tf_op jit(solution)/shard_map/ppermute | solution.py:231
  41.4 1.4 %shard_map.89.part_ref = f32[2,256,256]{2,1,0:T(8,128)S(1)} custom-call(s32[5,8]{1,0:T(8,128)S(1)} %pad_add_fusion.meta, bf16[8,256,256]{2,1,0:T(8,128)(2,1)S(1)} %shard_map.88.own_ref, bf16[8,256,256]{2,1,0:T(8,128)(2,1)S(1)} %collective-permute-done.14.other_ref, bf16[2,256,256]{2,1,0:T(8,128)(2,1)S(1)} %get-tuple-element.19.refs_2_.refs_0_, ...), custom_call_target="tpu_custom_call" | custom-call | flops 536870912 | bytes 6291456 | tf_op jit(solution)/shard_map/pallas_call | solution.py:23
  42.8 4.4 %collective-permute-done.4.same_ref = bf16[256,256]{1,0:T(8,128)(2,1)S(1)} collective-permute-done((bf16[256,256]{1,0:T(8,128)(2,1)S(1)}, bf16[256,256]{1,0:T(8,128)(2,1)S(1)}, u32[]{:S(2)}, u32[]{:S(2)}) %collective-permute-start.4) | collective-permute-done | bytes 131104 | tf_op jit(solution)/shard_map/ppermute | solution.py:231
  47.5 1.1 %collective-permute-start.16 = (bf16[2,256,256]{2,1,0:T(8,128)(2,1)S(1)}, bf16[2,256,256]{2,1,0:T(8,128)(2,1)S(1)}, u32[]{:S(2)}, u32[]{:S(2)}) collective-permute-start(bf16[2,256,256]{2,1,0:T(8,128)(2,1)S(1)} %get-tuple-element.22.refs_0_), channel_id=1, source_target_pairs={{16,0},{24,8},{0,16},{8,24},{17,1},{25,9},{1,17},{9,25},{18,2},{26... | collective-permute-start | bytes 786440 | tf_op jit(solution)/shard_map/ppermute | solution.py:214
  48.6 1.5 %collective-permute-start.15 = (bf16[2,256,256]{2,1,0:T(8,128)(2,1)S(1)}, bf16[2,256,256]{2,1,0:T(8,128)(2,1)S(1)}, u32[]{:S(2)}, u32[]{:S(2)}) collective-permute-start(bf16[2,256,256]{2,1,0:T(8,128)(2,1)S(1)} %get-tuple-element.22.refs_0_), channel_id=1, source_target_pairs={{8,0},{0,8},{24,16},{16,24},{9,1},{1,9},{25,17},{17,25},{10,2},{2,... | collective-permute-start | bytes 786440 | tf_op jit(solution)/shard_map/ppermute | solution.py:214
  51.5 4.3 %collective-permute-done.17.refs_3_ = bf16[2,256,256]{2,1,0:T(8,128)(2,1)S(1)} collective-permute-done((bf16[2,256,256]{2,1,0:T(8,128)(2,1)S(1)}, bf16[2,256,256]{2,1,0:T(8,128)(2,1)S(1)}, u32[]{:S(2)}, u32[]{:S(2)}) %collective-permute-start.17) | collective-permute-done | bytes 262176 | tf_op jit(solution)/shard_map/ppermute | solution.py:214
  55.9 4.8 %collective-permute-done.16.refs_2_ = bf16[2,256,256]{2,1,0:T(8,128)(2,1)S(1)} collective-permute-done((bf16[2,256,256]{2,1,0:T(8,128)(2,1)S(1)}, bf16[2,256,256]{2,1,0:T(8,128)(2,1)S(1)}, u32[]{:S(2)}, u32[]{:S(2)}) %collective-permute-start.16) | collective-permute-done | bytes 262176 | tf_op jit(solution)/shard_map/ppermute | solution.py:214
  61.4 1.5 %collective-permute-start.27 = (bf16[2,256,256]{2,1,0:T(8,128)(2,1)S(1)}, bf16[2,256,256]{2,1,0:T(8,128)(2,1)S(1)}, u32[]{:S(2)}, u32[]{:S(2)}) collective-permute-start(bf16[2,256,256]{2,1,0:T(8,128)(2,1)S(1)} %get-tuple-element.25.refs_2_.refs_0_), channel_id=1, source_target_pairs={{8,0},{0,8},{24,16},{16,24},{9,1},{1,9},{25,17},{17,25},{10,2},{2,... | collective-permute-start | bytes 786440 | tf_op jit(solution)/shard_map/ppermute | solution.py:214
  63.7 1.9 %collective-permute-start.24 = (bf16[2,256,256]{2,1,0:T(8,128)(2,1)S(1)}, bf16[2,256,256]{2,1,0:T(8,128)(2,1)S(1)}, u32[]{:S(2)}, u32[]{:S(2)}) collective-permute-start(bf16[2,256,256]{2,1,0:T(8,128)(2,1)S(1)} %shard_map.92.refs_2_), channel_id=1, source_target_pairs={{2,0},{3,1},{0,2},{1,3},{6,4},{7,5},{4,6},{5,7},{10,8},{11,9},{8,1... | collective-permute-start | bytes 786440 | tf_op jit(solution)/shard_map/ppermute | solution.py:223
  65.6 2.2 %collective-permute-start.18 = (bf16[256,256]{1,0:T(8,128)(2,1)S(1)}, bf16[256,256]{1,0:T(8,128)(2,1)S(1)}, u32[]{:S(2)}, u32[]{:S(2)}) collective-permute-start(bf16[256,256]{1,0:T(8,128)(2,1)S(1)} %get-tuple-element.23), channel_id=1, source_target_pairs={{0,0},{1,1},{2,8},{3,9},{4,4},{5,5},{6,12},{7,13},{8,2},{9,3},{10,... | collective-permute-start | bytes 393224 | tf_op jit(solution)/shard_map/ppermute | solution.py:231
  67.8 3.6 %collective-permute-start.20 = (bf16[256,256]{1,0:T(8,128)(2,1)S(1)}, bf16[256,256]{1,0:T(8,128)(2,1)S(1)}, u32[]{:S(2)}, u32[]{:S(2)}) collective-permute-start(bf16[256,256]{1,0:T(8,128)(2,1)S(1)} %get-tuple-element.24), channel_id=1, source_target_pairs={{0,0},{1,1},{2,2},{3,3},{4,16},{5,17},{6,18},{7,19},{8,8},{9,9},{1... | collective-permute-start | bytes 393224 | tf_op jit(solution)/shard_map/ppermute | solution.py:231
  71.7 2.0 %collective-permute-done.18.refs_6_ = bf16[256,256]{1,0:T(8,128)(2,1)S(1)} collective-permute-done((bf16[256,256]{1,0:T(8,128)(2,1)S(1)}, bf16[256,256]{1,0:T(8,128)(2,1)S(1)}, u32[]{:S(2)}, u32[]{:S(2)}) %collective-permute-start.18) | collective-permute-done | bytes 131104 | tf_op jit(solution)/shard_map/ppermute | solution.py:231
  73.7 4.9 %collective-permute-done.20.refs_7_ = bf16[256,256]{1,0:T(8,128)(2,1)S(1)} collective-permute-done((bf16[256,256]{1,0:T(8,128)(2,1)S(1)}, bf16[256,256]{1,0:T(8,128)(2,1)S(1)}, u32[]{:S(2)}, u32[]{:S(2)}) %collective-permute-start.20) | collective-permute-done | bytes 131104 | tf_op jit(solution)/shard_map/ppermute | solution.py:231
  78.7 2.1 %collective-permute-start.29 = (bf16[8,256,256]{2,1,0:T(8,128)(2,1)S(1)}, bf16[8,256,256]{2,1,0:T(8,128)(2,1)S(1)}, u32[]{:S(2)}, u32[]{:S(2)}) collective-permute-start(bf16[8,256,256]{2,1,0:T(8,128)(2,1)S(1)} %shard_map.93.own_ref), channel_id=1, source_target_pairs={{1,0},{0,1},{3,2},{2,3},{5,4},{4,5},{7,6},{6,7},{9,8},{8,9},{11,10... | collective-permute-start | bytes 3145736 | tf_op jit(solution)/shard_map/ppermute | solution.py:220
  80.8 3.1 %collective-permute-start.19 = (bf16[256,256]{1,0:T(8,128)(2,1)S(1)}, bf16[256,256]{1,0:T(8,128)(2,1)S(1)}, u32[]{:S(2)}, u32[]{:S(2)}) collective-permute-start(bf16[256,256]{1,0:T(8,128)(2,1)S(1)} %collective-permute-done.18.refs_6_), channel_id=1, source_target_pairs={{0,0},{1,1},{2,2},{3,3},{4,16},{5,17},{6,18},{7,19},{8,8},{9,9},{1... | collective-permute-start | bytes 393224 | tf_op jit(solution)/shard_map/ppermute | solution.py:231
  84.0 2.0 %collective-permute-start.21 = (bf16[256,256]{1,0:T(8,128)(2,1)S(1)}, bf16[256,256]{1,0:T(8,128)(2,1)S(1)}, u32[]{:S(2)}, u32[]{:S(2)}) collective-permute-start(bf16[256,256]{1,0:T(8,128)(2,1)S(1)} %collective-permute-done.20.refs_7_), channel_id=1, source_target_pairs={{0,1},{1,0},{2,9},{3,8},{4,5},{5,4},{6,13},{7,12},{8,3},{9,2},{10,... | collective-permute-start | bytes 393224 | tf_op jit(solution)/shard_map/ppermute | solution.py:231
  85.9 1.3 %shard_map.94.part_ref = f32[2,256,256]{2,1,0:T(8,128)S(1)} custom-call(s32[5,8]{1,0:T(8,128)S(1)} %pad_add_fusion.meta, bf16[8,256,256]{2,1,0:T(8,128)(2,1)S(1)} %shard_map.93.own_ref, bf16[8,256,256]{2,1,0:T(8,128)(2,1)S(1)} %collective-permute-done.29.other_ref, bf16[2,256,256]{2,1,0:T(8,128)(2,1)S(1)} %get-tuple-element.25.refs_2_.refs_0_, ...), custom_call_target="tpu_custom_call" | custom-call | flops 536870912 | bytes 6291456 | tf_op jit(solution)/shard_map/pallas_call | solution.py:23
  87.3 3.7 %collective-permute-done.19.same_ref = bf16[256,256]{1,0:T(8,128)(2,1)S(1)} collective-permute-done((bf16[256,256]{1,0:T(8,128)(2,1)S(1)}, bf16[256,256]{1,0:T(8,128)(2,1)S(1)}, u32[]{:S(2)}, u32[]{:S(2)}) %collective-permute-start.19) | collective-permute-done | bytes 131104 | tf_op jit(solution)/shard_map/ppermute | solution.py:231
  (65 shorter events, 12.3 us)
Async XLA Ops:
  0.0 9.1 %copy-start = (s32[2,8,8]{2,1,0:T(8,128)S(1)}, s32[2,8,8]{2,1,0:T(8,128)}, u32[]{:S(2)}) copy-start(s32[2,8,8]{2,1,0:T(8,128)} %param.12) | copy-start | bytes 1540
  1.1 19.7 %collective-permute-start.8 = (bf16[2,256,256]{2,1,0:T(8,128)(2,1)S(1)}, bf16[2,256,256]{2,1,0:T(8,128)(2,1)S(1)}, u32[]{:S(2)}, u32[]{:S(2)}) collective-permute-start(bf16[2,256,256]{2,1,0:T(8,128)(2,1)S(1)} %bitcast_convert_fusion.refs_0_), channel_id=1, source_target_pairs={{4,0},{5,1},{6,2},{7,3},{0,4},{1,5},{2,6},{3,7},{12,8},{13,9},{14,... | collective-permute-start | bytes 786440 | tf_op jit(solution)/shard_map/ppermute | solution.py:223
  3.5 17.3 %collective-permute-start.7 = (bf16[2,256,256]{2,1,0:T(8,128)(2,1)S(1)}, bf16[2,256,256]{2,1,0:T(8,128)(2,1)S(1)}, u32[]{:S(2)}, u32[]{:S(2)}) collective-permute-start(bf16[2,256,256]{2,1,0:T(8,128)(2,1)S(1)} %bitcast_convert_fusion.refs_0_), channel_id=1, source_target_pairs={{2,0},{3,1},{0,2},{1,3},{6,4},{7,5},{4,6},{5,7},{10,8},{11,9},{8,1... | collective-permute-start | bytes 786440 | tf_op jit(solution)/shard_map/ppermute | solution.py:223
  4.8 9.9 %collective-permute-start.2 = (bf16[2,256,256]{2,1,0:T(8,128)(2,1)S(1)}, bf16[2,256,256]{2,1,0:T(8,128)(2,1)S(1)}, u32[]{:S(2)}, u32[]{:S(2)}) collective-permute-start(bf16[2,256,256]{2,1,0:T(8,128)(2,1)S(1)} %bitcast_convert_fusion.refs_0_), channel_id=1, source_target_pairs={{24,0},{16,8},{8,16},{0,24},{25,1},{17,9},{9,17},{1,25},{26,2},{18... | collective-permute-start | bytes 786440 | tf_op jit(solution)/shard_map/ppermute | solution.py:214
  5.0 13.1 %collective-permute-start.1 = (bf16[2,256,256]{2,1,0:T(8,128)(2,1)S(1)}, bf16[2,256,256]{2,1,0:T(8,128)(2,1)S(1)}, u32[]{:S(2)}, u32[]{:S(2)}) collective-permute-start(bf16[2,256,256]{2,1,0:T(8,128)(2,1)S(1)} %bitcast_convert_fusion.refs_0_), channel_id=1, source_target_pairs={{16,0},{24,8},{0,16},{8,24},{17,1},{25,9},{1,17},{9,25},{18,2},{26... | collective-permute-start | bytes 786440 | tf_op jit(solution)/shard_map/ppermute | solution.py:214
  6.2 11.8 %collective-permute-start = (bf16[2,256,256]{2,1,0:T(8,128)(2,1)S(1)}, bf16[2,256,256]{2,1,0:T(8,128)(2,1)S(1)}, u32[]{:S(2)}, u32[]{:S(2)}) collective-permute-start(bf16[2,256,256]{2,1,0:T(8,128)(2,1)S(1)} %bitcast_convert_fusion.refs_0_), channel_id=1, source_target_pairs={{8,0},{0,8},{24,16},{16,24},{9,1},{1,9},{25,17},{17,25},{10,2},{2,... | collective-permute-start | bytes 786440 | tf_op jit(solution)/shard_map/ppermute | solution.py:214
  18.8 22.6 %copy-start.2 = (f32[2,1,256,256]{3,2,1,0:T(8,128)S(1)}, f32[2,1,256,256]{3,2,1,0:T(8,128)}, u32[]{:S(2)}) copy-start(f32[2,1,256,256]{3,2,1,0:T(8,128)} %param.8) | copy-start | bytes 1572868
  18.8 8.3 %collective-permute-start.12 = (bf16[2,256,256]{2,1,0:T(8,128)(2,1)S(1)}, bf16[2,256,256]{2,1,0:T(8,128)(2,1)S(1)}, u32[]{:S(2)}, u32[]{:S(2)}) collective-permute-start(bf16[2,256,256]{2,1,0:T(8,128)(2,1)S(1)} %get-tuple-element.19.refs_2_.refs_0_), channel_id=1, source_target_pairs={{8,0},{0,8},{24,16},{16,24},{9,1},{1,9},{25,17},{17,25},{10,2},{2,... | collective-permute-start | bytes 786440 | tf_op jit(solution)/shard_map/ppermute | solution.py:214
  20.6 7.3 %collective-permute-start.10 = (bf16[2,256,256]{2,1,0:T(8,128)(2,1)S(1)}, bf16[2,256,256]{2,1,0:T(8,128)(2,1)S(1)}, u32[]{:S(2)}, u32[]{:S(2)}) collective-permute-start(bf16[2,256,256]{2,1,0:T(8,128)(2,1)S(1)} %get-tuple-element.19.refs_2_.refs_0_), channel_id=1, source_target_pairs={{16,0},{24,8},{0,16},{8,24},{17,1},{25,9},{1,17},{9,25},{18,2},{26... | collective-permute-start | bytes 786440 | tf_op jit(solution)/shard_map/ppermute | solution.py:214
  20.8 13.7 %collective-permute-start.9 = (bf16[2,256,256]{2,1,0:T(8,128)(2,1)S(1)}, bf16[2,256,256]{2,1,0:T(8,128)(2,1)S(1)}, u32[]{:S(2)}, u32[]{:S(2)}) collective-permute-start(bf16[2,256,256]{2,1,0:T(8,128)(2,1)S(1)} %shard_map.87.refs_2_), channel_id=1, source_target_pairs={{2,0},{3,1},{0,2},{1,3},{6,4},{7,5},{4,6},{5,7},{10,8},{11,9},{8,1... | collective-permute-start | bytes 786440 | tf_op jit(solution)/shard_map/ppermute | solution.py:223
  21.0 9.9 %collective-permute-start.3 = (bf16[256,256]{1,0:T(8,128)(2,1)S(1)}, bf16[256,256]{1,0:T(8,128)(2,1)S(1)}, u32[]{:S(2)}, u32[]{:S(2)}) collective-permute-start(bf16[256,256]{1,0:T(8,128)(2,1)S(1)} %get-tuple-element.17), channel_id=1, source_target_pairs={{0,0},{1,1},{2,8},{3,9},{4,4},{5,5},{6,12},{7,13},{8,2},{9,3},{10,... | collective-permute-start | bytes 393224 | tf_op jit(solution)/shard_map/ppermute | solution.py:231
  25.1 9.4 %collective-permute-start.5 = (bf16[256,256]{1,0:T(8,128)(2,1)S(1)}, bf16[256,256]{1,0:T(8,128)(2,1)S(1)}, u32[]{:S(2)}, u32[]{:S(2)}) collective-permute-start(bf16[256,256]{1,0:T(8,128)(2,1)S(1)} %get-tuple-element.18), channel_id=1, source_target_pairs={{0,0},{1,1},{2,2},{3,3},{4,16},{5,17},{6,18},{7,19},{8,8},{9,9},{1... | collective-permute-start | bytes 393224 | tf_op jit(solution)/shard_map/ppermute | solution.py:231
  27.1 7.4 %collective-permute-start.13 = (bf16[1,256,256]{2,1,0:T(8,128)(2,1)S(1)}, bf16[1,256,256]{2,1,0:T(8,128)(2,1)S(1)}, u32[]{:S(2)}, u32[]{:S(2)}) collective-permute-start(bf16[1,256,256]{2,1,0:T(8,128)(2,1)S(1)} %slice.17), channel_id=1, source_target_pairs={{16,0},{24,8},{0,16},{8,24},{17,1},{25,9},{1,17},{9,25},{18,2},{26... | collective-permute-start | bytes 393224 | tf_op jit(solution)/shard_map/ppermute | solution.py:214
  27.9 6.6 %collective-permute-start.11 = (bf16[1,256,256]{2,1,0:T(8,128)(2,1)S(1)}, bf16[1,256,256]{2,1,0:T(8,128)(2,1)S(1)}, u32[]{:S(2)}, u32[]{:S(2)}) collective-permute-start(bf16[1,256,256]{2,1,0:T(8,128)(2,1)S(1)} %slice.16), channel_id=1, source_target_pairs={{8,0},{0,8},{24,16},{16,24},{9,1},{1,9},{25,17},{17,25},{10,2},{2,... | collective-permute-start | bytes 393224 | tf_op jit(solution)/shard_map/ppermute | solution.py:214
  34.6 6.8 %collective-permute-start.14 = (bf16[8,256,256]{2,1,0:T(8,128)(2,1)S(1)}, bf16[8,256,256]{2,1,0:T(8,128)(2,1)S(1)}, u32[]{:S(2)}, u32[]{:S(2)}) collective-permute-start(bf16[8,256,256]{2,1,0:T(8,128)(2,1)S(1)} %shard_map.88.own_ref), channel_id=1, source_target_pairs={{1,0},{0,1},{3,2},{2,3},{5,4},{4,5},{7,6},{6,7},{9,8},{8,9},{11,10... | collective-permute-start | bytes 3145736 | tf_op jit(solution)/shard_map/ppermute | solution.py:220
  37.2 10.0 %collective-permute-start.4 = (bf16[256,256]{1,0:T(8,128)(2,1)S(1)}, bf16[256,256]{1,0:T(8,128)(2,1)S(1)}, u32[]{:S(2)}, u32[]{:S(2)}) collective-permute-start(bf16[256,256]{1,0:T(8,128)(2,1)S(1)} %collective-permute-done.3.refs_6_), channel_id=1, source_target_pairs={{0,0},{1,1},{2,2},{3,3},{4,16},{5,17},{6,18},{7,19},{8,8},{9,9},{1... | collective-permute-start | bytes 393224 | tf_op jit(solution)/shard_map/ppermute | solution.py:231
  40.8 6.4 %collective-permute-start.6 = (bf16[256,256]{1,0:T(8,128)(2,1)S(1)}, bf16[256,256]{1,0:T(8,128)(2,1)S(1)}, u32[]{:S(2)}, u32[]{:S(2)}) collective-permute-start(bf16[256,256]{1,0:T(8,128)(2,1)S(1)} %collective-permute-done.5.refs_7_), channel_id=1, source_target_pairs={{0,1},{1,0},{2,9},{3,8},{4,5},{5,4},{6,13},{7,12},{8,3},{9,2},{10,... | collective-permute-start | bytes 393224 | tf_op jit(solution)/shard_map/ppermute | solution.py:231
  47.4 8.5 %collective-permute-start.17 = (bf16[2,256,256]{2,1,0:T(8,128)(2,1)S(1)}, bf16[2,256,256]{2,1,0:T(8,128)(2,1)S(1)}, u32[]{:S(2)}, u32[]{:S(2)}) collective-permute-start(bf16[2,256,256]{2,1,0:T(8,128)(2,1)S(1)} %get-tuple-element.22.refs_0_), channel_id=1, source_target_pairs={{24,0},{16,8},{8,16},{0,24},{25,1},{17,9},{9,17},{1,25},{26,2},{18... | collective-permute-start | bytes 786440 | tf_op jit(solution)/shard_map/ppermute | solution.py:214
  47.5 13.2 %collective-permute-start.16 = (bf16[2,256,256]{2,1,0:T(8,128)(2,1)S(1)}, bf16[2,256,256]{2,1,0:T(8,128)(2,1)S(1)}, u32[]{:S(2)}, u32[]{:S(2)}) collective-permute-start(bf16[2,256,256]{2,1,0:T(8,128)(2,1)S(1)} %get-tuple-element.22.refs_0_), channel_id=1, source_target_pairs={{16,0},{24,8},{0,16},{8,24},{17,1},{25,9},{1,17},{9,25},{18,2},{26... | collective-permute-start | bytes 786440 | tf_op jit(solution)/shard_map/ppermute | solution.py:214
  48.6 12.1 %collective-permute-start.15 = (bf16[2,256,256]{2,1,0:T(8,128)(2,1)S(1)}, bf16[2,256,256]{2,1,0:T(8,128)(2,1)S(1)}, u32[]{:S(2)}, u32[]{:S(2)}) collective-permute-start(bf16[2,256,256]{2,1,0:T(8,128)(2,1)S(1)} %get-tuple-element.22.refs_0_), channel_id=1, source_target_pairs={{8,0},{0,8},{24,16},{16,24},{9,1},{1,9},{25,17},{17,25},{10,2},{2,... | collective-permute-start | bytes 786440 | tf_op jit(solution)/shard_map/ppermute | solution.py:214
  50.1 13.6 %collective-permute-start.23 = (bf16[2,256,256]{2,1,0:T(8,128)(2,1)S(1)}, bf16[2,256,256]{2,1,0:T(8,128)(2,1)S(1)}, u32[]{:S(2)}, u32[]{:S(2)}) collective-permute-start(bf16[2,256,256]{2,1,0:T(8,128)(2,1)S(1)} %get-tuple-element.22.refs_0_), channel_id=1, source_target_pairs={{4,0},{5,1},{6,2},{7,3},{0,4},{1,5},{2,6},{3,7},{12,8},{13,9},{14,... | collective-permute-start | bytes 786440 | tf_op jit(solution)/shard_map/ppermute | solution.py:223
  50.8 12.9 %collective-permute-start.22 = (bf16[2,256,256]{2,1,0:T(8,128)(2,1)S(1)}, bf16[2,256,256]{2,1,0:T(8,128)(2,1)S(1)}, u32[]{:S(2)}, u32[]{:S(2)}) collective-permute-start(bf16[2,256,256]{2,1,0:T(8,128)(2,1)S(1)} %get-tuple-element.22.refs_0_), channel_id=1, source_target_pairs={{2,0},{3,1},{0,2},{1,3},{6,4},{7,5},{4,6},{5,7},{10,8},{11,9},{8,1... | collective-permute-start | bytes 786440 | tf_op jit(solution)/shard_map/ppermute | solution.py:223
  61.4 10.1 %collective-permute-start.27 = (bf16[2,256,256]{2,1,0:T(8,128)(2,1)S(1)}, bf16[2,256,256]{2,1,0:T(8,128)(2,1)S(1)}, u32[]{:S(2)}, u32[]{:S(2)}) collective-permute-start(bf16[2,256,256]{2,1,0:T(8,128)(2,1)S(1)} %get-tuple-element.25.refs_2_.refs_0_), channel_id=1, source_target_pairs={{8,0},{0,8},{24,16},{16,24},{9,1},{1,9},{25,17},{17,25},{10,2},{2,... | collective-permute-start | bytes 786440 | tf_op jit(solution)/shard_map/ppermute | solution.py:214
  62.9 8.6 %collective-permute-start.25 = (bf16[2,256,256]{2,1,0:T(8,128)(2,1)S(1)}, bf16[2,256,256]{2,1,0:T(8,128)(2,1)S(1)}, u32[]{:S(2)}, u32[]{:S(2)}) collective-permute-start(bf16[2,256,256]{2,1,0:T(8,128)(2,1)S(1)} %get-tuple-element.25.refs_2_.refs_0_), channel_id=1, source_target_pairs={{16,0},{24,8},{0,16},{8,24},{17,1},{25,9},{1,17},{9,25},{18,2},{26... | collective-permute-start | bytes 786440 | tf_op jit(solution)/shard_map/ppermute | solution.py:214
  63.7 14.9 %collective-permute-start.24 = (bf16[2,256,256]{2,1,0:T(8,128)(2,1)S(1)}, bf16[2,256,256]{2,1,0:T(8,128)(2,1)S(1)}, u32[]{:S(2)}, u32[]{:S(2)}) collective-permute-start(bf16[2,256,256]{2,1,0:T(8,128)(2,1)S(1)} %shard_map.92.refs_2_), channel_id=1, source_target_pairs={{2,0},{3,1},{0,2},{1,3},{6,4},{7,5},{4,6},{5,7},{10,8},{11,9},{8,1... | collective-permute-start | bytes 786440 | tf_op jit(solution)/shard_map/ppermute | solution.py:223
  65.6 8.0 %collective-permute-start.18 = (bf16[256,256]{1,0:T(8,128)(2,1)S(1)}, bf16[256,256]{1,0:T(8,128)(2,1)S(1)}, u32[]{:S(2)}, u32[]{:S(2)}) collective-permute-start(bf16[256,256]{1,0:T(8,128)(2,1)S(1)} %get-tuple-element.23), channel_id=1, source_target_pairs={{0,0},{1,1},{2,8},{3,9},{4,4},{5,5},{6,12},{7,13},{8,2},{9,3},{10,... | collective-permute-start | bytes 393224 | tf_op jit(solution)/shard_map/ppermute | solution.py:231
  67.8 10.8 %collective-permute-start.20 = (bf16[256,256]{1,0:T(8,128)(2,1)S(1)}, bf16[256,256]{1,0:T(8,128)(2,1)S(1)}, u32[]{:S(2)}, u32[]{:S(2)}) collective-permute-start(bf16[256,256]{1,0:T(8,128)(2,1)S(1)} %get-tuple-element.24), channel_id=1, source_target_pairs={{0,0},{1,1},{2,2},{3,3},{4,16},{5,17},{6,18},{7,19},{8,8},{9,9},{1... | collective-permute-start | bytes 393224 | tf_op jit(solution)/shard_map/ppermute | solution.py:231
  71.5 7.1 %collective-permute-start.28 = (bf16[1,256,256]{2,1,0:T(8,128)(2,1)S(1)}, bf16[1,256,256]{2,1,0:T(8,128)(2,1)S(1)}, u32[]{:S(2)}, u32[]{:S(2)}) collective-permute-start(bf16[1,256,256]{2,1,0:T(8,128)(2,1)S(1)} %slice.19), channel_id=1, source_target_pairs={{16,0},{24,8},{0,16},{8,24},{17,1},{25,9},{1,17},{9,25},{18,2},{26... | collective-permute-start | bytes 393224 | tf_op jit(solution)/shard_map/ppermute | solution.py:214
  71.6 7.0 %collective-permute-start.26 = (bf16[1,256,256]{2,1,0:T(8,128)(2,1)S(1)}, bf16[1,256,256]{2,1,0:T(8,128)(2,1)S(1)}, u32[]{:S(2)}, u32[]{:S(2)}) collective-permute-start(bf16[1,256,256]{2,1,0:T(8,128)(2,1)S(1)} %slice.18), channel_id=1, source_target_pairs={{8,0},{0,8},{24,16},{16,24},{9,1},{1,9},{25,17},{17,25},{10,2},{2,... | collective-permute-start | bytes 393224 | tf_op jit(solution)/shard_map/ppermute | solution.py:214
  78.7 7.2 %collective-permute-start.29 = (bf16[8,256,256]{2,1,0:T(8,128)(2,1)S(1)}, bf16[8,256,256]{2,1,0:T(8,128)(2,1)S(1)}, u32[]{:S(2)}, u32[]{:S(2)}) collective-permute-start(bf16[8,256,256]{2,1,0:T(8,128)(2,1)S(1)} %shard_map.93.own_ref), channel_id=1, source_target_pairs={{1,0},{0,1},{3,2},{2,3},{5,4},{4,5},{7,6},{6,7},{9,8},{8,9},{11,10... | collective-permute-start | bytes 3145736 | tf_op jit(solution)/shard_map/ppermute | solution.py:220
  80.8 10.1 %collective-permute-start.19 = (bf16[256,256]{1,0:T(8,128)(2,1)S(1)}, bf16[256,256]{1,0:T(8,128)(2,1)S(1)}, u32[]{:S(2)}, u32[]{:S(2)}) collective-permute-start(bf16[256,256]{1,0:T(8,128)(2,1)S(1)} %collective-permute-done.18.refs_6_), channel_id=1, source_target_pairs={{0,0},{1,1},{2,2},{3,3},{4,16},{5,17},{6,18},{7,19},{8,8},{9,9},{1... | collective-permute-start | bytes 393224 | tf_op jit(solution)/shard_map/ppermute | solution.py:231
  84.0 7.0 %collective-permute-start.21 = (bf16[256,256]{1,0:T(8,128)(2,1)S(1)}, bf16[256,256]{1,0:T(8,128)(2,1)S(1)}, u32[]{:S(2)}, u32[]{:S(2)}) collective-permute-start(bf16[256,256]{1,0:T(8,128)(2,1)S(1)} %collective-permute-done.20.refs_7_), channel_id=1, source_target_pairs={{0,1},{1,0},{2,9},{3,8},{4,5},{5,4},{6,13},{7,12},{8,3},{9,2},{10,... | collective-permute-start | bytes 393224 | tf_op jit(solution)/shard_map/ppermute | solution.py:231
  (3 other events, 2.9 us)
